TPU v7x, 32 devices: a whole 2x2x4 slice. The times are simulated.
32 devices in a mesh: seq: 4 (over y, core), fsdp: 8 (over z, x).
Axes of the slice: x: 2, y: 2, z: 4, core: 2. Of those that a mesh axis runs over, the one named last changes fastest.
Arguments:
- hidden_in: bfloat16 [8, 1024, 1024], P('fsdp', 'seq'), may hold values from -6 to 6
- memory: bfloat16 [8, 1024, 1024], P('fsdp', 'seq'), may hold values from -6 to 6
- lengths: int32 [8], P('fsdp'), may hold values from 256 to 1024, as said below
- out_grad: bfloat16 [8, 1024, 1024], P('fsdp', 'seq'), may hold values from -6 to 6
- self_in_weight: bfloat16 [1024, 3072], P('fsdp'), may hold values from -0.21875 to 0.21875
- self_query_bias: bfloat16 [1024], P('fsdp'), may hold values from -3 to 3
- self_value_bias: bfloat16 [1024], P('fsdp'), may hold values from -0.29882812 to 0.29882812
- self_out_weight: bfloat16 [1024, 1024], P('fsdp'), may hold values from -3 to 3
- self_out_bias: bfloat16 [1024], P('fsdp'), may hold values from -3 to 3
- cross_query_weight: bfloat16 [1024, 1024], P('fsdp'), may hold values from -0.21875 to 0.21875
- cross_query_bias: bfloat16 [1024], P('fsdp'), may hold values from -3 to 3
- memory_weight: bfloat16 [1024, 2048], P('fsdp'), may hold values from -0.21875 to 0.21875
- memory_value_bias: bfloat16 [1024], P('fsdp'), may hold values from -0.29882812 to 0.29882812
- cross_out_weight: bfloat16 [1024, 1024], P('fsdp'), may hold values from -3 to 3
- cross_out_bias: bfloat16 [1024], P('fsdp'), may hold values from -3 to 3
- ffn_in_weight: bfloat16 [1024, 4096], P('fsdp'), may hold values from -0.1875 to 0.1875
- ffn_in_bias: bfloat16 [4096], P('fsdp'), may hold values from -3 to 3
- ffn_out_weight: bfloat16 [4096, 1024], P('fsdp'), may hold values from -0.5 to 0.5
- ffn_out_bias: bfloat16 [1024], P('fsdp'), may hold values from -3 to 3
- norm_gain: bfloat16 [3, 1024], P(None, 'fsdp'), may hold values from 0.25 to 1.75
- norm_bias: bfloat16 [3, 1024], P(None, 'fsdp'), may hold values from -2 to 2
Outputs:
- layer_out: bfloat16 [8, 1024, 1024], P('fsdp', 'seq')
- input_grad: bfloat16 [8, 1024, 1024], P('fsdp', 'seq')
- memory_grad: bfloat16 [8, 1024, 1024], P('fsdp', 'seq')
- grad_self_in: float32 [1024, 3072], P('fsdp')
- grad_self_query_bias: float32 [1024], P('fsdp')
- grad_self_value_bias: float32 [1024], P('fsdp')
- grad_self_out: float32 [1024, 1024], P('fsdp')
- grad_self_out_bias: float32 [1024], P('fsdp')
- grad_cross_query: float32 [1024, 1024], P('fsdp')
- grad_cross_query_bias: float32 [1024], P('fsdp')
- grad_memory_weight: float32 [1024, 2048], P('fsdp')
- grad_memory_value_bias: float32 [1024], P('fsdp')
- grad_cross_out: float32 [1024, 1024], P('fsdp')
- grad_cross_out_bias: float32 [1024], P('fsdp')
- grad_ffn_in: float32 [1024, 4096], P('fsdp')
- grad_ffn_in_bias: float32 [4096], P('fsdp')
- grad_ffn_out: float32 [4096, 1024], P('fsdp')
- grad_ffn_out_bias: float32 [1024], P('fsdp')
- grad_norm_gain: float32 [3, 1024], P(None, 'fsdp')
- grad_norm_bias: float32 [3, 1024], P(None, 'fsdp')
Inputs may be any that keep to these rules, and one draw needn't show every extreme that they name: `lengths`: keys at positions at or beyond a sequence's length are masked; some sequence is full.
All inputs are finite; a program needn't handle non-finite values.
Results may differ from a plain program's by a relative error of at most 0.03.
Values may be sent and summed in bfloat16 or wider, within the bound.
No kernel may reach another device: no remote copies, remote signals or barrier semaphores. Data moves between devices by JAX's collectives and lax.ppermute only.
A program may use at most 192 MiB of HBM per device.

v0:
```python
import jax
import jax.numpy as jnp
from jax import lax
from jax.sharding import PartitionSpec as P

HD = 64
BLK = 256


alpha_scale = 300.0**0.25
layer_eps = 1e-05
score_scale = 0.125
masked_value = -1e30
gelu_coef = 0.7978845608028654
gelu_cube = 0.044715


def gelu_both(values):
    inner = gelu_coef * (values + gelu_cube * values * values * values)
    tangent = jnp.tanh(inner)
    output = 0.5 * values * (1.0 + tangent)
    slope = 0.5 * (1.0 + tangent) + 0.5 * values * (1.0 - tangent * tangent) * gelu_coef * (
        1.0 + 3.0 * gelu_cube * values * values
    )
    return (output, slope)


def layer_norm(values, gain_row, shift_row):
    center = values - jnp.mean(values, axis=-1, keepdims=True)
    inverse = lax.rsqrt(jnp.mean(center * center, axis=-1, keepdims=True) + layer_eps)
    normed = center * inverse
    return (normed * gain_row + shift_row, normed, inverse)


def norm_back(grad_rows, normed, inverse, gain_row):
    scaled = grad_rows * gain_row
    inner_term = scaled - jnp.mean(scaled, axis=-1, keepdims=True)
    inner_term = inner_term - normed * jnp.mean(scaled * normed, axis=-1, keepdims=True)
    return (
        inverse * inner_term,
        jnp.sum(grad_rows * normed, axis=(0, 1)),
        jnp.sum(grad_rows, axis=(0, 1)),
    )


def attend_forward(queries, key_rows, value_rows, allowed):
    seq_count, heads_dev, head_dim, total = queries.shape
    qblock = min(512, total)

    def visit(block_index, carried):
        out_buf, lse_buf = carried
        first_row = block_index * qblock
        query_part = lax.dynamic_slice_in_dim(queries, first_row, qblock, 3)
        scores = (
            jnp.einsum("bhdi,bhdj->bhij", query_part, key_rows, preferred_element_type=jnp.float32)
            * score_scale
        )
        if allowed is not None:
            scores = jnp.where(allowed(first_row, qblock), scores, masked_value)
        row_max = jnp.max(scores, axis=-1, keepdims=True)
        weights = jnp.exp(scores - row_max)
        totals = jnp.sum(weights, axis=-1, keepdims=True)
        weights_low = (weights / totals).astype(jnp.bfloat16)
        block_out = jnp.einsum(
            "bhij,bhdj->bhdi", weights_low, value_rows, preferred_element_type=jnp.float32
        ).astype(jnp.bfloat16)
        out_buf = lax.dynamic_update_slice_in_dim(out_buf, block_out, first_row, 3)
        lse_buf = lax.dynamic_update_slice_in_dim(
            lse_buf, (row_max + jnp.log(totals))[..., 0], first_row, 2
        )
        return (out_buf, lse_buf)

    initial = (
        jnp.zeros(queries.shape, jnp.bfloat16),
        jnp.zeros((seq_count, heads_dev, total), jnp.float32),
    )
    return lax.fori_loop(0, total // qblock, visit, initial)


def attend_back(queries, key_rows, value_rows, grad_out, lse_rows, allowed):
    seq_count, heads_dev, head_dim, total = queries.shape
    qblock = min(512, total)

    def visit(block_index, carried):
        query_grad, key_acc, value_acc = carried
        first_row = block_index * qblock
        query_part = lax.dynamic_slice_in_dim(queries, first_row, qblock, 3)
        grad_part = lax.dynamic_slice_in_dim(grad_out, first_row, qblock, 3)
        lse_part = lax.dynamic_slice_in_dim(lse_rows, first_row, qblock, 2)
        scores = (
            jnp.einsum("bhdi,bhdj->bhij", query_part, key_rows, preferred_element_type=jnp.float32)
            * score_scale
        )
        if allowed is not None:
            scores = jnp.where(allowed(first_row, qblock), scores, masked_value)
        weights = jnp.exp(scores - lse_part[..., None])
        weights_low = weights.astype(jnp.bfloat16)
        grad_weights = jnp.einsum(
            "bhdi,bhdj->bhij", grad_part, value_rows, preferred_element_type=jnp.float32
        )
        row_term = jnp.sum(grad_weights * weights, axis=-1, keepdims=True)
        grad_scores = (weights * (grad_weights - row_term)).astype(jnp.bfloat16)
        block_query = (
            jnp.einsum("bhij,bhdj->bhdi", grad_scores, key_rows, preferred_element_type=jnp.float32)
            * score_scale
        ).astype(jnp.bfloat16)
        query_grad = lax.dynamic_update_slice_in_dim(query_grad, block_query, first_row, 3)
        key_acc = (
            key_acc
            + jnp.einsum(
                "bhij,bhdi->bhdj", grad_scores, query_part, preferred_element_type=jnp.float32
            )
            * score_scale
        )
        value_acc = value_acc + jnp.einsum(
            "bhij,bhdi->bhdj", weights_low, grad_part, preferred_element_type=jnp.float32
        )
        return (query_grad, key_acc, value_acc)

    initial = (
        jnp.zeros(queries.shape, jnp.bfloat16),
        jnp.zeros(key_rows.shape, jnp.float32),
        jnp.zeros(value_rows.shape, jnp.float32),
    )
    query_grad, key_acc, value_acc = lax.fori_loop(0, total // qblock, visit, initial)
    return (query_grad, key_acc.astype(jnp.bfloat16), value_acc.astype(jnp.bfloat16))


def column_sum(array, axes):
    return jnp.sum(array.astype(jnp.float32), axis=axes)


def local(
    hidden_in,
    memory,
    lengths,
    out_grad,
    self_in_weight,
    self_query_bias,
    self_value_bias,
    self_out_weight,
    self_out_bias,
    cross_query_weight,
    cross_query_bias,
    memory_weight,
    memory_value_bias,
    cross_out_weight,
    cross_out_bias,
    ffn_in_weight,
    ffn_in_bias,
    ffn_out_weight,
    ffn_out_bias,
    norm_gain,
    norm_bias,
):
    (
        w_qkv,
        b_query,
        b_value,
        w_attn_out,
        b_attn_out,
        w_cross_q,
        b_cross_q,
        w_mem,
        b_mem_value,
        w_cross_out,
        b_cross_out,
        w_ffn_in,
        b_ffn_in,
        w_ffn_out,
        b_ffn_out,
        gain_all,
        shift_all,
    ) = (
        lax.all_gather(self_in_weight, "fsdp", axis=0, tiled=True),
        lax.all_gather(self_query_bias, "fsdp", axis=0, tiled=True),
        lax.all_gather(self_value_bias, "fsdp", axis=0, tiled=True),
        lax.all_gather(self_out_weight, "fsdp", axis=0, tiled=True),
        lax.all_gather(self_out_bias, "fsdp", axis=0, tiled=True),
        lax.all_gather(cross_query_weight, "fsdp", axis=0, tiled=True),
        lax.all_gather(cross_query_bias, "fsdp", axis=0, tiled=True),
        lax.all_gather(memory_weight, "fsdp", axis=0, tiled=True),
        lax.all_gather(memory_value_bias, "fsdp", axis=0, tiled=True),
        lax.all_gather(cross_out_weight, "fsdp", axis=0, tiled=True),
        lax.all_gather(cross_out_bias, "fsdp", axis=0, tiled=True),
        lax.all_gather(ffn_in_weight, "fsdp", axis=0, tiled=True),
        lax.all_gather(ffn_in_bias, "fsdp", axis=0, tiled=True),
        lax.all_gather(ffn_out_weight, "fsdp", axis=0, tiled=True),
        lax.all_gather(ffn_out_bias, "fsdp", axis=0, tiled=True),
        lax.all_gather(norm_gain, "fsdp", axis=1, tiled=True),
        lax.all_gather(norm_bias, "fsdp", axis=1, tiled=True),
    )
    seq_count, tok_count, width = hidden_in.shape
    mem_count = memory.shape[1]
    x_float = hidden_in.astype(jnp.float32)
    zeros_row = jnp.zeros((width,), jnp.float32)
    gains = gain_all.astype(jnp.float32)
    shifts = shift_all.astype(jnp.float32)
    qkv_bias = jnp.concatenate(
        [b_query.astype(jnp.float32), zeros_row, b_value.astype(jnp.float32)]
    )
    qkv_local = (
        (
            jnp.einsum("btd,dc->bct", hidden_in, w_qkv, preferred_element_type=jnp.float32)
            + qkv_bias[None, :, None]
        )
        .astype(jnp.bfloat16)
        .reshape(seq_count, 3, width, tok_count)
    )
    mem_bias = jnp.concatenate([zeros_row, b_mem_value.astype(jnp.float32)])
    mem_local = (
        (
            jnp.einsum("bmd,dc->bcm", memory, w_mem, preferred_element_type=jnp.float32)
            + mem_bias[None, :, None]
        )
        .astype(jnp.bfloat16)
        .reshape(seq_count, 2, width, mem_count)
    )
    qkv_heads, mem_heads = (
        lax.all_to_all(qkv_local, "seq", split_axis=2, concat_axis=3, tiled=True),
        lax.all_to_all(mem_local, "seq", split_axis=2, concat_axis=3, tiled=True),
    )
    head_width = qkv_heads.shape[2]
    heads_dev = head_width // HD
    total = qkv_heads.shape[3]

    def split_heads(array):
        return array.reshape(seq_count, heads_dev, HD, array.shape[-1])

    self_query = split_heads(qkv_heads[:, 0])
    self_key = split_heads(qkv_heads[:, 1])
    self_value = split_heads(qkv_heads[:, 2])
    key_pos = jnp.arange(total)

    def self_allowed(first_row, row_count):
        query_pos = first_row + jnp.arange(row_count)
        causal = key_pos[None, :] // BLK <= query_pos[:, None] // BLK
        live_keys = key_pos[None, :] < lengths[:, None]
        return (causal[None] & live_keys[:, None, :])[:, None]

    self_attn, self_lse = attend_forward(self_query, self_key, self_value, self_allowed)
    attn_tok = lax.all_to_all(
        self_attn.reshape(seq_count, head_width, total),
        "seq",
        split_axis=2,
        concat_axis=1,
        tiled=True,
    )
    branch = jnp.einsum(
        "bdt,de->bte", attn_tok, w_attn_out, preferred_element_type=jnp.float32
    ) + b_attn_out.astype(jnp.float32)
    first, normed_one, inverse_one = layer_norm(alpha_scale * x_float + branch, gains[0], shifts[0])
    first_low = first.astype(jnp.bfloat16)
    cq_local = (
        jnp.einsum("btd,de->bet", first_low, w_cross_q, preferred_element_type=jnp.float32)
        + b_cross_q.astype(jnp.float32)[None, :, None]
    ).astype(jnp.bfloat16)
    cq_heads = lax.all_to_all(
        cq_local.reshape(seq_count, 1, width, tok_count),
        "seq",
        split_axis=2,
        concat_axis=3,
        tiled=True,
    )
    cross_q = split_heads(cq_heads[:, 0])
    mem_key = split_heads(mem_heads[:, 0])
    mem_value = split_heads(mem_heads[:, 1])
    cross_attn, cross_lse = attend_forward(cross_q, mem_key, mem_value, None)
    cross_tok = lax.all_to_all(
        cross_attn.reshape(seq_count, head_width, total),
        "seq",
        split_axis=2,
        concat_axis=1,
        tiled=True,
    )
    cross_branch = jnp.einsum(
        "bdt,de->bte", cross_tok, w_cross_out, preferred_element_type=jnp.float32
    ) + b_cross_out.astype(jnp.float32)
    second, normed_two, inverse_two = layer_norm(
        alpha_scale * first + cross_branch, gains[1], shifts[1]
    )
    second_low = second.astype(jnp.bfloat16)
    pre_act = jnp.einsum(
        "btd,df->btf", second_low, w_ffn_in, preferred_element_type=jnp.float32
    ) + b_ffn_in.astype(jnp.float32)
    act_value, act_slope = gelu_both(pre_act)
    hidden_low = act_value.astype(jnp.bfloat16)
    ffn_branch = jnp.einsum(
        "btf,fd->btd", hidden_low, w_ffn_out, preferred_element_type=jnp.float32
    ) + b_ffn_out.astype(jnp.float32)
    result, normed_three, inverse_three = layer_norm(
        alpha_scale * second + ffn_branch, gains[2], shifts[2]
    )
    layer_out = result.astype(jnp.bfloat16)
    d_three, gain_three, shift_three = norm_back(
        out_grad.astype(jnp.float32), normed_three, inverse_three, gains[2]
    )
    d_ffn = d_three.astype(jnp.bfloat16)
    grad_ffn_out = jnp.einsum("btf,btd->fd", hidden_low, d_ffn, preferred_element_type=jnp.float32)
    grad_ffn_out_bias = column_sum(d_ffn, (0, 1))
    d_hidden = jnp.einsum("btd,fd->btf", d_ffn, w_ffn_out, preferred_element_type=jnp.float32)
    d_pre = (act_slope * d_hidden).astype(jnp.bfloat16)
    grad_ffn_in = jnp.einsum("btd,btf->df", second_low, d_pre, preferred_element_type=jnp.float32)
    grad_ffn_in_bias = column_sum(d_pre, (0, 1))
    d_second = alpha_scale * d_three + jnp.einsum(
        "btf,df->btd", d_pre, w_ffn_in, preferred_element_type=jnp.float32
    )
    d_two, gain_two, shift_two = norm_back(d_second, normed_two, inverse_two, gains[1])
    d_cross = d_two.astype(jnp.bfloat16)
    grad_cross_out = jnp.einsum(
        "bdt,bte->de", cross_tok, d_cross, preferred_element_type=jnp.float32
    )
    grad_cross_out_bias = column_sum(d_cross, (0, 1))
    d_cross_tok = jnp.einsum(
        "bte,de->bdt", d_cross, w_cross_out, preferred_element_type=jnp.float32
    ).astype(jnp.bfloat16)
    d_cross_heads = lax.all_to_all(d_cross_tok, "seq", split_axis=1, concat_axis=2, tiled=True)
    dq_cross, dk_mem, dv_mem = attend_back(
        cross_q, mem_key, mem_value, split_heads(d_cross_heads), cross_lse, None
    )
    dkv_heads = jnp.stack([dk_mem, dv_mem], axis=1).reshape(
        seq_count, 2, head_width, mem_key.shape[3]
    )
    d_cq_tok, d_mem_tok = (
        lax.all_to_all(
            dq_cross.reshape(seq_count, 1, head_width, total),
            "seq",
            split_axis=3,
            concat_axis=2,
            tiled=True,
        ),
        lax.all_to_all(dkv_heads, "seq", split_axis=3, concat_axis=2, tiled=True),
    )
    d_cq_flat = d_cq_tok[:, 0]
    grad_cross_query = jnp.einsum(
        "btd,bet->de", first_low, d_cq_flat, preferred_element_type=jnp.float32
    )
    grad_cross_query_bias = column_sum(d_cq_flat, (0, 2))
    d_mem_flat = d_mem_tok.reshape(seq_count, 2 * width, mem_count)
    grad_memory_weight = jnp.einsum(
        "bmd,bcm->dc", memory, d_mem_flat, preferred_element_type=jnp.float32
    )
    grad_memory_value_bias = column_sum(d_mem_tok[:, 1], (0, 2))
    memory_grad = jnp.einsum(
        "bcm,dc->bmd", d_mem_flat, w_mem, preferred_element_type=jnp.float32
    ).astype(jnp.bfloat16)
    d_first = alpha_scale * d_two + jnp.einsum(
        "bet,de->btd", d_cq_flat, w_cross_q, preferred_element_type=jnp.float32
    )
    d_one, gain_one, shift_one = norm_back(d_first, normed_one, inverse_one, gains[0])
    d_branch = d_one.astype(jnp.bfloat16)
    grad_self_out = jnp.einsum(
        "bdt,bte->de", attn_tok, d_branch, preferred_element_type=jnp.float32
    )
    grad_self_out_bias = column_sum(d_branch, (0, 1))
    d_attn_tok = jnp.einsum(
        "bte,de->bdt", d_branch, w_attn_out, preferred_element_type=jnp.float32
    ).astype(jnp.bfloat16)
    d_attn_heads = lax.all_to_all(d_attn_tok, "seq", split_axis=1, concat_axis=2, tiled=True)
    dq_self, dk_self, dv_self = attend_back(
        self_query, self_key, self_value, split_heads(d_attn_heads), self_lse, self_allowed
    )
    d_qkv_heads = jnp.stack([dq_self, dk_self, dv_self], axis=1).reshape(
        seq_count, 3, head_width, total
    )
    d_qkv_tok = lax.all_to_all(d_qkv_heads, "seq", split_axis=3, concat_axis=2, tiled=True)
    d_qkv_flat = d_qkv_tok.reshape(seq_count, 3 * width, tok_count)
    grad_self_in = jnp.einsum(
        "btd,bct->dc", hidden_in, d_qkv_flat, preferred_element_type=jnp.float32
    )
    grad_self_query_bias = column_sum(d_qkv_tok[:, 0], (0, 2))
    grad_self_value_bias = column_sum(d_qkv_tok[:, 2], (0, 2))
    input_grad = (
        alpha_scale * d_one
        + jnp.einsum("bct,dc->btd", d_qkv_flat, w_qkv, preferred_element_type=jnp.float32)
    ).astype(jnp.bfloat16)
    grad_norm_gain = jnp.stack([gain_one, gain_two, gain_three])
    grad_norm_bias = jnp.stack([shift_one, shift_two, shift_three])
    (
        own_a,
        own_b,
        own_c,
        own_d,
        own_e,
        own_f,
        own_g,
        own_h,
        own_i,
        own_j,
        own_k,
        own_l,
        own_m,
        own_n,
        own_o,
        own_p,
        own_q,
    ) = (
        lax.psum_scatter(
            grad_self_in.astype(jnp.bfloat16), "fsdp", scatter_dimension=0, tiled=True
        ).astype(jnp.float32),
        lax.psum_scatter(
            grad_self_query_bias.astype(jnp.bfloat16), "fsdp", scatter_dimension=0, tiled=True
        ).astype(jnp.float32),
        lax.psum_scatter(
            grad_self_value_bias.astype(jnp.bfloat16), "fsdp", scatter_dimension=0, tiled=True
        ).astype(jnp.float32),
        lax.psum_scatter(
            grad_self_out.astype(jnp.bfloat16), "fsdp", scatter_dimension=0, tiled=True
        ).astype(jnp.float32),
        lax.psum_scatter(
            grad_self_out_bias.astype(jnp.bfloat16), "fsdp", scatter_dimension=0, tiled=True
        ).astype(jnp.float32),
        lax.psum_scatter(
            grad_cross_query.astype(jnp.bfloat16), "fsdp", scatter_dimension=0, tiled=True
        ).astype(jnp.float32),
        lax.psum_scatter(
            grad_cross_query_bias.astype(jnp.bfloat16), "fsdp", scatter_dimension=0, tiled=True
        ).astype(jnp.float32),
        lax.psum_scatter(
            grad_memory_weight.astype(jnp.bfloat16), "fsdp", scatter_dimension=0, tiled=True
        ).astype(jnp.float32),
        lax.psum_scatter(
            grad_memory_value_bias.astype(jnp.bfloat16), "fsdp", scatter_dimension=0, tiled=True
        ).astype(jnp.float32),
        lax.psum_scatter(
            grad_cross_out.astype(jnp.bfloat16), "fsdp", scatter_dimension=0, tiled=True
        ).astype(jnp.float32),
        lax.psum_scatter(
            grad_cross_out_bias.astype(jnp.bfloat16), "fsdp", scatter_dimension=0, tiled=True
        ).astype(jnp.float32),
        lax.psum_scatter(
            grad_ffn_in.astype(jnp.bfloat16), "fsdp", scatter_dimension=0, tiled=True
        ).astype(jnp.float32),
        lax.psum_scatter(
            grad_ffn_in_bias.astype(jnp.bfloat16), "fsdp", scatter_dimension=0, tiled=True
        ).astype(jnp.float32),
        lax.psum_scatter(
            grad_ffn_out.astype(jnp.bfloat16), "fsdp", scatter_dimension=0, tiled=True
        ).astype(jnp.float32),
        lax.psum_scatter(
            grad_ffn_out_bias.astype(jnp.bfloat16), "fsdp", scatter_dimension=0, tiled=True
        ).astype(jnp.float32),
        lax.psum_scatter(
            grad_norm_gain.astype(jnp.bfloat16), "fsdp", scatter_dimension=1, tiled=True
        ).astype(jnp.float32),
        lax.psum_scatter(
            grad_norm_bias.astype(jnp.bfloat16), "fsdp", scatter_dimension=1, tiled=True
        ).astype(jnp.float32),
    )
    summed = (
        lax.psum(own_a.astype(jnp.bfloat16), "seq").astype(jnp.float32),
        lax.psum(own_b.astype(jnp.bfloat16), "seq").astype(jnp.float32),
        lax.psum(own_c.astype(jnp.bfloat16), "seq").astype(jnp.float32),
        lax.psum(own_d.astype(jnp.bfloat16), "seq").astype(jnp.float32),
        lax.psum(own_e.astype(jnp.bfloat16), "seq").astype(jnp.float32),
        lax.psum(own_f.astype(jnp.bfloat16), "seq").astype(jnp.float32),
        lax.psum(own_g.astype(jnp.bfloat16), "seq").astype(jnp.float32),
        lax.psum(own_h.astype(jnp.bfloat16), "seq").astype(jnp.float32),
        lax.psum(own_i.astype(jnp.bfloat16), "seq").astype(jnp.float32),
        lax.psum(own_j.astype(jnp.bfloat16), "seq").astype(jnp.float32),
        lax.psum(own_k.astype(jnp.bfloat16), "seq").astype(jnp.float32),
        lax.psum(own_l.astype(jnp.bfloat16), "seq").astype(jnp.float32),
        lax.psum(own_m.astype(jnp.bfloat16), "seq").astype(jnp.float32),
        lax.psum(own_n.astype(jnp.bfloat16), "seq").astype(jnp.float32),
        lax.psum(own_o.astype(jnp.bfloat16), "seq").astype(jnp.float32),
        lax.psum(own_p.astype(jnp.bfloat16), "seq").astype(jnp.float32),
        lax.psum(own_q.astype(jnp.bfloat16), "seq").astype(jnp.float32),
    )
    return (
        layer_out,
        input_grad,
        memory_grad,
        summed[0],
        summed[1],
        summed[2],
        summed[3],
        summed[4],
        summed[5],
        summed[6],
        summed[7],
        summed[8],
        summed[9],
        summed[10],
        summed[11],
        summed[12],
        summed[13],
        summed[14],
        summed[15],
        summed[16],
    )


def solution(mesh):
    in_specs = (
        P("fsdp", "seq", None),
        P("fsdp", "seq", None),
        P("fsdp"),
        P("fsdp", "seq", None),
        P("fsdp", None),
        P("fsdp"),
        P("fsdp"),
        P("fsdp", None),
        P("fsdp"),
        P("fsdp", None),
        P("fsdp"),
        P("fsdp", None),
        P("fsdp"),
        P("fsdp", None),
        P("fsdp"),
        P("fsdp", None),
        P("fsdp"),
        P("fsdp", None),
        P("fsdp"),
        P(None, "fsdp"),
        P(None, "fsdp"),
    )
    out_specs = (
        P("fsdp", "seq", None),
        P("fsdp", "seq", None),
        P("fsdp", "seq", None),
        P("fsdp", None),
        P("fsdp"),
        P("fsdp"),
        P("fsdp", None),
        P("fsdp"),
        P("fsdp", None),
        P("fsdp"),
        P("fsdp", None),
        P("fsdp"),
        P("fsdp", None),
        P("fsdp"),
        P("fsdp", None),
        P("fsdp"),
        P("fsdp", None),
        P("fsdp"),
        P(None, "fsdp"),
        P(None, "fsdp"),
    )
    return jax.shard_map(local, mesh=mesh, in_specs=in_specs, out_specs=out_specs, check_vma=False)
```

profile of v0, /device:TPU:0, one launch (start us, length us, event | category | flops | bytes accessed | tf_op | source)
XLA Modules:
  0.0 1705.9 jit_solution(1112801386113111253)
XLA Ops:
  11.2 22.4 %all-gather.1 = bf16[8,1,128]{2,1,0:T(2,128)(2,1)S(1)} all-gather(bf16[1,1,128]{2,1,0:T(2,128)(2,1)} %bitcast.485), channel_id=1, replica_groups=mesh['seq'=4,'fsdp'=8] {'fsdp'}, dimensions={0}, use_global_device_ids=true | all-gather | bytes 2304 | tf_op jit(solution)/shard_map/all_gather | solution.py:177
  33.6 16.7 all-gather
  50.3 61.8 %all-gather.16.cloned.1.call-done = bf16[1024,3072]{1,0:T(8,128)(2,1)} async-done(((bf16[128,3072]{1,0:T(8,128)(2,1)}), bf16[1024,3072]{1,0:T(8,128)(2,1)}) %all-gather.16.cloned.1.call-update) | async-done | bytes 6291472 | tf_op jit(solution)/shard_map/all_gather | solution.py:175
  112.0 5.0 fusion.122
  124.2 17.8 %all-gather.2 = bf16[8,1,128]{2,1,0:T(2,128)(2,1)S(1)} all-gather(bf16[1,1,128]{2,1,0:T(2,128)(2,1)S(1)} %bitcast.487), channel_id=1, replica_groups=mesh['seq'=4,'fsdp'=8] {'fsdp'}, dimensions={0}, use_global_device_ids=true | all-gather | bytes 2304 | tf_op jit(solution)/shard_map/all_gather | solution.py:179
  142.0 17.0 all-gather.3
  159.0 17.6 %all-gather.4 = bf16[8,1,128]{2,1,0:T(2,128)(2,1)S(1)} all-gather(bf16[1,1,128]{2,1,0:T(2,128)(2,1)S(1)} %bitcast.489), channel_id=1, replica_groups=mesh['seq'=4,'fsdp'=8] {'fsdp'}, dimensions={0}, use_global_device_ids=true | all-gather | bytes 2304 | tf_op jit(solution)/shard_map/all_gather | solution.py:183
  176.6 16.9 all_gather.56
  193.5 17.9 %all_gather.57 = bf16[3,1024]{1,0:T(4,128)(2,1)S(1)} all-gather(bf16[3,128]{1,0:T(4,128)(2,1)S(1)} %copy-done.74), channel_id=1, replica_groups=mesh['seq'=4,'fsdp'=8] {'fsdp'}, dimensions={1}, use_global_device_ids=true | all-gather | bytes 6912 | tf_op jit(solution)/shard_map/all_gather | solution.py:191
  218.3 16.5 while.76
  238.5 4.6 reduce.71
  248.6 3.7 fusion.123
  257.4 4.7 all-to-all-start.3
  265.8 19.8 %all-gather.20.cloned.1.call-done = bf16[1024,1024]{1,0:T(8,128)(2,1)} async-done(((bf16[128,1024]{1,0:T(8,128)(2,1)}), bf16[1024,1024]{1,0:T(8,128)(2,1)}) %all-gather.20.cloned.1.call-update) | async-done | bytes 2097168 | tf_op jit(solution)/shard_map/all_gather | solution.py:180
  290.0 4.8 reduce.72
  295.7 4.1 all-to-all-start.2
  317.1 12.0 while.75
  329.1 3.8 copy.166
  332.9 5.6 reduce.73
  340.4 4.2 all-to-all-start.4
  344.6 18.3 %all-gather.5 = bf16[8,1,128]{2,1,0:T(2,128)(2,1)S(1)} all-gather(bf16[1,1,128]{2,1,0:T(2,128)(2,1)S(1)} %bitcast.490), channel_id=1, replica_groups=mesh['seq'=4,'fsdp'=8] {'fsdp'}, dimensions={0}, use_global_device_ids=true | all-gather | bytes 2304 | tf_op jit(solution)/shard_map/all_gather | solution.py:185
  362.9 26.5 %all-gather.6 = bf16[8,1,512]{2,1,0:T(2,128)(2,1)S(1)} all-gather(bf16[1,1,512]{2,1,0:T(2,128)(2,1)S(1)} %reshape.1096), channel_id=1, replica_groups=mesh['seq'=4,'fsdp'=8] {'fsdp'}, dimensions={0}, use_global_device_ids=true | all-gather | bytes 9216 | tf_op jit(solution)/shard_map/all_gather | solution.py:187
  389.4 16.7 all-gather.7
  417.0 44.3 %all-gather.26.cloned.1.call-done = bf16[1024,4096]{1,0:T(8,128)(2,1)} async-done(((bf16[128,4096]{1,0:T(8,128)(2,1)}), bf16[1024,4096]{1,0:T(8,128)(2,1)}) %all-gather.26.cloned.1.call-update) | async-done | bytes 8388624 | tf_op jit(solution)/shard_map/all_gather | solution.py:186
  461.3 8.3 convolution_add_fusion
  469.6 117.0 %all-gather.28.cloned.1.call-done = bf16[4096,1024]{1,0:T(8,128)(2,1)} async-done(((bf16[512,1024]{1,0:T(8,128)(2,1)}), bf16[4096,1024]{1,0:T(8,128)(2,1)}) %all-gather.28.cloned.1.call-update) | async-done | bytes 8388624 | tf_op jit(solution)/shard_map/all_gather | solution.py:188
  586.6 7.6 fusion.177
  597.4 8.3 fusion.178
  612.5 3.8 reduce.74
  617.3 3.9 all-to-all-start.5
  621.2 8.8 all-to-all-done.5
  636.5 38.0 %while.77 = (s32[]{:T(128)}, bf16[1,4,64,1024]{3,2,1,0:T(8,128)(2,1)}, f32[1,4,64,1024]{3,2,1,0:T(8,128)S(1)}, f32[1,4,64,1024]{3,2,1,0:T(8,128)}, bf16[1,4,64,1...) while((s32[]{:T(128)}, ...), condition=%wide.region_20.21_spmd.clone, body=%wide.region_18.20_spmd.clone.sunk | while | flops 1368913920 | bytes 139256112 | solution.py:125
  647.7 4.6 fusion.256
  666.2 4.6 fusion.256
  676.9 3.8 reduce.75
  687.6 3.8 copy.177
  694.0 4.4 all-to-all-start.9
  709.7 3.8 reduce.76
  721.8 4.9 all-to-all-done.7
  734.7 6.6 copy.186
  742.7 43.6 %while.78 = (s32[]{:T(128)}, bf16[1,4,64,1024]{3,2,1,0:T(8,128)(2,1)}, f32[1,4,64,1024]{3,2,1,0:T(8,128)S(1)}, f32[1,4,64,1024]{3,2,1,0:T(8,128)}, s32[1]{0:T(12...) while((s32[]{:T(128)}, ...), condition=%wide.region_25.26_spmd.clone.clone, body=%wide.region_23.25_spmd.clone.clone.sunk | while | flops 1376271360 | bytes 145564032 | solution.py:125
  748.6 3.8 multiply_convert_fusion.8
  755.7 4.8 fusion.268
  769.8 3.8 multiply_convert_fusion.8
  776.9 4.7 fusion.268
  781.7 4.6 fusion.270
  793.0 28.2 %all_to_all.162 = bf16[1,3,256,1024]{2,1,0,3:T(4,128)(2,1)S(1)} all-to-all(bf16[1,3,256,1024]{2,1,0,3:T(4,128)(2,1)S(1)} %copy.174), channel_id=1, replica_groups=mesh['seq'=4,'fsdp'=8] {'seq'}, dimensions={3} | all-to-all | bytes 3145728 | tf_op jit(solution)/shard_map/all_to_all | solution.py:366
  824.2 4.5 convert_bitcast_fusion
  828.7 8.6 copy.184
  848.4 7.4 convolution_convert_fusion.1
  857.0 8.5 convolution_convert_fusion
  870.2 82.5 %reduce-scatter.28.cloned.1.call-done = bf16[128,3072]{1,0:T(8,128)(2,1)} async-done(((bf16[1024,3072]{1,0:T(8,128)(2,1)}), bf16[128,3072]{1,0:T(8,128)(2,1)}) %reduce-scatter.28.cloned.1.call-update) | async-done | bytes 786448
  955.0 68.5 %reduce-scatter.22.cloned.1.call-done = bf16[128,1024]{1,0:T(8,128)(2,1)} async-done(((bf16[1024,1024]{1,0:T(8,128)(2,1)}), bf16[128,1024]{1,0:T(8,128)(2,1)}) %reduce-scatter.22.cloned.1.call-update) | async-done | bytes 262160 | tf_op jit(solution)/shard_map/reduce_scatter | solution.py:425
  1023.5 71.4 %reduce-scatter.20.cloned.1.call-done = bf16[128,1024]{1,0:T(8,128)(2,1)} async-done(((bf16[1024,1024]{1,0:T(8,128)(2,1)}), bf16[128,1024]{1,0:T(8,128)(2,1)}) %reduce-scatter.20.cloned.1.call-update) | async-done | bytes 262160 | tf_op jit(solution)/shard_map/reduce_scatter | solution.py:413
  1094.9 71.2 %reduce-scatter.18.cloned.1.call-done = bf16[128,1024]{1,0:T(8,128)(2,1)} async-done(((bf16[1024,1024]{1,0:T(8,128)(2,1)}), bf16[128,1024]{1,0:T(8,128)(2,1)}) %reduce-scatter.18.cloned.1.call-update) | async-done | bytes 262160 | tf_op jit(solution)/shard_map/reduce_scatter | solution.py:407
  1166.1 152.1 %reduce-scatter.24.cloned.1.call-done = bf16[128,4096]{1,0:T(8,128)(2,1)} async-done(((bf16[1024,4096]{1,0:T(8,128)(2,1)}), bf16[128,4096]{1,0:T(8,128)(2,1)}) %reduce-scatter.24.cloned.1.call-update) | async-done | bytes 1048592 | tf_op jit(solution)/shard_map/reduce_scatter | solution.py:431
  1318.2 151.5 %reduce-scatter.26.cloned.1.call-done = bf16[512,1024]{1,0:T(8,128)(2,1)} async-done(((bf16[4096,1024]{1,0:T(8,128)(2,1)}), bf16[512,1024]{1,0:T(8,128)(2,1)}) %reduce-scatter.26.cloned.1.call-update) | async-done | bytes 1048592 | tf_op jit(solution)/shard_map/reduce_scatter | solution.py:437
  1472.8 61.3 %reduce-scatter.34.cloned.1.call-done = bf16[128,3]{1,0:T(8,128)(2,1)} async-done(((bf16[1024,3]{1,0:T(8,128)(2,1)}), bf16[128,3]{1,0:T(8,128)(2,1)}) %reduce-scatter.34.cloned.1.call-update) | async-done | bytes 784
  1534.9 63.5 %reduce-scatter.32.cloned.1.call-done = bf16[128,3]{1,0:T(8,128)(2,1)} async-done(((bf16[1024,3]{1,0:T(8,128)(2,1)}), bf16[128,3]{1,0:T(8,128)(2,1)}) %reduce-scatter.32.cloned.1.call-update) | async-done | bytes 784
  1599.6 4.3 fusion.139
  1604.2 35.3 %all-reduce.9 = (bf16[1024]{0:T(1024)(128)(2,1)S(1)}, bf16[1024]{0:T(1024)(128)(2,1)S(1)}, bf16[1024]{0:T(1024)(128)(2,1)S(1)}, bf16[1024]{0:T(1024)(128)(2,1)S(...) all-reduce(bf16[1024]{0:T(1024)(128)(2,1)S(1)} %get-tuple-element.1, ...), channel_id=3, replica_groups=mesh['seq'=4,'fsdp'=8] {'fsdp'}, use_global_device_ids=true, to_apply=%region_29.30.clone | all-reduce | flops 11264 | bytes 45056
  1640.1 6.0 all-reduce.10
  1651.5 6.2 fusion.136
  1657.7 30.3 %all-reduce.14.cloned.1.call-done = (bf16[128,3072]{0,1:T(8,128)(2,1)}, bf16[128,2048]{0,1:T(8,128)(2,1)}, bf16[128,1024]{1,0:T(8,128)(2,1)}, bf16[128,1024]{1,0...) async-done(((bf16[128,3072]{0,1:T(8,128)(2,1)}, bf16[128,2048]{0,1:T(8,128)(2,1)}, bf16[128,1024]{1,0:T(8,128)(2,1)}, ...) | async-done | bytes 4194320 | tf_op jit(solution)/shard_map/psum | solution.py:451
  (447 shorter events, 257.2 us)
Async XLA Ops:
  7.2 241.4 %copy-start = (bf16[1,256,1024]{2,1,0:T(8,128)(2,1)S(1)}, bf16[1,256,1024]{2,1,0:T(8,128)(2,1)}, u32[]{:S(2)}) copy-start(bf16[1,256,1024]{2,1,0:T(8,128)(2,1)} %param.30) | copy-start | bytes 1572868
  7.2 104.8 %all-gather.16.cloned.1.call-start = ((), (), s32[]{:S(2)}) async-start(), calls=%async_computation.19 | async-start | bytes 7077888 | tf_op jit(solution)/shard_map/all_gather | solution.py:175
  7.9 240.6 %all-gather.22.cloned.1.call-start = ((), (), s32[]{:S(2)}) async-start(), calls=%async_computation.22 | async-start | bytes 4718592 | tf_op jit(solution)/shard_map/all_gather | solution.py:182
  8.7 254.2 %all-gather.18.cloned.1.call-start = ((), (), s32[]{:S(2)}) async-start(), calls=%async_computation.20 | async-start | bytes 2359296 | tf_op jit(solution)/shard_map/all_gather | solution.py:178
  9.4 276.2 %all-gather.20.cloned.1.call-start = ((), (), s32[]{:S(2)}) async-start(), calls=%async_computation.21 | async-start | bytes 2359296 | tf_op jit(solution)/shard_map/all_gather | solution.py:180
  10.0 403.0 %all-gather.24.cloned.1.call-start = ((), (), s32[]{:S(2)}) async-start(), calls=%async_computation.23 | async-start | bytes 2359296 | tf_op jit(solution)/shard_map/all_gather | solution.py:184
  10.6 450.7 %all-gather.26.cloned.1.call-start = ((), (), s32[]{:S(2)}) async-start(), calls=%async_computation.24 | async-start | bytes 9437184 | tf_op jit(solution)/shard_map/all_gather | solution.py:186
  117.1 24.9 %copy-start.77 = (bf16[128]{0:T(256)(128)(2,1)S(1)}, bf16[128]{0:T(256)(128)(2,1)}, u32[]{:S(2)}) copy-start(bf16[128]{0:T(256)(128)(2,1)} %param.39) | copy-start | bytes 772
  117.1 41.9 %copy-start.78 = (bf16[128]{0:T(256)(128)(2,1)S(1)}, bf16[128]{0:T(256)(128)(2,1)}, u32[]{:S(2)}) copy-start(bf16[128]{0:T(256)(128)(2,1)} %param.41) | copy-start | bytes 772
  117.1 59.5 %copy-start.73 = (bf16[3,128]{1,0:T(4,128)(2,1)S(1)}, bf16[3,128]{1,0:T(4,128)(2,1)}, u32[]{:S(2)}) copy-start(bf16[3,128]{1,0:T(4,128)(2,1)} %param.48) | copy-start | bytes 2308
  117.1 76.4 %copy-start.74 = (bf16[3,128]{1,0:T(4,128)(2,1)S(1)}, bf16[3,128]{1,0:T(4,128)(2,1)}, u32[]{:S(2)}) copy-start(bf16[3,128]{1,0:T(4,128)(2,1)} %param.49) | copy-start | bytes 2308
  119.8 92.8 %all-to-all-start = ((bf16[1,3,1024,256]{3,1,0,2:T(4,128)(2,1)}), bf16[1,3,1024,256]{3,1,0,2:T(4,128)(2,1)S(1)}, u32[]{:S(2)}, u32[]{:S(2)}) async-start(bf16[1,3,1024,256]{3,1,0,2:T(4,128)(2,1)} %copy.151), calls=%async_computation | async-start | bytes 4194304 | tf_op jit(solution)/shard_map/all_to_all | solution.py:220
  123.4 463.2 %all-gather.28.cloned.1.call-start = ((), (), s32[]{:S(2)}) async-start(), calls=%async_computation.25 | async-start | bytes 9437184 | tf_op jit(solution)/shard_map/all_gather | solution.py:188
  211.9 201.1 %copy-start.49 = (f32[1,1024]{1,0:T(1,128)}, f32[1,1024]{1,0:T(1,128)S(1)}, u32[]{:S(2)}) copy-start(f32[1,1024]{1,0:T(1,128)S(1)} %get-tuple-element.1297) | copy-start | bytes 12292
  212.6 200.5 %copy-start.51 = (f32[1,1024]{1,0:T(1,128)}, f32[1,1024]{1,0:T(1,128)S(1)}, u32[]{:S(2)}) copy-start(f32[1,1024]{1,0:T(1,128)S(1)} %get-tuple-element.1300) | copy-start | bytes 12292
  234.8 17.5 %copy-start.5 = (bf16[1,4,64,1024]{3,2,1,0:T(8,128)(2,1)}, bf16[1,4,64,1024]{3,2,1,0:T(8,128)(2,1)S(1)}, u32[]{:S(2)}) copy-start(bf16[1,4,64,1024]{3,2,1,0:T(8,128)(2,1)S(1)} %get-tuple-element.1699) | copy-start | bytes 1572868
  234.8 17.5 %copy-start.7 = (bf16[1,4,64,1024]{3,2,1,0:T(8,128)(2,1)}, bf16[1,4,64,1024]{3,2,1,0:T(8,128)(2,1)S(1)}, u32[]{:S(2)}) copy-start(bf16[1,4,64,1024]{3,2,1,0:T(8,128)(2,1)S(1)} %get-tuple-element.1703) | copy-start | bytes 1572868
  234.8 17.5 %copy-start.15 = (bf16[1,4,64,1024]{3,2,1,0:T(8,128)(2,1)}, bf16[1,4,64,1024]{3,2,1,0:T(8,128)(2,1)S(1)}, u32[]{:S(2)}) copy-start(bf16[1,4,64,1024]{3,2,1,0:T(8,128)(2,1)S(1)} %get-tuple-element.1707) | copy-start | bytes 1572868
  245.1 12.3 all-to-all-start.1
  252.3 10.6 copy-start.33
  257.4 38.3 %all-to-all-start.3 = ((bf16[1,2,1024,256]{3,1,0,2:T(2,128)(2,1)}), bf16[1,2,1024,256]{3,1,0,2:T(2,128)(2,1)}, u32[]{:S(2)}, u32[]{:S(2)}) async-start(bf16[1,2,1024,256]{3,1,0,2:T(2,128)(2,1)} %copy.161), calls=%async_computation.3 | async-start | bytes 2097152 | tf_op jit(solution)/shard_map/all_to_all | solution.py:221
  262.9 25.1 %copy-start.28 = (bf16[1,4,256,256]{3,2,1,0:T(8,128)(2,1)}, bf16[1,4,256,256]{3,2,1,0:T(8,128)(2,1)S(1)}, u32[]{:S(2)}) copy-start(bf16[1,4,256,256]{3,2,1,0:T(8,128)(2,1)S(1)} %copy.158) | copy-start | bytes 1572868
  265.5 147.5 %copy-start.9 = (f32[1,256,1024]{2,1,0:T(8,128)}, f32[1,256,1024]{2,1,0:T(8,128)S(1)}, u32[]{:S(2)}) copy-start(f32[1,256,1024]{2,1,0:T(8,128)S(1)} %get-tuple-element.1302) | copy-start | bytes 3145732
  265.5 147.5 %copy-start.53 = (f32[256]{0:T(256)}, f32[256]{0:T(256)S(1)}, u32[]{:S(2)}) copy-start(f32[256]{0:T(256)S(1)} %broadcast_multiply_fusion.8) | copy-start | bytes 3076
  265.8 147.3 %copy-start.55 = (f32[256]{0:T(256)}, f32[256]{0:T(256)S(1)}, u32[]{:S(2)}) copy-start(f32[256]{0:T(256)S(1)} %add_rsqrt_fusion.2) | copy-start | bytes 3076
  295.7 13.1 all-to-all-start.2
  329.1 82.6 %copy-start.17 = (bf16[1,4,64,1024]{3,2,1,0:T(8,128)(2,1)}, bf16[1,4,64,1024]{3,2,1,0:T(8,128)(2,1)S(1)}, u32[]{:S(2)}) copy-start(bf16[1,4,64,1024]{3,2,1,0:T(8,128)(2,1)S(1)} %get-tuple-element.1708) | copy-start | bytes 1572868
  329.1 15.5 copy-start.79
  329.1 33.8 %copy-start.75 = (bf16[512]{0:T(512)(128)(2,1)S(1)}, bf16[512]{0:T(512)(128)(2,1)}, u32[]{:S(2)}) copy-start(bf16[512]{0:T(512)(128)(2,1)} %param.45) | copy-start | bytes 3076
  329.1 60.3 %copy-start.80 = (bf16[128]{0:T(256)(128)(2,1)S(1)}, bf16[128]{0:T(256)(128)(2,1)}, u32[]{:S(2)}) copy-start(bf16[128]{0:T(256)(128)(2,1)} %param.47) | copy-start | bytes 772
  340.4 65.7 %all-to-all-start.4 = ((bf16[4,2,32768]{2,1,0:T(2,128)(2,1)}), bf16[4,2,32768]{2,1,0:T(2,128)(2,1)}, u32[]{:S(2)}, u32[]{:S(2)}) async-start(bf16[4,2,32768]{2,1,0:T(2,128)(2,1)} %reshape.1141), calls=%async_computation.4 | async-start | bytes 1048576 | tf_op jit(solution)/shard_map/all_to_all | solution.py:269
  409.6 51.7 %copy-start.45 = (f32[1,1024]{1,0:T(1,128)S(1)}, f32[1,1024]{1,0:T(1,128)}, u32[]{:S(2)}) copy-start(f32[1,1024]{1,0:T(1,128)} %get-tuple-element.1296) | copy-start | bytes 12292
  409.6 51.7 %copy-start.47 = (f32[1,1024]{1,0:T(1,128)S(1)}, f32[1,1024]{1,0:T(1,128)}, u32[]{:S(2)}) copy-start(f32[1,1024]{1,0:T(1,128)} %get-tuple-element.1299) | copy-start | bytes 12292
  413.0 56.6 %copy-start.30 = (bf16[1,4,256,256]{3,2,1,0:T(8,128)(2,1)}, bf16[1,4,256,256]{3,2,1,0:T(8,128)(2,1)S(1)}, u32[]{:S(2)}) copy-start(bf16[1,4,256,256]{3,2,1,0:T(8,128)(2,1)S(1)} %copy.167) | copy-start | bytes 1572868
  415.8 193.2 %copy-start.58 = (f32[256]{0:T(256)}, f32[256]{0:T(256)S(1)}, u32[]{:S(2)}) copy-start(f32[256]{0:T(256)S(1)} %broadcast_multiply_fusion.7) | copy-start | bytes 3076
  417.0 192.0 %copy-start.60 = (f32[256]{0:T(256)}, f32[256]{0:T(256)S(1)}, u32[]{:S(2)}) copy-start(f32[256]{0:T(256)S(1)} %add_rsqrt_fusion.1) | copy-start | bytes 3076
  461.3 125.3 %copy-start.13 = (f32[1,256,1024]{2,1,0:T(8,128)S(1)}, f32[1,256,1024]{2,1,0:T(8,128)}, u32[]{:S(2)}) copy-start(f32[1,256,1024]{2,1,0:T(8,128)} %copy-done.12) | copy-start | bytes 3145732
  596.3 9.4 slice-start
  597.4 8.3 copy-start.36
  597.4 8.3 slice-start.1
  617.3 12.7 all-to-all-start.5
  681.7 12.3 all-to-all-start.6
  687.6 14.9 copy-start.10
  687.6 14.9 copy-start.23
  687.6 14.9 copy-start.50
  687.6 14.9 copy-start.54
  687.6 14.9 copy-start.56
  694.0 20.5 %all-to-all-start.9 = ((bf16[1,2,256,1024]{2,1,0,3:T(2,128)(2,1)}), bf16[1,2,256,1024]{2,1,0,3:T(2,128)(2,1)}, u32[]{:S(2)}, u32[]{:S(2)}) async-start(bf16[1,2,256,1024]{2,1,0,3:T(2,128)(2,1)} %copy.177), calls=%async_computation.9 | async-start | bytes 2097152 | tf_op jit(solution)/shard_map/all_to_all | solution.py:332
  714.5 12.3 all-to-all-start.7
  717.9 150.3 %reduce-scatter.30.cloned.1.call-start = ((), (), s32[]{:S(2)}) async-start(), calls=%async_computation.32 | async-start | bytes 4718592
  721.8 12.9 copy-start.19
  741.3 211.4 %reduce-scatter.28.cloned.1.call-start = ((), (), s32[]{:S(2)}) async-start(), calls=%async_computation.31 | async-start | bytes 7077888
  752.4 8.1 copy-start.4
  773.5 8.1 copy-start.4
  837.4 186.2 %reduce-scatter.22.cloned.1.call-start = ((), (), s32[]{:S(2)}) async-start(), calls=%async_computation.28 | async-start | bytes 2359296 | tf_op jit(solution)/shard_map/reduce_scatter | solution.py:425
  841.2 253.7 %reduce-scatter.20.cloned.1.call-start = ((), (), s32[]{:S(2)}) async-start(), calls=%async_computation.27 | async-start | bytes 2359296 | tf_op jit(solution)/shard_map/reduce_scatter | solution.py:413
  844.7 321.4 %reduce-scatter.18.cloned.1.call-start = ((), (), s32[]{:S(2)}) async-start(), calls=%async_computation.26 | async-start | bytes 2359296 | tf_op jit(solution)/shard_map/reduce_scatter | solution.py:407
  848.3 470.0 %reduce-scatter.24.cloned.1.call-start = ((), (), s32[]{:S(2)}) async-start(), calls=%async_computation.29 | async-start | bytes 9437184 | tf_op jit(solution)/shard_map/reduce_scatter | solution.py:431
  855.8 614.0 %reduce-scatter.26.cloned.1.call-start = ((), (), s32[]{:S(2)}) async-start(), calls=%async_computation.30 | async-start | bytes 9437184 | tf_op jit(solution)/shard_map/reduce_scatter | solution.py:437
  865.5 604.3 %copy-start.81 = (u32[32]{0:T(128)S(1)}, u32[32]{0:T(128)}, u32[]{:S(2)}) copy-start(u32[32]{0:T(128)} %constant.429) | copy-start | bytes 388
  865.5 668.6 %reduce-scatter.34.cloned.1.call-start = ((), (), s32[]{:S(2)}) async-start(), calls=%async_computation.34 | async-start | bytes 294912
  867.1 732.2 %copy-start.20 = (bf16[1,2,4,256,256]{4,3,2,1,0:T(8,128)(2,1)S(1)}, bf16[1,2,4,256,256]{4,3,2,1,0:T(8,128)(2,1)}, u32[]{:S(2)}) copy-start(bf16[1,2,4,256,256]{4,3,2,1,0:T(8,128)(2,1)} %copy-done.19) | copy-start | bytes 3145732
  867.1 731.3 %reduce-scatter.32.cloned.1.call-start = ((), (), s32[]{:S(2)}) async-start(), calls=%async_computation.33 | async-start | bytes 294912
  868.1 819.8 %all-reduce.14.cloned.1.call-start = ((), (), s32[]{:S(2)}) async-start(), calls=%async_computation.35 | async-start | bytes 8388608 | tf_op jit(solution)/shard_map/psum | solution.py:451
  (55 other events, 201.3 us)
Sparse Core Ops, SparseCore 0:
  10.2 101.7 all-gather.15
  114.2 71.8 all-gather.21
  188.2 47.5 all-gather.17
  237.8 47.8 all-gather.19
  287.6 47.7 all-gather.23
  337.4 123.8 all-gather.25
  463.4 123.1 all-gather.27
  741.4 85.1 reduce-scatter.29
  837.5 115.1 reduce-scatter.27
  956.5 66.9 reduce-scatter.21
  1028.1 66.7 reduce-scatter.19
  1099.3 66.7 reduce-scatter.17
  1170.2 147.9 reduce-scatter.23
  1321.7 147.9 reduce-scatter.25
  1473.9 60.2 reduce-scatter.33
  1538.2 60.2 reduce-scatter.31
  1602.0 85.9 all-reduce.13
where the time goes:
time: 1710 us
  waiting for transfers between devices  1020 us (60%)
  blocking collectives  257 us (15%)
  matrix products  175 us (10%)
  local copies, waits for them, and re-layouts  118 us (7%)
  other arithmetic  80.6 us (5%)
  starting transfers between devices  36.2 us (2%)
    unnamed x21, waiting for transfers between devices  212 us
    reduce_scatter x1, waiting for transfers between devices, local(): lax.psum_scatter(grad_ffn_in.astype(jnp.bfloat16), 'fsdp', scatter_dimens...  152 us
    reduce_scatter x1, waiting for transfers between devices, local(): lax.psum_scatter(grad_ffn_out.astype(jnp.bfloat16), 'fsdp', scatter_dimen...  152 us
    all_gather x1, waiting for transfers between devices, local(): lax.all_gather(ffn_out_weight, 'fsdp', axis=0, tiled=True)  117 us
    reduce_scatter x1, waiting for transfers between devices, local(): lax.psum_scatter(grad_cross_query.astype(jnp.bfloat16), 'fsdp', scatter_d...  71.4 us
    reduce_scatter x1, waiting for transfers between devices, local(): lax.psum_scatter(grad_self_out.astype(jnp.bfloat16), 'fsdp', scatter_dime...  71.2 us
    reduce_scatter x1, waiting for transfers between devices, local(): lax.psum_scatter(grad_cross_out.astype(jnp.bfloat16), 'fsdp', scatter_dim...  68.5 us
    all_gather x1, waiting for transfers between devices, local(): lax.all_gather(self_in_weight, 'fsdp', axis=0, tiled=True)  61.8 us
  transfers between devices with their start and end apart: 26, of which 18 were waited for; matrix products, arithmetic and copies ran while one was open for 15% of the time, Pallas kernels for 0%

commit v1 on v0

v1 whole, which is shorter than its diff:
```python
import functools

import jax
import jax.numpy as jnp
from jax import lax
from jax.experimental import pallas as pl
from jax.experimental.pallas import tpu as pltpu
from jax.sharding import PartitionSpec as P

HD = 64
BLK = 256
CORES = 2

alpha_scale = 300.0**0.25
layer_eps = 1e-05
score_scale = 0.125
masked_value = -1e30
gelu_coef = 0.7978845608028654
gelu_cube = 0.044715

f32 = jnp.float32
bf16 = jnp.bfloat16
vmem_limit = 56 * 1024 * 1024


def dot(left, right, dims):
    return lax.dot_general(left, right, (dims, ((), ())), preferred_element_type=f32)


nn = ((1,), (0,))
nt = ((1,), (1,))
tn = ((0,), (0,))


def key_cases(total_keys, causal, block_index, visit):
    if not causal:
        visit(total_keys)
        return
    blocks = total_keys // BLK
    cases = min(4, blocks)
    for case in range(cases):
        low, high = case * blocks // cases, (case + 1) * blocks // cases

        @pl.when((block_index >= low) & (block_index < high))
        def _(high=high):
            visit(high * BLK)


def mask_scores(scores, first_key, limit):
    key_pos = first_key + lax.broadcasted_iota(jnp.int32, scores.shape, 0)
    return jnp.where(key_pos < limit, scores, masked_value)


def forward_kernel(causal, heads, chunk, len_ref, q_ref, k_ref, v_ref, o_ref, lse_ref):
    block_index = pl.program_id(1)
    total_keys = k_ref.shape[0]
    limit = jnp.minimum(len_ref[0], (block_index + 1) * BLK) if causal else 0
    rows = q_ref.shape[0]

    if total_keys <= chunk:

        def visit(key_count):
            outs, lses = [], []
            for h in range(heads):
                cols = slice(h * HD, (h + 1) * HD)
                query = q_ref[:, cols] * jnp.asarray(score_scale, bf16)
                scores = dot(k_ref[:key_count, cols], query, nt)
                if causal:
                    scores = mask_scores(scores, 0, limit)
                top = jnp.max(scores, axis=0, keepdims=True)
                weights = jnp.exp(scores - top)
                totals = jnp.sum(weights, axis=0, keepdims=True)
                low = (weights * (1.0 / totals)).astype(bf16)
                outs.append(dot(low, v_ref[:key_count, cols], tn).astype(bf16))
                lses.append(top + jnp.log(totals))
            o_ref[...] = outs[0] if heads == 1 else jnp.concatenate(outs, axis=1)
            lse_ref[0] = lses[0] if heads == 1 else jnp.concatenate(lses, axis=0)

        key_cases(total_keys, causal, block_index, visit)
    else:
        live = ((block_index + 1) * BLK + chunk - 1) // chunk if causal else total_keys // chunk
        outs, lses = [], []
        for h in range(heads):
            cols = slice(h * HD, (h + 1) * HD)
            query = q_ref[:, cols] * jnp.asarray(score_scale, bf16)

            def step(n, carry, cols=cols, query=query):
                top, totals, acc = carry
                span = pl.ds(pl.multiple_of(n * chunk, chunk), chunk)
                scores = dot(k_ref[span, cols], query, nt)
                if causal:
                    scores = mask_scores(scores, n * chunk, limit)
                new_top = jnp.maximum(top, jnp.max(scores, axis=0, keepdims=True))
                decay = jnp.exp(top - new_top)
                weights = jnp.exp(scores - new_top)
                totals = totals * decay + jnp.sum(weights, axis=0, keepdims=True)
                acc = acc * decay + dot(v_ref[span, cols], weights.astype(bf16), tn)
                return new_top, totals, acc

            start = (
                jnp.full((1, rows), masked_value, f32),
                jnp.zeros((1, rows), f32),
                jnp.zeros((HD, rows), f32),
            )
            top, totals, acc = lax.fori_loop(0, live, step, start)
            outs.append((acc / totals).T.astype(bf16))
            lses.append(top + jnp.log(totals))
        o_ref[...] = outs[0] if heads == 1 else jnp.concatenate(outs, axis=1)
        lse_ref[0] = lses[0] if heads == 1 else jnp.concatenate(lses, axis=0)


def backward_kernel(
    causal, heads, chunk, len_ref, q_ref, k_ref, v_ref, g_ref, lse_ref, dq_ref, dk_ref, dv_ref,
    dk_acc, dv_acc
):
    block_index = pl.program_id(1)
    total_keys = k_ref.shape[0]
    limit = jnp.minimum(len_ref[0], (block_index + 1) * BLK) if causal else 0

    @pl.when(block_index == 0)
    def _():
        dk_acc[...] = jnp.zeros_like(dk_acc)
        dv_acc[...] = jnp.zeros_like(dv_acc)

    def probabilities(query, span, cols, first_key, lse):
        scores = dot(k_ref[span, cols], query, nt)
        if causal:
            scores = mask_scores(scores, first_key, limit)
        return jnp.exp(scores - lse)

    if total_keys <= chunk:

        def visit(key_count):
            span = slice(0, key_count)
            dqs = []
            for h in range(heads):
                cols = slice(h * HD, (h + 1) * HD)
                query = q_ref[:, cols] * jnp.asarray(score_scale, bf16)
                grad = g_ref[:, cols]
                weights = probabilities(query, span, cols, 0, lse_ref[0, h : h + 1, :])
                dv_acc[h, span, :] += dot(weights.astype(bf16), grad, nn)
                grad_weights = dot(v_ref[span, cols], grad, nt)
                row_term = jnp.sum(grad_weights * weights, axis=0, keepdims=True)
                low = (weights * (grad_weights - row_term)).astype(bf16)
                dk_acc[h, span, :] += dot(low, query, nn)
                dqs.append((dot(low, k_ref[span, cols], tn) * score_scale).astype(bf16))
            dq_ref[...] = dqs[0] if heads == 1 else jnp.concatenate(dqs, axis=1)

        key_cases(total_keys, causal, block_index, visit)
    else:
        live = ((block_index + 1) * BLK + chunk - 1) // chunk if causal else total_keys // chunk
        rows = q_ref.shape[0]
        dqs = []
        for h in range(heads):
            cols = slice(h * HD, (h + 1) * HD)
            query = q_ref[:, cols] * jnp.asarray(score_scale, bf16)
            grad = g_ref[:, cols]
            lse = lse_ref[0, h : h + 1, :]

            def sums(n, row_term, cols=cols, query=query, grad=grad, lse=lse):
                span = pl.ds(pl.multiple_of(n * chunk, chunk), chunk)
                weights = probabilities(query, span, cols, n * chunk, lse)
                grad_weights = dot(v_ref[span, cols], grad, nt)
                return row_term + jnp.sum(grad_weights * weights, axis=0, keepdims=True)

            row_term = lax.fori_loop(0, live, sums, jnp.zeros((1, rows), f32))

            def step(n, acc, h=h, cols=cols, query=query, grad=grad, lse=lse, row_term=row_term):
                span = pl.ds(pl.multiple_of(n * chunk, chunk), chunk)
                weights = probabilities(query, span, cols, n * chunk, lse)
                dv_acc[h, span, :] += dot(weights.astype(bf16), grad, nn)
                grad_weights = dot(v_ref[span, cols], grad, nt)
                low = (weights * (grad_weights - row_term)).astype(bf16)
                dk_acc[h, span, :] += dot(low, query, nn)
                return acc + dot(low, k_ref[span, cols], tn)

            acc = lax.fori_loop(0, live, step, jnp.zeros((rows, HD), f32))
            dqs.append((acc * score_scale).astype(bf16))
        dq_ref[...] = dqs[0] if heads == 1 else jnp.concatenate(dqs, axis=1)

    @pl.when(block_index == pl.num_programs(1) - 1)
    def _():
        for ref, acc in ((dk_ref, dk_acc), (dv_ref, dv_acc)):
            parts = [acc[h].astype(bf16) for h in range(heads)]
            ref[...] = parts[0] if heads == 1 else jnp.concatenate(parts, axis=1)


def attention_specs(total_q, total_k, width):
    block = min(2 * HD, width)
    heads = block // HD
    groups = width // block
    rows = min(BLK, total_q)
    chunk = min(1024, total_k)
    q_spec = pl.BlockSpec((rows, block), lambda g, i, _: (i, g))
    k_spec = pl.BlockSpec((total_k, block), lambda g, i, _: (0, g))
    l_spec = pl.BlockSpec((1, heads, rows), lambda g, i, _: (g, 0, i))
    return block, heads, groups, rows, chunk, q_spec, k_spec, l_spec


def attend_forward(queries, keys, values, lengths, causal):
    total_q, width = queries.shape
    total_k = keys.shape[0]
    block, heads, groups, rows, chunk, q_spec, k_spec, l_spec = attention_specs(
        total_q, total_k, width
    )
    work = total_q * total_k * width
    return pl.pallas_call(
        functools.partial(forward_kernel, causal, heads, chunk),
        grid_spec=pltpu.PrefetchScalarGridSpec(
            num_scalar_prefetch=1,
            grid=(groups, total_q // rows),
            in_specs=[q_spec, k_spec, k_spec],
            out_specs=[q_spec, l_spec],
        ),
        out_shape=[
            jax.ShapeDtypeStruct((total_q, width), bf16),
            jax.ShapeDtypeStruct((groups, heads, total_q), f32),
        ],
        compiler_params=pltpu.CompilerParams(vmem_limit_bytes=vmem_limit),
        cost_estimate=pl.CostEstimate(
            flops=4 * work, bytes_accessed=8 * total_k * width, transcendentals=work // HD
        ),
    )(lengths, queries, keys, values)


def attend_back(queries, keys, values, grads, lse, lengths, causal):
    total_q, width = queries.shape
    total_k = keys.shape[0]
    block, heads, groups, rows, chunk, q_spec, k_spec, l_spec = attention_specs(
        total_q, total_k, width
    )
    work = total_q * total_k * width
    return pl.pallas_call(
        functools.partial(backward_kernel, causal, heads, chunk),
        grid_spec=pltpu.PrefetchScalarGridSpec(
            num_scalar_prefetch=1,
            grid=(groups, total_q // rows),
            in_specs=[q_spec, k_spec, k_spec, q_spec, l_spec],
            out_specs=[q_spec, k_spec, k_spec],
            scratch_shapes=[
                pltpu.VMEM((heads, total_k, HD), f32),
                pltpu.VMEM((heads, total_k, HD), f32),
            ],
        ),
        out_shape=[
            jax.ShapeDtypeStruct((total_q, width), bf16),
            jax.ShapeDtypeStruct((total_k, width), bf16),
            jax.ShapeDtypeStruct((total_k, width), bf16),
        ],
        compiler_params=pltpu.CompilerParams(vmem_limit_bytes=vmem_limit),
        cost_estimate=pl.CostEstimate(
            flops=10 * work, bytes_accessed=16 * total_k * width, transcendentals=work // HD
        ),
    )(lengths, queries, keys, values, grads, lse)


def assemble(arrays, moves, shape):
    dtype = arrays[0].dtype
    if any(m[2] % 16 or m[4] % 128 or m[1] % 16 or m[3] % 128 for m in moves):
        result = jnp.zeros(shape, dtype)
        for index, row, rows, col, cols, to_row, to_col in moves:
            part = arrays[index][row : row + rows, col : col + cols]
            result = lax.dynamic_update_slice(result, part, (to_row, to_col))
        return result
    count = len(arrays)
    places = jnp.stack([jnp.asarray(p, jnp.int32) for m in moves for p in (m[5], m[6])])

    def kernel(places_ref, *refs):
        sources, target, sems = refs[:count], refs[count], refs[count + 1]
        copies = []
        for n, (index, row, rows, col, cols, _, _) in enumerate(moves):
            to_row = pl.multiple_of(places_ref[2 * n], rows)
            to_col = pl.multiple_of(places_ref[2 * n + 1], cols)
            copies.append(
                pltpu.make_async_copy(
                    sources[index].at[pl.ds(row, rows), pl.ds(col, cols)],
                    target.at[pl.ds(to_row, rows), pl.ds(to_col, cols)],
                    sems.at[n],
                )
            )
        for copy in copies:
            copy.start()
        for copy in copies:
            copy.wait()

    return pl.pallas_call(
        kernel,
        grid_spec=pltpu.PrefetchScalarGridSpec(
            num_scalar_prefetch=1,
            grid=(1,),
            in_specs=[pl.BlockSpec(memory_space=pl.ANY)] * count,
            out_specs=pl.BlockSpec(memory_space=pltpu.VMEM),
            scratch_shapes=[pltpu.SemaphoreType.DMA((len(moves),))],
        ),
        out_shape=jax.ShapeDtypeStruct(shape, dtype),
        compiler_params=pltpu.CompilerParams(vmem_limit_bytes=vmem_limit),
        cost_estimate=pl.CostEstimate(
            flops=0,
            bytes_accessed=2 * sum(a.size * a.dtype.itemsize for a in arrays),
            transcendentals=0,
        ),
    )(places, *arrays)


def gelu_both(values):
    inner = gelu_coef * (values + gelu_cube * values * values * values)
    tangent = jnp.tanh(inner)
    output = 0.5 * values * (1.0 + tangent)
    slope = 0.5 * (1.0 + tangent) + 0.5 * values * (1.0 - tangent * tangent) * gelu_coef * (
        1.0 + 3.0 * gelu_cube * values * values
    )
    return (output, slope)


def layer_norm(values, gain_row, shift_row):
    center = values - jnp.mean(values, axis=-1, keepdims=True)
    inverse = lax.rsqrt(jnp.mean(center * center, axis=-1, keepdims=True) + layer_eps)
    normed = center * inverse
    return (normed * gain_row + shift_row, normed, inverse)


def norm_back(grad_rows, normed, inverse, gain_row):
    scaled = grad_rows * gain_row
    inner_term = scaled - jnp.mean(scaled, axis=-1, keepdims=True)
    inner_term = inner_term - normed * jnp.mean(scaled * normed, axis=-1, keepdims=True)
    return (
        inverse * inner_term,
        jnp.sum(grad_rows * normed, axis=0),
        jnp.sum(grad_rows, axis=0),
    )


def column_sum(array):
    return jnp.sum(array.astype(f32), axis=0)


def after(value, *earlier):
    return lax.optimization_barrier((value, *earlier))[0]


def solution(mesh):
    S, F = mesh.shape["seq"], mesh.shape["fsdp"]
    Y = S // CORES
    Z = 4 if F % 4 == 0 else 1
    X = F // Z

    core_perm = [(n, n ^ 1) for n in range(S)]

    def y_perm(k):
        return [(y * CORES + c, (y + k) % Y * CORES + c) for y in range(Y) for c in range(CORES)]

    def z_perm(k):
        return [(z * X + x, (z + k) % Z * X + x) for z in range(Z) for x in range(X)]

    def x_perm(k):
        return [(z * X + x, z * X + (x + k) % X) for z in range(Z) for x in range(X)]

    def core_swap(array):
        return lax.ppermute(array, "seq", core_perm)

    def y_shift(array, k):
        return lax.ppermute(array, "seq", y_perm(k % Y)) if k % Y else array

    def z_shift(array, k):
        return lax.ppermute(array, "fsdp", z_perm(k % Z)) if k % Z else array

    def x_shift(array, k):
        return lax.ppermute(array, "fsdp", x_perm(k % X)) if k % X else array

    def local(
        hidden_in,
        memory,
        lengths,
        out_grad,
        self_in_weight,
        self_query_bias,
        self_value_bias,
        self_out_weight,
        self_out_bias,
        cross_query_weight,
        cross_query_bias,
        memory_weight,
        memory_value_bias,
        cross_out_weight,
        cross_out_bias,
        ffn_in_weight,
        ffn_in_bias,
        ffn_out_weight,
        ffn_out_bias,
        norm_gain,
        norm_bias,
    ):
        s = lax.axis_index("seq")
        y, c = s // CORES, s % CORES
        f = lax.axis_index("fsdp")
        z, x = f // X, f % X
        _, t, D = hidden_in.shape
        T = S * t
        hw = D // S
        FF = ffn_in_weight.shape[1]
        shard = D // F
        part = shard // S
        fw = FF // (F * S)
        hidden_in, memory, out_grad = hidden_in[0], memory[0], out_grad[0]

        relative = [(k, e) for e in range(CORES) for k in range(Y)]

        def seq_of(k, e):
            return lax.rem(y - k + Y, Y) * CORES + (c if e == 0 else 1 - c)

        def seq_gather(array):
            own = [y_shift(array, k) for k in range(Y)]
            return own + [core_swap(a) for a in own]

        def seq_scatter(parts):
            chip = []
            for k in reversed(range(Y)):
                other = core_swap(parts[(k, 1)].astype(bf16))
                chip.append((k, parts[(k, 0)].astype(f32) + other.astype(f32)))
            total = None
            for k, value in chip:
                value = y_shift(value.astype(bf16), -k).astype(f32) if k else value
                total = value if total is None else total + value
            return total

        def fsdp_gather(chunk):
            pieces = []
            for kz in range(Z):
                column = z_shift(chunk, kz)
                for kx in range(X):
                    pieces.append(x_shift(column, kx))
            return pieces

        def fsdp_place(pieces):
            rows, cols = pieces[0].shape
            moves = []
            for n in range(F):
                kz, kx = n // X, n % X
                where = lax.rem(z - kz + Z, Z) * X + lax.rem(x - kx + X, X)
                moves.append((n, 0, rows, 0, cols, where * rows, 0))
            return assemble(pieces, moves, (F * rows, cols))

        def fsdp_scatter(grads):
            rows, cols = grads.shape[0] // F, grads.shape[1]
            view = grads.reshape(Z, X, rows, cols)
            total = lax.dynamic_index_in_dim(view, x, 1, keepdims=False).astype(f32)
            for kx in range(1, X):
                sent = lax.dynamic_index_in_dim(view, lax.rem(x + kx, X), 1, keepdims=False)
                total = total + x_shift(sent.astype(bf16), kx).astype(f32)
            low = total.astype(bf16)
            own = lax.dynamic_index_in_dim(low, z, 0, keepdims=False).astype(f32)
            for kz in range(1, Z):
                sent = lax.dynamic_index_in_dim(low, lax.rem(z + kz, Z), 0, keepdims=False)
                own = own + z_shift(sent, kz).astype(f32)
            return own.astype(bf16)

        def finish(own):
            rows, cols = own.shape
            pieces = seq_gather(own)
            moves = [
                (n, 0, rows, 0, cols, seq_of(k, e) * rows, 0)
                for n, (k, e) in enumerate(relative)
            ]
            return assemble(pieces, moves, (S * rows, cols)).reshape(S, rows, cols).astype(f32)

        def pick(array, start, size):
            return lax.dynamic_slice_in_dim(array, start, size, 1)

        small_list = [
            self_query_bias, self_value_bias, self_out_bias, cross_query_bias, memory_value_bias,
            cross_out_bias, ffn_out_bias, norm_gain.reshape(-1), norm_bias.reshape(-1), ffn_in_bias,
        ]
        small = jnp.concatenate(small_list)
        small = lax.all_to_all(
            jnp.broadcast_to(small[None], (F, small.shape[0])), "fsdp", 0, 0, tiled=True
        ).astype(f32)
        smalls = []
        at = 0
        for _ in range(7):
            smalls.append(small[:, at : at + shard].reshape(D))
            at += shard
        b_query, b_value, b_attn_out, b_cross_q, b_mem_value, b_cross_out, b_ffn_out = smalls
        gains = small[:, at : at + 3 * shard].reshape(F, 3, shard).swapaxes(0, 1).reshape(3, D)
        at += 3 * shard
        shifts = small[:, at : at + 3 * shard].reshape(F, 3, shard).swapaxes(0, 1).reshape(3, D)
        at += 3 * shard
        b_ffn_in = lax.dynamic_index_in_dim(
            small[:, at:].reshape(F, S, fw), s, 1, keepdims=False
        ).reshape(F * fw)

        def group_row(row):
            return lax.dynamic_slice_in_dim(row, s * hw, hw, 0)

        chunk_qkv = jnp.concatenate(
            [pick(self_in_weight, m * D + s * hw, hw) for m in range(3)], axis=1
        )
        chunk_mid = jnp.concatenate(
            [pick(memory_weight, m * D + s * hw, hw) for m in range(2)]
            + [pick(cross_query_weight, s * hw, hw)],
            axis=1,
        )
        chunk_out = jnp.concatenate(
            [
                lax.dynamic_slice_in_dim(w, s * part, part, 0)
                for w in (self_out_weight, cross_out_weight)
            ],
            axis=0,
        )
        chunk_fin = lax.dynamic_index_in_dim(
            ffn_in_weight.reshape(shard, F, S, fw), s, 2, keepdims=False
        ).reshape(shard, F * fw)
        chunk_fout = lax.dynamic_slice_in_dim(ffn_out_weight, s * fw, fw, 0)

        got_qkv = fsdp_gather(chunk_qkv)
        x_blocks = seq_gather(hidden_in)
        got_mid = fsdp_gather(after(chunk_mid, got_qkv[-1]))
        m_blocks = seq_gather(after(memory, x_blocks[-1]))
        got_out = fsdp_gather(after(chunk_out, got_qkv[-1]))
        got_fin = fsdp_gather(after(chunk_fin, got_mid[-1]))
        got_fout = fsdp_gather(after(chunk_fout, got_fin[-1]))

        w_qkv = fsdp_place(got_qkv)
        block_moves = [
            (n, 0, t, 0, D, seq_of(k, e) * t, 0) for n, (k, e) in enumerate(relative)
        ]
        x_all = assemble(x_blocks, block_moves, (T, D))
        qkv_bias = jnp.concatenate([group_row(b_query), jnp.zeros((hw,), f32), group_row(b_value)])
        qkv = (dot(x_all, w_qkv, nn) + qkv_bias).astype(bf16)
        q_self, k_self, v_self = (qkv[:, m * hw : (m + 1) * hw] for m in range(3))
        self_attn, self_lse = attend_forward(q_self, k_self, v_self, lengths, True)

        w_mid = fsdp_place(got_mid)
        w_mem, cq_quarter = w_mid[:, : 2 * hw], w_mid[:, 2 * hw :]
        m_all = jnp.concatenate(m_blocks, axis=0)
        mem_bias = jnp.concatenate([jnp.zeros((hw,), f32), group_row(b_mem_value)])
        kv_mem = (dot(m_all, w_mem, nn) + mem_bias).astype(bf16)

        def all_rows(parts_of):
            return assemble(
                parts_of,
                [(n, 0, t, 0, hw, 0, seq_of(k, e) * hw) for n, (k, e) in enumerate(relative)],
                (t, D),
            )

        def heads_to_rows(array):
            blocks = array.reshape(S, t, hw)
            mine = []
            for k, e in relative:
                target = lax.rem(y + k, Y) * CORES + (c if e == 0 else 1 - c)
                sent = lax.dynamic_index_in_dim(blocks, target, 0, keepdims=False)
                sent = y_shift(sent, k)
                mine.append(core_swap(sent) if e else sent)
            return all_rows(mine)

        def rows_to_heads(array):
            mine = []
            for k, e in relative:
                target = lax.rem(y + k, Y) * CORES + (c if e == 0 else 1 - c)
                sent = y_shift(pick(array, target * hw, hw), k)
                mine.append(core_swap(sent) if e else sent)
            return assemble(
                mine,
                [(n, 0, t, 0, hw, seq_of(k, e) * t, 0) for n, (k, e) in enumerate(relative)],
                (T, hw),
            )

        attn_tok = heads_to_rows(self_attn)
        mem_chips = [y_shift(kv_mem, k) for k in range(Y)]
        mem_key = jnp.concatenate([m[:, :hw] for m in mem_chips], axis=1)
        mem_value = jnp.concatenate([m[:, hw:] for m in mem_chips], axis=1)

        out_quarter = fsdp_place(got_out)
        out_pieces = seq_gather(out_quarter)
        own_moves = [[], []]
        for n, (k, e) in enumerate(relative):
            for which in range(2):
                for shard_index in range(F):
                    own_moves[which].append(
                        (
                            n, shard_index * 2 * part + which * part, part, 0, D,
                            shard_index * shard + seq_of(k, e) * part, 0,
                        )
                    )
        w_attn_out = assemble(out_pieces, own_moves[0], (D, D))
        w_cross_out = assemble(out_pieces, own_moves[1], (D, D))
        cq_pieces = seq_gather(cq_quarter)
        w_cross_q = jnp.concatenate(cq_pieces, axis=1)
        b_cq = jnp.concatenate(
            [lax.dynamic_slice_in_dim(b_cross_q, seq_of(k, e) * hw, hw, 0) for k, e in relative]
        )
        half = Y * hw

        x_float = hidden_in.astype(f32)
        branch = dot(attn_tok, w_attn_out, nn) + b_attn_out
        first, normed_one, inverse_one = layer_norm(
            alpha_scale * x_float + branch, gains[0], shifts[0]
        )
        first_low = first.astype(bf16)
        cq_rows = (dot(first_low, w_cross_q, nn) + b_cq).astype(bf16)

        cross_q = jnp.concatenate([cq_rows[:, :half], core_swap(cq_rows[:, half:])], axis=0)
        cross_attn, cross_lse = attend_forward(cross_q, mem_key, mem_value, lengths, False)
        cross_other = core_swap(cross_attn[t:])
        cross_tok = assemble(
            [cross_attn, cross_other],
            [(e, 0, t, k * hw, hw, 0, seq_of(k, e) * hw) for k, e in relative],
            (t, D),
        )
        cross_branch = dot(cross_tok, w_cross_out, nn) + b_cross_out
        second, normed_two, inverse_two = layer_norm(
            alpha_scale * first + cross_branch, gains[1], shifts[1]
        )
        second_low = second.astype(bf16)

        w_fin = fsdp_place(got_fin)
        w_fout = fsdp_place(got_fout)
        second_all = jnp.concatenate(seq_gather(second_low), axis=0)
        pre_act = dot(second_all, w_fin, nn) + b_ffn_in
        act_value, act_slope = gelu_both(pre_act)
        hidden_low = act_value.astype(bf16)
        ffn_part = dot(hidden_low, w_fout, nn)

        def by_owner(array):
            return {ke: array[n * t : (n + 1) * t] for n, ke in enumerate(relative)}

        ffn_branch = seq_scatter(by_owner(ffn_part)) + b_ffn_out
        result, normed_three, inverse_three = layer_norm(
            alpha_scale * second + ffn_branch, gains[2], shifts[2]
        )
        layer_out = result.astype(bf16)

        d_three, gain_three, shift_three = norm_back(
            out_grad.astype(f32), normed_three, inverse_three, gains[2]
        )
        d_ffn = d_three.astype(bf16)
        d_ffn_all = jnp.concatenate(seq_gather(d_ffn), axis=0)
        d_hidden = dot(d_ffn_all, w_fout, nt)
        d_pre = (act_slope * d_hidden).astype(bf16)
        d_second_part = dot(d_pre, w_fin, nt)
        d_second = alpha_scale * d_three + seq_scatter(by_owner(d_second_part))
        grad_fout = dot(hidden_low, d_ffn_all, tn).astype(bf16)
        own_fout = fsdp_scatter(grad_fout)
        grad_fin = dot(second_all, d_pre, tn).astype(bf16)
        own_fin = fsdp_scatter(grad_fin)

        d_two, gain_two, shift_two = norm_back(d_second, normed_two, inverse_two, gains[1])
        d_cross = d_two.astype(bf16)
        d_cross_tok = dot(d_cross, w_cross_out, nt).astype(bf16)
        keep, send = (
            jnp.concatenate([pick(d_cross_tok, seq_of(k, e) * hw, hw) for k in range(Y)], axis=1)
            for e in range(CORES)
        )
        d_cross_heads = jnp.concatenate([keep, core_swap(send)], axis=0)
        dq_cross, dk_mem, dv_mem = attend_back(
            cross_q, mem_key, mem_value, d_cross_heads, cross_lse, lengths, False
        )
        d_cq_rows = jnp.concatenate([dq_cross[:t], core_swap(dq_cross[t:])], axis=1)
        d_first = alpha_scale * d_two + dot(d_cq_rows, w_cross_q, nt)
        grad_cross_out = dot(cross_tok, d_cross, tn)
        grad_cq = dot(first_low, d_cq_rows, tn)
        d_mem = None
        for k in range(Y):
            sent = jnp.concatenate([d[:, k * hw : (k + 1) * hw] for d in (dk_mem, dv_mem)], axis=1)
            got = y_shift(sent, -k).astype(f32)
            d_mem = got if d_mem is None else d_mem + got
        d_mem = d_mem.astype(bf16)
        grad_mem = dot(m_all, d_mem, tn).astype(bf16)
        memory_grad = seq_scatter(by_owner(dot(d_mem, w_mem, nt))).astype(bf16)

        d_one, gain_one, shift_one = norm_back(d_first, normed_one, inverse_one, gains[0])
        d_branch = d_one.astype(bf16)
        d_attn_heads = rows_to_heads(dot(d_branch, w_attn_out, nt).astype(bf16))
        grad_self_out = dot(attn_tok, d_branch, tn)
        dq_self, dk_self, dv_self = attend_back(
            q_self, k_self, v_self, d_attn_heads, self_lse, lengths, True
        )
        d_qkv = jnp.concatenate([dq_self, dk_self, dv_self], axis=1)
        grad_qkv = dot(x_all, d_qkv, tn).astype(bf16)
        own_qkv = fsdp_scatter(grad_qkv)
        input_part = dot(d_qkv, w_qkv, nt).reshape(S, t, D)
        input_sum = seq_scatter(
            {
                (k, e): lax.dynamic_index_in_dim(input_part, seq_of(k, e), 0, keepdims=False)
                for k, e in relative
            }
        )
        input_grad = (alpha_scale * d_one + input_sum).astype(bf16)

        def out_parts(grad):
            view = grad.astype(bf16).reshape(F, S, part, D)
            return {
                (k, e): lax.dynamic_index_in_dim(view, seq_of(k, e), 1, keepdims=False)
                for k, e in relative
            }

        own_cross_out = seq_scatter(out_parts(grad_cross_out)).astype(bf16)
        own_self_out = seq_scatter(out_parts(grad_self_out)).astype(bf16)
        own_cq = seq_scatter(
            {ke: grad_cq[:, n * hw : (n + 1) * hw] for n, ke in enumerate(relative)}
        ).astype(bf16)
        own_mid = fsdp_scatter(jnp.concatenate([grad_mem, own_cq], axis=1))
        own_out = fsdp_scatter(
            jnp.concatenate([own_self_out, own_cross_out], axis=1).reshape(F * 2 * part, D)
        )

        all_fout = finish(own_fout).reshape(S * fw, D)
        all_fin = (
            finish(own_fin).reshape(S, shard, F, fw).transpose(1, 2, 0, 3).reshape(shard, FF)
        )
        all_mid = finish(own_mid)
        all_mem = (
            all_mid[:, :, : 2 * hw]
            .reshape(S, shard, 2, hw)
            .transpose(1, 2, 0, 3)
            .reshape(shard, 2 * D)
        )
        all_cq = all_mid[:, :, 2 * hw :].transpose(1, 0, 2).reshape(shard, D)
        all_out = finish(own_out).reshape(S, 2, part, D)
        all_self_out = all_out[:, 0].reshape(shard, D)
        all_cross_out = all_out[:, 1].reshape(shard, D)
        all_qkv = (
            finish(own_qkv).reshape(S, shard, 3, hw).transpose(1, 2, 0, 3).reshape(shard, 3 * D)
        )

        def spread(row):
            return lax.dynamic_update_slice_in_dim(jnp.zeros((D,), f32), row, s * hw, 0)

        d_cq_sum = column_sum(d_cq_rows)
        cq_bias = jnp.zeros((D,), f32)
        for n, (k, e) in enumerate(relative):
            cq_bias = lax.dynamic_update_slice_in_dim(
                cq_bias, d_cq_sum[n * hw : (n + 1) * hw], seq_of(k, e) * hw, 0
            )
        fin_bias = lax.dynamic_update_slice_in_dim(
            jnp.zeros((F, S, fw), f32), column_sum(d_pre).reshape(F, 1, fw), s, 1
        ).reshape(F, S * fw)
        small_grads = jnp.concatenate(
            [
                row.reshape(F, shard)
                for row in (
                    spread(column_sum(dq_self)), spread(column_sum(dv_self)), column_sum(d_branch),
                    cq_bias, spread(column_sum(d_mem[:, hw:])), column_sum(d_cross),
                    column_sum(d_ffn), gain_one, gain_two, gain_three, shift_one, shift_two,
                    shift_three,
                )
            ]
            + [fin_bias],
            axis=1,
        )
        small_own = jnp.sum(lax.all_to_all(small_grads, "fsdp", 0, 0, tiled=True), axis=0)
        small_own = lax.psum(small_own, "seq")
        rows = [small_own[n * shard : (n + 1) * shard] for n in range(13)]
        return (
            layer_out[None],
            input_grad[None],
            memory_grad[None],
            all_qkv,
            rows[0],
            rows[1],
            all_self_out,
            rows[2],
            all_cq,
            rows[3],
            all_mem,
            rows[4],
            all_cross_out,
            rows[5],
            all_fin,
            small_own[13 * shard :],
            all_fout,
            rows[6],
            jnp.stack(rows[7:10]),
            jnp.stack(rows[10:13]),
        )

    by_row, rows_1d = P("fsdp", None), P("fsdp")
    tokens, norms = P("fsdp", "seq", None), P(None, "fsdp")
    in_specs = (
        tokens, tokens, rows_1d, tokens, by_row, rows_1d, rows_1d, by_row, rows_1d, by_row, rows_1d,
        by_row, rows_1d, by_row, rows_1d, by_row, rows_1d, by_row, rows_1d, norms, norms,
    )
    out_specs = (
        tokens, tokens, tokens, by_row, rows_1d, rows_1d, by_row, rows_1d, by_row, rows_1d, by_row,
        rows_1d, by_row, rows_1d, by_row, rows_1d, by_row, rows_1d, norms, norms,
    )
    return jax.shard_map(local, mesh=mesh, in_specs=in_specs, out_specs=out_specs, check_vma=False)
```

time: 1710 us -> 640 us (0.37)
  waiting for transfers between devices: 1020 us -> 161 us
  blocking collectives: 257 us -> 16.7 us
  Pallas kernels: 0 us -> 123 us
  matrix products: 175 us -> 64.5 us
  starting transfers between devices: 36.2 us -> 114 us
  local copies, waits for them, and re-layouts: 118 us -> 90.7 us
  other arithmetic: 80.6 us -> 57.3 us
    reduce_scatter x5 -> x0, waiting for transfers between devices: 515 us -> none  [the longest x1 152 us: local(): lax.psum_scatter(grad_ffn_in.astype(jnp.bfloat16), 'fsdp', scatter_dimens...]
    all_gather x7 -> x0, waiting for transfers between devices: 243 us -> none  [the longest x1 117 us: local(): lax.all_gather(ffn_out_weight, 'fsdp', axis=0, tiled=True)]
    unnamed x21 -> x0, waiting for transfers between devices: 212 us -> none
    all_gather x10 -> x0, blocking collectives: 188 us -> none  [the longest x1 26.5 us: local(): lax.all_gather(ffn_in_bias, 'fsdp', axis=0, tiled=True)]
    ppermute x0 -> x123, waiting for transfers between devices: none -> 161 us  [the longest x24 56.9 us: y_shift(): return lax.ppermute(array, 'seq', y_perm(k % Y)) if k % Y else array]
    pallas_call x0 -> x20, Pallas kernels: none -> 123 us  [the longest x16 50.1 us: assemble(): pl.pallas_call(kernel, grid_spec=pltpu.PrefetchScalarGridSpec(num_scalar_...]
    dot_general x49 -> x21, matrix products: 175 us -> 64.5 us  [dot(): lax.dot_general(left, right, (dims, ((), ())), preferred_element_type=f32)]
    ppermute x0 -> x123, starting transfers between devices: none -> 106 us  [the longest x30 46.8 us: z_shift(): return lax.ppermute(array, 'fsdp', z_perm(k % Z)) if k % Z else array]
  transfers between devices with their start and end apart: 26 -> 125, of which waited for: 18 -> 33; matrix products, arithmetic and copies ran while one was open for 15% -> 28% of each run, Pallas kernels for 0% -> 19%
where the time goes in v1:
time: 640 us; the launch traced here: 632 us
  waiting for transfers between devices  161 us (25%)
  Pallas kernels  123 us (19%)
  starting transfers between devices  114 us (18%)
  local copies, waits for them, and re-layouts  90.7 us (14%)
  matrix products  64.5 us (10%)
  other arithmetic  57.3 us (9%)
  blocking collectives  16.7 us (3%)
    dot_general x21, matrix products, dot(): lax.dot_general(left, right, (dims, ((), ())), preferred_element_type=f32)  64.5 us
    ppermute x24, waiting for transfers between devices, y_shift(): return lax.ppermute(array, 'seq', y_perm(k % Y)) if k % Y else array  56.9 us
    ppermute x25, waiting for transfers between devices, x_shift(): return lax.ppermute(array, 'fsdp', x_perm(k % X)) if k % X else array  52.3 us
    pallas_call x16, Pallas kernels, assemble(): pl.pallas_call(kernel, grid_spec=pltpu.PrefetchScalarGridSpec(num_scalar_...  50.1 us
    ppermute x30, waiting for transfers between devices, z_shift(): return lax.ppermute(array, 'fsdp', z_perm(k % Z)) if k % Z else array  49.7 us
    ppermute x30, starting transfers between devices, z_shift(): return lax.ppermute(array, 'fsdp', z_perm(k % Z)) if k % Z else array  46.8 us
    pallas_call x2, Pallas kernels, attend_back(): pl.pallas_call(functools.partial(backward_kernel, causal, heads, chunk),...  39.8 us
    pallas_call x2, Pallas kernels, attend_forward(): pl.pallas_call(functools.partial(forward_kernel, causal, heads, chunk), g...  33 us
  transfers between devices with their start and end apart: 125, of which 33 were waited for; matrix products, arithmetic and copies ran while one was open for 28% of the time, Pallas kernels for 19%

profile of v1, /device:TPU:0, one launch (start us, length us, event | category | flops | bytes accessed | tf_op | source)
XLA Modules:
  0.0 631.9 jit_solution(10646481059179974928)
XLA Ops:
  1.8 5.1 collective-permute-start.8
  19.9 4.1 all-to-all-start
  34.7 3.8 collective-permute-start.19
  51.4 3.5 collective-permute-done.14.refs_1_
  61.0 3.4 shard_map.357
  66.7 3.0 shard_map.360.refs_0_
  76.4 3.6 shard_map.356
  80.0 3.4 add_convert_fusion
  84.5 14.6 %shard_map.358 = (bf16[1024,256]{1,0:T(8,128)(2,1)}, f32[2,2,1024]{2,1,0:T(2,128)}) custom-call(s32[1]{0:T(128)S(6)} %copy.161.len_ref, bf16[1024,256]{1,0:T(8,128)(2,1)} %get-tuple-element.126.q_ref, bf16[1024,256]{1,0:T(8,128)(2,1)} %get-tuple-element.125.k_ref, bf16[1024,256]{1,0:T(8,128)(2,1)} %get-tuple-element.124.v_ref), custom_call_target="tpu_custom_call" | custom-call | flops 1073741824 | bytes 2097152 | tf_op jit(solution)/shard_map/pallas_call | solution.py:207
  103.7 4.3 collective-permute-done.26.refs_3_
  108.0 6.1 collective-permute-done.12
  115.4 3.5 shard_map.362
  123.6 2.7 shard_map.359
  130.2 5.3 collective-permute-done.31
  138.0 3.8 add_convert_fusion.2
  144.0 3.8 shard_map.361
  155.4 12.3 %collective-permute-done.38 = bf16[1024,512]{1,0:T(8,128)(2,1)S(1)} collective-permute-done((bf16[1024,512]{1,0:T(8,128)(2,1)}, bf16[1024,512]{1,0:T(8,128)(2,1)S(1)}, u32[]{:S(2)}, u32[]{:S(2)}) %collective-permute-start.38) | collective-permute-done | bytes 1048608 | tf_op jit(solution)/shard_map/ppermute | solution.py:362
  169.3 18.4 %shard_map.363 = (bf16[512,512]{1,0:T(8,128)(2,1)}, f32[4,2,512]{2,1,0:T(2,128)}) custom-call(s32[1]{0:T(128)S(6)} %copy.161.len_ref, bf16[512,512]{1,0:T(8,128)(2,1)} %pad_maximum_fusion.8.q_ref, bf16[1024,512]{1,0:T(8,128)(2,1)} %get-tuple-element.223.k_ref, bf16[1024,512]{1,0:T(8,128)(2,1)} %get-tuple-element.224.v_ref), custom_call_target="tpu_custom_call" | custom-call | flops 1073741824 | bytes 4194304 | tf_op jit(solution)/shard_map/pallas_call | solution.py:207
  191.7 3.8 shard_map.365
  204.7 5.0 collective-permute-done.46.refs_4_
  211.9 4.2 collective-permute-start.53
  216.0 3.1 collective-permute-done.47.refs_5_
  220.4 3.0 collective-permute-done.45.refs_3_
  224.9 9.3 %collective-permute-done.53.refs_4_ = bf16[128,1024]{1,0:T(8,128)(2,1)S(1)} collective-permute-done((bf16[128,1024]{1,0:T(8,128)(2,1)S(1)}, bf16[128,1024]{1,0:T(8,128)(2,1)S(1)}, u32[]{:S(2)}, u32[]{:S(2)}) %collective-permute-start.53) | collective-permute-done | bytes 262176 | tf_op jit(solution)/shard_map/ppermute | solution.py:365
  238.0 3.6 shard_map.366
  243.4 5.6 collective-permute-done.54.refs_5_
  249.1 3.6 collective-permute-done.52.refs_3_
  253.4 3.6 shard_map.367
  257.1 3.9 fusion.69
  261.0 2.8 fusion.109
  267.1 13.0 %collective-permute-done.58 = bf16[256,1024]{1,0:T(8,128)(2,1)S(1)} collective-permute-done((bf16[256,1024]{1,0:T(8,128)(2,1)S(1)}, bf16[256,1024]{1,0:T(8,128)(2,1)S(1)}, u32[]{:S(2)}, u32[]{:S(2)}) %collective-permute-start.58) | collective-permute-done | bytes 524320 | tf_op jit(solution)/shard_map/ppermute | solution.py:362
  284.9 12.5 %collective-permute-done.60 = bf16[256,1024]{1,0:T(8,128)(2,1)} collective-permute-done((bf16[256,1024]{1,0:T(8,128)(2,1)}, bf16[256,1024]{1,0:T(8,128)(2,1)}, u32[]{:S(2)}, u32[]{:S(2)}) %collective-permute-start.60) | collective-permute-done | bytes 524320 | tf_op jit(solution)/shard_map/ppermute | solution.py:362
  299.7 6.0 convolution_convert_fusion
  307.2 7.1 %convert_reduce_fusion = (f32[1024]{0:T(1024)S(1)}, bf16[1024,1024]{1,0:T(8,128)(2,1)S(1)}) fusion(bf16[1024,1024]{1,0:T(8,128)(2,1)S(1)} %copy-done.25, bf16[256,1024]{1,0:T(8,128)(2,1)} %collective-permute-done.62, bf16[256,1024]{1,0:T(8,128)(2,1)} %collective-permute-done.61, bf16[256,1024]{1,0:T(8,128)(2,1)} %collective-permute-done.60, ...), kind=kOutput, calls=%fused_computation.9 | convolution fusion | flops 2178939904 | bytes 10493952 | tf_op jit(solution)/shard_map/dot_general | solution.py:27
  317.8 3.8 convolution_convert_fusion.1
  325.0 6.8 %collective-permute-done.116 = bf16[4,128,1024]{2,1,0:T(8,128)(2,1)S(1)} collective-permute-done((bf16[4,128,1024]{2,1,0:T(8,128)(2,1)S(1)}, bf16[4,128,1024]{2,1,0:T(8,128)(2,1)S(1)}, u32[]{:S(2)}, u32[]{:S(2)}) %collective-permute-start.116) | collective-permute-done | bytes 1048608 | tf_op jit(solution)/shard_map/ppermute | solution.py:368
  332.4 3.8 collective-permute-start.119
  336.2 17.3 %collective-permute-done.109 = bf16[4,128,1024]{2,1,0:T(8,128)(2,1)S(1)} collective-permute-done((bf16[4,128,1024]{2,1,0:T(8,128)(2,1)S(1)}, bf16[4,128,1024]{2,1,0:T(8,128)(2,1)S(1)}, u32[]{:S(2)}, u32[]{:S(2)}) %collective-permute-start.109) | collective-permute-done | bytes 1048608 | tf_op jit(solution)/shard_map/ppermute | solution.py:368
  354.0 4.2 collective-permute-start.112
  366.5 4.3 collective-permute-done.118
  371.5 2.7 collective-permute-done.112
  375.2 11.4 %collective-permute-done.111 = bf16[128,1024]{1,0:T(8,128)(2,1)S(1)} collective-permute-done((bf16[128,1024]{1,0:T(8,128)(2,1)S(1)}, bf16[128,1024]{1,0:T(8,128)(2,1)S(1)}, u32[]{:S(2)}, u32[]{:S(2)}) %collective-permute-start.111) | collective-permute-done | bytes 262176 | tf_op jit(solution)/shard_map/ppermute | solution.py:365
  389.5 22.7 %shard_map.368 = (bf16[512,512]{1,0:T(8,128)(2,1)}, bf16[1024,512]{1,0:T(8,128)(2,1)}, bf16[1024,512]{1,0:T(8,128)(2,1)}) custom-call(s32[1]{0:T(128)S(6)} %copy.161.len_ref, bf16[512,512]{1,0:T(8,128)(2,1)} %pad_maximum_fusion.8.q_ref, bf16[1024,512]{1,0:T(8,128)(2,1)} %get-tuple-element.223.k_ref, bf16[1024,512]{1,0:T(8,128)(2,1)} %get-tuple-element.224.v_ref, ...), custom_call_target="tpu_custom_call" | custom-call | flops 2684354560 | bytes 8388608 | tf_op jit(solution)/shard_map/pallas_call | solution.py:233
  418.5 3.2 multiply_reduce_fusion.1
  424.3 2.9 fusion.112
  436.4 2.9 shard_map.374
  443.1 2.9 shard_map.375
  446.0 2.8 convert_element_type.561
  451.4 3.1 reshape.366
  458.2 17.1 %shard_map.370 = (bf16[1024,256]{1,0:T(8,128)(2,1)}, bf16[1024,256]{1,0:T(8,128)(2,1)}, bf16[1024,256]{1,0:T(8,128)(2,1)}) custom-call(s32[1]{0:T(128)S(6)} %copy.161.len_ref, bf16[1024,256]{1,0:T(8,128)(2,1)} %get-tuple-element.126.q_ref, bf16[1024,256]{1,0:T(8,128)(2,1)} %get-tuple-element.125.k_ref, bf16[1024,256]{1,0:T(8,128)(2,1)} %get-tuple-element.124.v_ref, ...), custom_call_target="tpu_custom_call" | custom-call | flops 2684354560 | bytes 4194304 | tf_op jit(solution)/shard_map/pallas_call | solution.py:233
  479.1 3.1 convolution_convert_fusion.4
  482.3 3.9 fusion.113
  486.9 2.8 fusion.53
  501.1 4.0 fusion.111
  506.1 4.4 all-to-all-start.1
  510.5 4.0 convolution_convert_fusion.5
  519.0 16.7 %psum.7 = f32[2176]{0:T(1024)S(1)} all-reduce(f32[2176]{0:T(1024)S(1)} %reduce_sum.269), channel_id=1, replica_groups=mesh['seq'=4,'fsdp'=8] {'seq'}, use_global_device_ids=true, to_apply=%region_27.28 | all-reduce | flops 2176 | bytes 17408 | tf_op jit(solution)/shard_map/psum | solution.py:751
  556.3 7.1 %collective-permute-done.81 = bf16[128,768]{1,0:T(8,128)(2,1)} collective-permute-done((bf16[128,768]{1,0:T(8,128)(2,1)}, bf16[128,768]{1,0:T(8,128)(2,1)}, u32[]{:S(2)}, u32[]{:S(2)}) %collective-permute-start.81) | collective-permute-done | bytes 196640 | tf_op jit(solution)/shard_map/ppermute | solution.py:365
  567.5 3.5 collective-permute-start.95
  576.3 4.8 collective-permute-done.94
  583.5 6.5 %collective-permute-done.73 = bf16[256,1024]{1,0:T(8,128)(2,1)S(1)} collective-permute-done((bf16[256,1024]{1,0:T(8,128)(2,1)S(1)}, bf16[256,1024]{1,0:T(8,128)(2,1)S(1)}, u32[]{:S(2)}, u32[]{:S(2)}) %collective-permute-start.73) | collective-permute-done | bytes 524320 | tf_op jit(solution)/shard_map/ppermute | solution.py:362
  591.0 4.0 collective-permute-start.105
  598.0 2.8 shard_map.371
  621.4 2.8 shard_map.373
  (632 shorter events, 251.3 us)
Async XLA Ops:
  1.8 24.7 %collective-permute-start.8 = (bf16[128,768]{1,0:T(8,128)(2,1)S(1)}, bf16[128,768]{1,0:T(8,128)(2,1)}, u32[]{:S(2)}, u32[]{:S(2)}) collective-permute-start(bf16[128,768]{1,0:T(8,128)(2,1)S(1)} %pad_maximum_fusion.18.refs_0_), channel_id=1, source_target_pairs={{0,6},{1,7},{2,0},{3,1},{4,2},{5,3},{6,4},{7,5},{8,14},{9,15},{10,... | collective-permute-start | bytes 589832 | tf_op jit(solution)/shard_map/ppermute | solution.py:365
  6.9 21.7 %collective-permute-start.6 = (bf16[128,768]{1,0:T(8,128)(2,1)S(1)}, bf16[128,768]{1,0:T(8,128)(2,1)}, u32[]{:S(2)}, u32[]{:S(2)}) collective-permute-start(bf16[128,768]{1,0:T(8,128)(2,1)S(1)} %pad_maximum_fusion.18.refs_0_), channel_id=1, source_target_pairs={{0,4},{1,5},{2,6},{3,7},{4,0},{5,1},{6,2},{7,3},{8,12},{9,13},{10,... | collective-permute-start | bytes 589832 | tf_op jit(solution)/shard_map/ppermute | solution.py:365
  6.9 23.3 %collective-permute-start.4 = (bf16[128,768]{1,0:T(8,128)(2,1)S(1)}, bf16[128,768]{1,0:T(8,128)(2,1)}, u32[]{:S(2)}, u32[]{:S(2)}) collective-permute-start(bf16[128,768]{1,0:T(8,128)(2,1)S(1)} %pad_maximum_fusion.18.refs_0_), channel_id=1, source_target_pairs={{0,2},{1,3},{2,4},{3,5},{4,6},{5,7},{6,0},{7,1},{8,10},{9,11},{10,... | collective-permute-start | bytes 589832 | tf_op jit(solution)/shard_map/ppermute | solution.py:365
  7.9 30.6 %collective-permute-start.3 = (bf16[128,768]{1,0:T(8,128)(2,1)S(1)}, bf16[128,768]{1,0:T(8,128)(2,1)}, u32[]{:S(2)}, u32[]{:S(2)}) collective-permute-start(bf16[128,768]{1,0:T(8,128)(2,1)S(1)} %pad_maximum_fusion.18.refs_0_), channel_id=1, source_target_pairs={{0,1},{1,0},{2,3},{3,2},{4,5},{5,4},{6,7},{7,6},{8,9},{9,8},{10,11... | collective-permute-start | bytes 589832 | tf_op jit(solution)/shard_map/ppermute | solution.py:368
  19.9 27.5 %all-to-all-start = ((bf16[8,2,1088]{2,1,0:T(2,128)(2,1)}), bf16[8,2,1088]{2,1,0:T(2,128)(2,1)}, u32[]{:S(2)}, u32[]{:S(2)}) async-start(bf16[8,2,1088]{2,1,0:T(2,128)(2,1)} %reshape.378), calls=%async_computation | async-start | bytes 73728 | tf_op jit(solution)/shard_map/all_to_all | solution.py:474
  24.0 27.4 %collective-permute-start = (bf16[256,1024]{1,0:T(8,128)(2,1)}, bf16[256,1024]{1,0:T(8,128)(2,1)}, u32[]{:S(2)}, u32[]{:S(2)}) collective-permute-start(bf16[256,1024]{1,0:T(8,128)(2,1)} %bitcast.408), channel_id=1, source_target_pairs={{0,16},{8,24},{16,0},{24,8},{1,17},{9,25},{17,1},{25,9},{2,18},{10... | collective-permute-start | bytes 1572872 | tf_op jit(solution)/shard_map/ppermute | solution.py:362
  30.2 18.2 %collective-permute-start.5 = (bf16[128,768]{1,0:T(8,128)(2,1)}, bf16[128,768]{1,0:T(8,128)(2,1)}, u32[]{:S(2)}, u32[]{:S(2)}) collective-permute-start(bf16[128,768]{1,0:T(8,128)(2,1)} %collective-permute-done.4.refs_2_), channel_id=1, source_target_pairs={{0,1},{1,0},{2,3},{3,2},{4,5},{5,4},{6,7},{7,6},{8,9},{9,8},{10,11... | collective-permute-start | bytes 589832 | tf_op jit(solution)/shard_map/ppermute | solution.py:368
  48.4 21.3 %collective-permute-start.1 = (bf16[256,1024]{1,0:T(8,128)(2,1)S(1)}, bf16[256,1024]{1,0:T(8,128)(2,1)S(1)}, u32[]{:S(2)}, u32[]{:S(2)}) collective-permute-start(bf16[256,1024]{1,0:T(8,128)(2,1)S(1)} %bitcast.410), channel_id=1, source_target_pairs={{0,8},{8,0},{16,24},{24,16},{1,9},{9,1},{17,25},{25,17},{2,10},{10... | collective-permute-start | bytes 1572872 | tf_op jit(solution)/shard_map/ppermute | solution.py:359
  51.4 24.1 %collective-permute-start.2 = (bf16[256,1024]{1,0:T(8,128)(2,1)}, bf16[256,1024]{1,0:T(8,128)(2,1)S(1)}, u32[]{:S(2)}, u32[]{:S(2)}) collective-permute-start(bf16[256,1024]{1,0:T(8,128)(2,1)} %collective-permute-done.refs_1_), channel_id=1, source_target_pairs={{0,8},{8,0},{16,24},{24,16},{1,9},{9,1},{17,25},{25,17},{2,10},{10... | collective-permute-start | bytes 1572872 | tf_op jit(solution)/shard_map/ppermute | solution.py:359
  65.3 33.9 %collective-permute-start.25 = (bf16[128,768]{1,0:T(8,128)(2,1)S(1)}, bf16[128,768]{1,0:T(8,128)(2,1)S(1)}, u32[]{:S(2)}, u32[]{:S(2)}) collective-permute-start(bf16[128,768]{1,0:T(8,128)(2,1)S(1)} %pad_maximum_fusion.19.refs_0_), channel_id=1, source_target_pairs={{0,2},{1,3},{2,4},{3,5},{4,6},{5,7},{6,0},{7,1},{8,10},{9,11},{10,... | collective-permute-start | bytes 589832 | tf_op jit(solution)/shard_map/ppermute | solution.py:365
  69.8 32.5 %collective-permute-start.24 = (bf16[128,768]{1,0:T(8,128)(2,1)S(1)}, bf16[128,768]{1,0:T(8,128)(2,1)S(1)}, u32[]{:S(2)}, u32[]{:S(2)}) collective-permute-start(bf16[128,768]{1,0:T(8,128)(2,1)S(1)} %pad_maximum_fusion.19.refs_0_), channel_id=1, source_target_pairs={{0,1},{1,0},{2,3},{3,2},{4,5},{5,4},{6,7},{7,6},{8,9},{9,8},{10,11... | collective-permute-start | bytes 589832 | tf_op jit(solution)/shard_map/ppermute | solution.py:368
  71.3 31.5 %collective-permute-start.30 = (bf16[128,768]{1,0:T(8,128)(2,1)S(1)}, bf16[128,768]{1,0:T(8,128)(2,1)S(1)}, u32[]{:S(2)}, u32[]{:S(2)}) collective-permute-start(bf16[128,768]{1,0:T(8,128)(2,1)S(1)} %collective-permute-done.29.refs_6_), channel_id=1, source_target_pairs={{0,1},{1,0},{2,3},{3,2},{4,5},{5,4},{6,7},{7,6},{8,9},{9,8},{10,11... | collective-permute-start | bytes 589832 | tf_op jit(solution)/shard_map/ppermute | solution.py:368
  74.1 29.6 %collective-permute-start.28 = (bf16[128,768]{1,0:T(8,128)(2,1)S(1)}, bf16[128,768]{1,0:T(8,128)(2,1)S(1)}, u32[]{:S(2)}, u32[]{:S(2)}) collective-permute-start(bf16[128,768]{1,0:T(8,128)(2,1)S(1)} %collective-permute-done.27.refs_4_), channel_id=1, source_target_pairs={{0,1},{1,0},{2,3},{3,2},{4,5},{5,4},{6,7},{7,6},{8,9},{9,8},{10,11... | collective-permute-start | bytes 589832 | tf_op jit(solution)/shard_map/ppermute | solution.py:368
  75.6 46.5 %collective-permute-start.21 = (bf16[512,1024]{1,0:T(8,128)(2,1)}, bf16[512,1024]{1,0:T(8,128)(2,1)S(1)}, u32[]{:S(2)}, u32[]{:S(2)}) collective-permute-start(bf16[512,1024]{1,0:T(8,128)(2,1)} %shard_map.360.refs_0_), channel_id=1, source_target_pairs={{0,16},{8,24},{16,0},{24,8},{1,17},{9,25},{17,1},{25,9},{2,18},{10... | collective-permute-start | bytes 3145736 | tf_op jit(solution)/shard_map/ppermute | solution.py:362
  99.2 22.9 %collective-permute-start.35 = (bf16[256,1024]{1,0:T(8,128)(2,1)S(1)}, bf16[256,1024]{1,0:T(8,128)(2,1)}, u32[]{:S(2)}, u32[]{:S(2)}) collective-permute-start(bf16[256,1024]{1,0:T(8,128)(2,1)S(1)} %bitcast.411), channel_id=1, source_target_pairs={{0,16},{8,24},{16,0},{24,8},{1,17},{9,25},{17,1},{25,9},{2,18},{10... | collective-permute-start | bytes 1572872 | tf_op jit(solution)/shard_map/ppermute | solution.py:362
  108.0 20.2 %collective-permute-start.36 = (bf16[256,1024]{1,0:T(8,128)(2,1)S(1)}, bf16[256,1024]{1,0:T(8,128)(2,1)}, u32[]{:S(2)}, u32[]{:S(2)}) collective-permute-start(bf16[256,1024]{1,0:T(8,128)(2,1)S(1)} %bitcast.412), channel_id=1, source_target_pairs={{0,8},{8,0},{16,24},{24,16},{1,9},{9,1},{17,25},{25,17},{2,10},{10... | collective-permute-start | bytes 1572872 | tf_op jit(solution)/shard_map/ppermute | solution.py:359
  120.7 21.1 %collective-permute-start.22 = (bf16[512,1024]{1,0:T(8,128)(2,1)S(1)}, bf16[512,1024]{1,0:T(8,128)(2,1)S(1)}, u32[]{:S(2)}, u32[]{:S(2)}) collective-permute-start(bf16[512,1024]{1,0:T(8,128)(2,1)S(1)} %copy-done.3), channel_id=1, source_target_pairs={{0,8},{8,0},{16,24},{24,16},{1,9},{9,1},{17,25},{25,17},{2,10},{10... | collective-permute-start | bytes 3145736 | tf_op jit(solution)/shard_map/ppermute | solution.py:359
  122.1 20.9 %collective-permute-start.23 = (bf16[512,1024]{1,0:T(8,128)(2,1)S(1)}, bf16[512,1024]{1,0:T(8,128)(2,1)S(1)}, u32[]{:S(2)}, u32[]{:S(2)}) collective-permute-start(bf16[512,1024]{1,0:T(8,128)(2,1)S(1)} %collective-permute-done.21.refs_1_), channel_id=1, source_target_pairs={{0,8},{8,0},{16,24},{24,16},{1,9},{9,1},{17,25},{25,17},{2,10},{10... | collective-permute-start | bytes 3145736 | tf_op jit(solution)/shard_map/ppermute | solution.py:359
  128.2 22.3 %collective-permute-start.32 = (bf16[1024,256]{1,0:T(8,128)(2,1)}, bf16[1024,256]{1,0:T(8,128)(2,1)}, u32[]{:S(2)}, u32[]{:S(2)}) collective-permute-start(bf16[1024,256]{1,0:T(8,128)(2,1)} %slice.319), channel_id=1, source_target_pairs={{0,8},{8,0},{16,24},{24,16},{1,9},{9,1},{17,25},{25,17},{2,10},{10... | collective-permute-start | bytes 1572872 | tf_op jit(solution)/shard_map/ppermute | solution.py:359
  135.5 55.3 %collective-permute-start.48 = (bf16[128,1024]{1,0:T(8,128)(2,1)S(1)}, bf16[128,1024]{1,0:T(8,128)(2,1)}, u32[]{:S(2)}, u32[]{:S(2)}) collective-permute-start(bf16[128,1024]{1,0:T(8,128)(2,1)S(1)} %bitcast.402), channel_id=1, source_target_pairs={{0,6},{1,7},{2,0},{3,1},{4,2},{5,3},{6,4},{7,5},{8,14},{9,15},{10,... | collective-permute-start | bytes 786440 | tf_op jit(solution)/shard_map/ppermute | solution.py:365
  141.9 25.9 %collective-permute-start.38 = (bf16[1024,512]{1,0:T(8,128)(2,1)}, bf16[1024,512]{1,0:T(8,128)(2,1)S(1)}, u32[]{:S(2)}, u32[]{:S(2)}) collective-permute-start(bf16[1024,512]{1,0:T(8,128)(2,1)} %add_convert_fusion.2), channel_id=1, source_target_pairs={{0,16},{8,24},{16,0},{24,8},{1,17},{9,25},{17,1},{25,9},{2,18},{10... | collective-permute-start | bytes 3145736 | tf_op jit(solution)/shard_map/ppermute | solution.py:362
  188.7 21.0 %collective-permute-start.46 = (bf16[128,1024]{1,0:T(8,128)(2,1)S(1)}, bf16[128,1024]{1,0:T(8,128)(2,1)}, u32[]{:S(2)}, u32[]{:S(2)}) collective-permute-start(bf16[128,1024]{1,0:T(8,128)(2,1)S(1)} %bitcast.403), channel_id=1, source_target_pairs={{0,4},{1,5},{2,6},{3,7},{4,0},{5,1},{6,2},{7,3},{8,12},{9,13},{10,... | collective-permute-start | bytes 786440 | tf_op jit(solution)/shard_map/ppermute | solution.py:365
  189.0 21.6 %collective-permute-start.44 = (bf16[128,1024]{1,0:T(8,128)(2,1)S(1)}, bf16[128,1024]{1,0:T(8,128)(2,1)}, u32[]{:S(2)}, u32[]{:S(2)}) collective-permute-start(bf16[128,1024]{1,0:T(8,128)(2,1)S(1)} %bitcast.404), channel_id=1, source_target_pairs={{0,2},{1,3},{2,4},{3,5},{4,6},{5,7},{6,0},{7,1},{8,10},{9,11},{10,... | collective-permute-start | bytes 786440 | tf_op jit(solution)/shard_map/ppermute | solution.py:365
  190.8 21.0 %collective-permute-start.49 = (bf16[128,1024]{1,0:T(8,128)(2,1)}, bf16[128,1024]{1,0:T(8,128)(2,1)}, u32[]{:S(2)}, u32[]{:S(2)}) collective-permute-start(bf16[128,1024]{1,0:T(8,128)(2,1)} %collective-permute-done.48.refs_6_), channel_id=1, source_target_pairs={{0,1},{1,0},{2,3},{3,2},{4,5},{5,4},{6,7},{7,6},{8,9},{9,8},{10,11... | collective-permute-start | bytes 786440 | tf_op jit(solution)/shard_map/ppermute | solution.py:368
  202.9 21.5 %collective-permute-start.40 = (bf16[256,1024]{1,0:T(8,128)(2,1)}, bf16[256,1024]{1,0:T(8,128)(2,1)}, u32[]{:S(2)}, u32[]{:S(2)}) collective-permute-start(bf16[256,1024]{1,0:T(8,128)(2,1)} %fusion.48), channel_id=1, source_target_pairs={{0,16},{8,24},{16,0},{24,8},{1,17},{9,25},{17,1},{25,9},{2,18},{10... | collective-permute-start | bytes 1572872 | tf_op jit(solution)/shard_map/ppermute | solution.py:362
  211.9 22.3 %collective-permute-start.53 = (bf16[128,1024]{1,0:T(8,128)(2,1)S(1)}, bf16[128,1024]{1,0:T(8,128)(2,1)S(1)}, u32[]{:S(2)}, u32[]{:S(2)}) collective-permute-start(bf16[128,1024]{1,0:T(8,128)(2,1)S(1)} %constant_dynamic-slice_fusion.8.refs_0_), channel_id=1, source_target_pairs={{0,4},{1,5},{2,6},{3,7},{4,0},{5,1},{6,2},{7,3},{8,12},{9,13},{10,... | collective-permute-start | bytes 786440 | tf_op jit(solution)/shard_map/ppermute | solution.py:365
  224.3 32.7 %collective-permute-start.41 = (bf16[256,1024]{1,0:T(8,128)(2,1)}, bf16[256,1024]{1,0:T(8,128)(2,1)S(1)}, u32[]{:S(2)}, u32[]{:S(2)}) collective-permute-start(bf16[256,1024]{1,0:T(8,128)(2,1)} %fusion.48), channel_id=1, source_target_pairs={{0,8},{8,0},{16,24},{24,16},{1,9},{9,1},{17,25},{25,17},{2,10},{10... | collective-permute-start | bytes 1572872 | tf_op jit(solution)/shard_map/ppermute | solution.py:359
  224.4 32.7 %collective-permute-start.42 = (bf16[256,1024]{1,0:T(8,128)(2,1)}, bf16[256,1024]{1,0:T(8,128)(2,1)}, u32[]{:S(2)}, u32[]{:S(2)}) collective-permute-start(bf16[256,1024]{1,0:T(8,128)(2,1)} %collective-permute-done.40), channel_id=1, source_target_pairs={{0,8},{8,0},{16,24},{24,16},{1,9},{9,1},{17,25},{25,17},{2,10},{10... | collective-permute-start | bytes 1572872 | tf_op jit(solution)/shard_map/ppermute | solution.py:359
  305.7 26.1 %collective-permute-start.116 = (bf16[4,128,1024]{2,1,0:T(8,128)(2,1)S(1)}, bf16[4,128,1024]{2,1,0:T(8,128)(2,1)S(1)}, u32[]{:S(2)}, u32[]{:S(2)}) collective-permute-start(bf16[4,128,1024]{2,1,0:T(8,128)(2,1)S(1)} %dynamic-slice_bitcast_fusion), channel_id=1, source_target_pairs={{0,1},{1,0},{2,3},{3,2},{4,5},{5,4},{6,7},{7,6},{8,9},{9,8},{10,11... | collective-permute-start | bytes 3145736 | tf_op jit(solution)/shard_map/ppermute | solution.py:368
  321.7 31.8 %collective-permute-start.109 = (bf16[4,128,1024]{2,1,0:T(8,128)(2,1)S(1)}, bf16[4,128,1024]{2,1,0:T(8,128)(2,1)S(1)}, u32[]{:S(2)}, u32[]{:S(2)}) collective-permute-start(bf16[4,128,1024]{2,1,0:T(8,128)(2,1)S(1)} %dynamic-slice_bitcast_fusion.1), channel_id=1, source_target_pairs={{0,1},{1,0},{2,3},{3,2},{4,5},{5,4},{6,7},{7,6},{8,9},{9,8},{10,11... | collective-permute-start | bytes 3145736 | tf_op jit(solution)/shard_map/ppermute | solution.py:368
  323.6 30.3 %collective-permute-start.65 = (bf16[256,1024]{1,0:T(8,128)(2,1)S(1)}, bf16[256,1024]{1,0:T(8,128)(2,1)S(1)}, u32[]{:S(2)}, u32[]{:S(2)}) collective-permute-start(bf16[256,1024]{1,0:T(8,128)(2,1)S(1)} %get-tuple-element.121), channel_id=1, source_target_pairs={{0,8},{8,0},{16,24},{24,16},{1,9},{9,1},{17,25},{25,17},{2,10},{10... | collective-permute-start | bytes 1572872 | tf_op jit(solution)/shard_map/ppermute | solution.py:359
  323.8 30.2 %collective-permute-start.64 = (bf16[256,1024]{1,0:T(8,128)(2,1)S(1)}, bf16[256,1024]{1,0:T(8,128)(2,1)S(1)}, u32[]{:S(2)}, u32[]{:S(2)}) collective-permute-start(bf16[256,1024]{1,0:T(8,128)(2,1)S(1)} %fusion.31), channel_id=1, source_target_pairs={{0,16},{8,24},{16,0},{24,8},{1,17},{9,25},{17,1},{25,9},{2,18},{10... | collective-permute-start | bytes 1572872 | tf_op jit(solution)/shard_map/ppermute | solution.py:362
  332.3 33.0 %collective-permute-start.117 = (bf16[128,1024]{1,0:T(8,128)(2,1)S(1)}, bf16[128,1024]{1,0:T(8,128)(2,1)S(1)}, u32[]{:S(2)}, u32[]{:S(2)}) collective-permute-start(bf16[128,1024]{1,0:T(8,128)(2,1)S(1)} %get-tuple-element.128), channel_id=1, source_target_pairs={{0,2},{1,3},{2,4},{3,5},{4,6},{5,7},{6,0},{7,1},{8,10},{9,11},{10,... | collective-permute-start | bytes 786440 | tf_op jit(solution)/shard_map/ppermute | solution.py:365
  332.4 34.0 %collective-permute-start.119 = (bf16[128,1024]{1,0:T(8,128)(2,1)S(1)}, bf16[128,1024]{1,0:T(8,128)(2,1)S(1)}, u32[]{:S(2)}, u32[]{:S(2)}) collective-permute-start(bf16[128,1024]{1,0:T(8,128)(2,1)S(1)} %get-tuple-element.129), channel_id=1, source_target_pairs={{0,6},{1,7},{2,0},{3,1},{4,2},{5,3},{6,4},{7,5},{8,14},{9,15},{10,... | collective-permute-start | bytes 786440 | tf_op jit(solution)/shard_map/ppermute | solution.py:365
  353.5 17.3 %collective-permute-start.118 = (bf16[128,1024]{1,0:T(8,128)(2,1)S(1)}, bf16[128,1024]{1,0:T(8,128)(2,1)S(1)}, u32[]{:S(2)}, u32[]{:S(2)}) collective-permute-start(bf16[128,1024]{1,0:T(8,128)(2,1)S(1)} %get-tuple-element.130), channel_id=1, source_target_pairs={{0,4},{1,5},{2,6},{3,7},{4,0},{5,1},{6,2},{7,3},{8,12},{9,13},{10,... | collective-permute-start | bytes 786440 | tf_op jit(solution)/shard_map/ppermute | solution.py:365
  353.9 17.0 %collective-permute-start.110 = (bf16[128,1024]{1,0:T(8,128)(2,1)S(1)}, bf16[128,1024]{1,0:T(8,128)(2,1)S(1)}, u32[]{:S(2)}, u32[]{:S(2)}) collective-permute-start(bf16[128,1024]{1,0:T(8,128)(2,1)S(1)} %get-tuple-element.131), channel_id=1, source_target_pairs={{0,2},{1,3},{2,4},{3,5},{4,6},{5,7},{6,0},{7,1},{8,10},{9,11},{10,... | collective-permute-start | bytes 786440 | tf_op jit(solution)/shard_map/ppermute | solution.py:365
  354.0 20.2 %collective-permute-start.112 = (bf16[128,1024]{1,0:T(8,128)(2,1)S(1)}, bf16[128,1024]{1,0:T(8,128)(2,1)S(1)}, u32[]{:S(2)}, u32[]{:S(2)}) collective-permute-start(bf16[128,1024]{1,0:T(8,128)(2,1)S(1)} %get-tuple-element.132), channel_id=1, source_target_pairs={{0,6},{1,7},{2,0},{3,1},{4,2},{5,3},{6,4},{7,5},{8,14},{9,15},{10,... | collective-permute-start | bytes 786440 | tf_op jit(solution)/shard_map/ppermute | solution.py:365
  365.3 21.4 %collective-permute-start.111 = (bf16[128,1024]{1,0:T(8,128)(2,1)S(1)}, bf16[128,1024]{1,0:T(8,128)(2,1)S(1)}, u32[]{:S(2)}, u32[]{:S(2)}) collective-permute-start(bf16[128,1024]{1,0:T(8,128)(2,1)S(1)} %get-tuple-element.133), channel_id=1, source_target_pairs={{0,4},{1,5},{2,6},{3,7},{4,0},{5,1},{6,2},{7,3},{8,12},{9,13},{10,... | collective-permute-start | bytes 786440 | tf_op jit(solution)/shard_map/ppermute | solution.py:365
  366.4 22.2 %collective-permute-start.66 = (bf16[256,512]{1,0:T(8,128)(2,1)S(1)}, bf16[256,512]{1,0:T(8,128)(2,1)S(1)}, u32[]{:S(2)}, u32[]{:S(2)}) collective-permute-start(bf16[256,512]{1,0:T(8,128)(2,1)S(1)} %pad_maximum_fusion.17), channel_id=1, source_target_pairs={{0,8},{8,0},{16,24},{24,16},{1,9},{9,1},{17,25},{25,17},{2,10},{10... | collective-permute-start | bytes 786440 | tf_op jit(solution)/shard_map/ppermute | solution.py:359
  370.8 59.1 %collective-permute-start.89 = (bf16[8,32,1024]{2,1,0:T(8,128)(2,1)}, bf16[8,32,1024]{2,1,0:T(8,128)(2,1)}, u32[]{:S(2)}, u32[]{:S(2)}) collective-permute-start(bf16[8,32,1024]{2,1,0:T(8,128)(2,1)} %get-tuple-element.116), channel_id=1, source_target_pairs={{0,8},{8,0},{16,24},{24,16},{1,9},{9,1},{17,25},{25,17},{2,10},{10... | collective-permute-start | bytes 1572872 | tf_op jit(solution)/shard_map/ppermute | solution.py:359
  371.0 70.4 %collective-permute-start.121 = (bf16[128,1024]{1,0:T(8,128)(2,1)S(1)}, bf16[128,1024]{1,0:T(8,128)(2,1)}, u32[]{:S(2)}, u32[]{:S(2)}) collective-permute-start(bf16[128,1024]{1,0:T(8,128)(2,1)S(1)} %fusion.59.refs_0_), channel_id=1, source_target_pairs={{0,8},{8,0},{16,24},{24,16},{1,9},{9,1},{17,25},{25,17},{2,10},{10... | collective-permute-start | bytes 786440 | tf_op jit(solution)/shard_map/ppermute | solution.py:359
  374.2 43.2 %collective-permute-start.120 = (bf16[128,1024]{1,0:T(8,128)(2,1)S(1)}, bf16[128,1024]{1,0:T(8,128)(2,1)}, u32[]{:S(2)}, u32[]{:S(2)}) collective-permute-start(bf16[128,1024]{1,0:T(8,128)(2,1)S(1)} %fusion.59.refs_0_), channel_id=1, source_target_pairs={{0,16},{8,24},{16,0},{24,8},{1,17},{9,25},{17,1},{25,9},{2,18},{10... | collective-permute-start | bytes 786440 | tf_op jit(solution)/shard_map/ppermute | solution.py:362
  387.6 30.4 %collective-permute-start.113 = (bf16[128,1024]{1,0:T(8,128)(2,1)}, bf16[128,1024]{1,0:T(8,128)(2,1)}, u32[]{:S(2)}, u32[]{:S(2)}) collective-permute-start(bf16[128,1024]{1,0:T(8,128)(2,1)} %fusion.62.refs_0_), channel_id=1, source_target_pairs={{0,16},{8,24},{16,0},{24,8},{1,17},{9,25},{17,1},{25,9},{2,18},{10... | collective-permute-start | bytes 786440 | tf_op jit(solution)/shard_map/ppermute | solution.py:362
  417.4 16.8 %collective-permute-start.114 = (bf16[128,1024]{1,0:T(8,128)(2,1)}, bf16[128,1024]{1,0:T(8,128)(2,1)}, u32[]{:S(2)}, u32[]{:S(2)}) collective-permute-start(bf16[128,1024]{1,0:T(8,128)(2,1)} %fusion.62.refs_0_), channel_id=1, source_target_pairs={{0,8},{8,0},{16,24},{24,16},{1,9},{9,1},{17,25},{25,17},{2,10},{10... | collective-permute-start | bytes 786440 | tf_op jit(solution)/shard_map/ppermute | solution.py:359
  417.9 24.0 %collective-permute-start.122 = (bf16[128,1024]{1,0:T(8,128)(2,1)}, bf16[128,1024]{1,0:T(8,128)(2,1)}, u32[]{:S(2)}, u32[]{:S(2)}) collective-permute-start(bf16[128,1024]{1,0:T(8,128)(2,1)} %collective-permute-done.120.refs_1_), channel_id=1, source_target_pairs={{0,8},{8,0},{16,24},{24,16},{1,9},{9,1},{17,25},{25,17},{2,10},{10... | collective-permute-start | bytes 786440 | tf_op jit(solution)/shard_map/ppermute | solution.py:359
  418.0 18.4 %collective-permute-start.115 = (bf16[128,1024]{1,0:T(8,128)(2,1)}, bf16[128,1024]{1,0:T(8,128)(2,1)}, u32[]{:S(2)}, u32[]{:S(2)}) collective-permute-start(bf16[128,1024]{1,0:T(8,128)(2,1)} %collective-permute-done.113.refs_1_), channel_id=1, source_target_pairs={{0,8},{8,0},{16,24},{24,16},{1,9},{9,1},{17,25},{25,17},{2,10},{10... | collective-permute-start | bytes 786440 | tf_op jit(solution)/shard_map/ppermute | solution.py:359
  434.3 20.2 %collective-permute-start.69 = (bf16[256,256]{1,0:T(8,128)(2,1)}, bf16[256,256]{1,0:T(8,128)(2,1)}, u32[]{:S(2)}, u32[]{:S(2)}) collective-permute-start(bf16[256,256]{1,0:T(8,128)(2,1)} %get-tuple-element.157), channel_id=1, source_target_pairs={{0,8},{8,0},{16,24},{24,16},{1,9},{9,1},{17,25},{25,17},{2,10},{10... | collective-permute-start | bytes 393224 | tf_op jit(solution)/shard_map/ppermute | solution.py:359
  435.5 19.0 %collective-permute-start.68 = (bf16[256,256]{1,0:T(8,128)(2,1)S(1)}, bf16[256,256]{1,0:T(8,128)(2,1)}, u32[]{:S(2)}, u32[]{:S(2)}) collective-permute-start(bf16[256,256]{1,0:T(8,128)(2,1)S(1)} %get-tuple-element.158), channel_id=1, source_target_pairs={{0,16},{8,24},{16,0},{24,8},{1,17},{9,25},{17,1},{25,9},{2,18},{10... | collective-permute-start | bytes 393224 | tf_op jit(solution)/shard_map/ppermute | solution.py:362
  436.4 19.1 %collective-permute-start.71 = (bf16[256,256]{1,0:T(8,128)(2,1)}, bf16[256,256]{1,0:T(8,128)(2,1)}, u32[]{:S(2)}, u32[]{:S(2)}) collective-permute-start(bf16[256,256]{1,0:T(8,128)(2,1)} %collective-permute-done.70), channel_id=1, source_target_pairs={{0,8},{8,0},{16,24},{24,16},{1,9},{9,1},{17,25},{25,17},{2,10},{10... | collective-permute-start | bytes 393224 | tf_op jit(solution)/shard_map/ppermute | solution.py:359
  441.4 51.6 %collective-permute-start.91 = (bf16[8,32,1024]{2,1,0:T(8,128)(2,1)}, bf16[8,32,1024]{2,1,0:T(8,128)(2,1)}, u32[]{:S(2)}, u32[]{:S(2)}) collective-permute-start(bf16[8,32,1024]{2,1,0:T(8,128)(2,1)} %get-tuple-element.117), channel_id=1, source_target_pairs={{0,8},{8,0},{16,24},{24,16},{1,9},{9,1},{17,25},{25,17},{2,10},{10... | collective-permute-start | bytes 1572872 | tf_op jit(solution)/shard_map/ppermute | solution.py:359
  442.0 56.3 %collective-permute-start.75 = (bf16[1024,512]{1,0:T(8,128)(2,1)}, bf16[1024,512]{1,0:T(8,128)(2,1)}, u32[]{:S(2)}, u32[]{:S(2)}) collective-permute-start(bf16[1024,512]{1,0:T(8,128)(2,1)} %pad_maximum_fusion.6), channel_id=1, source_target_pairs={{0,16},{8,24},{16,0},{24,8},{1,17},{9,25},{17,1},{25,9},{2,18},{10... | collective-permute-start | bytes 3145736 | tf_op jit(solution)/shard_map/ppermute | solution.py:362
  454.5 36.1 %collective-permute-start.86 = (bf16[8,32,1024]{2,1,0:T(8,128)(2,1)}, bf16[8,32,1024]{2,1,0:T(8,128)(2,1)}, u32[]{:S(2)}, u32[]{:S(2)}) collective-permute-start(bf16[8,32,1024]{2,1,0:T(8,128)(2,1)} %get-tuple-element.114), channel_id=1, source_target_pairs={{0,8},{8,0},{16,24},{24,16},{1,9},{9,1},{17,25},{25,17},{2,10},{10... | collective-permute-start | bytes 1572872 | tf_op jit(solution)/shard_map/ppermute | solution.py:359
  454.5 38.7 %collective-permute-start.90 = (bf16[8,32,1024]{2,1,0:T(8,128)(2,1)}, bf16[8,32,1024]{2,1,0:T(8,128)(2,1)}, u32[]{:S(2)}, u32[]{:S(2)}) collective-permute-start(bf16[8,32,1024]{2,1,0:T(8,128)(2,1)} %fusion.39), channel_id=1, source_target_pairs={{0,16},{8,24},{16,0},{24,8},{1,17},{9,25},{17,1},{25,9},{2,18},{10... | collective-permute-start | bytes 1572872 | tf_op jit(solution)/shard_map/ppermute | solution.py:362
  455.5 40.3 %collective-permute-start.99 = (bf16[1024,256]{0,1:T(8,128)(2,1)}, bf16[1024,256]{0,1:T(8,128)(2,1)}, u32[]{:S(2)}, u32[]{:S(2)}) collective-permute-start(bf16[1024,256]{0,1:T(8,128)(2,1)} %get-tuple-element.112), channel_id=1, source_target_pairs={{0,8},{8,0},{16,24},{24,16},{1,9},{9,1},{17,25},{25,17},{2,10},{10... | collective-permute-start | bytes 1572872 | tf_op jit(solution)/shard_map/ppermute | solution.py:359
  490.6 50.7 %collective-permute-start.88 = (bf16[8,32,1024]{2,1,0:T(8,128)(2,1)}, bf16[8,32,1024]{2,1,0:T(8,128)(2,1)}, u32[]{:S(2)}, u32[]{:S(2)}) collective-permute-start(bf16[8,32,1024]{2,1,0:T(8,128)(2,1)} %get-tuple-element.115), channel_id=1, source_target_pairs={{0,8},{8,0},{16,24},{24,16},{1,9},{9,1},{17,25},{25,17},{2,10},{10... | collective-permute-start | bytes 1572872 | tf_op jit(solution)/shard_map/ppermute | solution.py:359
  493.0 55.7 %collective-permute-start.101 = (bf16[1024,256]{0,1:T(8,128)(2,1)}, bf16[1024,256]{0,1:T(8,128)(2,1)}, u32[]{:S(2)}, u32[]{:S(2)}) collective-permute-start(bf16[1024,256]{0,1:T(8,128)(2,1)} %get-tuple-element.113), channel_id=1, source_target_pairs={{0,8},{8,0},{16,24},{24,16},{1,9},{9,1},{17,25},{25,17},{2,10},{10... | collective-permute-start | bytes 1572872 | tf_op jit(solution)/shard_map/ppermute | solution.py:359
  493.2 44.8 %collective-permute-start.79 = (bf16[4,128,768]{2,1,0:T(8,128)(2,1)}, bf16[4,128,768]{2,1,0:T(8,128)(2,1)S(1)}, u32[]{:S(2)}, u32[]{:S(2)}) collective-permute-start(bf16[4,128,768]{2,1,0:T(8,128)(2,1)} %dynamic-slice_bitcast_fusion.3), channel_id=1, source_target_pairs={{0,1},{1,0},{2,3},{3,2},{4,5},{5,4},{6,7},{7,6},{8,9},{9,8},{10,11... | collective-permute-start | bytes 2359304 | tf_op jit(solution)/shard_map/ppermute | solution.py:368
  495.8 19.7 %collective-permute-start.72 = (bf16[256,1024]{1,0:T(8,128)(2,1)}, bf16[256,1024]{1,0:T(8,128)(2,1)}, u32[]{:S(2)}, u32[]{:S(2)}) collective-permute-start(bf16[256,1024]{1,0:T(8,128)(2,1)} %get-tuple-element.110), channel_id=1, source_target_pairs={{0,8},{8,0},{16,24},{24,16},{1,9},{9,1},{17,25},{25,17},{2,10},{10... | collective-permute-start | bytes 1572872 | tf_op jit(solution)/shard_map/ppermute | solution.py:359
  498.3 44.8 %collective-permute-start.87 = (bf16[8,32,1024]{2,1,0:T(8,128)(2,1)}, bf16[8,32,1024]{2,1,0:T(8,128)(2,1)}, u32[]{:S(2)}, u32[]{:S(2)}) collective-permute-start(bf16[8,32,1024]{2,1,0:T(8,128)(2,1)} %fusion.42), channel_id=1, source_target_pairs={{0,16},{8,24},{16,0},{24,8},{1,17},{9,25},{17,1},{25,9},{2,18},{10... | collective-permute-start | bytes 1572872 | tf_op jit(solution)/shard_map/ppermute | solution.py:362
  515.7 33.8 %collective-permute-start.100 = (bf16[1024,256]{0,1:T(8,128)(2,1)S(1)}, bf16[1024,256]{0,1:T(8,128)(2,1)S(1)}, u32[]{:S(2)}, u32[]{:S(2)}) collective-permute-start(bf16[1024,256]{0,1:T(8,128)(2,1)S(1)} %copy-done.52), channel_id=1, source_target_pairs={{0,16},{8,24},{16,0},{24,8},{1,17},{9,25},{17,1},{25,9},{2,18},{10... | collective-permute-start | bytes 1572872 | tf_op jit(solution)/shard_map/ppermute | solution.py:362
  538.9 32.0 %collective-permute-start.76 = (bf16[256,1024]{1,0:T(8,128)(2,1)}, bf16[256,1024]{1,0:T(8,128)(2,1)}, u32[]{:S(2)}, u32[]{:S(2)}) collective-permute-start(bf16[256,1024]{1,0:T(8,128)(2,1)} %get-tuple-element.118), channel_id=1, source_target_pairs={{0,8},{8,0},{16,24},{24,16},{1,9},{9,1},{17,25},{25,17},{2,10},{10... | collective-permute-start | bytes 1572872 | tf_op jit(solution)/shard_map/ppermute | solution.py:359
  555.7 25.5 %collective-permute-start.102 = (bf16[4,128,768]{2,1,0:T(8,128)(2,1)S(1)}, bf16[4,128,768]{2,1,0:T(8,128)(2,1)S(1)}, u32[]{:S(2)}, u32[]{:S(2)}) collective-permute-start(bf16[4,128,768]{2,1,0:T(8,128)(2,1)S(1)} %dynamic-slice_bitcast_fusion.2), channel_id=1, source_target_pairs={{0,1},{1,0},{2,3},{3,2},{4,5},{5,4},{6,7},{7,6},{8,9},{9,8},{10,11... | collective-permute-start | bytes 2359304 | tf_op jit(solution)/shard_map/ppermute | solution.py:368
  583.3 27.6 %collective-permute-start.78 = (bf16[256,1024]{1,0:T(8,128)(2,1)}, bf16[256,1024]{1,0:T(8,128)(2,1)}, u32[]{:S(2)}, u32[]{:S(2)}) collective-permute-start(bf16[256,1024]{1,0:T(8,128)(2,1)} %get-tuple-element.119), channel_id=1, source_target_pairs={{0,8},{8,0},{16,24},{24,16},{1,9},{9,1},{17,25},{25,17},{2,10},{10... | collective-permute-start | bytes 1572872 | tf_op jit(solution)/shard_map/ppermute | solution.py:359
  590.0 20.9 %collective-permute-start.77 = (bf16[256,1024]{1,0:T(8,128)(2,1)}, bf16[256,1024]{1,0:T(8,128)(2,1)}, u32[]{:S(2)}, u32[]{:S(2)}) collective-permute-start(bf16[256,1024]{1,0:T(8,128)(2,1)} %fusion.28), channel_id=1, source_target_pairs={{0,16},{8,24},{16,0},{24,8},{1,17},{9,25},{17,1},{25,9},{2,18},{10... | collective-permute-start | bytes 1572872 | tf_op jit(solution)/shard_map/ppermute | solution.py:362
  (166 other events, 1922.0 us)

commit v2 on v1

--- a/solution.py
+++ b/solution.py
@@ -338,7 +338,7 @@
     return lax.optimization_barrier((value, *earlier))[0]
 
 
-def solution(mesh):
+def general_layer(mesh):
     S, F = mesh.shape["seq"], mesh.shape["fsdp"]
     Y = S // CORES
     Z = 4 if F % 4 == 0 else 1
@@ -773,6 +773,1101 @@
             jnp.stack(rows[10:13]),
         )
 
+    return local
+
+
+short = pl.CostEstimate(flops=1024, bytes_accessed=1024, transcendentals=0)
+
+small_rows = 24
+
+
+def hbm(array):
+    return ("hbm", array)
+
+
+def stage(body, where, ins, outs, scratch=(), limit=vmem_limit):
+    specs, arrays = [], []
+    for item in ins:
+        if isinstance(item, tuple):
+            specs.append(pl.BlockSpec(memory_space=pl.ANY))
+            arrays.append(item[1])
+        else:
+            specs.append(pl.BlockSpec(memory_space=pltpu.VMEM))
+            arrays.append(item)
+    n_in, n_out = len(arrays), len(outs)
+
+    def kernel(w, *refs):
+        body(w, refs[:n_in], refs[n_in : n_in + n_out], refs[n_in + n_out :])
+
+    return pl.pallas_call(
+        kernel,
+        grid_spec=pltpu.PrefetchScalarGridSpec(
+            num_scalar_prefetch=1,
+            grid=(1,),
+            in_specs=specs,
+            out_specs=[pl.BlockSpec(memory_space=pltpu.VMEM)] * n_out,
+            scratch_shapes=list(scratch),
+        ),
+        out_shape=[jax.ShapeDtypeStruct(shape, dtype) for shape, dtype in outs],
+        compiler_params=pltpu.CompilerParams(vmem_limit_bytes=limit),
+        cost_estimate=short,
+    )(where, *arrays)
+
+
+class Copies:
+    def __init__(self, sems):
+        self.sems, self.list = sems, []
+
+    def add(self, source, target):
+        copy = pltpu.make_async_copy(source, target, self.sems.at[len(self.list)])
+        copy.start()
+        self.list.append(copy)
+        return copy
+
+    def wait(self):
+        for copy in self.list:
+            copy.wait()
+        self.list = []
+
+
+def span(index, size):
+    return pl.ds(pl.multiple_of(index * size, size), size)
+
+
+def norm_rows(values, gain_row, shift_row):
+    center = values - jnp.mean(values, axis=-1, keepdims=True)
+    inverse = lax.rsqrt(jnp.mean(center * center, axis=-1, keepdims=True) + layer_eps)
+    normed = center * inverse
+    return normed * gain_row + shift_row, normed, inverse
+
+
+def norm_rows_back(grad_rows, normed, inverse, gain_row):
+    scaled = grad_rows * gain_row
+    inner = scaled - jnp.mean(scaled, axis=-1, keepdims=True)
+    inner = inner - normed * jnp.mean(scaled * normed, axis=-1, keepdims=True)
+    return (
+        inverse * inner,
+        jnp.sum(grad_rows * normed, axis=0, keepdims=True),
+        jnp.sum(grad_rows, axis=0, keepdims=True),
+    )
+
+
+def row_sum(array):
+    return jnp.sum(array.astype(f32), axis=0, keepdims=True)
+
+
+def tiled_layer(mesh):
+    S, F = mesh.shape["seq"], mesh.shape["fsdp"]
+    Z = 4 if F % 4 == 0 else 1
+    X = F // Z
+    SEQ, MINE, AT_X, LENGTH = 0, S, S + 1, S + 2
+
+    core_perm = [(n, n ^ 1) for n in range(S)]
+    y_perm = [(n, n ^ 2) for n in range(S)]
+
+    def core_swap(array):
+        return lax.ppermute(array, "seq", core_perm)
+
+    def y_swap(array):
+        return lax.ppermute(array, "seq", y_perm)
+
+    z_groups = [[z * X + x for z in range(Z)] for x in range(X)]
+
+    def z_exchange(array):
+        return lax.all_to_all(array, "fsdp", 0, 0, axis_index_groups=z_groups, tiled=True)
+
+    def x_shift(array, k):
+        perm = [(z * X + x, z * X + (x + k) % X) for z in range(Z) for x in range(X)]
+        return lax.ppermute(array, "fsdp", perm) if k % X else array
+
+    def seq_gather(array):
+        far = y_swap(array)
+        return [array, far, core_swap(array), core_swap(far)]
+
+    def tied(values):
+        return lax.optimization_barrier(list(values))
+
+    def z_gather(copies):
+        return z_exchange(copies)
+
+    def x_gather(column):
+        rows, cols = column.shape[0] // Z, column.shape[1]
+        return [a.reshape(Z, rows, cols) for a in (column, x_shift(column, 1))]
+
+    def heads_to_positions(array):
+        return lax.all_to_all(array, "seq", 0, 0, tiled=True)
+
+    def local(
+        hidden_in,
+        memory,
+        lengths,
+        out_grad,
+        self_in_weight,
+        self_query_bias,
+        self_value_bias,
+        self_out_weight,
+        self_out_bias,
+        cross_query_weight,
+        cross_query_bias,
+        memory_weight,
+        memory_value_bias,
+        cross_out_weight,
+        cross_out_bias,
+        ffn_in_weight,
+        ffn_in_bias,
+        ffn_out_weight,
+        ffn_out_bias,
+        norm_gain,
+        norm_bias,
+    ):
+        s, f = lax.axis_index("seq"), lax.axis_index("fsdp")
+        z, x = f // X, f % X
+        _, t, D = hidden_in.shape
+        T = S * t
+        hw = D // S
+        FF = ffn_in_weight.shape[1]
+        shard = D // F
+        fw = FF // (F * S)
+        half = 2 * hw
+        per_group = hw // shard
+        part = shard // S
+        deep = shard // 2
+        rest_cols = D + half
+        hidden_in, memory, out_grad = hidden_in[0], memory[0], out_grad[0]
+        where = jnp.stack(
+            [s, s ^ 2, s ^ 1, s ^ 3, s, x, lengths[0]]
+        ).astype(jnp.int32)
+
+        def prepare_qkv(w, ins, outs, _):
+            weight, out = ins[0], outs[0]
+            me = w[MINE]
+            for m in range(3):
+                lanes = pl.ds(pl.multiple_of(m * D + me * hw, hw), hw)
+                for k in range(Z):
+                    out[k, 0:shard, m * hw : (m + 1) * hw] = weight[:, lanes]
+            rows = [ins[n][...].reshape(1, shard) for n in range(1, 8)]
+            rows += [ins[8][...], ins[9][...]]
+            rows += [
+                ins[10][n * fw : (n + 1) * fw].reshape(1, fw) for n in range(S)
+            ]
+            packed = jnp.concatenate([r.astype(f32) for r in rows], axis=0)
+            first = packed[0:16].astype(bf16)
+            rest = jnp.concatenate(
+                [packed[16:], jnp.zeros((32 - packed.shape[0], shard), f32)], axis=0
+            ).astype(bf16)
+            below = jnp.concatenate(
+                [first, rest, jnp.zeros((16, 3 * hw - 2 * shard), bf16)], axis=1
+            )
+            for k in range(Z):
+                out[k, shard : shard + 16, :] = below
+
+        (chunk_qkv,) = stage(
+            prepare_qkv,
+            where,
+            [
+                self_in_weight, self_query_bias, self_value_bias, self_out_bias, cross_query_bias,
+                memory_value_bias, cross_out_bias, ffn_out_bias, norm_gain, norm_bias, ffn_in_bias,
+            ],
+            [((Z, shard + 16, 3 * hw), bf16)],
+        )
+
+        def prepare_rest(w, ins, outs, _):
+            query, own, cross = ins
+            out = outs[0]
+            core = lax.rem(w[MINE], 2)
+            out[0:deep, 0:D] = own[span(core, deep), :]
+            out[deep:, 0:D] = cross[span(core, deep), :]
+            out[:, D : D + hw] = query[:, span(w[SEQ], hw)]
+            out[:, D + hw :] = query[:, span(w[SEQ + 1], hw)]
+
+        (chunk_rest,) = stage(
+            prepare_rest,
+            where,
+            [cross_query_weight, self_out_weight, cross_out_weight],
+            [((shard, rest_cols), bf16)],
+        )
+
+        def prepare_mem(w, ins, outs, _):
+            for m in range(2):
+                lanes = pl.ds(pl.multiple_of(m * D + w[MINE] * hw, hw), hw)
+                for k in range(Z):
+                    outs[0][k, :, m * hw : (m + 1) * hw] = ins[0][:, lanes]
+
+        (chunk_mem,) = stage(prepare_mem, where, [memory_weight], [((Z, shard, 2 * hw), bf16)])
+
+        def prepare_ffn(w, ins, outs, _):
+            me = w[MINE]
+            for n in range(F):
+                lanes = pl.ds(pl.multiple_of(n * S * fw + me * fw, fw), fw)
+                outs[0][0:shard, n * fw : (n + 1) * fw] = ins[0][:, lanes]
+            outs[0][shard:, :] = ins[1][span(me, fw), :]
+
+        (chunk_ffn,) = stage(
+            prepare_ffn, where, [ffn_in_weight, ffn_out_weight], [((shard + fw, D), bf16)]
+        )
+
+        hidden_far = y_swap(after(hidden_in, chunk_qkv))
+        z_qkv = z_gather(chunk_qkv.reshape(Z * (shard + 16), 3 * hw))
+        z_qkv, hidden_far, chunk_rest, chunk_mem, chunk_ffn = tied(
+            [z_qkv, hidden_far, chunk_rest, chunk_mem, chunk_ffn]
+        )
+        rest_own = lax.all_gather(chunk_rest, "fsdp", axis=0, tiled=True)
+        x_blocks = [hidden_in, hidden_far, core_swap(hidden_in), core_swap(hidden_far)]
+        got_qkv = x_gather(z_qkv)
+        memory_far = y_swap(after(memory, hidden_far))
+        z_mem = z_gather(after(chunk_mem, z_qkv).reshape(Z * shard, 2 * hw))
+        got_qkv[0], z_mem, memory_far = tied([got_qkv[0], z_mem, memory_far])
+        m_blocks = [memory, memory_far, core_swap(memory), core_swap(memory_far)]
+        got_mem = x_gather(z_mem)
+
+        def project_qkv(w, ins, outs, scratch):
+            blocks, pieces = ins[:S], ins[S:]
+            qkv, small = outs
+            x_all, weight, packed, sems = scratch
+            copies = Copies(sems)
+            for k in range(2):
+                at = w[AT_X] if k == 0 else 1 - w[AT_X]
+                copies.add(pieces[k].at[:, pl.ds(0, shard)], weight.at[:, at])
+                copies.add(pieces[k].at[:, pl.ds(shard, 16), pl.ds(0, 2 * shard)], packed.at[:, at])
+            for n in range(S):
+                copies.add(blocks[n], x_all.at[span(w[SEQ + n], t)])
+            copies.wait()
+            small[...] = jnp.zeros_like(small)
+            for n in range(F):
+                lanes = slice(n * shard, (n + 1) * shard)
+                small[0:16, lanes] = packed[n // X, n % X, :, 0:shard].astype(f32)
+                small[16:24, lanes] = packed[n // X, n % X, 0:8, shard : 2 * shard].astype(f32)
+            mine = span(w[MINE], hw)
+            biases = [small[0:1, mine], jnp.zeros((1, hw), f32), small[1:2, mine]]
+            for n in range(S):
+                rows = slice(n * t, (n + 1) * t)
+                for m in range(3):
+                    cols = slice(m * hw, (m + 1) * hw)
+                    value = dot(x_all[rows, :], weight[..., cols].reshape(D, hw), nn) + biases[m]
+                    qkv[rows, cols] = value.astype(bf16)
+
+        qkv, small = stage(
+            project_qkv,
+            where,
+            [hbm(b) for b in x_blocks] + [hbm(p) for p in got_qkv],
+            [((T, 3 * hw), bf16), ((small_rows, D), f32)],
+            [
+                pltpu.VMEM((T, D), bf16),
+                pltpu.VMEM((Z, X, shard, 3 * hw), bf16),
+                pltpu.VMEM((Z, X, 16, 2 * shard), bf16),
+                pltpu.SemaphoreType.DMA((4 + S,)),
+            ],
+        )
+
+        pairs = hw // (2 * HD)
+        pair = 2 * HD
+
+        def qkv_spec(m):
+            return pl.BlockSpec((T, pair), lambda g, i, _: (0, m * pairs + g))
+
+        def self_forward(w, q_ref, k_ref, v_ref, o_ref, lse_ref):
+            i = pl.program_id(1)
+            limit = jnp.minimum(w[LENGTH], (i + 1) * BLK)
+
+            def visit(key_count):
+                parts, lses = [], []
+                for h in range(2):
+                    cols = slice(h * HD, (h + 1) * HD)
+                    query = q_ref[:, cols] * jnp.asarray(score_scale, bf16)
+                    scores = mask_scores(dot(k_ref[:key_count, cols], query, nt), 0, limit)
+                    top = jnp.max(scores, axis=0, keepdims=True)
+                    weights = jnp.exp(scores - top)
+                    totals = jnp.sum(weights, axis=0, keepdims=True)
+                    low = (weights * (1.0 / totals)).astype(bf16)
+                    parts.append(dot(low, v_ref[:key_count, cols], tn).astype(bf16))
+                    lses.append(top + jnp.log(totals))
+                o_ref[...] = jnp.concatenate(parts, axis=1)
+                lse_ref[0] = jnp.concatenate(lses, axis=0)
+
+            key_cases(T, True, i, visit)
+
+        q_block = pl.BlockSpec((t, pair), lambda g, i, _: (i, g))
+        row_block = pl.BlockSpec((t, pair), lambda g, i, _: (0, g))
+        lse_block = pl.BlockSpec((1, 2, t), lambda g, i, _: (g, 0, i))
+        self_attn, self_lse = pl.pallas_call(
+            self_forward,
+            grid_spec=pltpu.PrefetchScalarGridSpec(
+                num_scalar_prefetch=1,
+                grid=(pairs, S),
+                in_specs=[q_block, qkv_spec(1), qkv_spec(2)],
+                out_specs=[q_block, lse_block],
+            ),
+            out_shape=[
+                jax.ShapeDtypeStruct((T, hw), bf16),
+                jax.ShapeDtypeStruct((pairs, 2, T), f32),
+            ],
+            compiler_params=pltpu.CompilerParams(vmem_limit_bytes=vmem_limit),
+            cost_estimate=short,
+        )(where, qkv, qkv, qkv)
+        attn = heads_to_positions(self_attn)
+        rest_own = after(rest_own, self_attn)
+        rest_other = core_swap(rest_own)
+        rest = [r.reshape(F, shard, rest_cols) for r in (rest_own, rest_other)]
+
+        w_ffn = lax.all_gather(after(chunk_ffn, qkv), "fsdp", axis=0, tiled=True).reshape(
+            F, shard + fw, D
+        )
+        def project_memory(w, ins, outs, scratch):
+            blocks, pieces, small_ref = ins[:S], ins[S : S + 2], ins[S + 2]
+            kv, weight = outs
+            m_all, sems = scratch
+            copies = Copies(sems)
+            for k in range(2):
+                copies.add(pieces[k], weight.at[:, w[AT_X] if k == 0 else 1 - w[AT_X]])
+            for n in range(S):
+                copies.add(blocks[n], m_all.at[pl.ds(n * t, t)])
+            copies.wait()
+            bias = jnp.concatenate(
+                [jnp.zeros((1, hw), f32), small_ref[4:5, span(w[MINE], hw)]], axis=1
+            )
+            for n in range(S):
+                rows = slice(n * t, (n + 1) * t)
+                value = dot(m_all[rows, :], weight[...].reshape(D, 2 * hw), nn) + bias
+                kv[rows, :] = value.astype(bf16)
+
+        kv_own, w_mem = stage(
+            project_memory,
+            where,
+            [hbm(b) for b in m_blocks] + [hbm(p) for p in got_mem] + [after(small, attn)],
+            [((T, 2 * hw), bf16), ((Z, X, shard, 2 * hw), bf16)],
+            [pltpu.VMEM((T, D), bf16), pltpu.SemaphoreType.DMA((2 + S,))],
+        )
+        w_mem = w_mem.reshape(D, 2 * hw)
+        kv_far = y_swap(kv_own)
+
+        def load_out(copies, w, rest_refs, which, target):
+            core = lax.rem(w[MINE], 2)
+            for e in range(2):
+                copies.add(
+                    rest_refs[e].at[:, pl.ds(which * deep, deep), pl.ds(0, D)],
+                    target.at[:, core if e == 0 else 1 - core],
+                )
+
+        def group_rows(weight, group):
+            return weight[pl.ds(group * per_group, per_group)].reshape(hw, D)
+
+        out_scratch = pltpu.VMEM((F, 2, deep, D), bf16)
+        cq_scratch = pltpu.VMEM((2, F, shard, half), bf16)
+
+        def first_stage(w, ins, outs, scratch):
+            attn_ref, rest_refs, x_ref, small_ref = ins[0], ins[1:3], ins[3], ins[4]
+            normed_ref, inverse_ref, low_ref, keep_ref, send_ref = outs
+            weight, cq, sems = scratch
+            copies = Copies(sems)
+            load_out(copies, w, rest_refs, 0, weight)
+            for e in range(2):
+                copies.add(rest_refs[e].at[:, :, pl.ds(D, half)], cq.at[e])
+            copies.wait()
+            total = alpha_scale * x_ref[...].astype(f32) + small_ref[2:3, :]
+            for n in range(S):
+                total = total + dot(attn_ref[n * t : (n + 1) * t, :], group_rows(weight, n), nn)
+            value, normed, inverse = norm_rows(total, small_ref[7:8, :], small_ref[10:11, :])
+            normed_ref[...] = normed
+            inverse_ref[...] = inverse
+            low = value.astype(bf16)
+            low_ref[...] = low
+            for e, target in ((1, send_ref), (0, keep_ref)):
+                bias = jnp.concatenate(
+                    [small_ref[3:4, span(w[SEQ + 2 * e + k], hw)] for k in range(2)], axis=1
+                )
+                target[...] = (dot(low, cq[e].reshape(D, half), nn) + bias).astype(bf16)
+
+        normed_one, inverse_one, first_low, cq_keep, cq_send = stage(
+            first_stage,
+            where,
+            [attn] + [hbm(r) for r in rest] + [hidden_in, small],
+            [
+                ((t, D), f32), ((t, 1), f32), ((t, D), bf16), ((t, half), bf16), ((t, half), bf16),
+            ],
+            [out_scratch, cq_scratch, pltpu.SemaphoreType.DMA((4,))],
+        )
+        cq_other = core_swap(cq_send)
+
+        def kv_specs():
+            near = [
+                pl.BlockSpec((T, pair), lambda g, i, _, m=m: (0, m * pairs + jnp.minimum(g, pairs - 1)))
+                for m in range(2)
+            ]
+            far = [
+                pl.BlockSpec((T, pair), lambda g, i, _, m=m: (0, m * pairs + jnp.maximum(g - pairs, 0)))
+                for m in range(2)
+            ]
+            return near + far
+
+        cross_lse_block = pl.BlockSpec((1, 2, t), lambda g, i, _: (g, 0, i))
+
+        def cross_forward(w, qa_ref, qb_ref, k0, v0, k1, v1, oa_ref, ob_ref, lse_ref):
+            g, i = pl.program_id(0), pl.program_id(1)
+
+            def run(q_ref, k_ref, v_ref, o_ref):
+                parts, lses = [], []
+                for h in range(2):
+                    cols = slice(h * HD, (h + 1) * HD)
+                    query = q_ref[:, cols] * jnp.asarray(score_scale, bf16)
+                    scores = dot(k_ref[:, cols], query, nt)
+                    top = jnp.max(scores, axis=0, keepdims=True)
+                    weights = jnp.exp(scores - top)
+                    totals = jnp.sum(weights, axis=0, keepdims=True)
+                    low = (weights * (1.0 / totals)).astype(bf16)
+                    parts.append(dot(low, v_ref[:, cols], tn).astype(bf16))
+                    lses.append(top + jnp.log(totals))
+                o_ref[...] = jnp.concatenate(parts, axis=1)
+                lse_ref[0] = jnp.concatenate(lses, axis=0)
+
+            for gi, (k_ref, v_ref) in enumerate(((k0, v0), (k1, v1))):
+                for qi, (q_ref, o_ref) in enumerate(((qa_ref, oa_ref), (qb_ref, ob_ref))):
+
+                    @pl.when((g // pairs == gi) & (i == qi))
+                    def _(q_ref=q_ref, k_ref=k_ref, v_ref=v_ref, o_ref=o_ref):
+                        run(q_ref, k_ref, v_ref, o_ref)
+
+        cross_keep, cross_send, cross_lse = pl.pallas_call(
+            cross_forward,
+            grid_spec=pltpu.PrefetchScalarGridSpec(
+                num_scalar_prefetch=1,
+                grid=(2 * pairs, 2),
+                in_specs=[row_block, row_block] + kv_specs(),
+                out_specs=[row_block, row_block, cross_lse_block],
+            ),
+            out_shape=[jax.ShapeDtypeStruct((t, half), bf16)] * 2
+            + [jax.ShapeDtypeStruct((2 * pairs, 2, 2 * t), f32)],
+            compiler_params=pltpu.CompilerParams(vmem_limit_bytes=vmem_limit),
+            cost_estimate=short,
+        )(where, cq_keep, cq_other, kv_own, kv_own, kv_far, kv_far)
+        cross_other = core_swap(cross_send)
+
+        def halves(keep_ref, other_ref):
+            return [
+                ref[:, h * hw : (h + 1) * hw] for ref in (keep_ref, other_ref) for h in range(2)
+            ]
+
+        def second_stage(w, ins, outs, scratch):
+            keep_ref, other_ref, normed_one_ref, small_ref = ins[:4]
+            rest_refs = ins[4:]
+            normed_ref, inverse_ref, low_ref = outs
+            weight, sems = scratch
+            copies = Copies(sems)
+            load_out(copies, w, rest_refs, 1, weight)
+            copies.wait()
+            first = normed_one_ref[...] * small_ref[7:8, :] + small_ref[10:11, :]
+            total = alpha_scale * first + small_ref[5:6, :]
+            for n, piece in enumerate(halves(keep_ref, other_ref)):
+                total = total + dot(piece, group_rows(weight, w[SEQ + n]), nn)
+            value, normed, inverse = norm_rows(total, small_ref[8:9, :], small_ref[11:12, :])
+            normed_ref[...] = normed
+            inverse_ref[...] = inverse
+            low_ref[...] = value.astype(bf16)
+
+        normed_two, inverse_two, second_low = stage(
+            second_stage,
+            where,
+            [cross_keep, cross_other, normed_one, small] + [hbm(r) for r in rest],
+            [((t, D), f32), ((t, 1), f32), ((t, D), bf16)],
+            [out_scratch, pltpu.SemaphoreType.DMA((2,))],
+        )
+        second = seq_gather(second_low)
+
+        ffn_scratch = [
+            pltpu.VMEM((F, shard, D), bf16),
+            pltpu.VMEM((F, fw, D), bf16),
+            pltpu.SemaphoreType.DMA((2,)),
+        ]
+
+        def load_ffn(w_ref, scratch):
+            copies = Copies(scratch[2])
+            copies.add(w_ref.at[:, pl.ds(0, shard)], scratch[0])
+            copies.add(w_ref.at[:, pl.ds(shard, fw)], scratch[1])
+            copies.wait()
+            return scratch[0], scratch[1]
+
+        def ffn_forward(w, ins, outs, scratch):
+            block_refs, small_ref, w_ref = ins[:2], ins[2], ins[3]
+            part_refs, hidden_ref, slope_ref = outs[:2], outs[2], outs[3]
+            w_in, w_out = load_ffn(w_ref, scratch)
+            bias = small_ref[pl.ds(13 + w[MINE], 1), :]
+            for n in range(2):
+                rows = slice(n * t, (n + 1) * t)
+                pre = dot(block_refs[n][...], w_in[...].reshape(D, F * fw), nn) + bias
+                value, slope = gelu_both(pre)
+                low = value.astype(bf16)
+                hidden_ref[rows, :] = low
+                slope_ref[rows, :] = slope.astype(bf16)
+                out = dot(low, w_out[...].reshape(F * fw, D), nn)
+                part_refs[n][...] = out.astype(part_refs[n].dtype)
+
+        def ffn_call(blocks):
+            return stage(
+                ffn_forward,
+                where,
+                blocks + [small, hbm(w_ffn)],
+                [((t, D), bf16), ((t, D), bf16), ((2 * t, F * fw), bf16), ((2 * t, F * fw), bf16)],
+                ffn_scratch,
+            )
+
+        ffn_part_0, ffn_part_2, hidden_a, slope_a = ffn_call([second[0], second[2]])
+        ffn_near = core_swap(ffn_part_2)
+        ffn_part_1, ffn_part_3, hidden_b, slope_b = ffn_call([second[1], second[3]])
+
+        def add_pair(left, right):
+            return (left.astype(f32) + right.astype(f32)).astype(bf16)
+
+        ffn_far = y_swap(add_pair(ffn_part_1, core_swap(ffn_part_3)))
+
+        def third_stage(w, ins, outs, _):
+            a, b, far, normed_two_ref, small_ref, grad_ref = ins
+            out_ref, d_ref, low_ref, sums_ref = outs
+            second_rows = normed_two_ref[...] * small_ref[8:9, :] + small_ref[11:12, :]
+            branch = a[...].astype(f32) + b[...].astype(f32) + far[...].astype(f32)
+            total = alpha_scale * second_rows + branch + small_ref[6:7, :]
+            value, normed, inverse = norm_rows(total, small_ref[9:10, :], small_ref[12:13, :])
+            out_ref[...] = value.astype(bf16)
+            d, gain, shift = norm_rows_back(
+                grad_ref[...].astype(f32), normed, inverse, small_ref[9:10, :]
+            )
+            d_ref[...] = d
+            low = d.astype(bf16)
+            low_ref[...] = low
+            sums_ref[0:1, :] = row_sum(low)
+            sums_ref[1:2, :] = gain
+            sums_ref[2:3, :] = shift
+
+        layer_out, d_three, d_ffn_own, sums_three = stage(
+            third_stage,
+            where,
+            [ffn_part_0, ffn_near, ffn_far, normed_two, small, out_grad],
+            [((t, D), bf16), ((t, D), f32), ((t, D), bf16), ((8, D), f32)],
+        )
+        d_ffn = seq_gather(d_ffn_own)
+
+        def ffn_backward(w, ins, outs, scratch):
+            block_refs, slope_ref, w_ref = ins[:2], ins[2], ins[3]
+            part_refs, d_pre_ref = outs[:2], outs[2]
+            w_in, w_out = load_ffn(w_ref, scratch)
+            for n in range(2):
+                rows = slice(n * t, (n + 1) * t)
+                d_hidden = dot(block_refs[n][...], w_out[...].reshape(F * fw, D), nt)
+                d_pre = (slope_ref[rows, :].astype(f32) * d_hidden).astype(bf16)
+                d_pre_ref[rows, :] = d_pre
+                out = dot(d_pre, w_in[...].reshape(D, F * fw), nt)
+                part_refs[n][...] = out.astype(bf16)
+
+        def ffn_back_call(blocks, slope):
+            return stage(
+                ffn_backward,
+                where,
+                blocks + [slope, hbm(w_ffn)],
+                [((t, D), bf16), ((t, D), bf16), ((2 * t, F * fw), bf16)],
+                ffn_scratch,
+            )
+
+        d2_part_0, d2_part_2, d_pre_a = ffn_back_call([d_ffn[0], d_ffn[2]], slope_a)
+        d2_near = core_swap(d2_part_2)
+        d2_part_1, d2_part_3, d_pre_b = ffn_back_call([d_ffn[1], d_ffn[3]], slope_b)
+        d2_sent = add_pair(d2_part_1, core_swap(d2_part_3))
+        d2_far = y_swap(d2_sent)
+
+        def ffn_grads(w, ins, outs, scratch):
+            x_refs, g_refs, hidden_a_ref, hidden_b_ref, pre_a_ref, pre_b_ref = (
+                ins[0:4], ins[4:8], *ins[8:12],
+            )
+            grads, sums_ref = outs
+            x_rows, g_rows = scratch
+            for n in range(S):
+                at = (0, 2, 1, 3)[n] * t
+                x_rows[at : at + t, :] = x_refs[n][...]
+                g_rows[at : at + t, :] = g_refs[n][...]
+            for n in range(F):
+                cols = slice(n * fw, (n + 1) * fw)
+                rows = slice(n * shard, (n + 1) * shard)
+                value = dot(x_rows[: 2 * t, rows], pre_a_ref[...], tn)
+                value = value + dot(x_rows[2 * t :, rows], pre_b_ref[...], tn)
+                grads[n, 0:shard, :] = value.astype(bf16)
+                value = dot(hidden_a_ref[:, cols], g_rows[: 2 * t, :], tn)
+                value = value + dot(hidden_b_ref[:, cols], g_rows[2 * t :, :], tn)
+                grads[n, shard:, :] = value.astype(bf16)
+            sums_ref[0:1, :] = row_sum(pre_a_ref[...]) + row_sum(pre_b_ref[...])
+
+        grad_ffn, sums_ffn = stage(
+            ffn_grads,
+            where,
+            second + d_ffn + [after(hidden_a, d2_sent), hidden_b, d_pre_a, d_pre_b],
+            [((F, shard + fw, D), bf16), ((8, D), f32)],
+            [pltpu.VMEM((T, D), bf16), pltpu.VMEM((T, D), bf16)],
+        )
+        own_ffn = lax.psum_scatter(
+            grad_ffn.reshape(F * (shard + fw), D), "fsdp", scatter_dimension=0, tiled=True
+        )
+
+        def second_back(w, ins, outs, scratch):
+            a, b, far, d_three_ref, normed_ref, inverse_ref, small_ref = ins[:7]
+            rest_refs = ins[7:]
+            d_ref, low_ref, keep_ref, send_ref, sums_ref = outs
+            weight, sems = scratch
+            copies = Copies(sems)
+            load_out(copies, w, rest_refs, 1, weight)
+            total = alpha_scale * d_three_ref[...]
+            total = total + a[...].astype(f32) + b[...].astype(f32) + far[...].astype(f32)
+            d, gain, shift = norm_rows_back(
+                total, normed_ref[...], inverse_ref[...], small_ref[8:9, :]
+            )
+            d_ref[...] = d
+            low = d.astype(bf16)
+            low_ref[...] = low
+            sums_ref[0:1, :] = row_sum(low)
+            sums_ref[1:2, :] = gain
+            sums_ref[2:3, :] = shift
+            copies.wait()
+            for n in range(S):
+                target = keep_ref if n < 2 else send_ref
+                value = dot(low, group_rows(weight, w[SEQ + n]), nt)
+                target[:, (n % 2) * hw : (n % 2 + 1) * hw] = value.astype(bf16)
+
+        d_two, d_cross, dc_keep, dc_send, sums_two = stage(
+            second_back,
+            where,
+            [d2_part_0, d2_near, d2_far, after(d_three, grad_ffn), normed_two, inverse_two, small]
+            + [hbm(r) for r in rest],
+            [
+                ((t, D), f32), ((t, D), bf16), ((t, half), bf16), ((t, half), bf16), ((8, D), f32),
+            ],
+            [out_scratch, pltpu.SemaphoreType.DMA((2,))],
+        )
+        dc_other = core_swap(dc_send)
+
+        def backward_pair(q_ref, k_ref, v_ref, g_ref, lse_ref, key_count, limit, dk_acc, dv_acc):
+            dqs = []
+            for h in range(2):
+                cols = slice(h * HD, (h + 1) * HD)
+                query = q_ref[:, cols] * jnp.asarray(score_scale, bf16)
+                grad = g_ref[:, cols]
+                scores = dot(k_ref[:key_count, cols], query, nt)
+                if limit is not None:
+                    scores = mask_scores(scores, 0, limit)
+                weights = jnp.exp(scores - lse_ref[0, h : h + 1, :])
+                dv_acc[h, :key_count, :] += dot(weights.astype(bf16), grad, nn)
+                grad_weights = dot(v_ref[:key_count, cols], grad, nt)
+                row_term = jnp.sum(grad_weights * weights, axis=0, keepdims=True)
+                low = (weights * (grad_weights - row_term)).astype(bf16)
+                dk_acc[h, :key_count, :] += dot(low, query, nn)
+                dqs.append((dot(low, k_ref[:key_count, cols], tn) * score_scale).astype(bf16))
+            return jnp.concatenate(dqs, axis=1)
+
+        def sums_out(ref, acc):
+            ref[...] = jnp.concatenate([acc[h].astype(bf16) for h in range(2)], axis=1)
+
+        def cross_backward(
+            w, qa, qb, k0, v0, k1, v1, ga, gb, lse_ref, da, db, dk0, dv0, dk1, dv1, dk_acc, dv_acc
+        ):
+            g, i = pl.program_id(0), pl.program_id(1)
+
+            @pl.when(i == 0)
+            def _():
+                dk_acc[...] = jnp.zeros_like(dk_acc)
+                dv_acc[...] = jnp.zeros_like(dv_acc)
+
+            for gi, (k_ref, v_ref) in enumerate(((k0, v0), (k1, v1))):
+                for qi, (q_ref, g_ref, d_ref) in enumerate(((qa, ga, da), (qb, gb, db))):
+
+                    @pl.when((g // pairs == gi) & (i == qi))
+                    def _(q_ref=q_ref, g_ref=g_ref, d_ref=d_ref, k_ref=k_ref, v_ref=v_ref):
+                        d_ref[...] = backward_pair(
+                            q_ref, k_ref, v_ref, g_ref, lse_ref, T, None, dk_acc, dv_acc
+                        )
+
+            for gi, (dk_ref, dv_ref) in enumerate(((dk0, dv0), (dk1, dv1))):
+
+                @pl.when((g // pairs == gi) & (i == 1))
+                def _(dk_ref=dk_ref, dv_ref=dv_ref):
+                    sums_out(dk_ref, dk_acc)
+                    sums_out(dv_ref, dv_acc)
+
+        def near_block(m):
+            return pl.BlockSpec((T, pair), lambda g, i, _: (0, jnp.minimum(g, pairs - 1)))
+
+        def far_block(m):
+            return pl.BlockSpec((T, pair), lambda g, i, _: (0, jnp.maximum(g - pairs, 0)))
+
+        acc_scratch = [pltpu.VMEM((2, T, HD), f32), pltpu.VMEM((2, T, HD), f32)]
+        dq_keep, dq_send, dk_own, dv_own, dk_far, dv_far = pl.pallas_call(
+            cross_backward,
+            grid_spec=pltpu.PrefetchScalarGridSpec(
+                num_scalar_prefetch=1,
+                grid=(2 * pairs, 2),
+                in_specs=[row_block, row_block]
+                + kv_specs()
+                + [row_block, row_block, cross_lse_block],
+                out_specs=[row_block, row_block]
+                + [near_block(0), near_block(1), far_block(0), far_block(1)],
+                scratch_shapes=acc_scratch,
+            ),
+            out_shape=[jax.ShapeDtypeStruct((t, half), bf16)] * 2
+            + [jax.ShapeDtypeStruct((T, hw), bf16)] * 4,
+            compiler_params=pltpu.CompilerParams(vmem_limit_bytes=vmem_limit),
+            cost_estimate=short,
+        )(
+            where, cq_keep, cq_other, kv_own, kv_own, kv_far, kv_far, dc_keep, dc_other,
+            cross_lse,
+        )
+        dq_other = core_swap(dq_send)
+
+        def first_back(w, ins, outs, scratch):
+            keep_ref, other_ref, d_two_ref, normed_ref, inverse_ref, small_ref = ins[:6]
+            rest_refs = ins[6:]
+            d_ref, low_ref = outs[0], outs[1]
+            sent_ref, sums_ref = outs[2], outs[3]
+            weight, cq, sems = scratch
+            copies = Copies(sems)
+            for e in range(2):
+                copies.add(rest_refs[e].at[:, :, pl.ds(D, half)], cq.at[e])
+            load_out(copies, w, rest_refs, 0, weight)
+            copies.wait()
+            total = alpha_scale * d_two_ref[...]
+            for e, ref in enumerate((keep_ref, other_ref)):
+                total = total + dot(ref[...], cq[e].reshape(D, half), nt)
+            for n, piece in enumerate(halves(keep_ref, other_ref)):
+                sums_ref[3:4, span(w[SEQ + n], hw)] = row_sum(piece)
+            d, gain, shift = norm_rows_back(
+                total, normed_ref[...], inverse_ref[...], small_ref[7:8, :]
+            )
+            d_ref[...] = d
+            low = d.astype(bf16)
+            low_ref[...] = low
+            sums_ref[0:1, :] = row_sum(low)
+            sums_ref[1:2, :] = gain
+            sums_ref[2:3, :] = shift
+            for n in range(S):
+                value = dot(low, group_rows(weight, n), nt)
+                sent_ref[n * t : (n + 1) * t, :] = value.astype(bf16)
+
+        d_one, d_branch, d_attn_sent, sums_one = stage(
+            first_back,
+            where,
+            [dq_keep, dq_other, d_two, normed_one, inverse_one, small] + [hbm(r) for r in rest],
+            [((t, D), f32), ((t, D), bf16), ((T, hw), bf16), ((8, D), f32)],
+            [out_scratch, cq_scratch, pltpu.SemaphoreType.DMA((4,))],
+        )
+        d_attn = heads_to_positions(d_attn_sent)
+
+        def middle_grads(w, ins, outs, scratch):
+            dq_keep_ref, dq_other_ref, low_ref, attn_ref, d_one_ref, co_keep, co_other, d_two_ref = ins
+            own, cross = scratch
+            core = lax.rem(w[MINE], 2)
+            for e, ref in enumerate((dq_keep_ref, dq_other_ref)):
+                value = dot(low_ref[...], ref[...], tn)
+                outs[e][:, :, D:] = value.astype(bf16).reshape(F, shard, half)
+            for n, piece in enumerate(halves(co_keep, co_other)):
+                value = dot(piece, d_two_ref[...], tn).astype(bf16)
+                cross[pl.ds(w[SEQ + n] * per_group, per_group)] = value.reshape(
+                    per_group, 2, deep, D
+                )
+                value = dot(attn_ref[n * t : (n + 1) * t, :], d_one_ref[...], tn).astype(bf16)
+                own[n * per_group : (n + 1) * per_group] = value.reshape(per_group, 2, deep, D)
+            for e in range(2):
+                at = core if e == 0 else 1 - core
+                outs[e][:, 0:deep, 0:D] = own[:, at]
+                outs[e][:, deep:, 0:D] = cross[:, at]
+
+        middle_keep, middle_send = stage(
+            middle_grads,
+            where,
+            [dq_keep, dq_other, first_low, attn, after(d_branch, d_attn_sent), cross_keep]
+            + [cross_other, d_cross],
+            [((F, shard, rest_cols), bf16)] * 2,
+            [out_scratch, out_scratch],
+        )
+        middle_got = core_swap(middle_send)
+
+        def scatter_terms(parts):
+            return [parts[0], core_swap(parts[2]), y_swap(add_pair(parts[1], core_swap(parts[3])))]
+
+        def split_x(w, value, keep_ref, send_ref):
+            size = keep_ref.shape[0] // Z
+            for n in range(Z):
+                rows = slice(n * size, (n + 1) * size)
+                keep_ref[rows, :] = value[span(n * X + w[AT_X], size), :]
+                send_ref[rows, :] = value[span(n * X + 1 - w[AT_X], size), :]
+
+        def z_sum(sent):
+            rows, cols = sent.shape[0] // Z, sent.shape[1]
+            terms = z_exchange(sent).reshape(Z, rows, cols)
+            return jnp.sum(terms.astype(f32), axis=0).astype(bf16)
+
+        dk_got, dv_got = (y_swap(after(d, d_attn)) for d in (dk_far, dv_far))
+
+        def pack_rest(w, ins, outs, _):
+            for n in range(Z):
+                for out, at in ((outs[0], w[AT_X]), (outs[1], 1 - w[AT_X])):
+                    value = ins[0][n * X + at].astype(f32) + ins[1][n * X + at].astype(f32)
+                    out[n * shard : (n + 1) * shard, :] = value.astype(bf16)
+
+        rest_keep, rest_send = stage(
+            pack_rest,
+            where,
+            [middle_keep, middle_got],
+            [((Z * shard, rest_cols), bf16)] * 2,
+        )
+        rest_got = x_shift(rest_send, 1)
+
+        def self_backward(
+            w, q_ref, k_ref, v_ref, g_ref, lse_ref, dq_ref, dk_ref, dv_ref, dk_acc, dv_acc
+        ):
+            i = pl.program_id(1)
+
+            @pl.when(i == 0)
+            def _():
+                dk_acc[...] = jnp.zeros_like(dk_acc)
+                dv_acc[...] = jnp.zeros_like(dv_acc)
+
+            limit = jnp.minimum(w[LENGTH], (i + 1) * BLK)
+
+            def visit(key_count):
+                dq_ref[...] = backward_pair(
+                    q_ref, k_ref, v_ref, g_ref, lse_ref, key_count, limit, dk_acc, dv_acc
+                )
+
+            key_cases(T, True, i, visit)
+
+            @pl.when(i == S - 1)
+            def _():
+                sums_out(dk_ref, dk_acc)
+                sums_out(dv_ref, dv_acc)
+
+        key_block = pl.BlockSpec((T, pair), lambda g, i, _: (0, g))
+        dq_self, dk_self, dv_self = pl.pallas_call(
+            self_backward,
+            grid_spec=pltpu.PrefetchScalarGridSpec(
+                num_scalar_prefetch=1,
+                grid=(pairs, S),
+                in_specs=[q_block, qkv_spec(1), qkv_spec(2), q_block, lse_block],
+                out_specs=[q_block, key_block, key_block],
+                scratch_shapes=acc_scratch,
+            ),
+            out_shape=[jax.ShapeDtypeStruct((T, hw), bf16)] * 3,
+            compiler_params=pltpu.CompilerParams(vmem_limit_bytes=vmem_limit),
+            cost_estimate=short,
+        )(where, qkv, qkv, qkv, d_attn, after(self_lse, rest_keep))
+
+        tall = shard + 16
+
+        def place_small(small_sums, value):
+            for n in range(F):
+                lanes = slice(n * shard, (n + 1) * shard)
+                at = n * tall + shard
+                value[at : at + 16, 0:shard] = small_sums[0:16, lanes].astype(bf16)
+                rest_rows = [small_sums[16:, lanes], jnp.zeros((32 - small_rows, shard), f32)]
+                value[at : at + 16, shard : 2 * shard] = jnp.concatenate(
+                    rest_rows, axis=0
+                ).astype(bf16)
+
+        def last_grads(w, ins, outs, scratch):
+            dq, dk, dv, one, two, three, ffn = ins[:7]
+            mem_refs, weight = ins[7:11], ins[11]
+            blocks, mem_blocks = ins[12 : 12 + S], ins[12 + S :]
+            keep_ref, send_ref = outs[S], outs[S + 1]
+            x_all, m_all, d_all, value, small_sums, sems = scratch
+            copies = Copies(sems)
+            for n in range(S):
+                copies.add(blocks[n], x_all.at[span(w[SEQ + n], t)])
+            for n in range(S):
+                copies.add(mem_blocks[n], m_all.at[pl.ds(n * t, t)])
+            for m in range(2):
+                near, far = mem_refs[m], mem_refs[2 + m]
+                for n in range(S):
+                    rows = slice(n * t, (n + 1) * t)
+                    total = near[rows, :].astype(f32) + far[rows, :].astype(f32)
+                    d_all[rows, m * hw : (m + 1) * hw] = total.astype(bf16)
+            for n in (3, 2, 1, 0):
+                total = dot(d_all[n * t : (n + 1) * t, :], weight[...], nt)
+                outs[n][...] = total.astype(bf16)
+            copies.wait()
+
+            def store(grad, cols):
+                for n in range(F):
+                    value[n * tall : n * tall + shard, cols] = grad[n * shard : (n + 1) * shard]
+
+            for m, d in enumerate((dq, dk, dv)):
+                grad = dot(x_all[...], d[...], tn).astype(bf16)
+                store(grad, slice(m * hw, (m + 1) * hw))
+            grad = dot(m_all[...], d_all[...], tn).astype(bf16)
+            store(grad, slice(3 * hw, 5 * hw))
+            small_sums[...] = jnp.zeros_like(small_sums)
+            mine = span(w[MINE], hw)
+            small_sums[0:1, mine] = row_sum(dq[...])
+            small_sums[1:2, mine] = row_sum(dv[...])
+            small_sums[4:5, mine] = row_sum(d_all[:, hw:])
+            rows = [
+                (2, one, 0), (3, one, 3), (5, two, 0), (6, three, 0), (7, one, 1), (8, two, 1),
+                (9, three, 1), (10, one, 2), (11, two, 2), (12, three, 2),
+            ]
+            for at, ref, row in rows:
+                small_sums[at : at + 1, :] = ref[row : row + 1, :]
+            small_sums[pl.ds(13 + w[MINE], 1), :] = ffn[0:1, :]
+            place_small(small_sums, value)
+            split_x(w, value, keep_ref, send_ref)
+
+        *mem_parts, last_keep, last_send = stage(
+            last_grads,
+            where,
+            [dq_self, dk_self, dv_self, sums_one, sums_two, sums_three, sums_ffn]
+            + [dk_own, dv_own, dk_got, dv_got, w_mem]
+            + [hbm(b) for b in x_blocks + m_blocks],
+            [((t, D), bf16)] * S + [((Z * tall, 5 * hw), bf16)] * 2,
+            [
+                pltpu.VMEM((T, D), bf16),
+                pltpu.VMEM((T, D), bf16),
+                pltpu.VMEM((T, 2 * hw), bf16),
+                pltpu.VMEM((F * tall, 5 * hw), bf16),
+                pltpu.VMEM((small_rows, D), f32),
+                pltpu.SemaphoreType.DMA((2 * S,)),
+            ],
+        )
+        last_got = x_shift(last_send, 1)
+        rest_sent = add_pair(rest_keep, after(rest_got, last_keep))
+
+        def input_parts(w, ins, outs, scratch):
+            grads, pieces = ins[:3], ins[3:]
+            weight, sems = scratch
+            copies = Copies(sems)
+            for k in range(2):
+                at = w[AT_X] if k == 0 else 1 - w[AT_X]
+                copies.add(pieces[k].at[:, pl.ds(0, shard)], weight.at[:, at])
+            copies.wait()
+            for n in (3, 2, 1, 0):
+                rows = span(w[SEQ + n], t)
+                value = None
+                for m in range(3):
+                    part_of = weight[..., m * hw : (m + 1) * hw].reshape(D, hw)
+                    term = dot(grads[m][rows, :], part_of, nt)
+                    value = term if value is None else value + term
+                outs[n][...] = value.astype(bf16)
+
+        in_parts = stage(
+            input_parts,
+            where,
+            [after(dq_self, rest_sent), dk_self, dv_self] + [hbm(p) for p in got_qkv],
+            [((t, D), bf16)] * S,
+            [pltpu.VMEM((Z, X, shard, 3 * hw), bf16), pltpu.SemaphoreType.DMA((2,))],
+        )
+        in_terms = scatter_terms(in_parts)
+        memory_grad = sum(term.astype(f32) for term in scatter_terms(mem_parts)).astype(bf16)
+        input_grad = (
+            alpha_scale * d_one + sum(term.astype(f32) for term in in_terms)
+        ).astype(bf16)
+
+
+        def finish_ffn(w, ins, outs, _):
+            for n in range(S):
+                for m in range(F):
+                    lanes = pl.ds(pl.multiple_of(m * S * fw + w[SEQ + n] * fw, fw), fw)
+                    outs[0][:, lanes] = ins[n][0:shard, m * fw : (m + 1) * fw].astype(f32)
+                outs[1][span(w[SEQ + n], fw), :] = ins[n][shard:, :].astype(f32)
+
+        grad_fin, grad_fout = stage(
+            finish_ffn,
+            where,
+            seq_gather(after(own_ffn, last_keep)),
+            [((shard, FF), f32), ((S * fw, D), f32)],
+        )
+
+        own_rest = z_sum(rest_sent)
+        last_sent = add_pair(
+            last_keep, after(last_got, own_rest, grad_fin, input_grad, memory_grad)
+        )
+        own_last = z_sum(last_sent)
+
+        def sum_chips(w, ins, outs, _):
+            near, away = ins
+            out = outs[0]
+            out[:, 0:D] = (near[:, 0:D].astype(f32) + away[:, 0:D].astype(f32)).astype(bf16)
+            for k in range(2):
+                mine = slice(D + k * hw, D + (k + 1) * hw)
+                theirs = slice(D + (1 - k) * hw, D + (2 - k) * hw)
+                out[:, mine] = (near[:, mine].astype(f32) + away[:, theirs].astype(f32)).astype(bf16)
+
+        (rest_sum,) = stage(
+            sum_chips, where, [own_rest, y_swap(own_rest)], [((shard, rest_cols), bf16)]
+        )
+
+        def finish_rest(w, ins, outs, _):
+            query, own, cross = outs
+            core = lax.rem(w[MINE], 2)
+            for e in range(2):
+                rows = span(core if e == 0 else 1 - core, deep)
+                own[rows, :] = ins[e][0:deep, 0:D].astype(f32)
+                cross[rows, :] = ins[e][deep:, 0:D].astype(f32)
+                for k in range(2):
+                    query[:, span(w[SEQ + 2 * e + k], hw)] = ins[e][
+                        :, D + k * hw : D + (k + 1) * hw
+                    ].astype(f32)
+
+        grad_query, grad_self_out, grad_cross_out = stage(
+            finish_rest, where, [rest_sum, core_swap(rest_sum)], [((shard, D), f32)] * 3
+        )
+
+        def finish_last(w, ins, outs, _):
+            for n in range(S):
+                group = w[SEQ + n] * hw
+                for m in range(5):
+                    target, at = (outs[0], m) if m < 3 else (outs[1], m - 3)
+                    lanes = pl.ds(pl.multiple_of(at * D + group, hw), hw)
+                    target[:, lanes] = ins[n][0:shard, m * hw : (m + 1) * hw].astype(f32)
+            outs[2][0:16, :] = sum(ins[n][shard:, 0:shard].astype(f32) for n in range(S))
+            outs[2][16:, :] = sum(
+                ins[n][shard : shard + 8, shard : 2 * shard].astype(f32) for n in range(S)
+            )
+
+        grad_self_in, grad_memory, small_own = stage(
+            finish_last,
+            where,
+            seq_gather(own_last),
+            [((shard, 3 * D), f32), ((shard, 2 * D), f32), ((small_rows, shard), f32)],
+        )
+
+        rows = [small_own[n] for n in range(7)]
+        return (
+            layer_out[None],
+            input_grad[None],
+            memory_grad[None],
+            grad_self_in,
+            rows[0],
+            rows[1],
+            grad_self_out,
+            rows[2],
+            grad_query,
+            rows[3],
+            grad_memory,
+            rows[4],
+            grad_cross_out,
+            rows[5],
+            grad_fin,
+            small_own[13 : 13 + S].reshape(S * fw),
+            grad_fout,
+            rows[6],
+            small_own[7:10],
+            small_own[10:13],
+        )
+
+    return local
+
+
+def solution(mesh):
+    general, tiled = general_layer(mesh), tiled_layer(mesh)
+    S, F = mesh.shape["seq"], mesh.shape["fsdp"]
+
+    def local(*args):
+        _, t, D = args[0].shape
+        FF = args[15].shape[1]
+        blocks = (D // F, D // S, FF // (F * S))
+        whole_tiles = all(n % 128 == 0 for n in blocks) and D // F // 2 % 16 == 0
+        if whole_tiles and S == 4 and F == 8 and t == BLK:
+            return tiled(*args)
+        return general(*args)
+
     by_row, rows_1d = P("fsdp", None), P("fsdp")
     tokens, norms = P("fsdp", "seq", None), P(None, "fsdp")
     in_specs = (

time: 640 us -> 551 us (0.86)
  Pallas kernels: 123 us -> 220 us
  starting transfers between devices: 114 us -> 45.1 us
  local copies, waits for them, and re-layouts: 90.7 us -> 22.9 us
  matrix products: 64.5 us -> 0 us
  other arithmetic: 57.3 us -> 9 us
  waiting for transfers between devices: 161 us -> 205 us
  between operations: 3.83 us -> 15.1 us
  blocking collectives: 16.7 us -> 25.7 us
    pallas_call x20 -> x28, Pallas kernels: 123 us -> 220 us  [the longest x24 141 us: stage(): pl.pallas_call(kernel, grid_spec=pltpu.PrefetchScalarGridSpec(num_scalar_...]
    ppermute x79 -> x18, starting transfers between devices: 98.4 us -> 20.6 us  [the longest x14 16.2 us: y_swap(): return lax.ppermute(array, 'seq', y_perm)]
    dot_general x21 -> x0, matrix products: 64.5 us -> none  [dot(): lax.dot_general(left, right, (dims, ((), ())), preferred_element_type=f32)]
    all_to_all x2 -> x4, waiting for transfers between devices: 0.01 us -> 54.4 us  [z_exchange(): lax.all_to_all(array, 'fsdp', 0, 0, axis_index_groups=z_groups, tiled=True)]
    ppermute x79 -> x18, waiting for transfers between devices: 159 us -> 121 us  [the longest x14 118 us: y_swap(): return lax.ppermute(array, 'seq', y_perm)]
    all_to_all x0 -> x2, blocking collectives: none -> 25.7 us  [heads_to_positions(): return lax.all_to_all(array, 'seq', 0, 0, tiled=True)]
    convert_element_type x24 -> x8, other arithmetic: 30.2 us -> 8.51 us  [the longest x6 5.12 us: add_pair(): return (left.astype(f32) + right.astype(f32)).astype(bf16)]
    psum x1 -> x0, blocking collectives: 16.7 us -> none  [local(): small_own = lax.psum(small_own, 'seq')]
  transfers between devices with their start and end apart: 125 -> 52, of which waited for: 33 -> 25; matrix products, arithmetic and copies ran while one was open for 28% -> 1% of each run, Pallas kernels for 19% -> 36%
where the time goes in v2:
time: 551 us; the launch traced here: 543 us
  Pallas kernels  220 us (40%)
  waiting for transfers between devices  205 us (37%)
  starting transfers between devices  45.1 us (8%)
  blocking collectives  25.7 us (5%)
  local copies, waits for them, and re-layouts  22.9 us (4%)
  between operations  15.1 us (3%)
  other arithmetic  9 us (2%)
    pallas_call x24, Pallas kernels, stage(): pl.pallas_call(kernel, grid_spec=pltpu.PrefetchScalarGridSpec(num_scalar_...  141 us
    ppermute x14, waiting for transfers between devices, y_swap(): return lax.ppermute(array, 'seq', y_perm)  118 us
    all_to_all x4, waiting for transfers between devices, z_exchange(): lax.all_to_all(array, 'fsdp', 0, 0, axis_index_groups=z_groups, tiled=True)  54.4 us
    all_to_all x2, blocking collectives, heads_to_positions(): return lax.all_to_all(array, 'seq', 0, 0, tiled=True)  25.7 us
    pallas_call x1, Pallas kernels, local(): pl.pallas_call(cross_backward, grid_spec=pltpu.PrefetchScalarGridSpec(num...  25 us
    pallas_call x1, Pallas kernels, local(): pl.pallas_call(cross_forward, grid_spec=pltpu.PrefetchScalarGridSpec(num_...  20.6 us
    all_to_all x4, starting transfers between devices, z_exchange(): lax.all_to_all(array, 'fsdp', 0, 0, axis_index_groups=z_groups, tiled=True)  19.4 us
    unnamed x96, local copies, waits for them, and re-layouts  18.2 us
  transfers between devices with their start and end apart: 52, of which 25 were waited for; matrix products, arithmetic and copies ran while one was open for 1% of the time, Pallas kernels for 36%

profile of v2, /device:TPU:0, one launch (start us, length us, event | category | flops | bytes accessed | tf_op | source)
XLA Modules:
  0.0 542.9 jit_solution(16505464917521315376)
XLA Ops:
  8.5 3.0 shard_map.356
  11.4 6.3 %all-to-all-start = ((bf16[4,144,768]{2,1,0:T(8,128)(2,1)}), bf16[4,144,768]{2,1,0:T(8,128)(2,1)S(1)}, u32[]{:S(2)}, u32[]{:S(2)}) async-start(bf16[4,144,768]{2,1,0:T(8,128)(2,1)} %shard_map.356), calls=%async_computation | async-start | bytes 1769472 | tf_op jit(solution)/shard_map/all_to_all | solution.py:877
  17.8 1.6 collective-permute-start
  19.3 2.5 shard_map.358
  21.9 3.1 shard_map.359
  25.0 2.7 shard_map.357
  27.6 3.6 collective-permute-done.refs_1_.refs_13_
  31.2 8.8 %all-to-all-done = bf16[4,144,768]{2,1,0:T(8,128)(2,1)S(1)} async-done(((bf16[4,144,768]{2,1,0:T(8,128)(2,1)}), bf16[4,144,768]{2,1,0:T(8,128)(2,1)S(1)}, u32[]{:S(2)}, u32[]{:S(2)}) %all-to-all-start) | async-done | bytes 884768 | tf_op jit(solution)/shard_map/all_to_all | solution.py:877
  40.0 1.6 collective-permute-start.4
  41.6 4.1 all-to-all-start.1
  45.8 1.6 collective-permute-start.3
  47.9 10.7 %collective-permute-done.3.refs_1_.refs_17_ = bf16[256,1024]{1,0:T(8,128)(2,1)} collective-permute-done((bf16[256,1024]{1,0:T(8,128)(2,1)S(1)}, bf16[256,1024]{1,0:T(8,128)(2,1)}, u32[]{:S(2)}, u32[]{:S(2)}) %collective-permute-start.3) | collective-permute-done | bytes 524320 | tf_op jit(solution)/shard_map/ppermute | solution.py:872
  58.5 11.5 %all-to-all-done.1 = bf16[4,128,512]{2,1,0:T(8,128)(2,1)} async-done(((bf16[4,128,512]{2,1,0:T(8,128)(2,1)}), bf16[4,128,512]{2,1,0:T(8,128)(2,1)}, u32[]{:S(2)}, u32[]{:S(2)}) %all-to-all-start.1) | async-done | bytes 524320 | tf_op jit(solution)/shard_map/all_to_all | solution.py:877
  71.0 5.7 %shard_map.360 = (bf16[1024,768]{1,0:T(8,128)(2,1)}, f32[24,1024]{1,0:T(8,128)}) custom-call(s32[7]{0:T(128)} %stack.24.w, bf16[256,1024]{1,0:T(8,128)(2,1)} %bitcast.57, bf16[256,1024]{1,0:T(8,128)(2,1)} %copy-done.10, bf16[256,1024]{1,0:T(8,128)(2,1)} %collective-permute-done.1.refs_2_.refs_14_, bf16[256,1024]{1,0:T(8,128)(2,1)} %collective-permute-done.2.refs_3_.refs_15_, ...), custom_call_target="tpu_custom_call" | custom-call | flops 1024 | bytes 1024 | tf_op jit(solution)/shard_map/pallas_call | solution.py:802
  76.7 15.3 %shard_map.361 = (bf16[1024,256]{1,0:T(8,128)(2,1)}, f32[2,2,1024]{2,1,0:T(2,128)}) custom-call(s32[7]{0:T(128)} %stack.24.w, bf16[1024,768]{1,0:T(8,128)(2,1)} %get-tuple-element.128.q_ref.k_ref.v_ref, bf16[1024,768]{1,0:T(8,128)(2,1)} %get-tuple-element.128.q_ref.k_ref.v_ref, bf16[1024,768]{1,0:T(8,128)(2,1)} %get-tuple-element.128.q_ref.k_ref.v_ref), custom_call_target="tpu_custom_call" | custom-call | flops 1024 | bytes 1024 | tf_op jit(solution)/shard_map/pallas_call | solution.py:1092
  92.1 14.8 %all-gather.3.cloned.1.call-done = bf16[1024,1536]{1,0:T(8,128)(2,1)} async-done(((bf16[128,1536]{1,0:T(8,128)(2,1)}), bf16[1024,1536]{1,0:T(8,128)(2,1)}) %all-gather.3.cloned.1.call-update) | async-done | bytes 3145744 | tf_op jit(solution)/shard_map/all_gather | solution.py:1014
  108.2 13.3 %all_to_all.58 = bf16[4,256,256]{2,1,0:T(8,128)(2,1)} all-to-all(bf16[4,256,256]{2,1,0:T(8,128)(2,1)} %bitcast.74), channel_id=1, replica_groups=mesh['seq'=4,'fsdp'=8] {'seq'}, dimensions={0} | all-to-all | bytes 1048576 | tf_op jit(solution)/shard_map/all_to_all | solution.py:898
  121.6 2.8 collective-permute-done.9
  125.3 5.7 %shard_map.363 = (bf16[1024,512]{1,0:T(8,128)(2,1)}, bf16[4,2,128,512]{3,2,1,0:T(8,128)(2,1)}) custom-call(s32[7]{0:T(128)} %stack.24.w, bf16[256,1024]{1,0:T(8,128)(2,1)} %bitcast.67, bf16[256,1024]{1,0:T(8,128)(2,1)} %collective-permute-done.3.refs_1_.refs_17_, bf16[256,1024]{1,0:T(8,128)(2,1)} %copy-done.11, bf16[256,1024]{1,0:T(8,128)(2,1)} %copy-done.12, ...), custom_call_target="tpu_custom_call" | custom-call | flops 1024 | bytes 1024 | tf_op jit(solution)/shard_map/pallas_call | solution.py:802
  132.4 1.6 copy-done
  134.1 6.7 %shard_map.362 = (f32[256,1024]{1,0:T(8,128)}, f32[256,1]{1,0:T(8,128)}, bf16[256,1024]{1,0:T(8,128)(2,1)}, bf16[256,512]{1,0:T(8,128)(2,1)}, bf16[256,512]{1,0:T(8,128)(2,1)}) custom-call(s32[7]{0:T(128)} %stack.24.w, bf16[1024,256]{1,0:T(8,128)(2,1)} %bitcast.62, bf16[8,128,1536]{2,1,0:T(8,128)(2,1)} %bitcast.48, bf16[8,128,1536]{2,1,0:T(8,128)(2,1)} %bitcast.52, ...), custom_call_target="tpu_custom_call" | custom-call | flops 1024 | bytes 1024 | tf_op jit(solution)/shard_map/pallas_call | solution.py:802
  140.9 12.8 %collective-permute-done.10.k1.v1 = bf16[1024,512]{1,0:T(8,128)(2,1)S(1)} collective-permute-done((bf16[1024,512]{1,0:T(8,128)(2,1)}, bf16[1024,512]{1,0:T(8,128)(2,1)S(1)}, u32[]{:S(2)}, u32[]{:S(2)}) %collective-permute-start.10) | collective-permute-done | bytes 1048608 | tf_op jit(solution)/shard_map/ppermute | solution.py:872
  154.7 20.6 %shard_map.364 = (bf16[256,512]{1,0:T(8,128)(2,1)}, bf16[256,512]{1,0:T(8,128)(2,1)}, f32[4,2,512]{2,1,0:T(2,128)}) custom-call(s32[7]{0:T(128)} %stack.24.w, bf16[256,512]{1,0:T(8,128)(2,1)} %get-tuple-element.133.qa_ref.qa, bf16[256,512]{1,0:T(8,128)(2,1)} %copy-done.23, bf16[1024,512]{1,0:T(8,128)(2,1)} %get-tuple-element.138.k0.v0, ...), custom_call_target="tpu_custom_call" | custom-call | flops 1024 | bytes 1024 | tf_op jit(solution)/shard_map/pallas_call | solution.py:1229
  175.4 1.7 collective-permute-done.11.refs_1_.refs_6_
  177.9 5.8 %shard_map.365 = (f32[256,1024]{1,0:T(8,128)}, f32[256,1]{1,0:T(8,128)}, bf16[256,1024]{1,0:T(8,128)(2,1)}) custom-call(s32[7]{0:T(128)} %stack.24.w, bf16[256,512]{1,0:T(8,128)(2,1)} %get-tuple-element.139.refs_0_.refs_5_, bf16[256,512]{1,0:T(8,128)(2,1)} %copy-done.21, f32[256,1024]{1,0:T(8,128)} %get-tuple-element.141.refs_2_.refs_3_, ...), custom_call_target="tpu_custom_call" | custom-call | flops 1024 | bytes 1024 | tf_op jit(solution)/shard_map/pallas_call | solution.py:802
  185.1 12.8 %collective-permute-done.14.refs_0_.refs_1_ = bf16[256,1024]{1,0:T(8,128)(2,1)S(1)} collective-permute-done((bf16[256,1024]{1,0:T(8,128)(2,1)}, bf16[256,1024]{1,0:T(8,128)(2,1)S(1)}, u32[]{:S(2)}, u32[]{:S(2)}) %collective-permute-start.14) | collective-permute-done | bytes 524320 | tf_op jit(solution)/shard_map/ppermute | solution.py:872
  198.4 2.1 collective-permute-done.15.refs_1_.refs_3_
  201.4 8.3 %shard_map.367 = (bf16[256,1024]{1,0:T(8,128)(2,1)}, bf16[256,1024]{1,0:T(8,128)(2,1)}, bf16[512,1024]{1,0:T(8,128)(2,1)}, bf16[512,1024]{1,0:T(8,128)(2,1)}) custom-call(s32[7]{0:T(128)} %stack.24.w, bf16[256,1024]{1,0:T(8,128)(2,1)} %copy-done.13, bf16[256,1024]{1,0:T(8,128)(2,1)} %copy-done.14, ...), custom_call_target="tpu_custom_call" | custom-call | flops 1024 | bytes 1024 | tf_op jit(solution)/shard_map/pallas_call | solution.py:802
  210.8 8.3 %shard_map.366 = (bf16[256,1024]{1,0:T(8,128)(2,1)}, bf16[256,1024]{1,0:T(8,128)(2,1)}, bf16[512,1024]{1,0:T(8,128)(2,1)}, bf16[512,1024]{1,0:T(8,128)(2,1)}) custom-call(s32[7]{0:T(128)} %stack.24.w, bf16[256,1024]{1,0:T(8,128)(2,1)} %get-tuple-element.142.refs_0_, bf16[256,1024]{1,0:T(8,128)(2,1)} %copy-done.15, ...), custom_call_target="tpu_custom_call" | custom-call | flops 1024 | bytes 1024 | tf_op jit(solution)/shard_map/pallas_call | solution.py:802
  221.3 12.5 %collective-permute-done.17.refs_2_ = bf16[256,1024]{1,0:T(8,128)(2,1)S(1)} collective-permute-done((bf16[256,1024]{1,0:T(8,128)(2,1)S(1)}, bf16[256,1024]{1,0:T(8,128)(2,1)S(1)}, u32[]{:S(2)}, u32[]{:S(2)}) %collective-permute-start.17) | collective-permute-done | bytes 524320 | tf_op jit(solution)/shard_map/ppermute | solution.py:872
  234.6 4.9 shard_map.368
  240.9 12.0 %collective-permute-done.20.refs_0_.refs_5_ = bf16[256,1024]{1,0:T(8,128)(2,1)S(1)} collective-permute-done((bf16[256,1024]{1,0:T(8,128)(2,1)}, bf16[256,1024]{1,0:T(8,128)(2,1)S(1)}, u32[]{:S(2)}, u32[]{:S(2)}) %collective-permute-start.20) | collective-permute-done | bytes 524320 | tf_op jit(solution)/shard_map/ppermute | solution.py:872
  253.4 2.1 collective-permute-done.21.refs_1_.refs_7_
  256.3 8.0 %shard_map.370 = (bf16[256,1024]{1,0:T(8,128)(2,1)}, bf16[256,1024]{1,0:T(8,128)(2,1)}, bf16[512,1024]{1,0:T(8,128)(2,1)}) custom-call(s32[7]{0:T(128)} %stack.24.w, bf16[256,1024]{1,0:T(8,128)(2,1)} %copy-done.6, bf16[256,1024]{1,0:T(8,128)(2,1)} %copy-done.7, bf16[512,1024]{1,0:T(8,128)(2,1)} %get-tuple-element.155.refs_2_, bf16[8,256,1024]{2,1,0:T(8,128)(2,1)} %bitcast.46), custom_call_target="tpu_custom_call" | custom-call | flops 1024 | bytes 1024 | tf_op jit(solution)/shard_map/pallas_call | solution.py:802
  265.3 8.3 %shard_map.369 = (bf16[256,1024]{1,0:T(8,128)(2,1)}, bf16[256,1024]{1,0:T(8,128)(2,1)}, bf16[512,1024]{1,0:T(8,128)(2,1)}) custom-call(s32[7]{0:T(128)} %stack.24.w, bf16[256,1024]{1,0:T(8,128)(2,1)} %get-tuple-element.151.refs_0_.refs_4_, bf16[256,1024]{1,0:T(8,128)(2,1)} %copy-done.8, bf16[512,1024]{1,0:T(8,128)(2,1)} %get-tuple-element.152.refs_2_, ...), custom_call_target="tpu_custom_call" | custom-call | flops 1024 | bytes 1024 | tf_op jit(solution)/shard_map/pallas_call | solution.py:802
  273.8 10.8 %shard_map.371 = (bf16[8,256,1024]{2,1,0:T(8,128)(2,1)}, f32[8,1024]{1,0:T(8,128)}) custom-call(s32[7]{0:T(128)} %stack.24.w, bf16[256,1024]{1,0:T(8,128)(2,1)} %get-tuple-element.142.refs_0_, bf16[256,1024]{1,0:T(8,128)(2,1)} %copy-done.13, bf16[256,1024]{1,0:T(8,128)(2,1)} %copy-done.15, bf16[256,1024]{1,0:T(8,128)(2,1)} %copy-done.14, ...), custom_call_target="tpu_custom_call" | custom-call | flops 1024 | bytes 1024 | tf_op jit(solution)/shard_map/pallas_call | solution.py:802
  287.6 12.4 %collective-permute-done.23.refs_2_ = bf16[256,1024]{1,0:T(8,128)(2,1)S(1)} collective-permute-done((bf16[256,1024]{1,0:T(8,128)(2,1)S(1)}, bf16[256,1024]{1,0:T(8,128)(2,1)S(1)}, u32[]{:S(2)}, u32[]{:S(2)}) %collective-permute-start.23) | collective-permute-done | bytes 524320 | tf_op jit(solution)/shard_map/ppermute | solution.py:872
  300.9 5.8 %shard_map.372 = (f32[256,1024]{1,0:T(8,128)}, bf16[256,1024]{1,0:T(8,128)(2,1)}, bf16[256,512]{1,0:T(8,128)(2,1)}, bf16[256,512]{1,0:T(8,128)(2,1)}, f32[8,1024]{1,0:T(8,128)}) custom-call(s32[7]{0:T(128)} %stack.24.w, bf16[256,1024]{1,0:T(8,128)(2,1)} %get-tuple-element.153.refs_0_, bf16[256,1024]{1,0:T(8,128)(2,1)} %copy-done.29, ...), custom_call_target="tpu_custom_call" | custom-call | flops 1024 | bytes 1024 | tf_op jit(solution)/shard_map/pallas_call | solution.py:802
  306.8 1.7 collective-permute-done.24.gb
  309.3 25.0 %shard_map.373 = (bf16[256,512]{1,0:T(8,128)(2,1)}, bf16[256,512]{1,0:T(8,128)(2,1)}, bf16[1024,256]{1,0:T(8,128)(2,1)}, bf16[1024,256]{1,0:T(8,128)(2,1)}, bf16...) custom-call(s32[7]{0:T(128)} %stack.24.w, bf16[256,512]{1,0:T(8,128)(2,1)} %get-tuple-element.133.qa_ref.qa, ...), custom_call_target="tpu_custom_call" | custom-call | flops 1024 | bytes 1024 | tf_op jit(solution)/shard_map/pallas_call | solution.py:1496
  336.8 7.3 %shard_map.374 = (f32[256,1024]{1,0:T(8,128)}, bf16[256,1024]{1,0:T(8,128)(2,1)}, bf16[1024,256]{1,0:T(8,128)(2,1)}, f32[8,1024]{1,0:T(8,128)}) custom-call(s32[7]{0:T(128)} %stack.24.w, bf16[256,512]{1,0:T(8,128)(2,1)} %get-tuple-element.170.refs_0_, bf16[256,512]{1,0:T(8,128)(2,1)} %copy-done.22, f32[256,1024]{1,0:T(8,128)} %get-tuple-element.172.refs_2_, ...), custom_call_target="tpu_custom_call" | custom-call | flops 1024 | bytes 1024 | tf_op jit(solution)/shard_map/pallas_call | solution.py:802
  344.0 7.6 %shard_map.375 = (bf16[8,128,1536]{2,1,0:T(8,128)(2,1)}, bf16[8,128,1536]{2,1,0:T(8,128)(2,1)}) custom-call(s32[7]{0:T(128)} %stack.24.w, bf16[256,512]{1,0:T(8,128)(2,1)} %get-tuple-element.170.refs_0_, bf16[256,512]{1,0:T(8,128)(2,1)} %copy-done.22, bf16[256,1024]{1,0:T(8,128)(2,1)} %get-tuple-element.177.refs_2_, bf16[1024,256]{1,0:T(8,128)(2,1)} %bitcast.63, ...), custom_call_target="tpu_custom_call" | custom-call | flops 1024 | bytes 1024 | tf_op jit(solution)/shard_map/pallas_call | solution.py:802
  351.8 5.7 %collective-permute-done.26.refs_1_ = bf16[8,128,1536]{2,1,0:T(8,128)(2,1)S(1)} collective-permute-done((bf16[8,128,1536]{2,1,0:T(8,128)(2,1)}, bf16[8,128,1536]{2,1,0:T(8,128)(2,1)S(1)}, u32[]{:S(2)}, u32[]{:S(2)}) %collective-permute-start.26) | collective-permute-done | bytes 3145760 | tf_op jit(solution)/shard_map/ppermute | solution.py:869
  357.5 1.6 copy-done.5
  359.1 6.0 %shard_map.376 = (bf16[512,1536]{1,0:T(8,128)(2,1)}, bf16[512,1536]{1,0:T(8,128)(2,1)}) custom-call(s32[7]{0:T(128)} %stack.24.w, bf16[8,128,1536]{2,1,0:T(8,128)(2,1)} %get-tuple-element.181.refs_0_, bf16[8,128,1536]{2,1,0:T(8,128)(2,1)} %copy-done.5), custom_call_target="tpu_custom_call" | custom-call | flops 1024 | bytes 1024 | tf_op jit(solution)/shard_map/pallas_call | solution.py:802
  366.5 12.3 %all_to_all.59 = bf16[4,256,256]{2,1,0:T(8,128)(2,1)} all-to-all(bf16[4,256,256]{2,1,0:T(8,128)(2,1)S(1)} %bitcast.73), channel_id=1, replica_groups=mesh['seq'=4,'fsdp'=8] {'seq'}, dimensions={0} | all-to-all | bytes 1048576 | tf_op jit(solution)/shard_map/all_to_all | solution.py:898
  379.2 1.7 collective-permute-start.28
  380.9 18.0 %shard_map.377 = (bf16[1024,256]{1,0:T(8,128)(2,1)}, bf16[1024,256]{1,0:T(8,128)(2,1)}, bf16[1024,256]{1,0:T(8,128)(2,1)}) custom-call(s32[7]{0:T(128)} %stack.24.w, bf16[1024,768]{1,0:T(8,128)(2,1)} %get-tuple-element.128.q_ref.k_ref.v_ref, bf16[1024,768]{1,0:T(8,128)(2,1)} %get-tuple-element.128.q_ref.k_ref.v_ref, ...), custom_call_target="tpu_custom_call" | custom-call | flops 1024 | bytes 1024 | tf_op jit(solution)/shard_map/pallas_call | solution.py:1641
  398.9 4.7 collective-permute-done.28.refs_9_
  404.4 10.2 %shard_map.378 = (bf16[256,1024]{1,0:T(8,128)(2,1)}, bf16[256,1024]{1,0:T(8,128)(2,1)}, bf16[256,1024]{1,0:T(8,128)(2,1)}, bf16[256,1024]{1,0:T(8,128)(2,1)}, bf...) custom-call(s32[7]{0:T(128)} %stack.24.w, bf16[1024,256]{1,0:T(8,128)(2,1)} %get-tuple-element.202.refs_0_, ...), custom_call_target="tpu_custom_call" | custom-call | flops 1024 | bytes 1024 | tf_op jit(solution)/shard_map/pallas_call | solution.py:802
  416.2 3.9 all-to-all-start.4
  420.2 6.2 %shard_map.379 = (bf16[256,1024]{1,0:T(8,128)(2,1)}, bf16[256,1024]{1,0:T(8,128)(2,1)}, bf16[256,1024]{1,0:T(8,128)(2,1)}, bf16[256,1024]{1,0:T(8,128)(2,1)}) custom-call(s32[7]{0:T(128)} %stack.24.w, bf16[1024,256]{1,0:T(8,128)(2,1)} %get-tuple-element.202.refs_0_, bf16[1024,256]{1,0:T(8,128)(2,1)} %get-tuple-element.187.refs_1_, ...), custom_call_target="tpu_custom_call" | custom-call | flops 1024 | bytes 1024 | tf_op jit(solution)/shard_map/pallas_call | solution.py:802
  430.6 11.9 %collective-permute-done.35 = bf16[256,1024]{1,0:T(8,128)(2,1)} collective-permute-done((bf16[256,1024]{1,0:T(8,128)(2,1)S(1)}, bf16[256,1024]{1,0:T(8,128)(2,1)}, u32[]{:S(2)}, u32[]{:S(2)}) %collective-permute-start.35) | collective-permute-done | bytes 524320 | tf_op jit(solution)/shard_map/ppermute | solution.py:872
  442.5 11.2 %collective-permute-done.37.refs_1_ = bf16[256,1024]{1,0:T(8,128)(2,1)} collective-permute-done((bf16[256,1024]{1,0:T(8,128)(2,1)}, bf16[256,1024]{1,0:T(8,128)(2,1)}, u32[]{:S(2)}, u32[]{:S(2)}) %collective-permute-start.37) | collective-permute-done | bytes 524320 | tf_op jit(solution)/shard_map/ppermute | solution.py:872
  453.7 2.3 add_convert_fusion.2
  456.0 8.5 %collective-permute-done.32 = bf16[256,1024]{1,0:T(8,128)(2,1)S(1)} collective-permute-done((bf16[256,1024]{1,0:T(8,128)(2,1)S(1)}, bf16[256,1024]{1,0:T(8,128)(2,1)S(1)}, u32[]{:S(2)}, u32[]{:S(2)}) %collective-permute-start.32) | collective-permute-done | bytes 524320 | tf_op jit(solution)/shard_map/ppermute | solution.py:872
  465.9 4.7 shard_map.380
  470.6 2.8 add_convert_fusion.1
  473.4 5.1 all-to-all-start.5
  479.1 34.2 %all-to-all-done.5 = bf16[4,144,1280]{2,1,0:T(8,128)(2,1)S(1)} async-done(((bf16[4,144,1280]{2,1,0:T(8,128)(2,1)}), bf16[4,144,1280]{2,1,0:T(8,128)(2,1)S(1)}, u32[]{:S(2)}, u32[]{:S(2)}) %all-to-all-start.5) | async-done | bytes 1474592 | tf_op jit(solution)/shard_map/all_to_all | solution.py:877
  514.9 2.6 shard_map.382.refs_0_
  518.0 5.1 collective-permute-done.40.refs_1_
  523.9 3.0 shard_map.383
  528.4 3.7 shard_map.381
  (183 shorter events, 44.8 us)
Async XLA Ops:
  11.4 28.5 %all-to-all-start = ((bf16[4,144,768]{2,1,0:T(8,128)(2,1)}), bf16[4,144,768]{2,1,0:T(8,128)(2,1)S(1)}, u32[]{:S(2)}, u32[]{:S(2)}) async-start(bf16[4,144,768]{2,1,0:T(8,128)(2,1)} %shard_map.356), calls=%async_computation | async-start | bytes 1769472 | tf_op jit(solution)/shard_map/all_to_all | solution.py:877
  17.8 89.1 %all-gather.3.cloned.1.call-start = ((), (), s32[]{:S(2)}) async-start(), calls=%async_computation.7 | async-start | bytes 3538944 | tf_op jit(solution)/shard_map/all_gather | solution.py:1014
  17.8 13.4 %collective-permute-start = (bf16[256,1024]{1,0:T(8,128)(2,1)S(1)}, bf16[256,1024]{1,0:T(8,128)(2,1)S(1)}, u32[]{:S(2)}, u32[]{:S(2)}) collective-permute-start(bf16[256,1024]{1,0:T(8,128)(2,1)S(1)} %bitcast.60), channel_id=1, source_target_pairs={{0,16},{8,24},{16,0},{24,8},{1,17},{9,25},{17,1},{25,9},{2,18},{10... | collective-permute-start | bytes 1572872 | tf_op jit(solution)/shard_map/ppermute | solution.py:872
  25.0 20.8 %copy-start.9 = (bf16[1,256,1024]{2,1,0:T(8,128)(2,1)S(1)}, bf16[1,256,1024]{2,1,0:T(8,128)(2,1)}, u32[]{:S(2)}) copy-start(bf16[1,256,1024]{2,1,0:T(8,128)(2,1)} %param.22) | copy-start | bytes 1572868
  31.2 38.8 %copy-start.10 = (bf16[256,1024]{1,0:T(8,128)(2,1)}, bf16[256,1024]{1,0:T(8,128)(2,1)S(1)}, u32[]{:S(2)}) copy-start(bf16[256,1024]{1,0:T(8,128)(2,1)S(1)} %collective-permute-done.refs_1_.refs_13_) | copy-start | bytes 1572868
  40.0 30.1 %copy-start.2 = (bf16[4,144,768]{2,1,0:T(8,128)(2,1)}, bf16[4,144,768]{2,1,0:T(8,128)(2,1)S(1)}, u32[]{:S(2)}) copy-start(bf16[4,144,768]{2,1,0:T(8,128)(2,1)S(1)} %all-to-all-done) | copy-start | bytes 2654212
  40.0 30.0 %collective-permute-start.4 = (bf16[576,768]{1,0:T(8,128)(2,1)S(1)}, bf16[576,768]{1,0:T(8,128)(2,1)S(1)}, u32[]{:S(2)}, u32[]{:S(2)}) collective-permute-start(bf16[576,768]{1,0:T(8,128)(2,1)S(1)} %bitcast.56), channel_id=1, source_target_pairs={{0,1},{1,0},{2,3},{3,2},{4,5},{5,4},{6,7},{7,6},{8,9},{9,8},{10,11... | collective-permute-start | bytes 2654216 | tf_op jit(solution)/shard_map/ppermute | solution.py:881
  41.6 28.4 %all-to-all-start.1 = ((bf16[4,128,512]{2,1,0:T(8,128)(2,1)}), bf16[4,128,512]{2,1,0:T(8,128)(2,1)}, u32[]{:S(2)}, u32[]{:S(2)}) async-start(bf16[4,128,512]{2,1,0:T(8,128)(2,1)} %shard_map.358), calls=%async_computation.1 | async-start | bytes 1048576 | tf_op jit(solution)/shard_map/all_to_all | solution.py:877
  45.7 152.7 %all-gather.5.cloned.1.call-start = ((), (), s32[]{:S(2)}) async-start(), calls=%async_computation.8 | async-start | bytes 4718592 | tf_op jit(solution)/shard_map/all_gather | solution.py:1112
  45.8 12.8 %collective-permute-start.3 = (bf16[256,1024]{1,0:T(8,128)(2,1)S(1)}, bf16[256,1024]{1,0:T(8,128)(2,1)}, u32[]{:S(2)}, u32[]{:S(2)}) collective-permute-start(bf16[256,1024]{1,0:T(8,128)(2,1)S(1)} %bitcast.69), channel_id=1, source_target_pairs={{0,16},{8,24},{16,0},{24,8},{1,17},{9,25},{17,1},{25,9},{2,18},{10... | collective-permute-start | bytes 1572872 | tf_op jit(solution)/shard_map/ppermute | solution.py:872
  47.4 22.7 %collective-permute-start.1 = (bf16[256,1024]{1,0:T(8,128)(2,1)S(1)}, bf16[256,1024]{1,0:T(8,128)(2,1)}, u32[]{:S(2)}, u32[]{:S(2)}) collective-permute-start(bf16[256,1024]{1,0:T(8,128)(2,1)S(1)} %bitcast.61), channel_id=1, source_target_pairs={{0,8},{8,0},{16,24},{24,16},{1,9},{9,1},{17,25},{25,17},{2,10},{10... | collective-permute-start | bytes 1572872 | tf_op jit(solution)/shard_map/ppermute | solution.py:869
  47.4 22.7 %collective-permute-start.2 = (bf16[256,1024]{1,0:T(8,128)(2,1)S(1)}, bf16[256,1024]{1,0:T(8,128)(2,1)}, u32[]{:S(2)}, u32[]{:S(2)}) collective-permute-start(bf16[256,1024]{1,0:T(8,128)(2,1)S(1)} %collective-permute-done.refs_1_.refs_13_), channel_id=1, source_target_pairs={{0,8},{8,0},{16,24},{24,16},{1,9},{9,1},{17,25},{25,17},{2,10},{10... | collective-permute-start | bytes 1572872 | tf_op jit(solution)/shard_map/ppermute | solution.py:869
  76.7 351.6 %reduce-scatter.2.cloned.1.call-start = ((), (), s32[]{:S(2)}) async-start(), calls=%async_computation.9 | async-start | bytes 4718592 | tf_op jit(solution)/shard_map/reduce_scatter | solution.py:1402
  106.8 25.6 %collective-permute-start.5 = (bf16[1024,1536]{1,0:T(8,128)(2,1)}, bf16[1024,1536]{1,0:T(8,128)(2,1)S(1)}, u32[]{:S(2)}, u32[]{:S(2)}) collective-permute-start(bf16[1024,1536]{1,0:T(8,128)(2,1)} %all-gather.3.cloned.1.call-done), channel_id=1, source_target_pairs={{0,8},{8,0},{16,24},{24,16},{1,9},{9,1},{17,25},{25,17},{2,10},{10... | collective-permute-start | bytes 9437192 | tf_op jit(solution)/shard_map/ppermute | solution.py:869
  106.8 14.7 %collective-permute-start.7 = (bf16[256,1024]{1,0:T(8,128)(2,1)S(1)}, bf16[256,1024]{1,0:T(8,128)(2,1)S(1)}, u32[]{:S(2)}, u32[]{:S(2)}) collective-permute-start(bf16[256,1024]{1,0:T(8,128)(2,1)S(1)} %bitcast.70), channel_id=1, source_target_pairs={{0,8},{8,0},{16,24},{24,16},{1,9},{9,1},{17,25},{25,17},{2,10},{10... | collective-permute-start | bytes 1572872 | tf_op jit(solution)/shard_map/ppermute | solution.py:869
  107.3 17.0 %collective-permute-start.9 = (bf16[512,512]{1,0:T(8,128)(2,1)}, bf16[512,512]{1,0:T(8,128)(2,1)S(1)}, u32[]{:S(2)}, u32[]{:S(2)}) collective-permute-start(bf16[512,512]{1,0:T(8,128)(2,1)} %bitcast.8), channel_id=1, source_target_pairs={{0,1},{1,0},{2,3},{3,2},{4,5},{5,4},{6,7},{7,6},{8,9},{9,8},{10,11... | collective-permute-start | bytes 1572872 | tf_op jit(solution)/shard_map/ppermute | solution.py:881
  108.2 16.1 %collective-permute-start.8 = (bf16[256,1024]{1,0:T(8,128)(2,1)}, bf16[256,1024]{1,0:T(8,128)(2,1)S(1)}, u32[]{:S(2)}, u32[]{:S(2)}) collective-permute-start(bf16[256,1024]{1,0:T(8,128)(2,1)} %collective-permute-done.3.refs_1_.refs_17_), channel_id=1, source_target_pairs={{0,8},{8,0},{16,24},{24,16},{1,9},{9,1},{17,25},{25,17},{2,10},{10... | collective-permute-start | bytes 1572872 | tf_op jit(solution)/shard_map/ppermute | solution.py:869
  131.0 22.7 %collective-permute-start.10 = (bf16[1024,512]{1,0:T(8,128)(2,1)}, bf16[1024,512]{1,0:T(8,128)(2,1)S(1)}, u32[]{:S(2)}, u32[]{:S(2)}) collective-permute-start(bf16[1024,512]{1,0:T(8,128)(2,1)} %get-tuple-element.138.k0.v0), channel_id=1, source_target_pairs={{0,16},{8,24},{16,0},{24,8},{1,17},{9,25},{17,1},{25,9},{2,18},{10... | collective-permute-start | bytes 3145736 | tf_op jit(solution)/shard_map/ppermute | solution.py:872
  140.8 12.9 %collective-permute-start.6 = (bf16[256,512]{1,0:T(8,128)(2,1)}, bf16[256,512]{1,0:T(8,128)(2,1)S(1)}, u32[]{:S(2)}, u32[]{:S(2)}) collective-permute-start(bf16[256,512]{1,0:T(8,128)(2,1)} %get-tuple-element.134), channel_id=1, source_target_pairs={{0,8},{8,0},{16,24},{24,16},{1,9},{9,1},{17,25},{25,17},{2,10},{10... | collective-permute-start | bytes 786440 | tf_op jit(solution)/shard_map/ppermute | solution.py:869
  175.3 1.8 collective-permute-start.11
  183.7 14.2 %collective-permute-start.14 = (bf16[256,1024]{1,0:T(8,128)(2,1)}, bf16[256,1024]{1,0:T(8,128)(2,1)S(1)}, u32[]{:S(2)}, u32[]{:S(2)}) collective-permute-start(bf16[256,1024]{1,0:T(8,128)(2,1)} %get-tuple-element.142.refs_0_), channel_id=1, source_target_pairs={{0,16},{8,24},{16,0},{24,8},{1,17},{9,25},{17,1},{25,9},{2,18},{10... | collective-permute-start | bytes 1572872 | tf_op jit(solution)/shard_map/ppermute | solution.py:872
  197.9 2.6 collective-permute-start.15
  197.9 12.0 %collective-permute-start.12 = (bf16[256,1024]{1,0:T(8,128)(2,1)}, bf16[256,1024]{1,0:T(8,128)(2,1)S(1)}, u32[]{:S(2)}, u32[]{:S(2)}) collective-permute-start(bf16[256,1024]{1,0:T(8,128)(2,1)} %get-tuple-element.142.refs_0_), channel_id=1, source_target_pairs={{0,8},{8,0},{16,24},{24,16},{1,9},{9,1},{17,25},{25,17},{2,10},{10... | collective-permute-start | bytes 1572872 | tf_op jit(solution)/shard_map/ppermute | solution.py:869
  209.7 9.8 %collective-permute-start.16 = (bf16[256,1024]{1,0:T(8,128)(2,1)}, bf16[256,1024]{1,0:T(8,128)(2,1)S(1)}, u32[]{:S(2)}, u32[]{:S(2)}) collective-permute-start(bf16[256,1024]{1,0:T(8,128)(2,1)} %get-tuple-element.148), channel_id=1, source_target_pairs={{0,8},{8,0},{16,24},{24,16},{1,9},{9,1},{17,25},{25,17},{2,10},{10... | collective-permute-start | bytes 1572872 | tf_op jit(solution)/shard_map/ppermute | solution.py:869
  219.1 2.2 collective-permute-start.13
  219.8 14.0 %collective-permute-start.17 = (bf16[256,1024]{1,0:T(8,128)(2,1)S(1)}, bf16[256,1024]{1,0:T(8,128)(2,1)S(1)}, u32[]{:S(2)}, u32[]{:S(2)}) collective-permute-start(bf16[256,1024]{1,0:T(8,128)(2,1)S(1)} %add_convert_fusion.7), channel_id=1, source_target_pairs={{0,16},{8,24},{16,0},{24,8},{1,17},{9,25},{17,1},{25,9},{2,18},{10... | collective-permute-start | bytes 1572872 | tf_op jit(solution)/shard_map/ppermute | solution.py:872
  221.3 12.5 %copy-start.35 = (bf16[256,1024]{1,0:T(8,128)(2,1)}, bf16[256,1024]{1,0:T(8,128)(2,1)S(1)}, u32[]{:S(2)}) copy-start(bf16[256,1024]{1,0:T(8,128)(2,1)S(1)} %collective-permute-done.13.refs_1_) | copy-start | bytes 1572868
  239.5 13.4 %collective-permute-start.20 = (bf16[256,1024]{1,0:T(8,128)(2,1)}, bf16[256,1024]{1,0:T(8,128)(2,1)S(1)}, u32[]{:S(2)}, u32[]{:S(2)}) collective-permute-start(bf16[256,1024]{1,0:T(8,128)(2,1)} %get-tuple-element.151.refs_0_.refs_4_), channel_id=1, source_target_pairs={{0,16},{8,24},{16,0},{24,8},{1,17},{9,25},{17,1},{25,9},{2,18},{10... | collective-permute-start | bytes 1572872 | tf_op jit(solution)/shard_map/ppermute | solution.py:872
  252.9 2.6 collective-permute-start.21
  252.9 11.6 %collective-permute-start.18 = (bf16[256,1024]{1,0:T(8,128)(2,1)}, bf16[256,1024]{1,0:T(8,128)(2,1)S(1)}, u32[]{:S(2)}, u32[]{:S(2)}) collective-permute-start(bf16[256,1024]{1,0:T(8,128)(2,1)} %get-tuple-element.151.refs_0_.refs_4_), channel_id=1, source_target_pairs={{0,8},{8,0},{16,24},{24,16},{1,9},{9,1},{17,25},{25,17},{2,10},{10... | collective-permute-start | bytes 1572872 | tf_op jit(solution)/shard_map/ppermute | solution.py:869
  264.3 9.3 %collective-permute-start.22 = (bf16[256,1024]{1,0:T(8,128)(2,1)}, bf16[256,1024]{1,0:T(8,128)(2,1)S(1)}, u32[]{:S(2)}, u32[]{:S(2)}) collective-permute-start(bf16[256,1024]{1,0:T(8,128)(2,1)} %get-tuple-element.157), channel_id=1, source_target_pairs={{0,8},{8,0},{16,24},{24,16},{1,9},{9,1},{17,25},{25,17},{2,10},{10... | collective-permute-start | bytes 1572872 | tf_op jit(solution)/shard_map/ppermute | solution.py:869
  285.7 1.9 collective-permute-start.19
  286.1 14.0 %collective-permute-start.23 = (bf16[256,1024]{1,0:T(8,128)(2,1)S(1)}, bf16[256,1024]{1,0:T(8,128)(2,1)S(1)}, u32[]{:S(2)}, u32[]{:S(2)}) collective-permute-start(bf16[256,1024]{1,0:T(8,128)(2,1)S(1)} %add_convert_fusion.6), channel_id=1, source_target_pairs={{0,16},{8,24},{16,0},{24,8},{1,17},{9,25},{17,1},{25,9},{2,18},{10... | collective-permute-start | bytes 1572872 | tf_op jit(solution)/shard_map/ppermute | solution.py:872
  287.6 12.4 %copy-start.29 = (bf16[256,1024]{1,0:T(8,128)(2,1)}, bf16[256,1024]{1,0:T(8,128)(2,1)S(1)}, u32[]{:S(2)}) copy-start(bf16[256,1024]{1,0:T(8,128)(2,1)S(1)} %collective-permute-done.19.refs_1_) | copy-start | bytes 1572868
  306.8 1.8 collective-permute-start.24
  334.3 1.8 collective-permute-start.25
  351.6 5.9 %collective-permute-start.26 = (bf16[8,128,1536]{2,1,0:T(8,128)(2,1)}, bf16[8,128,1536]{2,1,0:T(8,128)(2,1)S(1)}, u32[]{:S(2)}, u32[]{:S(2)}) collective-permute-start(bf16[8,128,1536]{2,1,0:T(8,128)(2,1)} %get-tuple-element.182), channel_id=1, source_target_pairs={{0,8},{8,0},{16,24},{24,16},{1,9},{9,1},{17,25},{25,17},{2,10},{10... | collective-permute-start | bytes 9437192 | tf_op jit(solution)/shard_map/ppermute | solution.py:869
  359.1 19.8 %copy-start.45 = (bf16[1024,256]{1,0:T(8,128)(2,1)S(1)}, bf16[1024,256]{1,0:T(8,128)(2,1)}, u32[]{:S(2)}) copy-start(bf16[1024,256]{1,0:T(8,128)(2,1)} %get-tuple-element.198) | copy-start | bytes 1572868
  359.1 20.1 %copy-start.44 = (bf16[1024,256]{1,0:T(8,128)(2,1)S(1)}, bf16[1024,256]{1,0:T(8,128)(2,1)}, u32[]{:S(2)}) copy-start(bf16[1024,256]{1,0:T(8,128)(2,1)} %get-tuple-element.196) | copy-start | bytes 1572868
  365.1 49.5 %collective-permute-start.27 = (bf16[512,1536]{1,0:T(8,128)(2,1)}, bf16[512,1536]{1,0:T(8,128)(2,1)S(1)}, u32[]{:S(2)}, u32[]{:S(2)}) collective-permute-start(bf16[512,1536]{1,0:T(8,128)(2,1)} %get-tuple-element.186), channel_id=1, source_target_pairs={{0,1},{1,0},{2,3},{3,2},{4,5},{5,4},{6,7},{7,6},{8,9},{9,8},{10,11... | collective-permute-start | bytes 4718600 | tf_op jit(solution)/shard_map/ppermute | solution.py:881
  378.9 20.0 %collective-permute-start.29 = (bf16[1024,256]{1,0:T(8,128)(2,1)S(1)}, bf16[1024,256]{1,0:T(8,128)(2,1)S(1)}, u32[]{:S(2)}, u32[]{:S(2)}) collective-permute-start(bf16[1024,256]{1,0:T(8,128)(2,1)S(1)} %copy-done.45), channel_id=1, source_target_pairs={{0,16},{8,24},{16,0},{24,8},{1,17},{9,25},{17,1},{25,9},{2,18},{10... | collective-permute-start | bytes 1572872 | tf_op jit(solution)/shard_map/ppermute | solution.py:872
  379.2 24.4 %collective-permute-start.28 = (bf16[1024,256]{1,0:T(8,128)(2,1)S(1)}, bf16[1024,256]{1,0:T(8,128)(2,1)S(1)}, u32[]{:S(2)}, u32[]{:S(2)}) collective-permute-start(bf16[1024,256]{1,0:T(8,128)(2,1)S(1)} %copy-done.44), channel_id=1, source_target_pairs={{0,16},{8,24},{16,0},{24,8},{1,17},{9,25},{17,1},{25,9},{2,18},{10... | collective-permute-start | bytes 1572872 | tf_op jit(solution)/shard_map/ppermute | solution.py:872
  416.2 49.4 %all-to-all-start.4 = ((bf16[4,128,1536]{2,1,0:T(8,128)(2,1)}), bf16[4,128,1536]{2,1,0:T(8,128)(2,1)S(1)}, u32[]{:S(2)}, u32[]{:S(2)}) async-start(bf16[4,128,1536]{2,1,0:T(8,128)(2,1)} %bitcast.25), calls=%async_computation.4 | async-start | bytes 3145728 | tf_op jit(solution)/shard_map/all_to_all | solution.py:877
  420.1 7.3 %collective-permute-start.34 = (bf16[256,1024]{1,0:T(8,128)(2,1)S(1)}, bf16[256,1024]{1,0:T(8,128)(2,1)S(1)}, u32[]{:S(2)}, u32[]{:S(2)}) collective-permute-start(bf16[256,1024]{1,0:T(8,128)(2,1)S(1)} %copy-done.46), channel_id=1, source_target_pairs={{0,8},{8,0},{16,24},{24,16},{1,9},{9,1},{17,25},{25,17},{2,10},{10... | collective-permute-start | bytes 1572872 | tf_op jit(solution)/shard_map/ppermute | solution.py:869
  426.4 3.3 collective-permute-start.31
  426.8 43.8 %collective-permute-start.36 = (bf16[576,1280]{1,0:T(8,128)(2,1)}, bf16[576,1280]{1,0:T(8,128)(2,1)}, u32[]{:S(2)}, u32[]{:S(2)}) collective-permute-start(bf16[576,1280]{1,0:T(8,128)(2,1)} %get-tuple-element.211), channel_id=1, source_target_pairs={{0,1},{1,0},{2,3},{3,2},{4,5},{5,4},{6,7},{7,6},{8,9},{9,8},{10,11... | collective-permute-start | bytes 4423688 | tf_op jit(solution)/shard_map/ppermute | solution.py:881
  427.4 2.5 collective-permute-start.33
  427.6 14.9 %collective-permute-start.35 = (bf16[256,1024]{1,0:T(8,128)(2,1)S(1)}, bf16[256,1024]{1,0:T(8,128)(2,1)}, u32[]{:S(2)}, u32[]{:S(2)}) collective-permute-start(bf16[256,1024]{1,0:T(8,128)(2,1)S(1)} %add_convert_fusion.3), channel_id=1, source_target_pairs={{0,16},{8,24},{16,0},{24,8},{1,17},{9,25},{17,1},{25,9},{2,18},{10... | collective-permute-start | bytes 1572872 | tf_op jit(solution)/shard_map/ppermute | solution.py:872
  428.2 25.5 %copy-start.33 = (bf16[256,1024]{1,0:T(8,128)(2,1)S(1)}, bf16[256,1024]{1,0:T(8,128)(2,1)}, u32[]{:S(2)}) copy-start(bf16[256,1024]{1,0:T(8,128)(2,1)} %get-tuple-element.207) | copy-start | bytes 1572868
  428.3 25.5 %collective-permute-start.37 = (bf16[256,1024]{1,0:T(8,128)(2,1)}, bf16[256,1024]{1,0:T(8,128)(2,1)}, u32[]{:S(2)}, u32[]{:S(2)}) collective-permute-start(bf16[256,1024]{1,0:T(8,128)(2,1)} %reduce-scatter.2.cloned.1.call-done.refs_0_), channel_id=1, source_target_pairs={{0,16},{8,24},{16,0},{24,8},{1,17},{9,25},{17,1},{25,9},{2,18},{10... | collective-permute-start | bytes 1572872 | tf_op jit(solution)/shard_map/ppermute | solution.py:872
  429.7 26.3 %collective-permute-start.30 = (bf16[256,1024]{1,0:T(8,128)(2,1)}, bf16[256,1024]{1,0:T(8,128)(2,1)S(1)}, u32[]{:S(2)}, u32[]{:S(2)}) collective-permute-start(bf16[256,1024]{1,0:T(8,128)(2,1)} %get-tuple-element.204), channel_id=1, source_target_pairs={{0,8},{8,0},{16,24},{24,16},{1,9},{9,1},{17,25},{25,17},{2,10},{10... | collective-permute-start | bytes 1572872 | tf_op jit(solution)/shard_map/ppermute | solution.py:869
  429.7 34.8 %copy-start.20 = (f32[256,1024]{1,0:T(8,128)S(1)}, f32[256,1024]{1,0:T(8,128)}, u32[]{:S(2)}) copy-start(f32[256,1024]{1,0:T(8,128)} %get-tuple-element.174) | copy-start | bytes 3145732
  429.7 34.8 %copy-start.34 = (bf16[256,1024]{1,0:T(8,128)(2,1)S(1)}, bf16[256,1024]{1,0:T(8,128)(2,1)}, u32[]{:S(2)}) copy-start(bf16[256,1024]{1,0:T(8,128)(2,1)} %get-tuple-element.203) | copy-start | bytes 1572868
  429.9 34.5 %collective-permute-start.32 = (bf16[256,1024]{1,0:T(8,128)(2,1)S(1)}, bf16[256,1024]{1,0:T(8,128)(2,1)S(1)}, u32[]{:S(2)}, u32[]{:S(2)}) collective-permute-start(bf16[256,1024]{1,0:T(8,128)(2,1)S(1)} %add_convert_fusion.5), channel_id=1, source_target_pairs={{0,16},{8,24},{16,0},{24,8},{1,17},{9,25},{17,1},{25,9},{2,18},{10... | collective-permute-start | bytes 1572872 | tf_op jit(solution)/shard_map/ppermute | solution.py:872
  442.5 23.4 %collective-permute-start.38 = (bf16[256,1024]{1,0:T(8,128)(2,1)}, bf16[256,1024]{1,0:T(8,128)(2,1)}, u32[]{:S(2)}, u32[]{:S(2)}) collective-permute-start(bf16[256,1024]{1,0:T(8,128)(2,1)} %reduce-scatter.2.cloned.1.call-done.refs_0_), channel_id=1, source_target_pairs={{0,8},{8,0},{16,24},{24,16},{1,9},{9,1},{17,25},{25,17},{2,10},{10... | collective-permute-start | bytes 1572872 | tf_op jit(solution)/shard_map/ppermute | solution.py:869
  453.7 12.2 %collective-permute-start.39 = (bf16[256,1024]{1,0:T(8,128)(2,1)}, bf16[256,1024]{1,0:T(8,128)(2,1)}, u32[]{:S(2)}, u32[]{:S(2)}) collective-permute-start(bf16[256,1024]{1,0:T(8,128)(2,1)} %collective-permute-done.37.refs_1_), channel_id=1, source_target_pairs={{0,8},{8,0},{16,24},{24,16},{1,9},{9,1},{17,25},{25,17},{2,10},{10... | collective-permute-start | bytes 1572872 | tf_op jit(solution)/shard_map/ppermute | solution.py:869
  465.9 12.6 %copy-start.17 = (bf16[128,1536]{1,0:T(8,128)(2,1)}, bf16[128,1536]{1,0:T(8,128)(2,1)S(1)}, u32[]{:S(2)}) copy-start(bf16[128,1536]{1,0:T(8,128)(2,1)S(1)} %reduce_sum.24.refs_0_) | copy-start | bytes 1179652
  473.4 39.8 %all-to-all-start.5 = ((bf16[4,144,1280]{2,1,0:T(8,128)(2,1)}), bf16[4,144,1280]{2,1,0:T(8,128)(2,1)S(1)}, u32[]{:S(2)}, u32[]{:S(2)}) async-start(bf16[4,144,1280]{2,1,0:T(8,128)(2,1)} %bitcast.27), calls=%async_computation.6 | async-start | bytes 2949120 | tf_op jit(solution)/shard_map/all_to_all | solution.py:877
  478.5 35.6 %collective-permute-start.43 = (bf16[128,1536]{1,0:T(8,128)(2,1)S(1)}, bf16[128,1536]{1,0:T(8,128)(2,1)S(1)}, u32[]{:S(2)}, u32[]{:S(2)}) collective-permute-start(bf16[128,1536]{1,0:T(8,128)(2,1)S(1)} %reduce_sum.24.refs_0_), channel_id=1, source_target_pairs={{0,16},{8,24},{16,0},{24,8},{1,17},{9,25},{17,1},{25,9},{2,18},{10... | collective-permute-start | bytes 1179656 | tf_op jit(solution)/shard_map/ppermute | solution.py:872
  513.5 13.4 %copy-start.19 = (bf16[144,1280]{1,0:T(8,128)(2,1)}, bf16[144,1280]{1,0:T(8,128)(2,1)S(1)}, u32[]{:S(2)}) copy-start(bf16[144,1280]{1,0:T(8,128)(2,1)S(1)} %reduce_sum.25.refs_0_) | copy-start | bytes 1105924
  513.5 9.6 %collective-permute-start.40 = (bf16[144,1280]{1,0:T(8,128)(2,1)S(1)}, bf16[144,1280]{1,0:T(8,128)(2,1)S(1)}, u32[]{:S(2)}, u32[]{:S(2)}) collective-permute-start(bf16[144,1280]{1,0:T(8,128)(2,1)S(1)} %reduce_sum.25.refs_0_), channel_id=1, source_target_pairs={{0,16},{8,24},{16,0},{24,8},{1,17},{9,25},{17,1},{25,9},{2,18},{10... | collective-permute-start | bytes 1105928 | tf_op jit(solution)/shard_map/ppermute | solution.py:872
  517.5 5.6 %collective-permute-start.44 = (bf16[128,1536]{1,0:T(8,128)(2,1)}, bf16[128,1536]{1,0:T(8,128)(2,1)S(1)}, u32[]{:S(2)}, u32[]{:S(2)}) collective-permute-start(bf16[128,1536]{1,0:T(8,128)(2,1)} %shard_map.382.refs_0_), channel_id=1, source_target_pairs={{0,8},{8,0},{16,24},{24,16},{1,9},{9,1},{17,25},{25,17},{2,10},{10... | collective-permute-start | bytes 1179656 | tf_op jit(solution)/shard_map/ppermute | solution.py:869
  517.5 9.4 %collective-permute-start.41 = (bf16[144,1280]{1,0:T(8,128)(2,1)S(1)}, bf16[144,1280]{1,0:T(8,128)(2,1)S(1)}, u32[]{:S(2)}, u32[]{:S(2)}) collective-permute-start(bf16[144,1280]{1,0:T(8,128)(2,1)S(1)} %reduce_sum.25.refs_0_), channel_id=1, source_target_pairs={{0,8},{8,0},{16,24},{24,16},{1,9},{9,1},{17,25},{25,17},{2,10},{10... | collective-permute-start | bytes 1105928 | tf_op jit(solution)/shard_map/ppermute | solution.py:869
  523.1 3.8 collective-permute-start.42
  (36 other events, 101.2 us)
Sparse Core Ops, SparseCore 0:
  40.1 66.6 all-gather.2
  109.5 72.2 all-gather.4
  284.8 86.6 reduce-scatter.1

commit v3 on v2

--- a/solution.py
+++ b/solution.py
@@ -785,7 +785,7 @@
     return ("hbm", array)
 
 
-def stage(body, where, ins, outs, scratch=(), limit=vmem_limit):
+def stage(body, where, ins, outs, scratch=(), time=0):
     specs, arrays = [], []
     for item in ins:
         if isinstance(item, tuple):
@@ -809,8 +809,10 @@
             scratch_shapes=list(scratch),
         ),
         out_shape=[jax.ShapeDtypeStruct(shape, dtype) for shape, dtype in outs],
-        compiler_params=pltpu.CompilerParams(vmem_limit_bytes=limit),
-        cost_estimate=short,
+        compiler_params=pltpu.CompilerParams(vmem_limit_bytes=vmem_limit),
+        cost_estimate=pl.CostEstimate(
+            flops=1024, bytes_accessed=1024 + int(3.5e6 * time), transcendentals=0
+        ),
     )(where, *arrays)
 
 
@@ -864,6 +866,7 @@
 
     core_perm = [(n, n ^ 1) for n in range(S)]
     y_perm = [(n, n ^ 2) for n in range(S)]
+    diagonal_perm = [(n, n ^ 3) for n in range(S)]
 
     def core_swap(array):
         return lax.ppermute(array, "seq", core_perm)
@@ -894,8 +897,9 @@
         rows, cols = column.shape[0] // Z, column.shape[1]
         return [a.reshape(Z, rows, cols) for a in (column, x_shift(column, 1))]
 
-    def heads_to_positions(array):
-        return lax.all_to_all(array, "seq", 0, 0, tiled=True)
+    def exchange(parts):
+        got = [y_swap(parts[1]), core_swap(parts[2]), lax.ppermute(parts[3], "seq", diagonal_perm)]
+        return [parts[0], *tied(got)]
 
     def local(
         hidden_in,
@@ -938,6 +942,24 @@
             [s, s ^ 2, s ^ 1, s ^ 3, s, x, lengths[0]]
         ).astype(jnp.int32)
 
+        def prepare_rest(w, ins, outs, _):
+            query, own, cross = ins
+            out = outs[0]
+            core = lax.rem(w[MINE], 2)
+            out[0:deep, 0:D] = own[span(core, deep), :]
+            out[deep:, 0:D] = cross[span(core, deep), :]
+            out[:, D : D + hw] = query[:, span(w[SEQ], hw)]
+            out[:, D + hw :] = query[:, span(w[SEQ + 1], hw)]
+
+        (chunk_rest,) = stage(
+            prepare_rest,
+            where,
+            [cross_query_weight, self_out_weight, cross_out_weight],
+            [((shard, rest_cols), bf16)],
+        )
+
+        rest_own = lax.all_gather(chunk_rest, "fsdp", axis=0, tiled=True)
+
         def prepare_qkv(w, ins, outs, _):
             weight, out = ins[0], outs[0]
             me = w[MINE]
@@ -965,26 +987,10 @@
             prepare_qkv,
             where,
             [
-                self_in_weight, self_query_bias, self_value_bias, self_out_bias, cross_query_bias,
+                after(self_in_weight, chunk_rest), self_query_bias, self_value_bias, self_out_bias, cross_query_bias,
                 memory_value_bias, cross_out_bias, ffn_out_bias, norm_gain, norm_bias, ffn_in_bias,
             ],
             [((Z, shard + 16, 3 * hw), bf16)],
-        )
-
-        def prepare_rest(w, ins, outs, _):
-            query, own, cross = ins
-            out = outs[0]
-            core = lax.rem(w[MINE], 2)
-            out[0:deep, 0:D] = own[span(core, deep), :]
-            out[deep:, 0:D] = cross[span(core, deep), :]
-            out[:, D : D + hw] = query[:, span(w[SEQ], hw)]
-            out[:, D + hw :] = query[:, span(w[SEQ + 1], hw)]
-
-        (chunk_rest,) = stage(
-            prepare_rest,
-            where,
-            [cross_query_weight, self_out_weight, cross_out_weight],
-            [((shard, rest_cols), bf16)],
         )
 
         def prepare_mem(w, ins, outs, _):
@@ -1008,10 +1014,7 @@
 
         hidden_far = y_swap(after(hidden_in, chunk_qkv))
         z_qkv = z_gather(chunk_qkv.reshape(Z * (shard + 16), 3 * hw))
-        z_qkv, hidden_far, chunk_rest, chunk_mem, chunk_ffn = tied(
-            [z_qkv, hidden_far, chunk_rest, chunk_mem, chunk_ffn]
-        )
-        rest_own = lax.all_gather(chunk_rest, "fsdp", axis=0, tiled=True)
+        z_qkv, hidden_far, chunk_mem, chunk_ffn = tied([z_qkv, hidden_far, chunk_mem, chunk_ffn])
         x_blocks = [hidden_in, hidden_far, core_swap(hidden_in), core_swap(hidden_far)]
         got_qkv = x_gather(z_qkv)
         memory_far = y_swap(after(memory, hidden_far))
@@ -1065,49 +1068,68 @@
         def qkv_spec(m):
             return pl.BlockSpec((T, pair), lambda g, i, _: (0, m * pairs + g))
 
-        def self_forward(w, q_ref, k_ref, v_ref, o_ref, lse_ref):
+        rows_2 = 2 * t
+
+        def masked(w, i, scores):
+            key_pos = lax.broadcasted_iota(jnp.int32, scores.shape, 0)
+            query_pos = i * rows_2 + lax.broadcasted_iota(jnp.int32, (1, rows_2), 1)
+            limit = jnp.minimum(w[LENGTH], (query_pos // BLK + 1) * BLK)
+            return jnp.where(key_pos < limit, scores, masked_value)
+
+        def forward_pair(queries, k_ref, v_ref, key_count, mask, lse_ref):
+            parts, lses = [], []
+            for h in range(2):
+                cols = slice(h * HD, (h + 1) * HD)
+                query = queries[:, cols] * jnp.asarray(score_scale, bf16)
+                scores = mask(dot(k_ref[:key_count, cols], query, nt))
+                top = jnp.max(scores, axis=0, keepdims=True)
+                weights = jnp.exp(scores - top)
+                totals = jnp.sum(weights, axis=0, keepdims=True)
+                value = dot(v_ref[:key_count, cols], weights.astype(bf16), tn)
+                parts.append(value * (1.0 / totals))
+                lses.append(top + jnp.log(totals))
+            lse_ref[0] = jnp.concatenate(lses, axis=0)
+            return jnp.concatenate(parts, axis=0).T.astype(bf16)
+
+        def step_cases(i, visit):
+            for n in range(T // rows_2):
+
+                @pl.when(i == n)
+                def _(n=n):
+                    visit((n + 1) * rows_2)
+
+        def self_forward(w, q_ref, k_ref, v_ref, *outs):
             i = pl.program_id(1)
-            limit = jnp.minimum(w[LENGTH], (i + 1) * BLK)
 
             def visit(key_count):
-                parts, lses = [], []
-                for h in range(2):
-                    cols = slice(h * HD, (h + 1) * HD)
-                    query = q_ref[:, cols] * jnp.asarray(score_scale, bf16)
-                    scores = mask_scores(dot(k_ref[:key_count, cols], query, nt), 0, limit)
-                    top = jnp.max(scores, axis=0, keepdims=True)
-                    weights = jnp.exp(scores - top)
-                    totals = jnp.sum(weights, axis=0, keepdims=True)
-                    low = (weights * (1.0 / totals)).astype(bf16)
-                    parts.append(dot(low, v_ref[:key_count, cols], tn).astype(bf16))
-                    lses.append(top + jnp.log(totals))
-                o_ref[...] = jnp.concatenate(parts, axis=1)
-                lse_ref[0] = jnp.concatenate(lses, axis=0)
-
-            key_cases(T, True, i, visit)
-
-        q_block = pl.BlockSpec((t, pair), lambda g, i, _: (i, g))
+                mask = functools.partial(masked, w, i)
+                out = forward_pair(q_ref[...], k_ref, v_ref, key_count, mask, outs[S])
+                for n in range(S):
+                    for b in range(2):
+
+                        @pl.when(w[SEQ + n] == 2 * i + b)
+                        def _(n=n, b=b):
+                            outs[n][...] = out[b * t : (b + 1) * t]
+
+            step_cases(i, visit)
+
+        q_block = pl.BlockSpec((rows_2, pair), lambda g, i, _: (i, g))
         row_block = pl.BlockSpec((t, pair), lambda g, i, _: (0, g))
-        lse_block = pl.BlockSpec((1, 2, t), lambda g, i, _: (g, 0, i))
-        self_attn, self_lse = pl.pallas_call(
+        lse_block = pl.BlockSpec((1, 2, rows_2), lambda g, i, _: (g, 0, i))
+        *attn_sent, self_lse = pl.pallas_call(
             self_forward,
             grid_spec=pltpu.PrefetchScalarGridSpec(
                 num_scalar_prefetch=1,
-                grid=(pairs, S),
+                grid=(pairs, T // rows_2),
                 in_specs=[q_block, qkv_spec(1), qkv_spec(2)],
-                out_specs=[q_block, lse_block],
+                out_specs=[row_block] * S + [lse_block],
             ),
-            out_shape=[
-                jax.ShapeDtypeStruct((T, hw), bf16),
-                jax.ShapeDtypeStruct((pairs, 2, T), f32),
-            ],
+            out_shape=[jax.ShapeDtypeStruct((t, hw), bf16)] * S
+            + [jax.ShapeDtypeStruct((pairs, 2, T), f32)],
             compiler_params=pltpu.CompilerParams(vmem_limit_bytes=vmem_limit),
             cost_estimate=short,
         )(where, qkv, qkv, qkv)
-        attn = heads_to_positions(self_attn)
-        rest_own = after(rest_own, self_attn)
-        rest_other = core_swap(rest_own)
-        rest = [r.reshape(F, shard, rest_cols) for r in (rest_own, rest_other)]
+        attn = exchange(attn_sent)
 
         w_ffn = lax.all_gather(after(chunk_ffn, qkv), "fsdp", axis=0, tiled=True).reshape(
             F, shard + fw, D
@@ -1133,12 +1155,15 @@
         kv_own, w_mem = stage(
             project_memory,
             where,
-            [hbm(b) for b in m_blocks] + [hbm(p) for p in got_mem] + [after(small, attn)],
+            [hbm(b) for b in m_blocks] + [hbm(p) for p in got_mem] + [after(small, attn[1])],
             [((T, 2 * hw), bf16), ((Z, X, shard, 2 * hw), bf16)],
             [pltpu.VMEM((T, D), bf16), pltpu.SemaphoreType.DMA((2 + S,))],
         )
         w_mem = w_mem.reshape(D, 2 * hw)
         kv_far = y_swap(kv_own)
+        rest_own = after(rest_own, kv_own)
+        rest_other = core_swap(rest_own)
+        rest = [r.reshape(F, shard, rest_cols) for r in (rest_own, rest_other)]
 
         def load_out(copies, w, rest_refs, which, target):
             core = lax.rem(w[MINE], 2)
@@ -1155,7 +1180,7 @@
         cq_scratch = pltpu.VMEM((2, F, shard, half), bf16)
 
         def first_stage(w, ins, outs, scratch):
-            attn_ref, rest_refs, x_ref, small_ref = ins[0], ins[1:3], ins[3], ins[4]
+            pieces, rest_refs, x_ref, small_ref = ins[:S], ins[S : S + 2], ins[S + 2], ins[S + 3]
             normed_ref, inverse_ref, low_ref, keep_ref, send_ref = outs
             weight, cq, sems = scratch
             copies = Copies(sems)
@@ -1165,7 +1190,7 @@
             copies.wait()
             total = alpha_scale * x_ref[...].astype(f32) + small_ref[2:3, :]
             for n in range(S):
-                total = total + dot(attn_ref[n * t : (n + 1) * t, :], group_rows(weight, n), nn)
+                total = total + dot(pieces[n][...], group_rows(weight, w[SEQ + n]), nn)
             value, normed, inverse = norm_rows(total, small_ref[7:8, :], small_ref[10:11, :])
             normed_ref[...] = normed
             inverse_ref[...] = inverse
@@ -1180,7 +1205,7 @@
         normed_one, inverse_one, first_low, cq_keep, cq_send = stage(
             first_stage,
             where,
-            [attn] + [hbm(r) for r in rest] + [hidden_in, small],
+            attn + [hbm(r) for r in rest] + [hidden_in, small],
             [
                 ((t, D), f32), ((t, 1), f32), ((t, D), bf16), ((t, half), bf16), ((t, half), bf16),
             ],
@@ -1199,40 +1224,24 @@
             ]
             return near + far
 
-        cross_lse_block = pl.BlockSpec((1, 2, t), lambda g, i, _: (g, 0, i))
-
         def cross_forward(w, qa_ref, qb_ref, k0, v0, k1, v1, oa_ref, ob_ref, lse_ref):
-            g, i = pl.program_id(0), pl.program_id(1)
-
-            def run(q_ref, k_ref, v_ref, o_ref):
-                parts, lses = [], []
-                for h in range(2):
-                    cols = slice(h * HD, (h + 1) * HD)
-                    query = q_ref[:, cols] * jnp.asarray(score_scale, bf16)
-                    scores = dot(k_ref[:, cols], query, nt)
-                    top = jnp.max(scores, axis=0, keepdims=True)
-                    weights = jnp.exp(scores - top)
-                    totals = jnp.sum(weights, axis=0, keepdims=True)
-                    low = (weights * (1.0 / totals)).astype(bf16)
-                    parts.append(dot(low, v_ref[:, cols], tn).astype(bf16))
-                    lses.append(top + jnp.log(totals))
-                o_ref[...] = jnp.concatenate(parts, axis=1)
-                lse_ref[0] = jnp.concatenate(lses, axis=0)
-
+            g = pl.program_id(0)
             for gi, (k_ref, v_ref) in enumerate(((k0, v0), (k1, v1))):
-                for qi, (q_ref, o_ref) in enumerate(((qa_ref, oa_ref), (qb_ref, ob_ref))):
-
-                    @pl.when((g // pairs == gi) & (i == qi))
-                    def _(q_ref=q_ref, k_ref=k_ref, v_ref=v_ref, o_ref=o_ref):
-                        run(q_ref, k_ref, v_ref, o_ref)
+
+                @pl.when(g // pairs == gi)
+                def _(k_ref=k_ref, v_ref=v_ref):
+                    queries = jnp.concatenate([qa_ref[...], qb_ref[...]], axis=0)
+                    out = forward_pair(queries, k_ref, v_ref, T, lambda scores: scores, lse_ref)
+                    oa_ref[...] = out[:t]
+                    ob_ref[...] = out[t:]
 
         cross_keep, cross_send, cross_lse = pl.pallas_call(
             cross_forward,
             grid_spec=pltpu.PrefetchScalarGridSpec(
                 num_scalar_prefetch=1,
-                grid=(2 * pairs, 2),
+                grid=(2 * pairs, 1),
                 in_specs=[row_block, row_block] + kv_specs(),
-                out_specs=[row_block, row_block, cross_lse_block],
+                out_specs=[row_block, row_block, lse_block],
             ),
             out_shape=[jax.ShapeDtypeStruct((t, half), bf16)] * 2
             + [jax.ShapeDtypeStruct((2 * pairs, 2, 2 * t), f32)],
@@ -1270,7 +1279,8 @@
             [((t, D), f32), ((t, 1), f32), ((t, D), bf16)],
             [out_scratch, pltpu.SemaphoreType.DMA((2,))],
         )
-        second = seq_gather(second_low)
+        second_far = y_swap(second_low)
+        second = [second_low, second_far, core_swap(second_low), None]
 
         ffn_scratch = [
             pltpu.VMEM((F, shard, D), bf16),
@@ -1311,6 +1321,8 @@
 
         ffn_part_0, ffn_part_2, hidden_a, slope_a = ffn_call([second[0], second[2]])
         ffn_near = core_swap(ffn_part_2)
+        second[1] = after(second_far, ffn_part_0)
+        second[3] = core_swap(second[1])
         ffn_part_1, ffn_part_3, hidden_b, slope_b = ffn_call([second[1], second[3]])
 
         def add_pair(left, right):
@@ -1342,7 +1354,8 @@
             [ffn_part_0, ffn_near, ffn_far, normed_two, small, out_grad],
             [((t, D), bf16), ((t, D), f32), ((t, D), bf16), ((8, D), f32)],
         )
-        d_ffn = seq_gather(d_ffn_own)
+        d_ffn_far = y_swap(d_ffn_own)
+        d_ffn = [d_ffn_own, d_ffn_far, core_swap(d_ffn_own), None]
 
         def ffn_backward(w, ins, outs, scratch):
             block_refs, slope_ref, w_ref = ins[:2], ins[2], ins[3]
@@ -1367,6 +1380,8 @@
 
         d2_part_0, d2_part_2, d_pre_a = ffn_back_call([d_ffn[0], d_ffn[2]], slope_a)
         d2_near = core_swap(d2_part_2)
+        d_ffn[1] = after(d_ffn_far, d2_part_0)
+        d_ffn[3] = core_swap(d_ffn[1])
         d2_part_1, d2_part_3, d_pre_b = ffn_back_call([d_ffn[1], d_ffn[3]], slope_b)
         d2_sent = add_pair(d2_part_1, core_swap(d2_part_3))
         d2_far = y_swap(d2_sent)
@@ -1398,11 +1413,8 @@
             second + d_ffn + [after(hidden_a, d2_sent), hidden_b, d_pre_a, d_pre_b],
             [((F, shard + fw, D), bf16), ((8, D), f32)],
             [pltpu.VMEM((T, D), bf16), pltpu.VMEM((T, D), bf16)],
-        )
-        own_ffn = lax.psum_scatter(
-            grad_ffn.reshape(F * (shard + fw), D), "fsdp", scatter_dimension=0, tiled=True
-        )
-
+            time=12,
+        )
         def second_back(w, ins, outs, scratch):
             a, b, far, d_three_ref, normed_ref, inverse_ref, small_ref = ins[:7]
             rest_refs = ins[7:]
@@ -1438,24 +1450,28 @@
             [out_scratch, pltpu.SemaphoreType.DMA((2,))],
         )
         dc_other = core_swap(dc_send)
-
-        def backward_pair(q_ref, k_ref, v_ref, g_ref, lse_ref, key_count, limit, dk_acc, dv_acc):
+        own_ffn = lax.psum_scatter(
+            after(grad_ffn, d_cross).reshape(F * (shard + fw), D),
+            "fsdp",
+            scatter_dimension=0,
+            tiled=True,
+        )
+
+        def backward_pair(queries, k_ref, v_ref, grads, lse_ref, key_count, mask, dk_acc, dv_acc):
             dqs = []
             for h in range(2):
                 cols = slice(h * HD, (h + 1) * HD)
-                query = q_ref[:, cols] * jnp.asarray(score_scale, bf16)
-                grad = g_ref[:, cols]
-                scores = dot(k_ref[:key_count, cols], query, nt)
-                if limit is not None:
-                    scores = mask_scores(scores, 0, limit)
+                query = queries[:, cols] * jnp.asarray(score_scale, bf16)
+                grad = grads[:, cols]
+                scores = mask(dot(k_ref[:key_count, cols], query, nt))
                 weights = jnp.exp(scores - lse_ref[0, h : h + 1, :])
                 dv_acc[h, :key_count, :] += dot(weights.astype(bf16), grad, nn)
                 grad_weights = dot(v_ref[:key_count, cols], grad, nt)
                 row_term = jnp.sum(grad_weights * weights, axis=0, keepdims=True)
                 low = (weights * (grad_weights - row_term)).astype(bf16)
                 dk_acc[h, :key_count, :] += dot(low, query, nn)
-                dqs.append((dot(low, k_ref[:key_count, cols], tn) * score_scale).astype(bf16))
-            return jnp.concatenate(dqs, axis=1)
+                dqs.append(dot(k_ref[:key_count, cols], low, tn) * score_scale)
+            return jnp.concatenate(dqs, axis=0).T.astype(bf16)
 
         def sums_out(ref, acc):
             ref[...] = jnp.concatenate([acc[h].astype(bf16) for h in range(2)], axis=1)
@@ -1463,26 +1479,23 @@
         def cross_backward(
             w, qa, qb, k0, v0, k1, v1, ga, gb, lse_ref, da, db, dk0, dv0, dk1, dv1, dk_acc, dv_acc
         ):
-            g, i = pl.program_id(0), pl.program_id(1)
-
-            @pl.when(i == 0)
-            def _():
-                dk_acc[...] = jnp.zeros_like(dk_acc)
-                dv_acc[...] = jnp.zeros_like(dv_acc)
-
-            for gi, (k_ref, v_ref) in enumerate(((k0, v0), (k1, v1))):
-                for qi, (q_ref, g_ref, d_ref) in enumerate(((qa, ga, da), (qb, gb, db))):
-
-                    @pl.when((g // pairs == gi) & (i == qi))
-                    def _(q_ref=q_ref, g_ref=g_ref, d_ref=d_ref, k_ref=k_ref, v_ref=v_ref):
-                        d_ref[...] = backward_pair(
-                            q_ref, k_ref, v_ref, g_ref, lse_ref, T, None, dk_acc, dv_acc
-                        )
-
-            for gi, (dk_ref, dv_ref) in enumerate(((dk0, dv0), (dk1, dv1))):
-
-                @pl.when((g // pairs == gi) & (i == 1))
-                def _(dk_ref=dk_ref, dv_ref=dv_ref):
+            g = pl.program_id(0)
+            dk_acc[...] = jnp.zeros_like(dk_acc)
+            dv_acc[...] = jnp.zeros_like(dv_acc)
+            for gi, (k_ref, v_ref, dk_ref, dv_ref) in enumerate(
+                ((k0, v0, dk0, dv0), (k1, v1, dk1, dv1))
+            ):
+
+                @pl.when(g // pairs == gi)
+                def _(k_ref=k_ref, v_ref=v_ref, dk_ref=dk_ref, dv_ref=dv_ref):
+                    queries = jnp.concatenate([qa[...], qb[...]], axis=0)
+                    grads = jnp.concatenate([ga[...], gb[...]], axis=0)
+                    out = backward_pair(
+                        queries, k_ref, v_ref, grads, lse_ref, T, lambda scores: scores, dk_acc,
+                        dv_acc,
+                    )
+                    da[...] = out[:t]
+                    db[...] = out[t:]
                     sums_out(dk_ref, dk_acc)
                     sums_out(dv_ref, dv_acc)
 
@@ -1497,10 +1510,10 @@
             cross_backward,
             grid_spec=pltpu.PrefetchScalarGridSpec(
                 num_scalar_prefetch=1,
-                grid=(2 * pairs, 2),
+                grid=(2 * pairs, 1),
                 in_specs=[row_block, row_block]
                 + kv_specs()
-                + [row_block, row_block, cross_lse_block],
+                + [row_block, row_block, lse_block],
                 out_specs=[row_block, row_block]
                 + [near_block(0), near_block(1), far_block(0), far_block(1)],
                 scratch_shapes=acc_scratch,
@@ -1519,7 +1532,7 @@
             keep_ref, other_ref, d_two_ref, normed_ref, inverse_ref, small_ref = ins[:6]
             rest_refs = ins[6:]
             d_ref, low_ref = outs[0], outs[1]
-            sent_ref, sums_ref = outs[2], outs[3]
+            sent_refs, sums_ref = outs[2 : 2 + S], outs[2 + S]
             weight, cq, sems = scratch
             copies = Copies(sems)
             for e in range(2):
@@ -1541,20 +1554,21 @@
             sums_ref[1:2, :] = gain
             sums_ref[2:3, :] = shift
             for n in range(S):
-                value = dot(low, group_rows(weight, n), nt)
-                sent_ref[n * t : (n + 1) * t, :] = value.astype(bf16)
-
-        d_one, d_branch, d_attn_sent, sums_one = stage(
+                value = dot(low, group_rows(weight, w[SEQ + n]), nt)
+                sent_refs[n][...] = value.astype(bf16)
+
+        d_one, d_branch, *d_attn_sent, sums_one = stage(
             first_back,
             where,
             [dq_keep, dq_other, d_two, normed_one, inverse_one, small] + [hbm(r) for r in rest],
-            [((t, D), f32), ((t, D), bf16), ((T, hw), bf16), ((8, D), f32)],
+            [((t, D), f32), ((t, D), bf16)] + [((t, hw), bf16)] * S + [((8, D), f32)],
             [out_scratch, cq_scratch, pltpu.SemaphoreType.DMA((4,))],
         )
-        d_attn = heads_to_positions(d_attn_sent)
+        d_attn = exchange(d_attn_sent)
 
         def middle_grads(w, ins, outs, scratch):
-            dq_keep_ref, dq_other_ref, low_ref, attn_ref, d_one_ref, co_keep, co_other, d_two_ref = ins
+            dq_keep_ref, dq_other_ref, low_ref, d_one_ref, co_keep, co_other, d_two_ref = ins[:7]
+            attn_refs = ins[7:]
             own, cross = scratch
             core = lax.rem(w[MINE], 2)
             for e, ref in enumerate((dq_keep_ref, dq_other_ref)):
@@ -1565,8 +1579,8 @@
                 cross[pl.ds(w[SEQ + n] * per_group, per_group)] = value.reshape(
                     per_group, 2, deep, D
                 )
-                value = dot(attn_ref[n * t : (n + 1) * t, :], d_one_ref[...], tn).astype(bf16)
-                own[n * per_group : (n + 1) * per_group] = value.reshape(per_group, 2, deep, D)
+                value = dot(attn_refs[n][...], d_one_ref[...], tn).astype(bf16)
+                own[pl.ds(w[SEQ + n] * per_group, per_group)] = value.reshape(per_group, 2, deep, D)
             for e in range(2):
                 at = core if e == 0 else 1 - core
                 outs[e][:, 0:deep, 0:D] = own[:, at]
@@ -1575,8 +1589,8 @@
         middle_keep, middle_send = stage(
             middle_grads,
             where,
-            [dq_keep, dq_other, first_low, attn, after(d_branch, d_attn_sent), cross_keep]
-            + [cross_other, d_cross],
+            [dq_keep, dq_other, first_low, after(d_branch, d_attn_sent[1]), cross_keep, cross_other]
+            + [d_cross, *attn],
             [((F, shard, rest_cols), bf16)] * 2,
             [out_scratch, out_scratch],
         )
@@ -1597,7 +1611,7 @@
             terms = z_exchange(sent).reshape(Z, rows, cols)
             return jnp.sum(terms.astype(f32), axis=0).astype(bf16)
 
-        dk_got, dv_got = (y_swap(after(d, d_attn)) for d in (dk_far, dv_far))
+        dk_got, dv_got = (y_swap(after(d, d_attn[1])) for d in (dk_far, dv_far))
 
         def pack_rest(w, ins, outs, _):
             for n in range(Z):
@@ -1608,31 +1622,32 @@
         rest_keep, rest_send = stage(
             pack_rest,
             where,
-            [middle_keep, middle_got],
+            [after(middle_keep, d_attn[1]), middle_got],
             [((Z * shard, rest_cols), bf16)] * 2,
         )
         rest_got = x_shift(rest_send, 1)
 
-        def self_backward(
-            w, q_ref, k_ref, v_ref, g_ref, lse_ref, dq_ref, dk_ref, dv_ref, dk_acc, dv_acc
-        ):
+        def self_backward(w, q_ref, k_ref, v_ref, *refs):
+            grads, lse_ref = refs[:S], refs[S]
+            dq_ref, dk_ref, dv_ref, dk_acc, dv_acc, g_rows = refs[S + 1 :]
             i = pl.program_id(1)
 
             @pl.when(i == 0)
             def _():
                 dk_acc[...] = jnp.zeros_like(dk_acc)
                 dv_acc[...] = jnp.zeros_like(dv_acc)
-
-            limit = jnp.minimum(w[LENGTH], (i + 1) * BLK)
+                for n in range(S):
+                    g_rows[span(w[SEQ + n], t), :] = grads[n][...]
 
             def visit(key_count):
                 dq_ref[...] = backward_pair(
-                    q_ref, k_ref, v_ref, g_ref, lse_ref, key_count, limit, dk_acc, dv_acc
+                    q_ref[...], k_ref, v_ref, g_rows[span(i, rows_2), :], lse_ref, key_count,
+                    functools.partial(masked, w, i), dk_acc, dv_acc,
                 )
 
-            key_cases(T, True, i, visit)
-
-            @pl.when(i == S - 1)
+            step_cases(i, visit)
+
+            @pl.when(i == T // rows_2 - 1)
             def _():
                 sums_out(dk_ref, dk_acc)
                 sums_out(dv_ref, dv_acc)
@@ -1642,15 +1657,15 @@
             self_backward,
             grid_spec=pltpu.PrefetchScalarGridSpec(
                 num_scalar_prefetch=1,
-                grid=(pairs, S),
-                in_specs=[q_block, qkv_spec(1), qkv_spec(2), q_block, lse_block],
+                grid=(pairs, T // rows_2),
+                in_specs=[q_block, qkv_spec(1), qkv_spec(2)] + [row_block] * S + [lse_block],
                 out_specs=[q_block, key_block, key_block],
-                scratch_shapes=acc_scratch,
+                scratch_shapes=acc_scratch + [pltpu.VMEM((T, pair), bf16)],
             ),
             out_shape=[jax.ShapeDtypeStruct((T, hw), bf16)] * 3,
             compiler_params=pltpu.CompilerParams(vmem_limit_bytes=vmem_limit),
             cost_estimate=short,
-        )(where, qkv, qkv, qkv, d_attn, after(self_lse, rest_keep))
+        )(where, qkv, qkv, qkv, *d_attn, after(self_lse, rest_keep))
 
         tall = shard + 16
 
@@ -1749,7 +1764,7 @@
         in_parts = stage(
             input_parts,
             where,
-            [after(dq_self, rest_sent), dk_self, dv_self] + [hbm(p) for p in got_qkv],
+            [after(dq_self, last_got), dk_self, dv_self] + [hbm(p) for p in got_qkv],
             [((t, D), bf16)] * S,
             [pltpu.VMEM((Z, X, shard, 3 * hw), bf16), pltpu.SemaphoreType.DMA((2,))],
         )
@@ -1776,7 +1791,7 @@
 
         own_rest = z_sum(rest_sent)
         last_sent = add_pair(
-            last_keep, after(last_got, own_rest, grad_fin, input_grad, memory_grad)
+            last_keep, after(last_got, own_rest, grad_fin, memory_grad)
         )
         own_last = z_sum(last_sent)
 

time: 551 us -> 498 us (0.904)
  blocking collectives: 25.7 us -> 0 us
  Pallas kernels: 220 us -> 198 us
  waiting for transfers between devices: 205 us -> 193 us
  starting transfers between devices: 45.1 us -> 50.8 us
    ppermute x14 -> x16, waiting for transfers between devices: 118 us -> 89.8 us  [y_swap(): return lax.ppermute(array, 'seq', y_perm)]
    all_to_all x2 -> x0, blocking collectives: 25.7 us -> none  [heads_to_positions(): return lax.all_to_all(array, 'seq', 0, 0, tiled=True)]
    all_gather x1, waiting for transfers between devices: 14.8 us -> 0.02 us  [local(): rest_own = lax.all_gather(chunk_rest, 'fsdp', axis=0, tiled=True)]
    all_to_all x4, waiting for transfers between devices: 54.4 us -> 65.1 us  [z_exchange(): lax.all_to_all(array, 'fsdp', 0, 0, axis_index_groups=z_groups, tiled=True)]
    pallas_call x1, Pallas kernels: 20.6 us -> 11.2 us  [local(): pl.pallas_call(cross_forward, grid_spec=pltpu.PrefetchScalarGridSpec(num_...]
    ppermute x4, waiting for transfers between devices: 2.78 us -> 10.6 us  [x_shift(): return lax.ppermute(array, 'fsdp', perm) if k % X else array]
    ppermute x0 -> x2, waiting for transfers between devices: none -> 6.74 us  [exchange(): lax.ppermute(parts[3], 'seq', diagonal_perm)]
    ppermute x27 -> x29, waiting for transfers between devices: 15.2 us -> 21 us  [core_swap(): return lax.ppermute(array, 'seq', core_perm)]
  transfers between devices with their start and end apart: 52 -> 58, of which waited for: 25 -> 33; matrix products, arithmetic and copies ran while one was open for 1% -> 2% of each run, Pallas kernels for 36% -> 33%
where the time goes in v3:
time: 498 us; the launch traced here: 493 us
  Pallas kernels  198 us (40%)
  waiting for transfers between devices  193 us (39%)
  starting transfers between devices  50.8 us (10%)
  local copies, waits for them, and re-layouts  22 us (4%)
  between operations  15.2 us (3%)
  other arithmetic  14.2 us (3%)
    pallas_call x24, Pallas kernels, stage(): pl.pallas_call(kernel, grid_spec=pltpu.PrefetchScalarGridSpec(num_scalar_...  141 us
    ppermute x16, waiting for transfers between devices, y_swap(): return lax.ppermute(array, 'seq', y_perm)  89.8 us
    all_to_all x4, waiting for transfers between devices, z_exchange(): lax.all_to_all(array, 'fsdp', 0, 0, axis_index_groups=z_groups, tiled=True)  65.1 us
    ppermute x16, starting transfers between devices, y_swap(): return lax.ppermute(array, 'seq', y_perm)  21.1 us
    ppermute x29, waiting for transfers between devices, core_swap(): return lax.ppermute(array, 'seq', core_perm)  21 us
    pallas_call x1, Pallas kernels, local(): pl.pallas_call(cross_backward, grid_spec=pltpu.PrefetchScalarGridSpec(num...  19.5 us
    all_to_all x4, starting transfers between devices, z_exchange(): lax.all_to_all(array, 'fsdp', 0, 0, axis_index_groups=z_groups, tiled=True)  18 us
    unnamed x104, local copies, waits for them, and re-layouts  17.3 us
  transfers between devices with their start and end apart: 58, of which 33 were waited for; matrix products, arithmetic and copies ran while one was open for 2% of the time, Pallas kernels for 33%

profile of v3, /device:TPU:0, one launch (start us, length us, event | category | flops | bytes accessed | tf_op | source)
XLA Modules:
  0.0 493.3 jit_solution(7760444211519790400)
XLA Ops:
  8.5 2.5 shard_map.356
  11.1 3.0 shard_map.357
  14.1 6.3 %all-to-all-start = ((bf16[4,144,768]{2,1,0:T(8,128)(2,1)}), bf16[4,144,768]{2,1,0:T(8,128)(2,1)S(1)}, u32[]{:S(2)}, u32[]{:S(2)}) async-start(bf16[4,144,768]{2,1,0:T(8,128)(2,1)} %shard_map.357), calls=%async_computation | async-start | bytes 1769472 | tf_op jit(solution)/shard_map/all_to_all | solution.py:880
  21.9 2.5 shard_map.358
  24.5 3.2 shard_map.359
  27.7 6.1 %collective-permute-done.refs_1_.refs_13_ = bf16[256,1024]{1,0:T(8,128)(2,1)S(1)} collective-permute-done((bf16[256,1024]{1,0:T(8,128)(2,1)S(1)}, bf16[256,1024]{1,0:T(8,128)(2,1)S(1)}, u32[]{:S(2)}, u32[]{:S(2)}) %collective-permute-start) | collective-permute-done | bytes 524320 | tf_op jit(solution)/shard_map/ppermute | solution.py:875
  33.8 21.5 %all-to-all-done = bf16[4,144,768]{2,1,0:T(8,128)(2,1)S(1)} async-done(((bf16[4,144,768]{2,1,0:T(8,128)(2,1)}), bf16[4,144,768]{2,1,0:T(8,128)(2,1)S(1)}, u32[]{:S(2)}, u32[]{:S(2)}) %all-to-all-start) | async-done | bytes 884768 | tf_op jit(solution)/shard_map/all_to_all | solution.py:880
  56.7 4.2 all-to-all-start.1
  63.1 10.6 %collective-permute-done.3.refs_1_.refs_17_ = bf16[256,1024]{1,0:T(8,128)(2,1)} collective-permute-done((bf16[256,1024]{1,0:T(8,128)(2,1)S(1)}, bf16[256,1024]{1,0:T(8,128)(2,1)}, u32[]{:S(2)}, u32[]{:S(2)}) %collective-permute-start.3) | collective-permute-done | bytes 524320 | tf_op jit(solution)/shard_map/ppermute | solution.py:875
  73.7 14.0 %all-to-all-done.1 = bf16[4,128,512]{2,1,0:T(8,128)(2,1)} async-done(((bf16[4,128,512]{2,1,0:T(8,128)(2,1)}), bf16[4,128,512]{2,1,0:T(8,128)(2,1)}, u32[]{:S(2)}, u32[]{:S(2)}) %all-to-all-start.1) | async-done | bytes 524320 | tf_op jit(solution)/shard_map/all_to_all | solution.py:880
  87.8 4.9 collective-permute-done.4
  93.6 5.7 %shard_map.360 = (bf16[1024,768]{1,0:T(8,128)(2,1)}, f32[24,1024]{1,0:T(8,128)}) custom-call(s32[7]{0:T(128)} %stack.24.w, bf16[256,1024]{1,0:T(8,128)(2,1)} %bitcast.54, bf16[256,1024]{1,0:T(8,128)(2,1)} %copy-done.10, bf16[256,1024]{1,0:T(8,128)(2,1)} %collective-permute-done.1.refs_2_.refs_14_, bf16[256,1024]{1,0:T(8,128)(2,1)} %collective-permute-done.2.refs_3_.refs_15_, ...), custom_call_target="tpu_custom_call" | custom-call | flops 1024 | bytes 1024 | tf_op jit(solution)/shard_map/pallas_call | solution.py:802
  101.4 10.2 %shard_map.361 = (bf16[256,256]{1,0:T(8,128)(2,1)}, bf16[256,256]{1,0:T(8,128)(2,1)}, bf16[256,256]{1,0:T(8,128)(2,1)}, bf16[256,256]{1,0:T(8,128)(2,1)}, f32[2,2,1024]{2,1,0:T(2,128)}) custom-call(s32[7]{0:T(128)} %stack.24.w, bf16[1024,768]{1,0:T(8,128)(2,1)} %get-tuple-element.145.q_ref.k_ref.v_ref, ...), custom_call_target="tpu_custom_call" | custom-call | flops 1024 | bytes 1024 | tf_op jit(solution)/shard_map/pallas_call | solution.py:1119
  113.3 4.4 collective-permute-done.5.refs_1_.refs_8_
  118.4 5.2 %collective-permute-done.7.refs_3_.refs_10_ = bf16[256,256]{1,0:T(8,128)(2,1)S(1)} collective-permute-done((bf16[256,256]{1,0:T(8,128)(2,1)}, bf16[256,256]{1,0:T(8,128)(2,1)S(1)}, u32[]{:S(2)}, u32[]{:S(2)}) %collective-permute-start.7) | collective-permute-done | bytes 131104 | tf_op jit(solution)/shard_map/ppermute | solution.py:901
  124.7 5.7 %shard_map.362 = (bf16[1024,512]{1,0:T(8,128)(2,1)}, bf16[4,2,128,512]{3,2,1,0:T(8,128)(2,1)}) custom-call(s32[7]{0:T(128)} %stack.24.w, bf16[256,1024]{1,0:T(8,128)(2,1)} %bitcast.62, bf16[256,1024]{1,0:T(8,128)(2,1)} %collective-permute-done.3.refs_1_.refs_17_, bf16[256,1024]{1,0:T(8,128)(2,1)} %copy-done.11, bf16[256,1024]{1,0:T(8,128)(2,1)} %copy-done.12, ...), custom_call_target="tpu_custom_call" | custom-call | flops 1024 | bytes 1024 | tf_op jit(solution)/shard_map/pallas_call | solution.py:802
  132.0 4.4 collective-permute-done.11
  138.0 7.0 %shard_map.363 = (f32[256,1024]{1,0:T(8,128)}, f32[256,1]{1,0:T(8,128)}, bf16[256,1024]{1,0:T(8,128)(2,1)}, bf16[256,512]{1,0:T(8,128)(2,1)}, bf16[256,512]{1,0:T(8,128)(2,1)}) custom-call(s32[7]{0:T(128)} %stack.24.w, bf16[256,256]{1,0:T(8,128)(2,1)} %get-tuple-element.146.refs_0_.refs_7_, bf16[256,256]{1,0:T(8,128)(2,1)} %copy-done.24, ...), custom_call_target="tpu_custom_call" | custom-call | flops 1024 | bytes 1024 | tf_op jit(solution)/shard_map/pallas_call | solution.py:802
  145.4 10.9 %collective-permute-done.13.k1.v1 = bf16[1024,512]{1,0:T(8,128)(2,1)S(1)} collective-permute-done((bf16[1024,512]{1,0:T(8,128)(2,1)}, bf16[1024,512]{1,0:T(8,128)(2,1)S(1)}, u32[]{:S(2)}, u32[]{:S(2)}) %collective-permute-start.13) | collective-permute-done | bytes 1048608 | tf_op jit(solution)/shard_map/ppermute | solution.py:875
  157.3 11.2 %shard_map.364 = (bf16[256,512]{1,0:T(8,128)(2,1)}, bf16[256,512]{1,0:T(8,128)(2,1)}, f32[4,2,512]{2,1,0:T(2,128)}) custom-call(s32[7]{0:T(128)} %stack.24.w, bf16[256,512]{1,0:T(8,128)(2,1)} %get-tuple-element.159.qa_ref.qa, bf16[256,512]{1,0:T(8,128)(2,1)} %copy-done.23, bf16[1024,512]{1,0:T(8,128)(2,1)} %get-tuple-element.157.k0.v0, ...), custom_call_target="tpu_custom_call" | custom-call | flops 1024 | bytes 1024 | tf_op jit(solution)/shard_map/pallas_call | solution.py:1238
  168.7 1.7 collective-permute-done.14.refs_1_.refs_5_
  171.1 5.8 %shard_map.365 = (f32[256,1024]{1,0:T(8,128)}, f32[256,1]{1,0:T(8,128)}, bf16[256,1024]{1,0:T(8,128)(2,1)}) custom-call(s32[7]{0:T(128)} %stack.24.w, bf16[256,512]{1,0:T(8,128)(2,1)} %get-tuple-element.161.refs_0_.refs_4_, bf16[256,512]{1,0:T(8,128)(2,1)} %copy-done.21, f32[256,1024]{1,0:T(8,128)} %get-tuple-element.163.refs_2_.refs_3_, ...), custom_call_target="tpu_custom_call" | custom-call | flops 1024 | bytes 1024 | tf_op jit(solution)/shard_map/pallas_call | solution.py:802
  179.9 8.3 %shard_map.366 = (bf16[256,1024]{1,0:T(8,128)(2,1)}, bf16[256,1024]{1,0:T(8,128)(2,1)}, bf16[512,1024]{1,0:T(8,128)(2,1)}, bf16[512,1024]{1,0:T(8,128)(2,1)}) custom-call(s32[7]{0:T(128)} %stack.24.w, bf16[256,1024]{1,0:T(8,128)(2,1)} %get-tuple-element.164.refs_0_, bf16[256,1024]{1,0:T(8,128)(2,1)} %copy-done.13, ...), custom_call_target="tpu_custom_call" | custom-call | flops 1024 | bytes 1024 | tf_op jit(solution)/shard_map/pallas_call | solution.py:802
  188.2 3.3 collective-permute-done.17.refs_0_.refs_1_
  191.5 1.9 collective-permute-done.18.refs_1_.refs_3_
  194.3 8.3 %shard_map.367 = (bf16[256,1024]{1,0:T(8,128)(2,1)}, bf16[256,1024]{1,0:T(8,128)(2,1)}, bf16[512,1024]{1,0:T(8,128)(2,1)}, bf16[512,1024]{1,0:T(8,128)(2,1)}) custom-call(s32[7]{0:T(128)} %stack.24.w, bf16[256,1024]{1,0:T(8,128)(2,1)} %copy-done.14, bf16[256,1024]{1,0:T(8,128)(2,1)} %copy-done.15, ...), custom_call_target="tpu_custom_call" | custom-call | flops 1024 | bytes 1024 | tf_op jit(solution)/shard_map/pallas_call | solution.py:802
  207.5 12.5 %collective-permute-done.20.refs_2_ = bf16[256,1024]{1,0:T(8,128)(2,1)S(1)} collective-permute-done((bf16[256,1024]{1,0:T(8,128)(2,1)S(1)}, bf16[256,1024]{1,0:T(8,128)(2,1)S(1)}, u32[]{:S(2)}, u32[]{:S(2)}) %collective-permute-start.20) | collective-permute-done | bytes 524320 | tf_op jit(solution)/shard_map/ppermute | solution.py:875
  220.9 4.9 shard_map.368
  228.7 8.0 %shard_map.369 = (bf16[256,1024]{1,0:T(8,128)(2,1)}, bf16[256,1024]{1,0:T(8,128)(2,1)}, bf16[512,1024]{1,0:T(8,128)(2,1)}) custom-call(s32[7]{0:T(128)} %stack.24.w, bf16[256,1024]{1,0:T(8,128)(2,1)} %get-tuple-element.174.refs_0_.refs_4_, bf16[256,1024]{1,0:T(8,128)(2,1)} %copy-done.6, bf16[512,1024]{1,0:T(8,128)(2,1)} %get-tuple-element.175.refs_2_, ...), custom_call_target="tpu_custom_call" | custom-call | flops 1024 | bytes 1024 | tf_op jit(solution)/shard_map/pallas_call | solution.py:802
  236.7 3.6 collective-permute-done.23.refs_0_.refs_5_
  240.3 1.9 collective-permute-done.24.refs_1_.refs_7_
  243.0 8.5 %shard_map.370 = (bf16[256,1024]{1,0:T(8,128)(2,1)}, bf16[256,1024]{1,0:T(8,128)(2,1)}, bf16[512,1024]{1,0:T(8,128)(2,1)}) custom-call(s32[7]{0:T(128)} %stack.24.w, bf16[256,1024]{1,0:T(8,128)(2,1)} %copy-done.7, bf16[256,1024]{1,0:T(8,128)(2,1)} %copy-done.8, bf16[512,1024]{1,0:T(8,128)(2,1)} %get-tuple-element.179.refs_2_, bf16[8,256,1024]{2,1,0:T(8,128)(2,1)} %bitcast.44), custom_call_target="tpu_custom_call" | custom-call | flops 1024 | bytes 1024 | tf_op jit(solution)/shard_map/pallas_call | solution.py:802
  256.5 10.8 %shard_map.371 = (bf16[8,256,1024]{2,1,0:T(8,128)(2,1)}, f32[8,1024]{1,0:T(8,128)}) custom-call(s32[7]{0:T(128)} %stack.24.w, bf16[256,1024]{1,0:T(8,128)(2,1)} %get-tuple-element.164.refs_0_, bf16[256,1024]{1,0:T(8,128)(2,1)} %copy-done.14, bf16[256,1024]{1,0:T(8,128)(2,1)} %copy-done.13, bf16[256,1024]{1,0:T(8,128)(2,1)} %copy-done.15, ...), custom_call_target="tpu_custom_call" | custom-call | flops 1024 | bytes 42001024 | tf_op jit(solution)/shard_map/pallas_call | solution.py:802
  267.3 1.7 collective-permute-done.26.refs_2_
  269.8 5.8 %shard_map.372 = (f32[256,1024]{1,0:T(8,128)}, bf16[256,1024]{1,0:T(8,128)(2,1)}, bf16[256,512]{1,0:T(8,128)(2,1)}, bf16[256,512]{1,0:T(8,128)(2,1)}, f32[8,1024]{1,0:T(8,128)}) custom-call(s32[7]{0:T(128)} %stack.24.w, bf16[256,1024]{1,0:T(8,128)(2,1)} %get-tuple-element.176.refs_0_, bf16[256,1024]{1,0:T(8,128)(2,1)} %copy-done.28, ...), custom_call_target="tpu_custom_call" | custom-call | flops 1024 | bytes 1024 | tf_op jit(solution)/shard_map/pallas_call | solution.py:802
  278.8 19.5 %shard_map.373 = (bf16[256,512]{1,0:T(8,128)(2,1)}, bf16[256,512]{1,0:T(8,128)(2,1)}, bf16[1024,256]{1,0:T(8,128)(2,1)}, bf16[1024,256]{1,0:T(8,128)(2,1)}, bf16...) custom-call(s32[7]{0:T(128)} %stack.24.w, bf16[256,512]{1,0:T(8,128)(2,1)} %get-tuple-element.159.qa_ref.qa, ...), custom_call_target="tpu_custom_call" | custom-call | flops 1024 | bytes 1024 | tf_op jit(solution)/shard_map/pallas_call | solution.py:1509
  300.8 7.3 %shard_map.374 = (f32[256,1024]{1,0:T(8,128)}, bf16[256,1024]{1,0:T(8,128)(2,1)}, bf16[256,256]{1,0:T(8,128)(2,1)}, bf16[256,256]{1,0:T(8,128)(2,1)}, bf16[256,2...) custom-call(s32[7]{0:T(128)} %stack.24.w, bf16[256,512]{1,0:T(8,128)(2,1)} %get-tuple-element.194.refs_0_, ...), custom_call_target="tpu_custom_call" | custom-call | flops 1024 | bytes 1024 | tf_op jit(solution)/shard_map/pallas_call | solution.py:802
  308.1 7.3 %shard_map.375 = (bf16[8,128,1536]{2,1,0:T(8,128)(2,1)}, bf16[8,128,1536]{2,1,0:T(8,128)(2,1)}) custom-call(s32[7]{0:T(128)} %stack.24.w, bf16[256,512]{1,0:T(8,128)(2,1)} %get-tuple-element.194.refs_0_, bf16[256,512]{1,0:T(8,128)(2,1)} %copy-done.22, bf16[256,1024]{1,0:T(8,128)(2,1)} %get-tuple-element.207.refs_2_, ...), custom_call_target="tpu_custom_call" | custom-call | flops 1024 | bytes 1024 | tf_op jit(solution)/shard_map/pallas_call | solution.py:802
  317.8 1.9 collective-permute-done.30.refs_2_
  321.3 3.2 collective-permute-done.29.refs_1_
  324.5 1.6 copy-done.5
  326.1 5.8 %shard_map.376 = (bf16[512,1536]{1,0:T(8,128)(2,1)}, bf16[512,1536]{1,0:T(8,128)(2,1)}) custom-call(s32[7]{0:T(128)} %stack.24.w, bf16[8,128,1536]{2,1,0:T(8,128)(2,1)} %get-tuple-element.212.refs_0_, bf16[8,128,1536]{2,1,0:T(8,128)(2,1)} %copy-done.5), custom_call_target="tpu_custom_call" | custom-call | flops 1024 | bytes 1024 | tf_op jit(solution)/shard_map/pallas_call | solution.py:802
  334.4 16.3 %shard_map.377 = (bf16[1024,256]{1,0:T(8,128)(2,1)}, bf16[1024,256]{1,0:T(8,128)(2,1)}, bf16[1024,256]{1,0:T(8,128)(2,1)}) custom-call(s32[7]{0:T(128)} %stack.24.w, bf16[1024,768]{1,0:T(8,128)(2,1)} %get-tuple-element.145.q_ref.k_ref.v_ref, bf16[1024,768]{1,0:T(8,128)(2,1)} %get-tuple-element.145.q_ref.k_ref.v_ref, ...), custom_call_target="tpu_custom_call" | custom-call | flops 1024 | bytes 1024 | tf_op jit(solution)/shard_map/pallas_call | solution.py:1656
  350.7 6.3 %collective-permute-done.34.refs_10_ = bf16[1024,256]{1,0:T(8,128)(2,1)S(1)} collective-permute-done((bf16[1024,256]{1,0:T(8,128)(2,1)S(1)}, bf16[1024,256]{1,0:T(8,128)(2,1)S(1)}, u32[]{:S(2)}, u32[]{:S(2)}) %collective-permute-start.34) | collective-permute-done | bytes 524320 | tf_op jit(solution)/shard_map/ppermute | solution.py:875
  357.8 10.3 %shard_map.378 = (bf16[256,1024]{1,0:T(8,128)(2,1)}, bf16[256,1024]{1,0:T(8,128)(2,1)}, bf16[256,1024]{1,0:T(8,128)(2,1)}, bf16[256,1024]{1,0:T(8,128)(2,1)}, bf...) custom-call(s32[7]{0:T(128)} %stack.24.w, bf16[1024,256]{1,0:T(8,128)(2,1)} %get-tuple-element.231.refs_0_, ...), custom_call_target="tpu_custom_call" | custom-call | flops 1024 | bytes 1024 | tf_op jit(solution)/shard_map/pallas_call | solution.py:802
  368.1 5.7 %collective-permute-done.42 = bf16[512,1536]{1,0:T(8,128)(2,1)S(1)} collective-permute-done((bf16[512,1536]{1,0:T(8,128)(2,1)}, bf16[512,1536]{1,0:T(8,128)(2,1)S(1)}, u32[]{:S(2)}, u32[]{:S(2)}) %collective-permute-start.42) | collective-permute-done | bytes 1572896 | tf_op jit(solution)/shard_map/ppermute | solution.py:884
  375.3 3.9 all-to-all-start.2
  383.4 11.8 %collective-permute-done.43.refs_1_ = bf16[256,1024]{1,0:T(8,128)(2,1)} collective-permute-done((bf16[256,1024]{1,0:T(8,128)(2,1)}, bf16[256,1024]{1,0:T(8,128)(2,1)}, u32[]{:S(2)}, u32[]{:S(2)}) %collective-permute-start.43) | collective-permute-done | bytes 524320 | tf_op jit(solution)/shard_map/ppermute | solution.py:875
  395.2 10.6 %collective-permute-done.41 = bf16[256,1024]{1,0:T(8,128)(2,1)S(1)} collective-permute-done((bf16[256,1024]{1,0:T(8,128)(2,1)S(1)}, bf16[256,1024]{1,0:T(8,128)(2,1)S(1)}, u32[]{:S(2)}, u32[]{:S(2)}) %collective-permute-start.41) | collective-permute-done | bytes 524320 | tf_op jit(solution)/shard_map/ppermute | solution.py:875
  405.8 2.1 add_convert_fusion.2
  407.9 7.6 %all-to-all-done.2 = bf16[4,128,1536]{2,1,0:T(8,128)(2,1)S(1)} async-done(((bf16[4,128,1536]{2,1,0:T(8,128)(2,1)}), bf16[4,128,1536]{2,1,0:T(8,128)(2,1)S(1)}, u32[]{:S(2)}, u32[]{:S(2)}) %all-to-all-start.2) | async-done | bytes 1572896 | tf_op jit(solution)/shard_map/all_to_all | solution.py:880
  415.7 4.6 shard_map.380
  420.3 2.8 add_convert_fusion.1
  423.2 3.6 all-to-all-start.3
  426.7 6.0 %shard_map.379 = (bf16[256,1024]{1,0:T(8,128)(2,1)}, bf16[256,1024]{1,0:T(8,128)(2,1)}, bf16[256,1024]{1,0:T(8,128)(2,1)}, bf16[256,1024]{1,0:T(8,128)(2,1)}) custom-call(s32[7]{0:T(128)} %stack.24.w, bf16[1024,256]{1,0:T(8,128)(2,1)} %get-tuple-element.231.refs_0_, bf16[1024,256]{1,0:T(8,128)(2,1)} %get-tuple-element.217.refs_1_, ...), custom_call_target="tpu_custom_call" | custom-call | flops 1024 | bytes 1024 | tf_op jit(solution)/shard_map/pallas_call | solution.py:802
  434.9 2.0 add_convert_fusion.5
  437.0 1.7 collective-permute-start.38
  439.0 22.0 %all-to-all-done.3 = bf16[4,144,1280]{2,1,0:T(8,128)(2,1)S(1)} async-done(((bf16[4,144,1280]{2,1,0:T(8,128)(2,1)}), bf16[4,144,1280]{2,1,0:T(8,128)(2,1)S(1)}, u32[]{:S(2)}, u32[]{:S(2)}) %all-to-all-start.3) | async-done | bytes 1474592 | tf_op jit(solution)/shard_map/all_to_all | solution.py:880
  461.3 1.8 collective-permute-start.46
  463.1 2.6 shard_map.382.refs_0_
  466.2 4.7 collective-permute-done.46.refs_1_
  470.9 2.6 fusion
  474.3 3.0 shard_map.383
  478.8 3.7 shard_map.381
  (201 shorter events, 65.2 us)
Async XLA Ops:
  7.2 123.3 %all-gather.3.cloned.1.call-start = ((), (), s32[]{:S(2)}) async-start(), calls=%async_computation.5 | async-start | bytes 3538944 | tf_op jit(solution)/shard_map/all_gather | solution.py:961
  14.1 41.2 %all-to-all-start = ((bf16[4,144,768]{2,1,0:T(8,128)(2,1)}), bf16[4,144,768]{2,1,0:T(8,128)(2,1)S(1)}, u32[]{:S(2)}, u32[]{:S(2)}) async-start(bf16[4,144,768]{2,1,0:T(8,128)(2,1)} %shard_map.357), calls=%async_computation | async-start | bytes 1769472 | tf_op jit(solution)/shard_map/all_to_all | solution.py:880
  20.4 13.4 %collective-permute-start = (bf16[256,1024]{1,0:T(8,128)(2,1)S(1)}, bf16[256,1024]{1,0:T(8,128)(2,1)S(1)}, u32[]{:S(2)}, u32[]{:S(2)}) collective-permute-start(bf16[256,1024]{1,0:T(8,128)(2,1)S(1)} %bitcast.57), channel_id=1, source_target_pairs={{0,16},{8,24},{16,0},{24,8},{1,17},{9,25},{17,1},{25,9},{2,18},{10... | collective-permute-start | bytes 1572872 | tf_op jit(solution)/shard_map/ppermute | solution.py:875
  24.5 36.5 %copy-start.9 = (bf16[1,256,1024]{2,1,0:T(8,128)(2,1)S(1)}, bf16[1,256,1024]{2,1,0:T(8,128)(2,1)}, u32[]{:S(2)}) copy-start(bf16[1,256,1024]{2,1,0:T(8,128)(2,1)} %param.22) | copy-start | bytes 1572868
  33.8 58.9 %copy-start.10 = (bf16[256,1024]{1,0:T(8,128)(2,1)}, bf16[256,1024]{1,0:T(8,128)(2,1)S(1)}, u32[]{:S(2)}) copy-start(bf16[256,1024]{1,0:T(8,128)(2,1)S(1)} %collective-permute-done.refs_1_.refs_13_) | copy-start | bytes 1572868
  55.2 37.4 %copy-start.2 = (bf16[4,144,768]{2,1,0:T(8,128)(2,1)}, bf16[4,144,768]{2,1,0:T(8,128)(2,1)S(1)}, u32[]{:S(2)}) copy-start(bf16[4,144,768]{2,1,0:T(8,128)(2,1)S(1)} %all-to-all-done) | copy-start | bytes 2654212
  55.2 37.4 %collective-permute-start.4 = (bf16[576,768]{1,0:T(8,128)(2,1)S(1)}, bf16[576,768]{1,0:T(8,128)(2,1)S(1)}, u32[]{:S(2)}, u32[]{:S(2)}) collective-permute-start(bf16[576,768]{1,0:T(8,128)(2,1)S(1)} %bitcast.53), channel_id=1, source_target_pairs={{0,1},{1,0},{2,3},{3,2},{4,5},{5,4},{6,7},{7,6},{8,9},{9,8},{10,11... | collective-permute-start | bytes 2654216 | tf_op jit(solution)/shard_map/ppermute | solution.py:884
  56.7 31.0 %all-to-all-start.1 = ((bf16[4,128,512]{2,1,0:T(8,128)(2,1)}), bf16[4,128,512]{2,1,0:T(8,128)(2,1)}, u32[]{:S(2)}, u32[]{:S(2)}) async-start(bf16[4,128,512]{2,1,0:T(8,128)(2,1)} %shard_map.358), calls=%async_computation.1 | async-start | bytes 1048576 | tf_op jit(solution)/shard_map/all_to_all | solution.py:880
  60.9 117.6 %all-gather.5.cloned.1.call-start = ((), (), s32[]{:S(2)}) async-start(), calls=%async_computation.6 | async-start | bytes 4718592 | tf_op jit(solution)/shard_map/all_gather | solution.py:1134
  61.0 12.8 %collective-permute-start.3 = (bf16[256,1024]{1,0:T(8,128)(2,1)S(1)}, bf16[256,1024]{1,0:T(8,128)(2,1)}, u32[]{:S(2)}, u32[]{:S(2)}) collective-permute-start(bf16[256,1024]{1,0:T(8,128)(2,1)S(1)} %bitcast.64), channel_id=1, source_target_pairs={{0,16},{8,24},{16,0},{24,8},{1,17},{9,25},{17,1},{25,9},{2,18},{10... | collective-permute-start | bytes 1572872 | tf_op jit(solution)/shard_map/ppermute | solution.py:875
  62.6 25.2 %collective-permute-start.1 = (bf16[256,1024]{1,0:T(8,128)(2,1)S(1)}, bf16[256,1024]{1,0:T(8,128)(2,1)}, u32[]{:S(2)}, u32[]{:S(2)}) collective-permute-start(bf16[256,1024]{1,0:T(8,128)(2,1)S(1)} %bitcast.58), channel_id=1, source_target_pairs={{0,8},{8,0},{16,24},{24,16},{1,9},{9,1},{17,25},{25,17},{2,10},{10... | collective-permute-start | bytes 1572872 | tf_op jit(solution)/shard_map/ppermute | solution.py:872
  62.6 25.2 %collective-permute-start.2 = (bf16[256,1024]{1,0:T(8,128)(2,1)S(1)}, bf16[256,1024]{1,0:T(8,128)(2,1)}, u32[]{:S(2)}, u32[]{:S(2)}) collective-permute-start(bf16[256,1024]{1,0:T(8,128)(2,1)S(1)} %collective-permute-done.refs_1_.refs_13_), channel_id=1, source_target_pairs={{0,8},{8,0},{16,24},{24,16},{1,9},{9,1},{17,25},{25,17},{2,10},{10... | collective-permute-start | bytes 1572872 | tf_op jit(solution)/shard_map/ppermute | solution.py:872
  99.3 280.8 %reduce-scatter.2.cloned.1.call-start = ((), (), s32[]{:S(2)}) async-start(), calls=%async_computation.7 | async-start | bytes 4718592 | tf_op jit(solution)/shard_map/reduce_scatter | solution.py:1453
  99.5 24.1 %collective-permute-start.8 = (bf16[256,1024]{1,0:T(8,128)(2,1)S(1)}, bf16[256,1024]{1,0:T(8,128)(2,1)S(1)}, u32[]{:S(2)}, u32[]{:S(2)}) collective-permute-start(bf16[256,1024]{1,0:T(8,128)(2,1)S(1)} %bitcast.65), channel_id=1, source_target_pairs={{0,8},{8,0},{16,24},{24,16},{1,9},{9,1},{17,25},{25,17},{2,10},{10... | collective-permute-start | bytes 1572872 | tf_op jit(solution)/shard_map/ppermute | solution.py:872
  99.6 24.0 %collective-permute-start.10 = (bf16[512,512]{1,0:T(8,128)(2,1)}, bf16[512,512]{1,0:T(8,128)(2,1)S(1)}, u32[]{:S(2)}, u32[]{:S(2)}) collective-permute-start(bf16[512,512]{1,0:T(8,128)(2,1)} %bitcast.8), channel_id=1, source_target_pairs={{0,1},{1,0},{2,3},{3,2},{4,5},{5,4},{6,7},{7,6},{8,9},{9,8},{10,11... | collective-permute-start | bytes 1572872 | tf_op jit(solution)/shard_map/ppermute | solution.py:884
  101.3 22.4 %collective-permute-start.9 = (bf16[256,1024]{1,0:T(8,128)(2,1)}, bf16[256,1024]{1,0:T(8,128)(2,1)S(1)}, u32[]{:S(2)}, u32[]{:S(2)}) collective-permute-start(bf16[256,1024]{1,0:T(8,128)(2,1)} %collective-permute-done.3.refs_1_.refs_17_), channel_id=1, source_target_pairs={{0,8},{8,0},{16,24},{24,16},{1,9},{9,1},{17,25},{25,17},{2,10},{10... | collective-permute-start | bytes 1572872 | tf_op jit(solution)/shard_map/ppermute | solution.py:872
  111.6 6.0 %collective-permute-start.5 = (bf16[256,256]{1,0:T(8,128)(2,1)}, bf16[256,256]{1,0:T(8,128)(2,1)S(1)}, u32[]{:S(2)}, u32[]{:S(2)}) collective-permute-start(bf16[256,256]{1,0:T(8,128)(2,1)} %get-tuple-element.147), channel_id=1, source_target_pairs={{0,16},{8,24},{16,0},{24,8},{1,17},{9,25},{17,1},{25,9},{2,18},{10... | collective-permute-start | bytes 393224 | tf_op jit(solution)/shard_map/ppermute | solution.py:875
  113.2 5.2 %collective-permute-start.6 = (bf16[256,256]{1,0:T(8,128)(2,1)}, bf16[256,256]{1,0:T(8,128)(2,1)S(1)}, u32[]{:S(2)}, u32[]{:S(2)}) collective-permute-start(bf16[256,256]{1,0:T(8,128)(2,1)} %get-tuple-element.148), channel_id=1, source_target_pairs={{0,8},{8,0},{16,24},{24,16},{1,9},{9,1},{17,25},{25,17},{2,10},{10... | collective-permute-start | bytes 393224 | tf_op jit(solution)/shard_map/ppermute | solution.py:872
  117.7 5.9 %collective-permute-start.7 = (bf16[256,256]{1,0:T(8,128)(2,1)}, bf16[256,256]{1,0:T(8,128)(2,1)S(1)}, u32[]{:S(2)}, u32[]{:S(2)}) collective-permute-start(bf16[256,256]{1,0:T(8,128)(2,1)} %get-tuple-element.149), channel_id=1, source_target_pairs={{0,24},{8,16},{16,8},{24,0},{1,25},{9,17},{17,9},{25,1},{2,26},{10... | collective-permute-start | bytes 393224 | tf_op jit(solution)/shard_map/ppermute | solution.py:901
  130.5 5.9 %collective-permute-start.11 = (bf16[1024,1536]{1,0:T(8,128)(2,1)}, bf16[1024,1536]{1,0:T(8,128)(2,1)S(1)}, u32[]{:S(2)}, u32[]{:S(2)}) collective-permute-start(bf16[1024,1536]{1,0:T(8,128)(2,1)} %all-gather.3.cloned.1.call-done), channel_id=1, source_target_pairs={{0,8},{8,0},{16,24},{24,16},{1,9},{9,1},{17,25},{25,17},{2,10},{10... | collective-permute-start | bytes 9437192 | tf_op jit(solution)/shard_map/ppermute | solution.py:872
  130.8 25.5 %collective-permute-start.13 = (bf16[1024,512]{1,0:T(8,128)(2,1)}, bf16[1024,512]{1,0:T(8,128)(2,1)S(1)}, u32[]{:S(2)}, u32[]{:S(2)}) collective-permute-start(bf16[1024,512]{1,0:T(8,128)(2,1)} %get-tuple-element.157.k0.v0), channel_id=1, source_target_pairs={{0,16},{8,24},{16,0},{24,8},{1,17},{9,25},{17,1},{25,9},{2,18},{10... | collective-permute-start | bytes 3145736 | tf_op jit(solution)/shard_map/ppermute | solution.py:875
  145.0 11.3 %collective-permute-start.12 = (bf16[256,512]{1,0:T(8,128)(2,1)}, bf16[256,512]{1,0:T(8,128)(2,1)S(1)}, u32[]{:S(2)}, u32[]{:S(2)}) collective-permute-start(bf16[256,512]{1,0:T(8,128)(2,1)} %get-tuple-element.160), channel_id=1, source_target_pairs={{0,8},{8,0},{16,24},{24,16},{1,9},{9,1},{17,25},{25,17},{2,10},{10... | collective-permute-start | bytes 786440 | tf_op jit(solution)/shard_map/ppermute | solution.py:872
  168.6 1.8 collective-permute-start.14
  176.9 2.2 collective-permute-start.15
  177.1 14.4 %collective-permute-start.17 = (bf16[256,1024]{1,0:T(8,128)(2,1)}, bf16[256,1024]{1,0:T(8,128)(2,1)S(1)}, u32[]{:S(2)}, u32[]{:S(2)}) collective-permute-start(bf16[256,1024]{1,0:T(8,128)(2,1)} %get-tuple-element.164.refs_0_), channel_id=1, source_target_pairs={{0,16},{8,24},{16,0},{24,8},{1,17},{9,25},{17,1},{25,9},{2,18},{10... | collective-permute-start | bytes 1572872 | tf_op jit(solution)/shard_map/ppermute | solution.py:875
  191.5 1.9 collective-permute-start.18
  202.6 2.2 collective-permute-start.19
  202.8 4.7 collective-permute-start.16
  206.0 14.0 %collective-permute-start.20 = (bf16[256,1024]{1,0:T(8,128)(2,1)S(1)}, bf16[256,1024]{1,0:T(8,128)(2,1)S(1)}, u32[]{:S(2)}, u32[]{:S(2)}) collective-permute-start(bf16[256,1024]{1,0:T(8,128)(2,1)S(1)} %add_convert_fusion.7), channel_id=1, source_target_pairs={{0,16},{8,24},{16,0},{24,8},{1,17},{9,25},{17,1},{25,9},{2,18},{10... | collective-permute-start | bytes 1572872 | tf_op jit(solution)/shard_map/ppermute | solution.py:875
  225.8 2.1 collective-permute-start.21
  225.8 14.5 %collective-permute-start.23 = (bf16[256,1024]{1,0:T(8,128)(2,1)}, bf16[256,1024]{1,0:T(8,128)(2,1)S(1)}, u32[]{:S(2)}, u32[]{:S(2)}) collective-permute-start(bf16[256,1024]{1,0:T(8,128)(2,1)} %get-tuple-element.174.refs_0_.refs_4_), channel_id=1, source_target_pairs={{0,16},{8,24},{16,0},{24,8},{1,17},{9,25},{17,1},{25,9},{2,18},{10... | collective-permute-start | bytes 1572872 | tf_op jit(solution)/shard_map/ppermute | solution.py:875
  240.3 1.9 collective-permute-start.24
  251.6 2.2 collective-permute-start.25
  251.8 15.5 %collective-permute-start.22 = (bf16[256,1024]{1,0:T(8,128)(2,1)S(1)}, bf16[256,1024]{1,0:T(8,128)(2,1)S(1)}, u32[]{:S(2)}, u32[]{:S(2)}) collective-permute-start(bf16[256,1024]{1,0:T(8,128)(2,1)S(1)} %copy-done.46), channel_id=1, source_target_pairs={{0,8},{8,0},{16,24},{24,16},{1,9},{9,1},{17,25},{25,17},{2,10},{10... | collective-permute-start | bytes 1572872 | tf_op jit(solution)/shard_map/ppermute | solution.py:872
  255.0 14.0 %collective-permute-start.26 = (bf16[256,1024]{1,0:T(8,128)(2,1)S(1)}, bf16[256,1024]{1,0:T(8,128)(2,1)S(1)}, u32[]{:S(2)}, u32[]{:S(2)}) collective-permute-start(bf16[256,1024]{1,0:T(8,128)(2,1)S(1)} %add_convert_fusion.6), channel_id=1, source_target_pairs={{0,16},{8,24},{16,0},{24,8},{1,17},{9,25},{17,1},{25,9},{2,18},{10... | collective-permute-start | bytes 1572872 | tf_op jit(solution)/shard_map/ppermute | solution.py:875
  276.6 1.5 collective-permute-start.27
  298.2 1.8 collective-permute-start.28
  315.3 9.1 %collective-permute-start.32 = (bf16[8,128,1536]{2,1,0:T(8,128)(2,1)}, bf16[8,128,1536]{2,1,0:T(8,128)(2,1)S(1)}, u32[]{:S(2)}, u32[]{:S(2)}) collective-permute-start(bf16[8,128,1536]{2,1,0:T(8,128)(2,1)} %get-tuple-element.213), channel_id=1, source_target_pairs={{0,8},{8,0},{16,24},{24,16},{1,9},{9,1},{17,25},{25,17},{2,10},{10... | collective-permute-start | bytes 9437192 | tf_op jit(solution)/shard_map/ppermute | solution.py:872
  315.6 4.1 collective-permute-start.30
  315.8 5.4 %collective-permute-start.31 = (bf16[256,256]{1,0:T(8,128)(2,1)S(1)}, bf16[256,256]{1,0:T(8,128)(2,1)S(1)}, u32[]{:S(2)}, u32[]{:S(2)}) collective-permute-start(bf16[256,256]{1,0:T(8,128)(2,1)S(1)} %copy-done.50), channel_id=1, source_target_pairs={{0,24},{8,16},{16,8},{24,0},{1,25},{9,17},{17,9},{25,1},{2,26},{10... | collective-permute-start | bytes 393224 | tf_op jit(solution)/shard_map/ppermute | solution.py:901
  317.2 7.2 %collective-permute-start.29 = (bf16[256,256]{1,0:T(8,128)(2,1)S(1)}, bf16[256,256]{1,0:T(8,128)(2,1)S(1)}, u32[]{:S(2)}, u32[]{:S(2)}) collective-permute-start(bf16[256,256]{1,0:T(8,128)(2,1)S(1)} %copy-done.49), channel_id=1, source_target_pairs={{0,16},{8,24},{16,0},{24,8},{1,17},{9,25},{17,1},{25,9},{2,18},{10... | collective-permute-start | bytes 393224 | tf_op jit(solution)/shard_map/ppermute | solution.py:875
  331.9 41.9 %collective-permute-start.42 = (bf16[512,1536]{1,0:T(8,128)(2,1)}, bf16[512,1536]{1,0:T(8,128)(2,1)S(1)}, u32[]{:S(2)}, u32[]{:S(2)}) collective-permute-start(bf16[512,1536]{1,0:T(8,128)(2,1)} %get-tuple-element.241), channel_id=1, source_target_pairs={{0,1},{1,0},{2,3},{3,2},{4,5},{5,4},{6,7},{7,6},{8,9},{9,8},{10,11... | collective-permute-start | bytes 4718600 | tf_op jit(solution)/shard_map/ppermute | solution.py:884
  332.3 18.3 %collective-permute-start.33 = (bf16[1024,256]{1,0:T(8,128)(2,1)S(1)}, bf16[1024,256]{1,0:T(8,128)(2,1)S(1)}, u32[]{:S(2)}, u32[]{:S(2)}) collective-permute-start(bf16[1024,256]{1,0:T(8,128)(2,1)S(1)} %copy-done.45), channel_id=1, source_target_pairs={{0,16},{8,24},{16,0},{24,8},{1,17},{9,25},{17,1},{25,9},{2,18},{10... | collective-permute-start | bytes 1572872 | tf_op jit(solution)/shard_map/ppermute | solution.py:875
  333.8 23.1 %collective-permute-start.34 = (bf16[1024,256]{1,0:T(8,128)(2,1)S(1)}, bf16[1024,256]{1,0:T(8,128)(2,1)S(1)}, u32[]{:S(2)}, u32[]{:S(2)}) collective-permute-start(bf16[1024,256]{1,0:T(8,128)(2,1)S(1)} %copy-done.44), channel_id=1, source_target_pairs={{0,16},{8,24},{16,0},{24,8},{1,17},{9,25},{17,1},{25,9},{2,18},{10... | collective-permute-start | bytes 1572872 | tf_op jit(solution)/shard_map/ppermute | solution.py:875
  375.3 40.2 %all-to-all-start.2 = ((bf16[4,128,1536]{2,1,0:T(8,128)(2,1)}), bf16[4,128,1536]{2,1,0:T(8,128)(2,1)S(1)}, u32[]{:S(2)}, u32[]{:S(2)}) async-start(bf16[4,128,1536]{2,1,0:T(8,128)(2,1)} %bitcast.21), calls=%async_computation.2 | async-start | bytes 3145728 | tf_op jit(solution)/shard_map/all_to_all | solution.py:880
  379.3 26.5 %copy-start.32 = (bf16[256,1024]{1,0:T(8,128)(2,1)S(1)}, bf16[256,1024]{1,0:T(8,128)(2,1)}, u32[]{:S(2)}) copy-start(bf16[256,1024]{1,0:T(8,128)(2,1)} %get-tuple-element.236) | copy-start | bytes 1572868
  379.3 2.4 collective-permute-start.40
  379.4 41.0 %collective-permute-start.35 = (bf16[576,1280]{1,0:T(8,128)(2,1)}, bf16[576,1280]{1,0:T(8,128)(2,1)}, u32[]{:S(2)}, u32[]{:S(2)}) collective-permute-start(bf16[576,1280]{1,0:T(8,128)(2,1)} %get-tuple-element.230), channel_id=1, source_target_pairs={{0,1},{1,0},{2,3},{3,2},{4,5},{5,4},{6,7},{7,6},{8,9},{9,8},{10,11... | collective-permute-start | bytes 4423688 | tf_op jit(solution)/shard_map/ppermute | solution.py:884
  380.0 15.2 %collective-permute-start.39 = (bf16[256,1024]{1,0:T(8,128)(2,1)}, bf16[256,1024]{1,0:T(8,128)(2,1)}, u32[]{:S(2)}, u32[]{:S(2)}) collective-permute-start(bf16[256,1024]{1,0:T(8,128)(2,1)} %get-tuple-element.237), channel_id=1, source_target_pairs={{0,8},{8,0},{16,24},{24,16},{1,9},{9,1},{17,25},{25,17},{2,10},{10... | collective-permute-start | bytes 1572872 | tf_op jit(solution)/shard_map/ppermute | solution.py:872
  380.1 15.1 %collective-permute-start.43 = (bf16[256,1024]{1,0:T(8,128)(2,1)}, bf16[256,1024]{1,0:T(8,128)(2,1)}, u32[]{:S(2)}, u32[]{:S(2)}) collective-permute-start(bf16[256,1024]{1,0:T(8,128)(2,1)} %reduce-scatter.2.cloned.1.call-done.refs_0_), channel_id=1, source_target_pairs={{0,16},{8,24},{16,0},{24,8},{1,17},{9,25},{17,1},{25,9},{2,18},{10... | collective-permute-start | bytes 1572872 | tf_op jit(solution)/shard_map/ppermute | solution.py:875
  381.8 23.9 %collective-permute-start.41 = (bf16[256,1024]{1,0:T(8,128)(2,1)S(1)}, bf16[256,1024]{1,0:T(8,128)(2,1)S(1)}, u32[]{:S(2)}, u32[]{:S(2)}) collective-permute-start(bf16[256,1024]{1,0:T(8,128)(2,1)S(1)} %add_convert_fusion.3), channel_id=1, source_target_pairs={{0,16},{8,24},{16,0},{24,8},{1,17},{9,25},{17,1},{25,9},{2,18},{10... | collective-permute-start | bytes 1572872 | tf_op jit(solution)/shard_map/ppermute | solution.py:875
  383.4 32.3 %collective-permute-start.44 = (bf16[256,1024]{1,0:T(8,128)(2,1)}, bf16[256,1024]{1,0:T(8,128)(2,1)}, u32[]{:S(2)}, u32[]{:S(2)}) collective-permute-start(bf16[256,1024]{1,0:T(8,128)(2,1)} %reduce-scatter.2.cloned.1.call-done.refs_0_), channel_id=1, source_target_pairs={{0,8},{8,0},{16,24},{24,16},{1,9},{9,1},{17,25},{25,17},{2,10},{10... | collective-permute-start | bytes 1572872 | tf_op jit(solution)/shard_map/ppermute | solution.py:872
  395.2 20.6 %collective-permute-start.45 = (bf16[256,1024]{1,0:T(8,128)(2,1)}, bf16[256,1024]{1,0:T(8,128)(2,1)}, u32[]{:S(2)}, u32[]{:S(2)}) collective-permute-start(bf16[256,1024]{1,0:T(8,128)(2,1)} %collective-permute-done.43.refs_1_), channel_id=1, source_target_pairs={{0,8},{8,0},{16,24},{24,16},{1,9},{9,1},{17,25},{25,17},{2,10},{10... | collective-permute-start | bytes 1572872 | tf_op jit(solution)/shard_map/ppermute | solution.py:872
  415.7 23.0 %copy-start.17 = (bf16[128,1536]{1,0:T(8,128)(2,1)}, bf16[128,1536]{1,0:T(8,128)(2,1)S(1)}, u32[]{:S(2)}) copy-start(bf16[128,1536]{1,0:T(8,128)(2,1)S(1)} %reduce_sum.24.refs_0_) | copy-start | bytes 1179652
  423.2 37.9 %all-to-all-start.3 = ((bf16[4,144,1280]{2,1,0:T(8,128)(2,1)}), bf16[4,144,1280]{2,1,0:T(8,128)(2,1)S(1)}, u32[]{:S(2)}, u32[]{:S(2)}) async-start(bf16[4,144,1280]{2,1,0:T(8,128)(2,1)} %bitcast.23), calls=%async_computation.4 | async-start | bytes 2949120 | tf_op jit(solution)/shard_map/all_to_all | solution.py:880
  432.8 2.2 collective-permute-start.37
  432.8 38.1 %collective-permute-start.36 = (bf16[256,1024]{1,0:T(8,128)(2,1)}, bf16[256,1024]{1,0:T(8,128)(2,1)}, u32[]{:S(2)}, u32[]{:S(2)}) collective-permute-start(bf16[256,1024]{1,0:T(8,128)(2,1)} %get-tuple-element.233), channel_id=1, source_target_pairs={{0,8},{8,0},{16,24},{24,16},{1,9},{9,1},{17,25},{25,17},{2,10},{10... | collective-permute-start | bytes 1572872 | tf_op jit(solution)/shard_map/ppermute | solution.py:872
  437.0 33.9 %copy-start.20 = (f32[256,1024]{1,0:T(8,128)S(1)}, f32[256,1024]{1,0:T(8,128)}, u32[]{:S(2)}) copy-start(f32[256,1024]{1,0:T(8,128)} %get-tuple-element.198) | copy-start | bytes 3145732
  437.0 33.9 %collective-permute-start.38 = (bf16[256,1024]{1,0:T(8,128)(2,1)}, bf16[256,1024]{1,0:T(8,128)(2,1)}, u32[]{:S(2)}, u32[]{:S(2)}) collective-permute-start(bf16[256,1024]{1,0:T(8,128)(2,1)} %add_convert_fusion.5), channel_id=1, source_target_pairs={{0,16},{8,24},{16,0},{24,8},{1,17},{9,25},{17,1},{25,9},{2,18},{10... | collective-permute-start | bytes 1572872 | tf_op jit(solution)/shard_map/ppermute | solution.py:875
  438.7 24.4 %collective-permute-start.49 = (bf16[128,1536]{1,0:T(8,128)(2,1)S(1)}, bf16[128,1536]{1,0:T(8,128)(2,1)}, u32[]{:S(2)}, u32[]{:S(2)}) collective-permute-start(bf16[128,1536]{1,0:T(8,128)(2,1)S(1)} %reduce_sum.24.refs_0_), channel_id=1, source_target_pairs={{0,16},{8,24},{16,0},{24,8},{1,17},{9,25},{17,1},{25,9},{2,18},{10... | collective-permute-start | bytes 1179656 | tf_op jit(solution)/shard_map/ppermute | solution.py:875
  461.3 9.6 %collective-permute-start.46 = (bf16[144,1280]{1,0:T(8,128)(2,1)S(1)}, bf16[144,1280]{1,0:T(8,128)(2,1)S(1)}, u32[]{:S(2)}, u32[]{:S(2)}) collective-permute-start(bf16[144,1280]{1,0:T(8,128)(2,1)S(1)} %reduce_sum.25.refs_0_), channel_id=1, source_target_pairs={{0,16},{8,24},{16,0},{24,8},{1,17},{9,25},{17,1},{25,9},{2,18},{10... | collective-permute-start | bytes 1105928 | tf_op jit(solution)/shard_map/ppermute | solution.py:875
  465.7 7.9 %collective-permute-start.50 = (bf16[128,1536]{1,0:T(8,128)(2,1)}, bf16[128,1536]{1,0:T(8,128)(2,1)S(1)}, u32[]{:S(2)}, u32[]{:S(2)}) collective-permute-start(bf16[128,1536]{1,0:T(8,128)(2,1)} %shard_map.382.refs_0_), channel_id=1, source_target_pairs={{0,8},{8,0},{16,24},{24,16},{1,9},{9,1},{17,25},{25,17},{2,10},{10... | collective-permute-start | bytes 1179656 | tf_op jit(solution)/shard_map/ppermute | solution.py:872
  465.7 11.6 %collective-permute-start.47 = (bf16[144,1280]{1,0:T(8,128)(2,1)S(1)}, bf16[144,1280]{1,0:T(8,128)(2,1)S(1)}, u32[]{:S(2)}, u32[]{:S(2)}) collective-permute-start(bf16[144,1280]{1,0:T(8,128)(2,1)S(1)} %reduce_sum.25.refs_0_), channel_id=1, source_target_pairs={{0,8},{8,0},{16,24},{24,16},{1,9},{9,1},{17,25},{25,17},{2,10},{10... | collective-permute-start | bytes 1105928 | tf_op jit(solution)/shard_map/ppermute | solution.py:872
  470.9 6.4 %collective-permute-start.48 = (bf16[144,1280]{1,0:T(8,128)(2,1)S(1)}, bf16[144,1280]{1,0:T(8,128)(2,1)S(1)}, u32[]{:S(2)}, u32[]{:S(2)}) collective-permute-start(bf16[144,1280]{1,0:T(8,128)(2,1)S(1)} %collective-permute-done.46.refs_1_), channel_id=1, source_target_pairs={{0,8},{8,0},{16,24},{24,16},{1,9},{9,1},{17,25},{25,17},{2,10},{10... | collective-permute-start | bytes 1105928 | tf_op jit(solution)/shard_map/ppermute | solution.py:872
  (46 other events, 252.8 us)
Sparse Core Ops, SparseCore 0:
  11.2 91.1 all-gather.2
  105.1 73.4 all-gather.4
  275.8 91.1 reduce-scatter.1

commit v4 on v3

--- a/solution.py
+++ b/solution.py
@@ -818,18 +818,20 @@
 
 class Copies:
     def __init__(self, sems):
-        self.sems, self.list = sems, []
+        self.sems, self.count, self.lots = sems, 0, [[]]
 
     def add(self, source, target):
-        copy = pltpu.make_async_copy(source, target, self.sems.at[len(self.list)])
+        copy = pltpu.make_async_copy(source, target, self.sems.at[self.count])
         copy.start()
-        self.list.append(copy)
-        return copy
+        self.count += 1
+        self.lots[-1].append(copy)
+
+    def split(self):
+        self.lots.append([])
 
     def wait(self):
-        for copy in self.list:
+        for copy in self.lots.pop(0):
             copy.wait()
-        self.list = []
 
 
 def span(index, size):
@@ -945,19 +947,20 @@
         def prepare_rest(w, ins, outs, _):
             query, own, cross = ins
             out = outs[0]
-            core = lax.rem(w[MINE], 2)
-            out[0:deep, 0:D] = own[span(core, deep), :]
-            out[deep:, 0:D] = cross[span(core, deep), :]
-            out[:, D : D + hw] = query[:, span(w[SEQ], hw)]
-            out[:, D + hw :] = query[:, span(w[SEQ + 1], hw)]
+            me = w[MINE]
+            out[:, 0:hw] = query[:, span(me, hw)]
+            rows = span(me, part)
+            for h in range(2):
+                for m, source in enumerate((own, cross)):
+                    at = (2 * h + m) * part
+                    out[at : at + part, hw:] = source[rows, h * (D // 2) : (h + 1) * (D // 2)]
 
         (chunk_rest,) = stage(
             prepare_rest,
             where,
             [cross_query_weight, self_out_weight, cross_out_weight],
-            [((shard, rest_cols), bf16)],
-        )
-
+            [((shard, 3 * hw), bf16)],
+        )
         rest_own = lax.all_gather(chunk_rest, "fsdp", axis=0, tiled=True)
 
         def prepare_qkv(w, ins, outs, _):
@@ -1128,8 +1131,10 @@
             + [jax.ShapeDtypeStruct((pairs, 2, T), f32)],
             compiler_params=pltpu.CompilerParams(vmem_limit_bytes=vmem_limit),
             cost_estimate=short,
-        )(where, qkv, qkv, qkv)
+        )(where, after(qkv, m_blocks[2], m_blocks[3]), qkv, qkv)
         attn = exchange(attn_sent)
+        rest_own = after(rest_own, qkv)
+        rest_far = y_swap(rest_own)
 
         w_ffn = lax.all_gather(after(chunk_ffn, qkv), "fsdp", axis=0, tiled=True).reshape(
             F, shard + fw, D
@@ -1155,38 +1160,40 @@
         kv_own, w_mem = stage(
             project_memory,
             where,
-            [hbm(b) for b in m_blocks] + [hbm(p) for p in got_mem] + [after(small, attn[1])],
+            [hbm(b) for b in m_blocks] + [hbm(p) for p in got_mem] + [after(small, attn_sent[1])],
             [((T, 2 * hw), bf16), ((Z, X, shard, 2 * hw), bf16)],
             [pltpu.VMEM((T, D), bf16), pltpu.SemaphoreType.DMA((2 + S,))],
         )
         w_mem = w_mem.reshape(D, 2 * hw)
-        kv_far = y_swap(kv_own)
-        rest_own = after(rest_own, kv_own)
-        rest_other = core_swap(rest_own)
-        rest = [r.reshape(F, shard, rest_cols) for r in (rest_own, rest_other)]
+        kv_far = y_swap(after(kv_own, attn[1]))
+        rest_core = [core_swap(after(r, kv_own)) for r in (rest_own, rest_far)]
+        rest = [r.reshape(F, shard, 3 * hw) for r in (rest_own, rest_far, *rest_core)]
 
         def load_out(copies, w, rest_refs, which, target):
-            core = lax.rem(w[MINE], 2)
-            for e in range(2):
-                copies.add(
-                    rest_refs[e].at[:, pl.ds(which * deep, deep), pl.ds(0, D)],
-                    target.at[:, core if e == 0 else 1 - core],
-                )
+            for n in range(S):
+                for h in range(2):
+                    at = (2 * h + which) * part
+                    copies.add(
+                        rest_refs[n].at[:, pl.ds(at, part), pl.ds(hw, D // 2)],
+                        target.at[:, w[SEQ + n], :, pl.ds(h * (D // 2), D // 2)],
+                    )
 
         def group_rows(weight, group):
             return weight[pl.ds(group * per_group, per_group)].reshape(hw, D)
 
-        out_scratch = pltpu.VMEM((F, 2, deep, D), bf16)
-        cq_scratch = pltpu.VMEM((2, F, shard, half), bf16)
+        out_scratch = pltpu.VMEM((F, S, part, D), bf16)
+        half_scratch = pltpu.VMEM((F, 2, deep, D), bf16)
+        cq_scratch = pltpu.VMEM((S, F, shard, hw), bf16)
 
         def first_stage(w, ins, outs, scratch):
-            pieces, rest_refs, x_ref, small_ref = ins[:S], ins[S : S + 2], ins[S + 2], ins[S + 3]
+            pieces, rest_refs, x_ref, small_ref = ins[:S], ins[S : 2 * S], ins[2 * S], ins[2 * S + 1]
             normed_ref, inverse_ref, low_ref, keep_ref, send_ref = outs
             weight, cq, sems = scratch
             copies = Copies(sems)
             load_out(copies, w, rest_refs, 0, weight)
-            for e in range(2):
-                copies.add(rest_refs[e].at[:, :, pl.ds(D, half)], cq.at[e])
+            copies.split()
+            for n in range(S):
+                copies.add(rest_refs[n].at[:, :, pl.ds(0, hw)], cq.at[n])
             copies.wait()
             total = alpha_scale * x_ref[...].astype(f32) + small_ref[2:3, :]
             for n in range(S):
@@ -1196,11 +1203,12 @@
             inverse_ref[...] = inverse
             low = value.astype(bf16)
             low_ref[...] = low
-            for e, target in ((1, send_ref), (0, keep_ref)):
-                bias = jnp.concatenate(
-                    [small_ref[3:4, span(w[SEQ + 2 * e + k], hw)] for k in range(2)], axis=1
-                )
-                target[...] = (dot(low, cq[e].reshape(D, half), nn) + bias).astype(bf16)
+            copies.wait()
+            for n in (2, 3, 0, 1):
+                bias = small_ref[3:4, span(w[SEQ + n], hw)]
+                query = (dot(low, cq[n].reshape(D, hw), nn) + bias).astype(bf16)
+                target = keep_ref if n < 2 else send_ref
+                target[:, (n % 2) * hw : (n % 2 + 1) * hw] = query
 
         normed_one, inverse_one, first_low, cq_keep, cq_send = stage(
             first_stage,
@@ -1209,7 +1217,7 @@
             [
                 ((t, D), f32), ((t, 1), f32), ((t, D), bf16), ((t, half), bf16), ((t, half), bf16),
             ],
-            [out_scratch, cq_scratch, pltpu.SemaphoreType.DMA((4,))],
+            [out_scratch, cq_scratch, pltpu.SemaphoreType.DMA((3 * S,))],
         )
         cq_other = core_swap(cq_send)
 
@@ -1277,7 +1285,7 @@
             where,
             [cross_keep, cross_other, normed_one, small] + [hbm(r) for r in rest],
             [((t, D), f32), ((t, 1), f32), ((t, D), bf16)],
-            [out_scratch, pltpu.SemaphoreType.DMA((2,))],
+            [out_scratch, pltpu.SemaphoreType.DMA((2 * S,))],
         )
         second_far = y_swap(second_low)
         second = [second_low, second_far, core_swap(second_low), None]
@@ -1288,17 +1296,20 @@
             pltpu.SemaphoreType.DMA((2,)),
         ]
 
-        def load_ffn(w_ref, scratch):
+        def load_ffn(w_ref, scratch, backward):
             copies = Copies(scratch[2])
-            copies.add(w_ref.at[:, pl.ds(0, shard)], scratch[0])
-            copies.add(w_ref.at[:, pl.ds(shard, fw)], scratch[1])
+            order = (1, 0) if backward else (0, 1)
+            for m in order:
+                at, rows = (0, shard) if m == 0 else (shard, fw)
+                copies.add(w_ref.at[:, pl.ds(at, rows)], scratch[m])
+                copies.split()
             copies.wait()
-            return scratch[0], scratch[1]
+            return scratch[0], scratch[1], copies
 
         def ffn_forward(w, ins, outs, scratch):
             block_refs, small_ref, w_ref = ins[:2], ins[2], ins[3]
             part_refs, hidden_ref, slope_ref = outs[:2], outs[2], outs[3]
-            w_in, w_out = load_ffn(w_ref, scratch)
+            w_in, w_out, copies = load_ffn(w_ref, scratch, False)
             bias = small_ref[pl.ds(13 + w[MINE], 1), :]
             for n in range(2):
                 rows = slice(n * t, (n + 1) * t)
@@ -1307,6 +1318,8 @@
                 low = value.astype(bf16)
                 hidden_ref[rows, :] = low
                 slope_ref[rows, :] = slope.astype(bf16)
+                if n == 0:
+                    copies.wait()
                 out = dot(low, w_out[...].reshape(F * fw, D), nn)
                 part_refs[n][...] = out.astype(part_refs[n].dtype)
 
@@ -1360,12 +1373,14 @@
         def ffn_backward(w, ins, outs, scratch):
             block_refs, slope_ref, w_ref = ins[:2], ins[2], ins[3]
             part_refs, d_pre_ref = outs[:2], outs[2]
-            w_in, w_out = load_ffn(w_ref, scratch)
+            w_in, w_out, copies = load_ffn(w_ref, scratch, True)
             for n in range(2):
                 rows = slice(n * t, (n + 1) * t)
                 d_hidden = dot(block_refs[n][...], w_out[...].reshape(F * fw, D), nt)
                 d_pre = (slope_ref[rows, :].astype(f32) * d_hidden).astype(bf16)
                 d_pre_ref[rows, :] = d_pre
+                if n == 0:
+                    copies.wait()
                 out = dot(d_pre, w_in[...].reshape(D, F * fw), nt)
                 part_refs[n][...] = out.astype(bf16)
 
@@ -1447,7 +1462,7 @@
             [
                 ((t, D), f32), ((t, D), bf16), ((t, half), bf16), ((t, half), bf16), ((8, D), f32),
             ],
-            [out_scratch, pltpu.SemaphoreType.DMA((2,))],
+            [out_scratch, pltpu.SemaphoreType.DMA((2 * S,))],
         )
         dc_other = core_swap(dc_send)
         own_ffn = lax.psum_scatter(
@@ -1535,14 +1550,14 @@
             sent_refs, sums_ref = outs[2 : 2 + S], outs[2 + S]
             weight, cq, sems = scratch
             copies = Copies(sems)
-            for e in range(2):
-                copies.add(rest_refs[e].at[:, :, pl.ds(D, half)], cq.at[e])
+            for n in range(S):
+                copies.add(rest_refs[n].at[:, :, pl.ds(0, hw)], cq.at[n])
+            copies.split()
             load_out(copies, w, rest_refs, 0, weight)
             copies.wait()
             total = alpha_scale * d_two_ref[...]
-            for e, ref in enumerate((keep_ref, other_ref)):
-                total = total + dot(ref[...], cq[e].reshape(D, half), nt)
             for n, piece in enumerate(halves(keep_ref, other_ref)):
+                total = total + dot(piece, cq[n].reshape(D, hw), nt)
                 sums_ref[3:4, span(w[SEQ + n], hw)] = row_sum(piece)
             d, gain, shift = norm_rows_back(
                 total, normed_ref[...], inverse_ref[...], small_ref[7:8, :]
@@ -1553,6 +1568,7 @@
             sums_ref[0:1, :] = row_sum(low)
             sums_ref[1:2, :] = gain
             sums_ref[2:3, :] = shift
+            copies.wait()
             for n in range(S):
                 value = dot(low, group_rows(weight, w[SEQ + n]), nt)
                 sent_refs[n][...] = value.astype(bf16)
@@ -1562,7 +1578,7 @@
             where,
             [dq_keep, dq_other, d_two, normed_one, inverse_one, small] + [hbm(r) for r in rest],
             [((t, D), f32), ((t, D), bf16)] + [((t, hw), bf16)] * S + [((8, D), f32)],
-            [out_scratch, cq_scratch, pltpu.SemaphoreType.DMA((4,))],
+            [out_scratch, cq_scratch, pltpu.SemaphoreType.DMA((3 * S,))],
         )
         d_attn = exchange(d_attn_sent)
 
@@ -1592,7 +1608,7 @@
             [dq_keep, dq_other, first_low, after(d_branch, d_attn_sent[1]), cross_keep, cross_other]
             + [d_cross, *attn],
             [((F, shard, rest_cols), bf16)] * 2,
-            [out_scratch, out_scratch],
+            [half_scratch, half_scratch],
         )
         middle_got = core_swap(middle_send)
 
@@ -1611,7 +1627,7 @@
             terms = z_exchange(sent).reshape(Z, rows, cols)
             return jnp.sum(terms.astype(f32), axis=0).astype(bf16)
 
-        dk_got, dv_got = (y_swap(after(d, d_attn[1])) for d in (dk_far, dv_far))
+        dk_got, dv_got = (y_swap(d) for d in (dk_far, dv_far))
 
         def pack_rest(w, ins, outs, _):
             for n in range(Z):
@@ -1681,10 +1697,10 @@
 
         def last_grads(w, ins, outs, scratch):
             dq, dk, dv, one, two, three, ffn = ins[:7]
-            mem_refs, weight = ins[7:11], ins[11]
-            blocks, mem_blocks = ins[12 : 12 + S], ins[12 + S :]
-            keep_ref, send_ref = outs[S], outs[S + 1]
-            x_all, m_all, d_all, value, small_sums, sems = scratch
+            mem_refs = ins[7:11]
+            blocks, mem_blocks = ins[11 : 11 + S], ins[11 + S :]
+            keep_ref, send_ref, d_all = outs
+            x_all, m_all, value, small_sums, sems = scratch
             copies = Copies(sems)
             for n in range(S):
                 copies.add(blocks[n], x_all.at[span(w[SEQ + n], t)])
@@ -1696,9 +1712,6 @@
                     rows = slice(n * t, (n + 1) * t)
                     total = near[rows, :].astype(f32) + far[rows, :].astype(f32)
                     d_all[rows, m * hw : (m + 1) * hw] = total.astype(bf16)
-            for n in (3, 2, 1, 0):
-                total = dot(d_all[n * t : (n + 1) * t, :], weight[...], nt)
-                outs[n][...] = total.astype(bf16)
             copies.wait()
 
             def store(grad, cols):
@@ -1725,17 +1738,16 @@
             place_small(small_sums, value)
             split_x(w, value, keep_ref, send_ref)
 
-        *mem_parts, last_keep, last_send = stage(
+        last_keep, last_send, d_mem = stage(
             last_grads,
             where,
             [dq_self, dk_self, dv_self, sums_one, sums_two, sums_three, sums_ffn]
-            + [dk_own, dv_own, dk_got, dv_got, w_mem]
+            + [dk_own, dv_own, dk_got, dv_got]
             + [hbm(b) for b in x_blocks + m_blocks],
-            [((t, D), bf16)] * S + [((Z * tall, 5 * hw), bf16)] * 2,
+            [((Z * tall, 5 * hw), bf16)] * 2 + [((T, 2 * hw), bf16)],
             [
                 pltpu.VMEM((T, D), bf16),
                 pltpu.VMEM((T, D), bf16),
-                pltpu.VMEM((T, 2 * hw), bf16),
                 pltpu.VMEM((F * tall, 5 * hw), bf16),
                 pltpu.VMEM((small_rows, D), f32),
                 pltpu.SemaphoreType.DMA((2 * S,)),
@@ -1743,6 +1755,16 @@
         )
         last_got = x_shift(last_send, 1)
         rest_sent = add_pair(rest_keep, after(rest_got, last_keep))
+
+        def memory_parts(w, ins, outs, _):
+            d_ref, weight = ins
+            for n in (3, 2, 1, 0):
+                value = dot(d_ref[n * t : (n + 1) * t, :], weight[...], nt)
+                outs[n][...] = value.astype(bf16)
+
+        mem_parts = stage(
+            memory_parts, where, [after(d_mem, rest_sent), w_mem], [((t, D), bf16)] * S
+        )
 
         def input_parts(w, ins, outs, scratch):
             grads, pieces = ins[:3], ins[3:]
@@ -1831,19 +1853,26 @@
                     target, at = (outs[0], m) if m < 3 else (outs[1], m - 3)
                     lanes = pl.ds(pl.multiple_of(at * D + group, hw), hw)
                     target[:, lanes] = ins[n][0:shard, m * hw : (m + 1) * hw].astype(f32)
-            outs[2][0:16, :] = sum(ins[n][shard:, 0:shard].astype(f32) for n in range(S))
-            outs[2][16:, :] = sum(
-                ins[n][shard : shard + 8, shard : 2 * shard].astype(f32) for n in range(S)
-            )
-
-        grad_self_in, grad_memory, small_own = stage(
+            total = sum(ins[n][shard:, 0:shard].astype(f32) for n in range(S))
+            below = sum(ins[n][shard : shard + 8, shard : 2 * shard].astype(f32) for n in range(S))
+            for n in range(7):
+                outs[2 + n][...] = total[n : n + 1, :].reshape(shard)
+            outs[9][...] = total[7:10, :]
+            outs[10][...] = total[10:13, :]
+            for n in range(S):
+                row = total[13 + n : 14 + n, :] if n < 3 else below[n - 3 : n - 2, :]
+                outs[11][n * fw : (n + 1) * fw] = row.reshape(fw)
+
+        grad_self_in, grad_memory, *rows, grad_gain, grad_shift, grad_fin_bias = stage(
             finish_last,
             where,
             seq_gather(own_last),
-            [((shard, 3 * D), f32), ((shard, 2 * D), f32), ((small_rows, shard), f32)],
-        )
-
-        rows = [small_own[n] for n in range(7)]
+            [((shard, 3 * D), f32), ((shard, 2 * D), f32)]
+            + [((shard,), f32)] * 7
+            + [((3, shard), f32)] * 2
+            + [((S * fw,), f32)],
+        )
+
         return (
             layer_out[None],
             input_grad[None],
@@ -1860,11 +1889,11 @@
             grad_cross_out,
             rows[5],
             grad_fin,
-            small_own[13 : 13 + S].reshape(S * fw),
+            grad_fin_bias,
             grad_fout,
             rows[6],
-            small_own[7:10],
-            small_own[10:13],
+            grad_gain,
+            grad_shift,
         )
 
     return local

time: 498 us -> 492 us (0.988)
  waiting for transfers between devices: 193 us -> 186 us
    all_to_all x4, waiting for transfers between devices: 65.1 us -> 46.6 us  [z_exchange(): lax.all_to_all(array, 'fsdp', 0, 0, axis_index_groups=z_groups, tiled=True)]
    ppermute x16 -> x17, waiting for transfers between devices: 89.8 us -> 100 us  [y_swap(): return lax.ppermute(array, 'seq', y_perm)]
    ppermute x4, waiting for transfers between devices: 10.6 us -> 16.4 us  [x_shift(): return lax.ppermute(array, 'fsdp', perm) if k % X else array]
    ppermute x29 -> x30, waiting for transfers between devices: 21 us -> 18.8 us  [core_swap(): return lax.ppermute(array, 'seq', core_perm)]
    pallas_call x24 -> x25, Pallas kernels: 141 us -> 142 us  [stage(): pl.pallas_call(kernel, grid_spec=pltpu.PrefetchScalarGridSpec(num_scalar_...]
    unnamed x104 -> x114, local copies, waits for them, and re-layouts: 17.3 us -> 17.2 us
    ppermute x16 -> x17, starting transfers between devices: 21.1 us -> 21.3 us  [y_swap(): return lax.ppermute(array, 'seq', y_perm)]
  transfers between devices with their start and end apart: 58 -> 60, of which waited for: 33 -> 37; matrix products, arithmetic and copies ran while one was open for 2% -> 2% of each run, Pallas kernels for 33% -> 34%
where the time goes in v4:
time: 492 us; the launch traced here: 487 us
  Pallas kernels  200 us (41%)
  waiting for transfers between devices  186 us (38%)
  starting transfers between devices  54.1 us (11%)
  local copies, waits for them, and re-layouts  17.8 us (4%)
  between operations  15.2 us (3%)
  other arithmetic  14.3 us (3%)
    pallas_call x25, Pallas kernels, stage(): pl.pallas_call(kernel, grid_spec=pltpu.PrefetchScalarGridSpec(num_scalar_...  142 us
    ppermute x17, waiting for transfers between devices, y_swap(): return lax.ppermute(array, 'seq', y_perm)  100 us
    all_to_all x4, waiting for transfers between devices, z_exchange(): lax.all_to_all(array, 'fsdp', 0, 0, axis_index_groups=z_groups, tiled=True)  46.6 us
    ppermute x17, starting transfers between devices, y_swap(): return lax.ppermute(array, 'seq', y_perm)  21.3 us
    pallas_call x1, Pallas kernels, local(): pl.pallas_call(cross_backward, grid_spec=pltpu.PrefetchScalarGridSpec(num...  19.5 us
    ppermute x30, waiting for transfers between devices, core_swap(): return lax.ppermute(array, 'seq', core_perm)  18.8 us
    all_to_all x4, starting transfers between devices, z_exchange(): lax.all_to_all(array, 'fsdp', 0, 0, axis_index_groups=z_groups, tiled=True)  17.6 us
    unnamed x114, local copies, waits for them, and re-layouts  17.2 us
  transfers between devices with their start and end apart: 60, of which 37 were waited for; matrix products, arithmetic and copies ran while one was open for 2% of the time, Pallas kernels for 34%

profile of v4, /device:TPU:0, one launch (start us, length us, event | category | flops | bytes accessed | tf_op | source)
XLA Modules:
  0.0 487.4 jit_solution(12215197246374004758)
XLA Ops:
  8.6 2.5 shard_map.356
  11.1 3.0 shard_map.357
  14.0 6.3 %all-to-all-start = ((bf16[4,144,768]{2,1,0:T(8,128)(2,1)}), bf16[4,144,768]{2,1,0:T(8,128)(2,1)S(1)}, u32[]{:S(2)}, u32[]{:S(2)}) async-start(bf16[4,144,768]{2,1,0:T(8,128)(2,1)} %shard_map.357), calls=%async_computation | async-start | bytes 1769472 | tf_op jit(solution)/shard_map/all_to_all | solution.py:882
  21.9 2.5 shard_map.358
  24.4 3.2 shard_map.359
  27.6 6.1 %collective-permute-done.refs_1_.refs_12_ = bf16[256,1024]{1,0:T(8,128)(2,1)S(1)} collective-permute-done((bf16[256,1024]{1,0:T(8,128)(2,1)S(1)}, bf16[256,1024]{1,0:T(8,128)(2,1)S(1)}, u32[]{:S(2)}, u32[]{:S(2)}) %collective-permute-start) | collective-permute-done | bytes 524320 | tf_op jit(solution)/shard_map/ppermute | solution.py:877
  33.8 15.1 %all-to-all-done = bf16[4,144,768]{2,1,0:T(8,128)(2,1)S(1)} async-done(((bf16[4,144,768]{2,1,0:T(8,128)(2,1)}), bf16[4,144,768]{2,1,0:T(8,128)(2,1)S(1)}, u32[]{:S(2)}, u32[]{:S(2)}) %all-to-all-start) | async-done | bytes 884768 | tf_op jit(solution)/shard_map/all_to_all | solution.py:882
  50.4 4.1 all-to-all-start.1
  56.7 10.7 %collective-permute-done.3.refs_1_.refs_16_ = bf16[256,1024]{1,0:T(8,128)(2,1)} collective-permute-done((bf16[256,1024]{1,0:T(8,128)(2,1)S(1)}, bf16[256,1024]{1,0:T(8,128)(2,1)}, u32[]{:S(2)}, u32[]{:S(2)}) %collective-permute-start.3) | collective-permute-done | bytes 524320 | tf_op jit(solution)/shard_map/ppermute | solution.py:877
  67.4 5.8 %all-to-all-done.1 = bf16[4,128,512]{2,1,0:T(8,128)(2,1)} async-done(((bf16[4,128,512]{2,1,0:T(8,128)(2,1)}), bf16[4,128,512]{2,1,0:T(8,128)(2,1)}, u32[]{:S(2)}, u32[]{:S(2)}) %all-to-all-start.1) | async-done | bytes 524320 | tf_op jit(solution)/shard_map/all_to_all | solution.py:882
  73.2 4.7 collective-permute-done.4
  78.9 5.7 %shard_map.360 = (bf16[1024,768]{1,0:T(8,128)(2,1)}, f32[24,1024]{1,0:T(8,128)}) custom-call(s32[7]{0:T(128)} %stack.24.w, bf16[256,1024]{1,0:T(8,128)(2,1)} %bitcast.48, bf16[256,1024]{1,0:T(8,128)(2,1)} %copy-done.13, bf16[256,1024]{1,0:T(8,128)(2,1)} %collective-permute-done.1.refs_2_.refs_13_, bf16[256,1024]{1,0:T(8,128)(2,1)} %collective-permute-done.2.refs_3_.refs_14_, ...), custom_call_target="tpu_custom_call" | custom-call | flops 1024 | bytes 1024 | tf_op jit(solution)/shard_map/pallas_call | solution.py:802
  89.4 10.3 %shard_map.361 = (bf16[256,256]{1,0:T(8,128)(2,1)}, bf16[256,256]{1,0:T(8,128)(2,1)}, bf16[256,256]{1,0:T(8,128)(2,1)}, bf16[256,256]{1,0:T(8,128)(2,1)}, f32[2,2,1024]{2,1,0:T(2,128)}) custom-call(s32[7]{0:T(128)} %stack.24.w, bf16[1024,768]{1,0:T(8,128)(2,1)} %get-tuple-element.160.q_ref.k_ref.v_ref, ...), custom_call_target="tpu_custom_call" | custom-call | flops 1024 | bytes 1024 | tf_op jit(solution)/shard_map/pallas_call | solution.py:1122
  99.7 7.0 %collective-permute-done.11 = bf16[512,512]{1,0:T(8,128)(2,1)S(1)} collective-permute-done((bf16[512,512]{1,0:T(8,128)(2,1)}, bf16[512,512]{1,0:T(8,128)(2,1)S(1)}, u32[]{:S(2)}, u32[]{:S(2)}) %collective-permute-start.11) | collective-permute-done | bytes 524320 | tf_op jit(solution)/shard_map/ppermute | solution.py:886
  107.5 5.8 %shard_map.362 = (bf16[1024,512]{1,0:T(8,128)(2,1)}, bf16[4,2,128,512]{3,2,1,0:T(8,128)(2,1)}) custom-call(s32[7]{0:T(128)} %stack.24.w, bf16[256,1024]{1,0:T(8,128)(2,1)} %bitcast.56, bf16[256,1024]{1,0:T(8,128)(2,1)} %collective-permute-done.3.refs_1_.refs_16_, bf16[256,1024]{1,0:T(8,128)(2,1)} %copy-done.14, bf16[256,1024]{1,0:T(8,128)(2,1)} %copy-done.15, ...), custom_call_target="tpu_custom_call" | custom-call | flops 1024 | bytes 1024 | tf_op jit(solution)/shard_map/pallas_call | solution.py:802
  113.4 6.4 %collective-permute-done.10 = bf16[1024,768]{1,0:T(8,128)(2,1)S(1)} collective-permute-done((bf16[1024,768]{1,0:T(8,128)(2,1)}, bf16[1024,768]{1,0:T(8,128)(2,1)S(1)}, u32[]{:S(2)}, u32[]{:S(2)}) %collective-permute-start.10) | collective-permute-done | bytes 1572896 | tf_op jit(solution)/shard_map/ppermute | solution.py:877
  123.5 2.5 collective-permute-done.9.refs_3_.refs_10_
  125.9 3.1 collective-permute-done.7.refs_1_.refs_8_
  132.3 6.2 %shard_map.363 = (f32[256,1024]{1,0:T(8,128)}, f32[256,1]{1,0:T(8,128)}, bf16[256,1024]{1,0:T(8,128)(2,1)}, bf16[256,512]{1,0:T(8,128)(2,1)}, bf16[256,512]{1,0:T(8,128)(2,1)}) custom-call(s32[7]{0:T(128)} %stack.24.w, bf16[256,256]{1,0:T(8,128)(2,1)} %get-tuple-element.161.refs_0_.refs_7_, bf16[256,256]{1,0:T(8,128)(2,1)} %copy-done.29, ...), custom_call_target="tpu_custom_call" | custom-call | flops 1024 | bytes 1024 | tf_op jit(solution)/shard_map/pallas_call | solution.py:802
  138.6 15.7 %collective-permute-done.15.k1.v1 = bf16[1024,512]{1,0:T(8,128)(2,1)S(1)} collective-permute-done((bf16[1024,512]{1,0:T(8,128)(2,1)}, bf16[1024,512]{1,0:T(8,128)(2,1)S(1)}, u32[]{:S(2)}, u32[]{:S(2)}) %collective-permute-start.15) | collective-permute-done | bytes 1048608 | tf_op jit(solution)/shard_map/ppermute | solution.py:877
  155.3 11.6 %shard_map.364 = (bf16[256,512]{1,0:T(8,128)(2,1)}, bf16[256,512]{1,0:T(8,128)(2,1)}, f32[4,2,512]{2,1,0:T(2,128)}) custom-call(s32[7]{0:T(128)} %stack.24.w, bf16[256,512]{1,0:T(8,128)(2,1)} %get-tuple-element.175.qa_ref.qa, bf16[256,512]{1,0:T(8,128)(2,1)} %copy-done.26, bf16[1024,512]{1,0:T(8,128)(2,1)} %get-tuple-element.177.k0.v0, ...), custom_call_target="tpu_custom_call" | custom-call | flops 1024 | bytes 1024 | tf_op jit(solution)/shard_map/pallas_call | solution.py:1246
  167.0 1.7 collective-permute-done.16.refs_1_.refs_5_
  169.4 5.8 %shard_map.365 = (f32[256,1024]{1,0:T(8,128)}, f32[256,1]{1,0:T(8,128)}, bf16[256,1024]{1,0:T(8,128)(2,1)}) custom-call(s32[7]{0:T(128)} %stack.24.w, bf16[256,512]{1,0:T(8,128)(2,1)} %get-tuple-element.178.refs_0_.refs_4_, bf16[256,512]{1,0:T(8,128)(2,1)} %copy-done.24, f32[256,1024]{1,0:T(8,128)} %get-tuple-element.180.refs_2_.refs_3_, ...), custom_call_target="tpu_custom_call" | custom-call | flops 1024 | bytes 1024 | tf_op jit(solution)/shard_map/pallas_call | solution.py:802
  178.2 8.2 %shard_map.366 = (bf16[256,1024]{1,0:T(8,128)(2,1)}, bf16[256,1024]{1,0:T(8,128)(2,1)}, bf16[512,1024]{1,0:T(8,128)(2,1)}, bf16[512,1024]{1,0:T(8,128)(2,1)}) custom-call(s32[7]{0:T(128)} %stack.24.w, bf16[256,1024]{1,0:T(8,128)(2,1)} %get-tuple-element.181.refs_0_, bf16[256,1024]{1,0:T(8,128)(2,1)} %copy-done.16, ...), custom_call_target="tpu_custom_call" | custom-call | flops 1024 | bytes 1024 | tf_op jit(solution)/shard_map/pallas_call | solution.py:802
  186.4 3.5 collective-permute-done.19.refs_0_.refs_1_
  189.9 1.9 collective-permute-done.20.refs_1_.refs_3_
  192.6 8.1 %shard_map.367 = (bf16[256,1024]{1,0:T(8,128)(2,1)}, bf16[256,1024]{1,0:T(8,128)(2,1)}, bf16[512,1024]{1,0:T(8,128)(2,1)}, bf16[512,1024]{1,0:T(8,128)(2,1)}) custom-call(s32[7]{0:T(128)} %stack.24.w, bf16[256,1024]{1,0:T(8,128)(2,1)} %copy-done.17, bf16[256,1024]{1,0:T(8,128)(2,1)} %copy-done.18, ...), custom_call_target="tpu_custom_call" | custom-call | flops 1024 | bytes 1024 | tf_op jit(solution)/shard_map/pallas_call | solution.py:802
  205.8 12.4 %collective-permute-done.22.refs_2_ = bf16[256,1024]{1,0:T(8,128)(2,1)S(1)} collective-permute-done((bf16[256,1024]{1,0:T(8,128)(2,1)S(1)}, bf16[256,1024]{1,0:T(8,128)(2,1)S(1)}, u32[]{:S(2)}, u32[]{:S(2)}) %collective-permute-start.22) | collective-permute-done | bytes 524320 | tf_op jit(solution)/shard_map/ppermute | solution.py:877
  219.0 5.0 %shard_map.368 = (bf16[256,1024]{1,0:T(8,128)(2,1)}, f32[256,1024]{1,0:T(8,128)}, bf16[256,1024]{1,0:T(8,128)(2,1)}, f32[8,1024]{1,0:T(8,128)}) custom-call(s32[7]{0:T(128)} %stack.24.w, bf16[256,1024]{1,0:T(8,128)(2,1)} %get-tuple-element.184.refs_0_, bf16[256,1024]{1,0:T(8,128)(2,1)} %copy-done.35, bf16[256,1024]{1,0:T(8,128)(2,1)} %copy-done.37, ...), custom_call_target="tpu_custom_call" | custom-call | flops 1024 | bytes 1024 | tf_op jit(solution)/shard_map/pallas_call | solution.py:802
  226.9 7.6 %shard_map.369 = (bf16[256,1024]{1,0:T(8,128)(2,1)}, bf16[256,1024]{1,0:T(8,128)(2,1)}, bf16[512,1024]{1,0:T(8,128)(2,1)}) custom-call(s32[7]{0:T(128)} %stack.24.w, bf16[256,1024]{1,0:T(8,128)(2,1)} %get-tuple-element.191.refs_0_.refs_4_, bf16[256,1024]{1,0:T(8,128)(2,1)} %copy-done.9, bf16[512,1024]{1,0:T(8,128)(2,1)} %get-tuple-element.192.refs_2_, ...), custom_call_target="tpu_custom_call" | custom-call | flops 1024 | bytes 1024 | tf_op jit(solution)/shard_map/pallas_call | solution.py:802
  234.4 4.1 collective-permute-done.25.refs_0_.refs_5_
  238.5 1.9 collective-permute-done.26.refs_1_.refs_7_
  241.3 7.9 %shard_map.370 = (bf16[256,1024]{1,0:T(8,128)(2,1)}, bf16[256,1024]{1,0:T(8,128)(2,1)}, bf16[512,1024]{1,0:T(8,128)(2,1)}) custom-call(s32[7]{0:T(128)} %stack.24.w, bf16[256,1024]{1,0:T(8,128)(2,1)} %copy-done.10, bf16[256,1024]{1,0:T(8,128)(2,1)} %copy-done.11, bf16[512,1024]{1,0:T(8,128)(2,1)} %get-tuple-element.196.refs_2_, bf16[8,256,1024]{2,1,0:T(8,128)(2,1)} %bitcast.30), custom_call_target="tpu_custom_call" | custom-call | flops 1024 | bytes 1024 | tf_op jit(solution)/shard_map/pallas_call | solution.py:802
  254.2 10.8 %shard_map.371 = (bf16[8,256,1024]{2,1,0:T(8,128)(2,1)}, f32[8,1024]{1,0:T(8,128)}) custom-call(s32[7]{0:T(128)} %stack.24.w, bf16[256,1024]{1,0:T(8,128)(2,1)} %get-tuple-element.181.refs_0_, bf16[256,1024]{1,0:T(8,128)(2,1)} %copy-done.17, bf16[256,1024]{1,0:T(8,128)(2,1)} %copy-done.16, bf16[256,1024]{1,0:T(8,128)(2,1)} %copy-done.18, ...), custom_call_target="tpu_custom_call" | custom-call | flops 1024 | bytes 42001024 | tf_op jit(solution)/shard_map/pallas_call | solution.py:802
  267.4 5.8 %shard_map.372 = (f32[256,1024]{1,0:T(8,128)}, bf16[256,1024]{1,0:T(8,128)(2,1)}, bf16[256,512]{1,0:T(8,128)(2,1)}, bf16[256,512]{1,0:T(8,128)(2,1)}, f32[8,1024]{1,0:T(8,128)}) custom-call(s32[7]{0:T(128)} %stack.24.w, bf16[256,1024]{1,0:T(8,128)(2,1)} %get-tuple-element.193.refs_0_, bf16[256,1024]{1,0:T(8,128)(2,1)} %copy-done.30, ...), custom_call_target="tpu_custom_call" | custom-call | flops 1024 | bytes 1024 | tf_op jit(solution)/shard_map/pallas_call | solution.py:802
  276.4 19.5 %shard_map.373 = (bf16[256,512]{1,0:T(8,128)(2,1)}, bf16[256,512]{1,0:T(8,128)(2,1)}, bf16[1024,256]{1,0:T(8,128)(2,1)}, bf16[1024,256]{1,0:T(8,128)(2,1)}, bf16...) custom-call(s32[7]{0:T(128)} %stack.24.w, bf16[256,512]{1,0:T(8,128)(2,1)} %get-tuple-element.175.qa_ref.qa, ...), custom_call_target="tpu_custom_call" | custom-call | flops 1024 | bytes 1024 | tf_op jit(solution)/shard_map/pallas_call | solution.py:1524
  298.4 6.8 %shard_map.374 = (f32[256,1024]{1,0:T(8,128)}, bf16[256,1024]{1,0:T(8,128)(2,1)}, bf16[256,256]{1,0:T(8,128)(2,1)}, bf16[256,256]{1,0:T(8,128)(2,1)}, bf16[256,2...) custom-call(s32[7]{0:T(128)} %stack.24.w, bf16[256,512]{1,0:T(8,128)(2,1)} %get-tuple-element.211.refs_0_, ...), custom_call_target="tpu_custom_call" | custom-call | flops 1024 | bytes 1024 | tf_op jit(solution)/shard_map/pallas_call | solution.py:802
  305.3 7.3 %shard_map.375 = (bf16[8,128,1536]{2,1,0:T(8,128)(2,1)}, bf16[8,128,1536]{2,1,0:T(8,128)(2,1)}) custom-call(s32[7]{0:T(128)} %stack.24.w, bf16[256,512]{1,0:T(8,128)(2,1)} %get-tuple-element.211.refs_0_, bf16[256,512]{1,0:T(8,128)(2,1)} %copy-done.25, bf16[256,1024]{1,0:T(8,128)(2,1)} %get-tuple-element.224.refs_2_, ...), custom_call_target="tpu_custom_call" | custom-call | flops 1024 | bytes 1024 | tf_op jit(solution)/shard_map/pallas_call | solution.py:802
  314.9 2.1 collective-permute-done.32.refs_2_
  318.6 3.1 collective-permute-done.31.refs_1_
  321.7 1.6 copy-done.8
  323.4 6.0 %shard_map.376 = (bf16[512,1536]{1,0:T(8,128)(2,1)}, bf16[512,1536]{1,0:T(8,128)(2,1)}) custom-call(s32[7]{0:T(128)} %stack.24.w, bf16[8,128,1536]{2,1,0:T(8,128)(2,1)} %get-tuple-element.229.refs_0_, bf16[8,128,1536]{2,1,0:T(8,128)(2,1)} %copy-done.8), custom_call_target="tpu_custom_call" | custom-call | flops 1024 | bytes 1024 | tf_op jit(solution)/shard_map/pallas_call | solution.py:802
  329.3 2.4 collective-permute-start.41
  333.7 16.2 %shard_map.377 = (bf16[1024,256]{1,0:T(8,128)(2,1)}, bf16[1024,256]{1,0:T(8,128)(2,1)}, bf16[1024,256]{1,0:T(8,128)(2,1)}) custom-call(s32[7]{0:T(128)} %stack.24.w, bf16[1024,768]{1,0:T(8,128)(2,1)} %get-tuple-element.160.q_ref.k_ref.v_ref, bf16[1024,768]{1,0:T(8,128)(2,1)} %get-tuple-element.160.q_ref.k_ref.v_ref, ...), custom_call_target="tpu_custom_call" | custom-call | flops 1024 | bytes 1024 | tf_op jit(solution)/shard_map/pallas_call | solution.py:1672
  350.0 6.4 %collective-permute-done.36.refs_10_ = bf16[1024,256]{1,0:T(8,128)(2,1)S(1)} collective-permute-done((bf16[1024,256]{1,0:T(8,128)(2,1)S(1)}, bf16[1024,256]{1,0:T(8,128)(2,1)S(1)}, u32[]{:S(2)}, u32[]{:S(2)}) %collective-permute-start.36) | collective-permute-done | bytes 524320 | tf_op jit(solution)/shard_map/ppermute | solution.py:877
  357.1 10.2 %shard_map.378 = (bf16[576,1280]{1,0:T(8,128)(2,1)}, bf16[576,1280]{1,0:T(8,128)(2,1)}, bf16[1024,512]{1,0:T(8,128)(2,1)}) custom-call(s32[7]{0:T(128)} %stack.24.w, bf16[1024,256]{1,0:T(8,128)(2,1)} %get-tuple-element.245.refs_0_, bf16[1024,256]{1,0:T(8,128)(2,1)} %get-tuple-element.234.refs_1_, bf16[1024,256]{1,0:T(8,128)(2,1)} %get-tuple-element.235.refs_2_, ...), custom_call_target="tpu_custom_call" | custom-call | flops 1024 | bytes 1024 | tf_op jit(solution)/shard_map/pallas_call | solution.py:802
  367.3 4.6 collective-permute-done.41
  373.4 3.6 all-to-all-start.2
  377.0 4.4 shard_map.380
  381.4 1.8 collective-permute-start.37
  386.7 11.7 %collective-permute-done.45.refs_1_ = bf16[256,1024]{1,0:T(8,128)(2,1)} collective-permute-done((bf16[256,1024]{1,0:T(8,128)(2,1)}, bf16[256,1024]{1,0:T(8,128)(2,1)}, u32[]{:S(2)}, u32[]{:S(2)}) %collective-permute-start.45) | collective-permute-done | bytes 524320 | tf_op jit(solution)/shard_map/ppermute | solution.py:877
  398.4 10.6 %collective-permute-done.44 = bf16[256,1024]{1,0:T(8,128)(2,1)S(1)} collective-permute-done((bf16[256,1024]{1,0:T(8,128)(2,1)S(1)}, bf16[256,1024]{1,0:T(8,128)(2,1)S(1)}, u32[]{:S(2)}, u32[]{:S(2)}) %collective-permute-start.44) | collective-permute-done | bytes 524320 | tf_op jit(solution)/shard_map/ppermute | solution.py:877
  410.1 3.6 all-to-all-done.2
  414.0 4.6 shard_map.381
  418.5 2.8 add_convert_fusion.1
  421.4 3.6 all-to-all-start.3
  424.9 6.0 %shard_map.379 = (bf16[256,1024]{1,0:T(8,128)(2,1)}, bf16[256,1024]{1,0:T(8,128)(2,1)}, bf16[256,1024]{1,0:T(8,128)(2,1)}, bf16[256,1024]{1,0:T(8,128)(2,1)}) custom-call(s32[7]{0:T(128)} %stack.24.w, bf16[1024,256]{1,0:T(8,128)(2,1)} %get-tuple-element.245.refs_0_, bf16[1024,256]{1,0:T(8,128)(2,1)} %get-tuple-element.234.refs_1_, ...), custom_call_target="tpu_custom_call" | custom-call | flops 1024 | bytes 1024 | tf_op jit(solution)/shard_map/pallas_call | solution.py:802
  433.2 2.0 add_convert_fusion.5
  437.2 22.0 %all-to-all-done.3 = bf16[4,144,1280]{2,1,0:T(8,128)(2,1)S(1)} async-done(((bf16[4,144,1280]{2,1,0:T(8,128)(2,1)}), bf16[4,144,1280]{2,1,0:T(8,128)(2,1)S(1)}, u32[]{:S(2)}, u32[]{:S(2)}) %all-to-all-start.3) | async-done | bytes 1474592 | tf_op jit(solution)/shard_map/all_to_all | solution.py:882
  461.0 2.6 shard_map.383.refs_0_
  464.1 5.0 %collective-permute-done.48.refs_1_ = bf16[144,1280]{1,0:T(8,128)(2,1)S(1)} collective-permute-done((bf16[144,1280]{1,0:T(8,128)(2,1)S(1)}, bf16[144,1280]{1,0:T(8,128)(2,1)S(1)}, u32[]{:S(2)}, u32[]{:S(2)}) %collective-permute-start.48) | collective-permute-done | bytes 368672 | tf_op jit(solution)/shard_map/ppermute | solution.py:877
  469.1 2.6 fusion
  472.5 3.0 shard_map.384
  477.0 3.7 shard_map.382
  (213 shorter events, 69.7 us)
Async XLA Ops:
  7.2 77.8 %all-gather.3.cloned.1.call-start = ((), (), s32[]{:S(2)}) async-start(), calls=%async_computation.5 | async-start | bytes 1769472 | tf_op jit(solution)/shard_map/all_gather | solution.py:964
  14.0 34.9 %all-to-all-start = ((bf16[4,144,768]{2,1,0:T(8,128)(2,1)}), bf16[4,144,768]{2,1,0:T(8,128)(2,1)S(1)}, u32[]{:S(2)}, u32[]{:S(2)}) async-start(bf16[4,144,768]{2,1,0:T(8,128)(2,1)} %shard_map.357), calls=%async_computation | async-start | bytes 1769472 | tf_op jit(solution)/shard_map/all_to_all | solution.py:882
  20.4 13.4 %collective-permute-start = (bf16[256,1024]{1,0:T(8,128)(2,1)S(1)}, bf16[256,1024]{1,0:T(8,128)(2,1)S(1)}, u32[]{:S(2)}, u32[]{:S(2)}) collective-permute-start(bf16[256,1024]{1,0:T(8,128)(2,1)S(1)} %bitcast.51), channel_id=1, source_target_pairs={{0,16},{8,24},{16,0},{24,8},{1,17},{9,25},{17,1},{25,9},{2,18},{10... | collective-permute-start | bytes 1572872 | tf_op jit(solution)/shard_map/ppermute | solution.py:877
  24.4 30.2 %copy-start.12 = (bf16[1,256,1024]{2,1,0:T(8,128)(2,1)S(1)}, bf16[1,256,1024]{2,1,0:T(8,128)(2,1)}, u32[]{:S(2)}) copy-start(bf16[1,256,1024]{2,1,0:T(8,128)(2,1)} %param.22) | copy-start | bytes 1572868
  33.8 44.2 %copy-start.13 = (bf16[256,1024]{1,0:T(8,128)(2,1)}, bf16[256,1024]{1,0:T(8,128)(2,1)S(1)}, u32[]{:S(2)}) copy-start(bf16[256,1024]{1,0:T(8,128)(2,1)S(1)} %collective-permute-done.refs_1_.refs_12_) | copy-start | bytes 1572868
  48.9 29.1 %copy-start.5 = (bf16[4,144,768]{2,1,0:T(8,128)(2,1)}, bf16[4,144,768]{2,1,0:T(8,128)(2,1)S(1)}, u32[]{:S(2)}) copy-start(bf16[4,144,768]{2,1,0:T(8,128)(2,1)S(1)} %all-to-all-done) | copy-start | bytes 2654212
  48.9 29.0 %collective-permute-start.4 = (bf16[576,768]{1,0:T(8,128)(2,1)S(1)}, bf16[576,768]{1,0:T(8,128)(2,1)S(1)}, u32[]{:S(2)}, u32[]{:S(2)}) collective-permute-start(bf16[576,768]{1,0:T(8,128)(2,1)S(1)} %bitcast.47), channel_id=1, source_target_pairs={{0,1},{1,0},{2,3},{3,2},{4,5},{5,4},{6,7},{7,6},{8,9},{9,8},{10,11... | collective-permute-start | bytes 2654216 | tf_op jit(solution)/shard_map/ppermute | solution.py:886
  50.4 22.8 %all-to-all-start.1 = ((bf16[4,128,512]{2,1,0:T(8,128)(2,1)}), bf16[4,128,512]{2,1,0:T(8,128)(2,1)}, u32[]{:S(2)}, u32[]{:S(2)}) async-start(bf16[4,128,512]{2,1,0:T(8,128)(2,1)} %shard_map.358), calls=%async_computation.1 | async-start | bytes 1048576 | tf_op jit(solution)/shard_map/all_to_all | solution.py:882
  54.5 122.9 %all-gather.5.cloned.1.call-start = ((), (), s32[]{:S(2)}) async-start(), calls=%async_computation.6 | async-start | bytes 4718592 | tf_op jit(solution)/shard_map/all_gather | solution.py:1139
  54.6 12.8 %collective-permute-start.3 = (bf16[256,1024]{1,0:T(8,128)(2,1)S(1)}, bf16[256,1024]{1,0:T(8,128)(2,1)}, u32[]{:S(2)}, u32[]{:S(2)}) collective-permute-start(bf16[256,1024]{1,0:T(8,128)(2,1)S(1)} %bitcast.58), channel_id=1, source_target_pairs={{0,16},{8,24},{16,0},{24,8},{1,17},{9,25},{17,1},{25,9},{2,18},{10... | collective-permute-start | bytes 1572872 | tf_op jit(solution)/shard_map/ppermute | solution.py:877
  56.2 17.0 %collective-permute-start.1 = (bf16[256,1024]{1,0:T(8,128)(2,1)S(1)}, bf16[256,1024]{1,0:T(8,128)(2,1)}, u32[]{:S(2)}, u32[]{:S(2)}) collective-permute-start(bf16[256,1024]{1,0:T(8,128)(2,1)S(1)} %bitcast.52), channel_id=1, source_target_pairs={{0,8},{8,0},{16,24},{24,16},{1,9},{9,1},{17,25},{25,17},{2,10},{10... | collective-permute-start | bytes 1572872 | tf_op jit(solution)/shard_map/ppermute | solution.py:874
  56.2 17.0 %collective-permute-start.2 = (bf16[256,1024]{1,0:T(8,128)(2,1)S(1)}, bf16[256,1024]{1,0:T(8,128)(2,1)}, u32[]{:S(2)}, u32[]{:S(2)}) collective-permute-start(bf16[256,1024]{1,0:T(8,128)(2,1)S(1)} %collective-permute-done.refs_1_.refs_12_), channel_id=1, source_target_pairs={{0,8},{8,0},{16,24},{24,16},{1,9},{9,1},{17,25},{25,17},{2,10},{10... | collective-permute-start | bytes 1572872 | tf_op jit(solution)/shard_map/ppermute | solution.py:874
  84.6 298.8 %reduce-scatter.2.cloned.1.call-start = ((), (), s32[]{:S(2)}) async-start(), calls=%async_computation.7 | async-start | bytes 4718592 | tf_op jit(solution)/shard_map/reduce_scatter | solution.py:1468
  85.0 34.9 %collective-permute-start.10 = (bf16[1024,768]{1,0:T(8,128)(2,1)}, bf16[1024,768]{1,0:T(8,128)(2,1)S(1)}, u32[]{:S(2)}, u32[]{:S(2)}) collective-permute-start(bf16[1024,768]{1,0:T(8,128)(2,1)} %all-gather.3.cloned.1.call-done), channel_id=1, source_target_pairs={{0,16},{8,24},{16,0},{24,8},{1,17},{9,25},{17,1},{25,9},{2,18},{10... | collective-permute-start | bytes 4718600 | tf_op jit(solution)/shard_map/ppermute | solution.py:877
  86.5 2.6 collective-permute-start.5
  86.5 2.9 collective-permute-start.6
  87.1 19.7 %collective-permute-start.11 = (bf16[512,512]{1,0:T(8,128)(2,1)}, bf16[512,512]{1,0:T(8,128)(2,1)S(1)}, u32[]{:S(2)}, u32[]{:S(2)}) collective-permute-start(bf16[512,512]{1,0:T(8,128)(2,1)} %bitcast.8), channel_id=1, source_target_pairs={{0,1},{1,0},{2,3},{3,2},{4,5},{5,4},{6,7},{7,6},{8,9},{9,8},{10,11... | collective-permute-start | bytes 1572872 | tf_op jit(solution)/shard_map/ppermute | solution.py:886
  113.3 17.2 %collective-permute-start.12 = (bf16[1024,768]{1,0:T(8,128)(2,1)S(1)}, bf16[1024,768]{1,0:T(8,128)(2,1)S(1)}, u32[]{:S(2)}, u32[]{:S(2)}) collective-permute-start(bf16[1024,768]{1,0:T(8,128)(2,1)S(1)} %copy-done), channel_id=1, source_target_pairs={{0,8},{8,0},{16,24},{24,16},{1,9},{9,1},{17,25},{25,17},{2,10},{10... | collective-permute-start | bytes 4718600 | tf_op jit(solution)/shard_map/ppermute | solution.py:874
  119.9 10.7 %collective-permute-start.13 = (bf16[1024,768]{1,0:T(8,128)(2,1)S(1)}, bf16[1024,768]{1,0:T(8,128)(2,1)S(1)}, u32[]{:S(2)}, u32[]{:S(2)}) collective-permute-start(bf16[1024,768]{1,0:T(8,128)(2,1)S(1)} %collective-permute-done.10), channel_id=1, source_target_pairs={{0,8},{8,0},{16,24},{24,16},{1,9},{9,1},{17,25},{25,17},{2,10},{10... | collective-permute-start | bytes 4718600 | tf_op jit(solution)/shard_map/ppermute | solution.py:874
  119.9 3.6 collective-permute-start.8
  120.4 5.5 %collective-permute-start.9 = (bf16[256,256]{1,0:T(8,128)(2,1)S(1)}, bf16[256,256]{1,0:T(8,128)(2,1)S(1)}, u32[]{:S(2)}, u32[]{:S(2)}) collective-permute-start(bf16[256,256]{1,0:T(8,128)(2,1)S(1)} %copy-done.55), channel_id=1, source_target_pairs={{0,24},{8,16},{16,8},{24,0},{1,25},{9,17},{17,9},{25,1},{2,26},{10... | collective-permute-start | bytes 393224 | tf_op jit(solution)/shard_map/ppermute | solution.py:903
  121.6 7.4 %collective-permute-start.7 = (bf16[256,256]{1,0:T(8,128)(2,1)S(1)}, bf16[256,256]{1,0:T(8,128)(2,1)S(1)}, u32[]{:S(2)}, u32[]{:S(2)}) collective-permute-start(bf16[256,256]{1,0:T(8,128)(2,1)S(1)} %copy-done.54), channel_id=1, source_target_pairs={{0,16},{8,24},{16,0},{24,8},{1,17},{9,25},{17,1},{25,9},{2,18},{10... | collective-permute-start | bytes 393224 | tf_op jit(solution)/shard_map/ppermute | solution.py:877
  129.0 25.2 %collective-permute-start.15 = (bf16[1024,512]{1,0:T(8,128)(2,1)}, bf16[1024,512]{1,0:T(8,128)(2,1)S(1)}, u32[]{:S(2)}, u32[]{:S(2)}) collective-permute-start(bf16[1024,512]{1,0:T(8,128)(2,1)} %get-tuple-element.177.k0.v0), channel_id=1, source_target_pairs={{0,16},{8,24},{16,0},{24,8},{1,17},{9,25},{17,1},{25,9},{2,18},{10... | collective-permute-start | bytes 3145736 | tf_op jit(solution)/shard_map/ppermute | solution.py:877
  138.5 15.7 %collective-permute-start.14 = (bf16[256,512]{1,0:T(8,128)(2,1)}, bf16[256,512]{1,0:T(8,128)(2,1)S(1)}, u32[]{:S(2)}, u32[]{:S(2)}) collective-permute-start(bf16[256,512]{1,0:T(8,128)(2,1)} %get-tuple-element.176), channel_id=1, source_target_pairs={{0,8},{8,0},{16,24},{24,16},{1,9},{9,1},{17,25},{25,17},{2,10},{10... | collective-permute-start | bytes 786440 | tf_op jit(solution)/shard_map/ppermute | solution.py:874
  166.9 1.8 collective-permute-start.16
  175.3 2.2 collective-permute-start.17
  175.5 14.4 %collective-permute-start.19 = (bf16[256,1024]{1,0:T(8,128)(2,1)}, bf16[256,1024]{1,0:T(8,128)(2,1)S(1)}, u32[]{:S(2)}, u32[]{:S(2)}) collective-permute-start(bf16[256,1024]{1,0:T(8,128)(2,1)} %get-tuple-element.181.refs_0_), channel_id=1, source_target_pairs={{0,16},{8,24},{16,0},{24,8},{1,17},{9,25},{17,1},{25,9},{2,18},{10... | collective-permute-start | bytes 1572872 | tf_op jit(solution)/shard_map/ppermute | solution.py:877
  189.9 1.9 collective-permute-start.20
  200.7 2.2 collective-permute-start.21
  200.9 4.9 collective-permute-start.18
  204.2 14.0 %collective-permute-start.22 = (bf16[256,1024]{1,0:T(8,128)(2,1)S(1)}, bf16[256,1024]{1,0:T(8,128)(2,1)S(1)}, u32[]{:S(2)}, u32[]{:S(2)}) collective-permute-start(bf16[256,1024]{1,0:T(8,128)(2,1)S(1)} %add_convert_fusion.7), channel_id=1, source_target_pairs={{0,16},{8,24},{16,0},{24,8},{1,17},{9,25},{17,1},{25,9},{2,18},{10... | collective-permute-start | bytes 1572872 | tf_op jit(solution)/shard_map/ppermute | solution.py:877
  224.0 2.1 collective-permute-start.23
  224.0 14.5 %collective-permute-start.25 = (bf16[256,1024]{1,0:T(8,128)(2,1)}, bf16[256,1024]{1,0:T(8,128)(2,1)S(1)}, u32[]{:S(2)}, u32[]{:S(2)}) collective-permute-start(bf16[256,1024]{1,0:T(8,128)(2,1)} %get-tuple-element.191.refs_0_.refs_4_), channel_id=1, source_target_pairs={{0,16},{8,24},{16,0},{24,8},{1,17},{9,25},{17,1},{25,9},{2,18},{10... | collective-permute-start | bytes 1572872 | tf_op jit(solution)/shard_map/ppermute | solution.py:877
  238.5 1.9 collective-permute-start.26
  249.1 2.2 collective-permute-start.27
  249.3 15.7 %collective-permute-start.24 = (bf16[256,1024]{1,0:T(8,128)(2,1)S(1)}, bf16[256,1024]{1,0:T(8,128)(2,1)S(1)}, u32[]{:S(2)}, u32[]{:S(2)}) collective-permute-start(bf16[256,1024]{1,0:T(8,128)(2,1)S(1)} %copy-done.48), channel_id=1, source_target_pairs={{0,8},{8,0},{16,24},{24,16},{1,9},{9,1},{17,25},{25,17},{2,10},{10... | collective-permute-start | bytes 1572872 | tf_op jit(solution)/shard_map/ppermute | solution.py:874
  252.6 14.0 %collective-permute-start.28 = (bf16[256,1024]{1,0:T(8,128)(2,1)S(1)}, bf16[256,1024]{1,0:T(8,128)(2,1)S(1)}, u32[]{:S(2)}, u32[]{:S(2)}) collective-permute-start(bf16[256,1024]{1,0:T(8,128)(2,1)S(1)} %add_convert_fusion.6), channel_id=1, source_target_pairs={{0,16},{8,24},{16,0},{24,8},{1,17},{9,25},{17,1},{25,9},{2,18},{10... | collective-permute-start | bytes 1572872 | tf_op jit(solution)/shard_map/ppermute | solution.py:877
  274.1 1.5 collective-permute-start.29
  295.9 1.8 collective-permute-start.30
  312.6 9.1 %collective-permute-start.34 = (bf16[8,128,1536]{2,1,0:T(8,128)(2,1)}, bf16[8,128,1536]{2,1,0:T(8,128)(2,1)S(1)}, u32[]{:S(2)}, u32[]{:S(2)}) collective-permute-start(bf16[8,128,1536]{2,1,0:T(8,128)(2,1)} %get-tuple-element.230), channel_id=1, source_target_pairs={{0,8},{8,0},{16,24},{24,16},{1,9},{9,1},{17,25},{25,17},{2,10},{10... | collective-permute-start | bytes 9437192 | tf_op jit(solution)/shard_map/ppermute | solution.py:874
  312.8 4.2 collective-permute-start.32
  313.1 5.5 %collective-permute-start.33 = (bf16[256,256]{1,0:T(8,128)(2,1)S(1)}, bf16[256,256]{1,0:T(8,128)(2,1)S(1)}, u32[]{:S(2)}, u32[]{:S(2)}) collective-permute-start(bf16[256,256]{1,0:T(8,128)(2,1)S(1)} %copy-done.52), channel_id=1, source_target_pairs={{0,24},{8,16},{16,8},{24,0},{1,25},{9,17},{17,9},{25,1},{2,26},{10... | collective-permute-start | bytes 393224 | tf_op jit(solution)/shard_map/ppermute | solution.py:903
  314.4 7.2 %collective-permute-start.31 = (bf16[256,256]{1,0:T(8,128)(2,1)S(1)}, bf16[256,256]{1,0:T(8,128)(2,1)S(1)}, u32[]{:S(2)}, u32[]{:S(2)}) collective-permute-start(bf16[256,256]{1,0:T(8,128)(2,1)S(1)} %copy-done.51), channel_id=1, source_target_pairs={{0,16},{8,24},{16,0},{24,8},{1,17},{9,25},{17,1},{25,9},{2,18},{10... | collective-permute-start | bytes 393224 | tf_op jit(solution)/shard_map/ppermute | solution.py:877
  329.3 42.6 %collective-permute-start.41 = (bf16[512,1536]{1,0:T(8,128)(2,1)}, bf16[512,1536]{1,0:T(8,128)(2,1)S(1)}, u32[]{:S(2)}, u32[]{:S(2)}) collective-permute-start(bf16[512,1536]{1,0:T(8,128)(2,1)} %get-tuple-element.251), channel_id=1, source_target_pairs={{0,1},{1,0},{2,3},{3,2},{4,5},{5,4},{6,7},{7,6},{8,9},{9,8},{10,11... | collective-permute-start | bytes 4718600 | tf_op jit(solution)/shard_map/ppermute | solution.py:886
  331.7 18.3 %collective-permute-start.35 = (bf16[1024,256]{1,0:T(8,128)(2,1)S(1)}, bf16[1024,256]{1,0:T(8,128)(2,1)S(1)}, u32[]{:S(2)}, u32[]{:S(2)}) collective-permute-start(bf16[1024,256]{1,0:T(8,128)(2,1)S(1)} %copy-done.47), channel_id=1, source_target_pairs={{0,16},{8,24},{16,0},{24,8},{1,17},{9,25},{17,1},{25,9},{2,18},{10... | collective-permute-start | bytes 1572872 | tf_op jit(solution)/shard_map/ppermute | solution.py:877
  333.1 23.2 %collective-permute-start.36 = (bf16[1024,256]{1,0:T(8,128)(2,1)S(1)}, bf16[1024,256]{1,0:T(8,128)(2,1)S(1)}, u32[]{:S(2)}, u32[]{:S(2)}) collective-permute-start(bf16[1024,256]{1,0:T(8,128)(2,1)S(1)} %copy-done.46), channel_id=1, source_target_pairs={{0,16},{8,24},{16,0},{24,8},{1,17},{9,25},{17,1},{25,9},{2,18},{10... | collective-permute-start | bytes 1572872 | tf_op jit(solution)/shard_map/ppermute | solution.py:877
  373.4 40.2 %all-to-all-start.2 = ((bf16[4,128,1536]{2,1,0:T(8,128)(2,1)}), bf16[4,128,1536]{2,1,0:T(8,128)(2,1)S(1)}, u32[]{:S(2)}, u32[]{:S(2)}) async-start(bf16[4,128,1536]{2,1,0:T(8,128)(2,1)} %bitcast.23), calls=%async_computation.2 | async-start | bytes 3145728 | tf_op jit(solution)/shard_map/all_to_all | solution.py:882
  381.4 3.4 collective-permute-start.43
  381.4 37.1 %collective-permute-start.37 = (bf16[576,1280]{1,0:T(8,128)(2,1)}, bf16[576,1280]{1,0:T(8,128)(2,1)}, u32[]{:S(2)}, u32[]{:S(2)}) collective-permute-start(bf16[576,1280]{1,0:T(8,128)(2,1)} %get-tuple-element.244), channel_id=1, source_target_pairs={{0,1},{1,0},{2,3},{3,2},{4,5},{5,4},{6,7},{7,6},{8,9},{9,8},{10,11... | collective-permute-start | bytes 4423688 | tf_op jit(solution)/shard_map/ppermute | solution.py:886
  383.2 15.2 %collective-permute-start.42 = (bf16[256,1024]{1,0:T(8,128)(2,1)}, bf16[256,1024]{1,0:T(8,128)(2,1)S(1)}, u32[]{:S(2)}, u32[]{:S(2)}) collective-permute-start(bf16[256,1024]{1,0:T(8,128)(2,1)} %get-tuple-element.257), channel_id=1, source_target_pairs={{0,8},{8,0},{16,24},{24,16},{1,9},{9,1},{17,25},{25,17},{2,10},{10... | collective-permute-start | bytes 1572872 | tf_op jit(solution)/shard_map/ppermute | solution.py:874
  383.4 15.1 %collective-permute-start.45 = (bf16[256,1024]{1,0:T(8,128)(2,1)}, bf16[256,1024]{1,0:T(8,128)(2,1)}, u32[]{:S(2)}, u32[]{:S(2)}) collective-permute-start(bf16[256,1024]{1,0:T(8,128)(2,1)} %reduce-scatter.2.cloned.1.call-done.refs_0_), channel_id=1, source_target_pairs={{0,16},{8,24},{16,0},{24,8},{1,17},{9,25},{17,1},{25,9},{2,18},{10... | collective-permute-start | bytes 1572872 | tf_op jit(solution)/shard_map/ppermute | solution.py:877
  386.0 22.9 %collective-permute-start.44 = (bf16[256,1024]{1,0:T(8,128)(2,1)S(1)}, bf16[256,1024]{1,0:T(8,128)(2,1)S(1)}, u32[]{:S(2)}, u32[]{:S(2)}) collective-permute-start(bf16[256,1024]{1,0:T(8,128)(2,1)S(1)} %add_convert_fusion.3), channel_id=1, source_target_pairs={{0,16},{8,24},{16,0},{24,8},{1,17},{9,25},{17,1},{25,9},{2,18},{10... | collective-permute-start | bytes 1572872 | tf_op jit(solution)/shard_map/ppermute | solution.py:877
  386.7 27.3 %collective-permute-start.46 = (bf16[256,1024]{1,0:T(8,128)(2,1)}, bf16[256,1024]{1,0:T(8,128)(2,1)}, u32[]{:S(2)}, u32[]{:S(2)}) collective-permute-start(bf16[256,1024]{1,0:T(8,128)(2,1)} %reduce-scatter.2.cloned.1.call-done.refs_0_), channel_id=1, source_target_pairs={{0,8},{8,0},{16,24},{24,16},{1,9},{9,1},{17,25},{25,17},{2,10},{10... | collective-permute-start | bytes 1572872 | tf_op jit(solution)/shard_map/ppermute | solution.py:874
  398.4 15.5 %collective-permute-start.47 = (bf16[256,1024]{1,0:T(8,128)(2,1)}, bf16[256,1024]{1,0:T(8,128)(2,1)}, u32[]{:S(2)}, u32[]{:S(2)}) collective-permute-start(bf16[256,1024]{1,0:T(8,128)(2,1)} %collective-permute-done.45.refs_1_), channel_id=1, source_target_pairs={{0,8},{8,0},{16,24},{24,16},{1,9},{9,1},{17,25},{25,17},{2,10},{10... | collective-permute-start | bytes 1572872 | tf_op jit(solution)/shard_map/ppermute | solution.py:874
  421.4 37.9 %all-to-all-start.3 = ((bf16[4,144,1280]{2,1,0:T(8,128)(2,1)}), bf16[4,144,1280]{2,1,0:T(8,128)(2,1)S(1)}, u32[]{:S(2)}, u32[]{:S(2)}) async-start(bf16[4,144,1280]{2,1,0:T(8,128)(2,1)} %bitcast.25), calls=%async_computation.4 | async-start | bytes 2949120 | tf_op jit(solution)/shard_map/all_to_all | solution.py:882
  431.0 2.2 collective-permute-start.39
  431.0 38.0 %collective-permute-start.38 = (bf16[256,1024]{1,0:T(8,128)(2,1)}, bf16[256,1024]{1,0:T(8,128)(2,1)}, u32[]{:S(2)}, u32[]{:S(2)}) collective-permute-start(bf16[256,1024]{1,0:T(8,128)(2,1)} %get-tuple-element.247), channel_id=1, source_target_pairs={{0,8},{8,0},{16,24},{24,16},{1,9},{9,1},{17,25},{25,17},{2,10},{10... | collective-permute-start | bytes 1572872 | tf_op jit(solution)/shard_map/ppermute | solution.py:874
  435.2 33.9 %copy-start.23 = (f32[256,1024]{1,0:T(8,128)S(1)}, f32[256,1024]{1,0:T(8,128)}, u32[]{:S(2)}) copy-start(f32[256,1024]{1,0:T(8,128)} %get-tuple-element.215) | copy-start | bytes 3145732
  435.2 33.9 %collective-permute-start.40 = (bf16[256,1024]{1,0:T(8,128)(2,1)}, bf16[256,1024]{1,0:T(8,128)(2,1)}, u32[]{:S(2)}, u32[]{:S(2)}) collective-permute-start(bf16[256,1024]{1,0:T(8,128)(2,1)} %add_convert_fusion.5), channel_id=1, source_target_pairs={{0,16},{8,24},{16,0},{24,8},{1,17},{9,25},{17,1},{25,9},{2,18},{10... | collective-permute-start | bytes 1572872 | tf_op jit(solution)/shard_map/ppermute | solution.py:877
  436.6 24.4 %collective-permute-start.51 = (bf16[128,1536]{1,0:T(8,128)(2,1)S(1)}, bf16[128,1536]{1,0:T(8,128)(2,1)}, u32[]{:S(2)}, u32[]{:S(2)}) collective-permute-start(bf16[128,1536]{1,0:T(8,128)(2,1)S(1)} %reduce_sum.24.refs_0_), channel_id=1, source_target_pairs={{0,16},{8,24},{16,0},{24,8},{1,17},{9,25},{17,1},{25,9},{2,18},{10... | collective-permute-start | bytes 1179656 | tf_op jit(solution)/shard_map/ppermute | solution.py:877
  459.5 9.6 %collective-permute-start.48 = (bf16[144,1280]{1,0:T(8,128)(2,1)S(1)}, bf16[144,1280]{1,0:T(8,128)(2,1)S(1)}, u32[]{:S(2)}, u32[]{:S(2)}) collective-permute-start(bf16[144,1280]{1,0:T(8,128)(2,1)S(1)} %reduce_sum.25.refs_0_), channel_id=1, source_target_pairs={{0,16},{8,24},{16,0},{24,8},{1,17},{9,25},{17,1},{25,9},{2,18},{10... | collective-permute-start | bytes 1105928 | tf_op jit(solution)/shard_map/ppermute | solution.py:877
  463.6 8.2 %collective-permute-start.52 = (bf16[128,1536]{1,0:T(8,128)(2,1)}, bf16[128,1536]{1,0:T(8,128)(2,1)S(1)}, u32[]{:S(2)}, u32[]{:S(2)}) collective-permute-start(bf16[128,1536]{1,0:T(8,128)(2,1)} %shard_map.383.refs_0_), channel_id=1, source_target_pairs={{0,8},{8,0},{16,24},{24,16},{1,9},{9,1},{17,25},{25,17},{2,10},{10... | collective-permute-start | bytes 1179656 | tf_op jit(solution)/shard_map/ppermute | solution.py:874
  463.6 11.9 %collective-permute-start.49 = (bf16[144,1280]{1,0:T(8,128)(2,1)S(1)}, bf16[144,1280]{1,0:T(8,128)(2,1)S(1)}, u32[]{:S(2)}, u32[]{:S(2)}) collective-permute-start(bf16[144,1280]{1,0:T(8,128)(2,1)S(1)} %reduce_sum.25.refs_0_), channel_id=1, source_target_pairs={{0,8},{8,0},{16,24},{24,16},{1,9},{9,1},{17,25},{25,17},{2,10},{10... | collective-permute-start | bytes 1105928 | tf_op jit(solution)/shard_map/ppermute | solution.py:874
  469.1 6.4 %collective-permute-start.50 = (bf16[144,1280]{1,0:T(8,128)(2,1)S(1)}, bf16[144,1280]{1,0:T(8,128)(2,1)S(1)}, u32[]{:S(2)}, u32[]{:S(2)}) collective-permute-start(bf16[144,1280]{1,0:T(8,128)(2,1)S(1)} %collective-permute-done.48.refs_1_), channel_id=1, source_target_pairs={{0,8},{8,0},{16,24},{24,16},{1,9},{9,1},{17,25},{25,17},{2,10},{10... | collective-permute-start | bytes 1105928 | tf_op jit(solution)/shard_map/ppermute | solution.py:874
  (53 other events, 340.4 us)
Sparse Core Ops, SparseCore 0:
  11.2 66.5 all-gather.2
  84.7 74.0 all-gather.4
  273.3 91.9 reduce-scatter.1
